TPU v7x, 128 devices: a whole 4x4x4 slice. The times are simulated.
128 devices in a mesh: section: 2 (over x_lo), dp: 16 (over x_hi, z, core), tensor: 4 (over y).
Axes of the slice: x: 4 (x_hi: 2, x_lo: 2; x = x_hi * 2 + x_lo), y: 4, z: 4, core: 2. Of those that a mesh axis runs over, the one named last changes fastest.
Arguments:
- tokens: bfloat16 [32, 256, 1536], P('dp', 'tensor'), may hold values from -6 to 6
- cotangent: bfloat16 [32, 256, 1536], P('dp', 'tensor'), may hold values from -6 to 6
- route_experts: int32 [2, 32, 256, 6], P('section', 'dp'), may hold values from 0 to 15, as said below
- route_slots: int32 [2, 32, 256, 6], P('section', 'dp'), may hold values from 0 to 127, as said below
- gain_attn: bfloat16 [2, 1536], P('section', ('dp', 'tensor')), may hold values from 0.5 to 1.5
- w_query: bfloat16 [2, 1536, 1536], P('section', 'dp', 'tensor'), may hold values from -0.15625 to 0.15625
- w_key: bfloat16 [2, 1536, 512], P('section', 'dp', 'tensor'), may hold values from -0.15625 to 0.15625
- w_value: bfloat16 [2, 1536, 512], P('section', 'dp', 'tensor'), may hold values from -0.15625 to 0.15625
- w_out: bfloat16 [2, 1536, 1536], P('section', 'tensor', 'dp'), may hold values from -0.625 to 0.625
- gain_ffn: bfloat16 [2, 1536], P('section', ('dp', 'tensor')), may hold values from 0.5 to 1.5
- w_router: bfloat16 [2, 1536, 16], P('section', ('dp', 'tensor')), may hold values from -0.078125 to 0.078125
- w_shared_in: bfloat16 [2, 1536, 2, 1024], P('section', 'dp', None, 'tensor'), may hold values from -0.15625 to 0.15625
- w_shared_down: bfloat16 [2, 1024, 1536], P('section', 'tensor', 'dp'), may hold values from -0.25 to 0.25
- w_expert_in: bfloat16 [2, 1536, 16, 2, 512], P('section', 'dp', None, None, 'tensor'), may hold values from -0.15625 to 0.15625
- w_expert_down: bfloat16 [2, 16, 512, 1536], P('section', None, 'tensor', 'dp'), may hold values from -0.75 to 0.75
Outputs:
- layer_out: bfloat16 [2, 32, 256, 1536], P('section', 'dp', 'tensor')
- layer_in_grad: bfloat16 [2, 32, 256, 1536], P('section', 'dp', 'tensor')
- grad_gain_attn: float32 [2, 1536], P('section', ('dp', 'tensor'))
- grad_query: float32 [2, 1536, 1536], P('section', 'dp', 'tensor')
- grad_key: float32 [2, 1536, 512], P('section', 'dp', 'tensor')
- grad_value: float32 [2, 1536, 512], P('section', 'dp', 'tensor')
- grad_out: float32 [2, 1536, 1536], P('section', 'tensor', 'dp')
- grad_gain_ffn: float32 [2, 1536], P('section', ('dp', 'tensor'))
- grad_router: float32 [2, 1536, 16], P('section', ('dp', 'tensor'))
- grad_shared_in: float32 [2, 1536, 2, 1024], P('section', 'dp', None, 'tensor')
- grad_shared_down: float32 [2, 1024, 1536], P('section', 'tensor', 'dp')
- grad_expert_in: float32 [2, 1536, 16, 2, 512], P('section', 'dp', None, None, 'tensor')
- grad_expert_down: float32 [2, 16, 512, 1536], P('section', None, 'tensor', 'dp')
Inputs may be any that keep to these rules, and one draw needn't show every extreme that they name: `route_experts`: in each layer and sequence a token names 6 different experts; every expert is named by 96 - 96 // 3 to 128 tokens of the sequence, and in every sequence some expert by exactly 128. `route_slots`: in each layer and sequence the slots of an expert's routes are 0 to its number of routes - 1, each once.
All inputs are finite; a program needn't handle non-finite values.
Results may differ from a plain program's by a relative error of at most 0.035.
Values may be sent and summed in bfloat16 or wider, within the bound.
No kernel may reach another device: no remote copies, remote signals or barrier semaphores. Data moves between devices by JAX's collectives and lax.ppermute only.
A program may use at most 320 MiB of HBM per device.

v0:
```python
import jax
import jax.numpy as jnp
from jax import lax
from jax.sharding import PartitionSpec as P

HQ = 12
HK = 4
HD = 128
TOPK = 6
E = 16


NORM_EPSILON = 1e-05
MASK_VALUE = -1e30
BLOCK_LIMIT = 512


def from_behind(block, axis, distance):
    devices = range(lax.axis_size(axis))
    route = [(i - distance, i) for i in devices if i - distance in devices]
    return lax.ppermute(block, axis, route)


def normalize(rows_in, gain_vec):
    factor = lax.rsqrt(jnp.mean(rows_in * rows_in, axis=-1, keepdims=True) + NORM_EPSILON)
    return (rows_in * factor * gain_vec, factor)


def norm_backward(rows_in, factor, gain_vec, upstream):
    unit_rows = rows_in * factor
    scaled = upstream * gain_vec
    rows_grad = factor * (scaled - unit_rows * jnp.mean(scaled * unit_rows, axis=-1, keepdims=True))
    return (rows_grad, jnp.sum(upstream * unit_rows, axis=0))


def swiglu(gate_part, up_part):
    return jax.nn.silu(gate_part) * up_part


def swiglu_backward(gate_part, up_part, upstream):
    sigmoid = jax.nn.sigmoid(gate_part)
    gate_grad = upstream * up_part * sigmoid * (1.0 + gate_part * (1.0 - sigmoid))
    return (gate_grad, upstream * gate_part * sigmoid)


def softmax_last(values):
    shifted = jnp.exp(values - jnp.max(values, axis=-1, keepdims=True))
    return shifted / jnp.sum(shifted, axis=-1, keepdims=True)


def block_scores(query_blk, keys_all, row_start):
    scores = jnp.einsum(
        "qgid,kgd->giqk", query_blk, keys_all, preferred_element_type=jnp.float32
    ) * HD ** (-0.5)
    causal = (
        jnp.arange(keys_all.shape[0])[None, :]
        <= (row_start + jnp.arange(query_blk.shape[0]))[:, None]
    )
    return jnp.where(causal, scores, MASK_VALUE)


def gather_tokens(rows_in):
    return lax.all_gather(rows_in, "tensor", axis=0, tiled=True)


def sum_branch(partial_rows):
    return lax.psum_scatter(
        partial_rows.astype(jnp.bfloat16), "tensor", scatter_dimension=0, tiled=True
    ).astype(jnp.float32)


def pass_section(rows_in, offset):
    return from_behind(rows_in, "section", offset)


def gather_weights(params):
    (
        gain_attn,
        w_query,
        w_key,
        w_value,
        w_out,
        gain_ffn,
        w_router,
        w_shared_in,
        w_shared_down,
        w_expert_in,
        w_expert_down,
    ) = params
    gathered = (
        lax.all_gather(w_query[:, None, None], "dp", axis=3, tiled=True),
        lax.all_gather(w_key[:, None, None], "dp", axis=3, tiled=True),
        lax.all_gather(w_value[:, None, None], "dp", axis=3, tiled=True),
        lax.all_gather(w_shared_in[:, None, None], "dp", axis=3, tiled=True),
        lax.all_gather(w_out[:, None], "dp", axis=3, tiled=True),
        lax.all_gather(w_shared_down[:, None], "dp", axis=3, tiled=True),
    )
    small_parts = (
        lax.all_gather(gain_attn, ("dp", "tensor"), axis=1, tiled=True),
        lax.all_gather(gain_ffn, ("dp", "tensor"), axis=1, tiled=True),
        lax.all_gather(w_router, ("dp", "tensor"), axis=1, tiled=True),
    )
    expert_set = (
        lax.all_gather(w_expert_in[:, None, None], "dp", axis=3, tiled=True),
        lax.all_gather(w_expert_down, "dp", axis=3, tiled=True),
    )
    expert_in = expert_set[0][0, 0, 0]
    expert_down = expert_set[1][0]
    return (
        small_parts[0][0],
        gathered[0][0, 0, 0],
        gathered[1][0, 0, 0],
        gathered[2][0, 0, 0],
        gathered[4][0, 0],
        small_parts[1][0],
        small_parts[2][0],
        gathered[3][0, 0, 0],
        gathered[5][0, 0],
        expert_in,
        expert_down,
    )


def reduce_grads(grad_set):
    (
        grad_gain_attn,
        grad_query,
        grad_key,
        grad_value,
        grad_out,
        grad_gain_ffn,
        grad_router,
        grad_shared_in,
        grad_shared_down,
        grad_expert_in,
        grad_expert_down,
    ) = grad_set
    summed = (
        lax.psum_scatter(
            grad_query[None, None, None].astype(jnp.bfloat16), "dp", scatter_dimension=3, tiled=True
        ).astype(jnp.float32),
        lax.psum_scatter(
            grad_key[None, None, None].astype(jnp.bfloat16), "dp", scatter_dimension=3, tiled=True
        ).astype(jnp.float32),
        lax.psum_scatter(
            grad_value[None, None, None].astype(jnp.bfloat16), "dp", scatter_dimension=3, tiled=True
        ).astype(jnp.float32),
        lax.psum_scatter(
            grad_shared_in[None, None, None].astype(jnp.bfloat16),
            "dp",
            scatter_dimension=3,
            tiled=True,
        ).astype(jnp.float32),
        lax.psum_scatter(
            grad_out[None, None].astype(jnp.bfloat16), "dp", scatter_dimension=3, tiled=True
        ).astype(jnp.float32),
        lax.psum_scatter(
            grad_shared_down[None, None].astype(jnp.bfloat16), "dp", scatter_dimension=3, tiled=True
        ).astype(jnp.float32),
    )
    small_parts = (
        lax.psum_scatter(grad_gain_attn[None], ("dp", "tensor"), scatter_dimension=1, tiled=True),
        lax.psum_scatter(grad_gain_ffn[None], ("dp", "tensor"), scatter_dimension=1, tiled=True),
        lax.psum_scatter(grad_router[None], ("dp", "tensor"), scatter_dimension=1, tiled=True),
    )
    expert_set = (
        lax.psum_scatter(
            grad_expert_in[None, None, None].astype(jnp.bfloat16),
            "dp",
            scatter_dimension=3,
            tiled=True,
        ).astype(jnp.float32),
        lax.psum_scatter(
            grad_expert_down[None].astype(jnp.bfloat16), "dp", scatter_dimension=3, tiled=True
        ).astype(jnp.float32),
    )
    expert_in_sum = expert_set[0][:, 0, 0]
    expert_down_sum = expert_set[1]
    return (
        small_parts[0],
        summed[0][:, 0, 0],
        summed[1][:, 0, 0],
        summed[2][:, 0, 0],
        summed[4][:, 0],
        small_parts[1],
        small_parts[2],
        summed[3][:, 0, 0],
        summed[5][:, 0],
        expert_in_sum,
        expert_down_sum,
    )


def layer_forward(hidden_in, weights, experts, slot_ids):
    (
        gain_attn,
        w_query,
        w_key,
        w_value,
        w_out,
        gain_ffn,
        w_router,
        w_shared_in,
        w_shared_down,
        w_expert_in,
        w_expert_down,
    ) = weights
    normed, factor_attn = normalize(hidden_in, gain_attn)
    normed_rows = gather_tokens(normed.astype(jnp.bfloat16))
    length = normed_rows.shape[0]
    kv_local = w_key.shape[1] // HD
    groups = HQ // HK
    queries = jnp.dot(normed_rows, w_query, preferred_element_type=jnp.float32).astype(jnp.bfloat16)
    queries = queries.reshape(length, kv_local, groups, HD)
    keys_all = jnp.dot(normed_rows, w_key, preferred_element_type=jnp.float32).astype(jnp.bfloat16)
    keys_all = keys_all.reshape(length, kv_local, HD)
    values_all = jnp.dot(normed_rows, w_value, preferred_element_type=jnp.float32).astype(
        jnp.bfloat16
    )
    values_all = values_all.reshape(length, kv_local, HD)
    scores = block_scores(queries, keys_all, 0)
    row_max = jnp.max(scores, axis=-1, keepdims=True)
    shifted = jnp.exp(scores - row_max)
    row_total = jnp.sum(shifted, axis=-1, keepdims=True)
    attn_probs = (shifted / row_total).astype(jnp.bfloat16)
    outputs = jnp.einsum(
        "giqk,kgd->qgid", attn_probs, values_all, preferred_element_type=jnp.float32
    )
    log_totals = [row_max + jnp.log(row_total)]
    attended = outputs.astype(jnp.bfloat16).reshape(length, -1)
    attn_part = jnp.dot(attended, w_out, preferred_element_type=jnp.float32)
    mid_rows = hidden_in + sum_branch(attn_part)
    normed_ffn, factor_ffn = normalize(mid_rows, gain_ffn)
    ffn_rows = gather_tokens(normed_ffn.astype(jnp.bfloat16))
    logits = jnp.dot(ffn_rows, w_router, preferred_element_type=jnp.float32)
    one_hot = (experts[:, :, None] == jnp.arange(E)[None, None, :]).astype(jnp.float32)
    gate_weights = softmax_last(jnp.sum(one_hot * logits[:, None, :], axis=-1))
    average = length * TOPK // E
    capacity = average + average // 3
    flat_slots = (experts * capacity + slot_ids).reshape(-1)
    owners = jnp.arange(length * TOPK, dtype=jnp.int32) // TOPK
    slot_token = jnp.full((E * capacity,), length, jnp.int32).at[flat_slots].set(owners)
    slot_gate = jnp.zeros((E * capacity,), jnp.float32).at[flat_slots].set(gate_weights.reshape(-1))
    padded = jnp.concatenate([ffn_rows, jnp.zeros((1, ffn_rows.shape[1]), jnp.bfloat16)], axis=0)
    dispatched = padded[slot_token].reshape(E, capacity, -1)
    gate_up = jnp.einsum(
        "ecd,dekf->eckf", dispatched, w_expert_in, preferred_element_type=jnp.float32
    )
    expert_hidden = swiglu(gate_up[:, :, 0], gate_up[:, :, 1]).astype(jnp.bfloat16)
    expert_out = jnp.einsum(
        "ecf,efd->ecd", expert_hidden, w_expert_down, preferred_element_type=jnp.float32
    )
    picked = expert_out.reshape(E * capacity, -1)[flat_slots].reshape(length, TOPK, -1)
    routed = jnp.sum(gate_weights[:, :, None] * picked, axis=1)
    shared_in = jnp.einsum("td,dkf->tkf", ffn_rows, w_shared_in, preferred_element_type=jnp.float32)
    shared_hidden = swiglu(shared_in[:, 0], shared_in[:, 1]).astype(jnp.bfloat16)
    shared_out = jnp.dot(shared_hidden, w_shared_down, preferred_element_type=jnp.float32)
    result = mid_rows + sum_branch(routed + shared_out)
    saved_state = (
        hidden_in,
        factor_attn,
        normed_rows,
        queries,
        keys_all,
        values_all,
        tuple(log_totals),
        attended,
        mid_rows,
        factor_ffn,
        ffn_rows,
        one_hot,
        gate_weights,
        flat_slots,
        slot_token,
        slot_gate,
        dispatched,
        gate_up,
        expert_hidden,
        picked,
        shared_in,
        shared_hidden,
    )
    return (result, saved_state)


def layer_backward(out_grad, saved_state, weights, tensor_rank):
    (
        gain_attn,
        w_query,
        w_key,
        w_value,
        w_out,
        gain_ffn,
        w_router,
        w_shared_in,
        w_shared_down,
        w_expert_in,
        w_expert_down,
    ) = weights
    (
        hidden_in,
        factor_attn,
        normed_rows,
        queries,
        keys_all,
        values_all,
        log_totals,
        attended,
        mid_rows,
        factor_ffn,
        ffn_rows,
        one_hot,
        gate_weights,
        flat_slots,
        slot_token,
        slot_gate,
        expert_inputs,
        gate_up,
        expert_hidden,
        picked,
        shared_in,
        shared_hidden,
    ) = saved_state
    length = normed_rows.shape[0]
    rows_dev = hidden_in.shape[0]
    capacity = slot_gate.shape[0] // E
    ffn_grad = gather_tokens(out_grad.astype(jnp.bfloat16))
    shared_hidden_grad = jnp.einsum(
        "td,fd->tf", ffn_grad, w_shared_down, preferred_element_type=jnp.float32
    )
    shared_gate_grad, shared_up_grad = swiglu_backward(
        shared_in[:, 0], shared_in[:, 1], shared_hidden_grad
    )
    shared_in_grad = jnp.stack([shared_gate_grad, shared_up_grad], axis=1).astype(jnp.bfloat16)
    rows_grad = jnp.einsum(
        "tkf,dkf->td", shared_in_grad, w_shared_in, preferred_element_type=jnp.float32
    )
    zero_row = jnp.zeros((1, ffn_grad.shape[1]), jnp.bfloat16)
    padded_grad = jnp.concatenate([ffn_grad, zero_row], axis=0)
    slot_grad = (
        (slot_gate[:, None] * padded_grad[slot_token]).astype(jnp.bfloat16).reshape(E, capacity, -1)
    )
    gate_part = jnp.einsum("td,tjd->tj", ffn_grad, picked, preferred_element_type=jnp.float32)
    gate_grad = lax.psum(gate_part, "tensor")
    chosen_grad = gate_weights * (
        gate_grad - jnp.sum(gate_weights * gate_grad, axis=1, keepdims=True)
    )
    logits_grad = jnp.sum(one_hot * chosen_grad[:, :, None], axis=1).astype(jnp.bfloat16)
    hidden_grad = jnp.einsum(
        "ecd,efd->ecf", slot_grad, w_expert_down, preferred_element_type=jnp.float32
    )
    expert_gate_grad, expert_up_grad = swiglu_backward(
        gate_up[:, :, 0], gate_up[:, :, 1], hidden_grad
    )
    gate_up_grad = jnp.stack([expert_gate_grad, expert_up_grad], axis=2).astype(jnp.bfloat16)
    expert_back = jnp.einsum(
        "eckf,dekf->ecd", gate_up_grad, w_expert_in, preferred_element_type=jnp.float32
    )
    dispatched_grad = expert_back
    dispatched_grad = dispatched_grad.reshape(E * capacity, -1)
    rows_grad = rows_grad + jnp.sum(dispatched_grad[flat_slots].reshape(length, TOPK, -1), axis=1)
    row_first = tensor_rank * rows_dev
    own_logits_grad = lax.dynamic_slice_in_dim(logits_grad, row_first, rows_dev, 0)
    own_rows = lax.dynamic_slice_in_dim(ffn_rows, row_first, rows_dev, 0)
    ffn_in_grad = sum_branch(rows_grad) + jnp.einsum(
        "te,de->td", own_logits_grad, w_router, preferred_element_type=jnp.float32
    )
    mid_norm_grad, grad_gain_ffn = norm_backward(mid_rows, factor_ffn, gain_ffn, ffn_in_grad)
    mid_grad = out_grad + mid_norm_grad
    attn_grad = gather_tokens(mid_grad.astype(jnp.bfloat16))
    attended_grad = jnp.einsum("td,ad->ta", attn_grad, w_out, preferred_element_type=jnp.float32)
    attended_grad = attended_grad.astype(jnp.bfloat16)
    kv_local = keys_all.shape[1]
    groups = queries.shape[2]
    attended_grad = attended_grad.reshape(length, kv_local, groups, HD)
    block_rows = min(length, BLOCK_LIMIT)
    query_parts = []
    key_grad = jnp.zeros((length, kv_local, HD), jnp.float32)
    value_grad = jnp.zeros((length, kv_local, HD), jnp.float32)
    for block_index, row_start in enumerate(range(0, length, block_rows)):
        attn_probs = jnp.exp(block_scores(queries, keys_all, row_start) - log_totals[block_index])
        value_grad = jnp.einsum(
            "giqk,qgid->kgd",
            attn_probs.astype(jnp.bfloat16),
            attended_grad,
            preferred_element_type=jnp.float32,
        )
        prob_grad = jnp.einsum(
            "qgid,kgd->giqk", attended_grad, values_all, preferred_element_type=jnp.float32
        )
        score_grad = attn_probs * (
            prob_grad - jnp.sum(attn_probs * prob_grad, axis=-1, keepdims=True)
        )
        score_grad = (score_grad * HD ** (-0.5)).astype(jnp.bfloat16)
        query_parts.append(
            jnp.einsum("giqk,kgd->qgid", score_grad, keys_all, preferred_element_type=jnp.float32)
        )
        key_grad = jnp.einsum(
            "giqk,qgid->kgd", score_grad, queries, preferred_element_type=jnp.float32
        )
    query_grad = query_parts[0].astype(jnp.bfloat16).reshape(length, -1)
    key_grad = key_grad.astype(jnp.bfloat16).reshape(length, -1)
    value_grad = value_grad.astype(jnp.bfloat16).reshape(length, -1)
    rows_grad = jnp.einsum("ta,da->td", query_grad, w_query, preferred_element_type=jnp.float32)
    rows_grad = rows_grad + jnp.einsum(
        "ta,da->td", key_grad, w_key, preferred_element_type=jnp.float32
    )
    rows_grad = rows_grad + jnp.einsum(
        "ta,da->td", value_grad, w_value, preferred_element_type=jnp.float32
    )
    normed_grad = sum_branch(rows_grad)
    hidden_norm_grad, grad_gain_attn = norm_backward(hidden_in, factor_attn, gain_attn, normed_grad)
    in_grad = mid_grad + hidden_norm_grad
    pieces = (
        grad_gain_attn,
        grad_gain_ffn,
        normed_rows,
        query_grad,
        key_grad,
        value_grad,
        attended,
        attn_grad,
        own_rows,
        own_logits_grad,
        ffn_rows,
        shared_in_grad,
        shared_hidden,
        ffn_grad,
        expert_inputs,
        gate_up_grad,
        expert_hidden,
        slot_grad,
    )
    return (in_grad, pieces)


def weight_grads(pieces):
    (
        grad_gain_attn,
        grad_gain_ffn,
        normed_rows,
        query_grad,
        key_grad,
        value_grad,
        attended,
        attn_grad,
        own_rows,
        own_logits_grad,
        ffn_rows,
        shared_in_grad,
        shared_hidden,
        ffn_grad,
        expert_inputs,
        gate_up_grad,
        expert_hidden,
        expert_grad_in,
    ) = pieces
    grad_query = jnp.einsum(
        "td,ta->da", normed_rows, query_grad, preferred_element_type=jnp.float32
    )
    grad_key = jnp.einsum("td,ta->da", normed_rows, key_grad, preferred_element_type=jnp.float32)
    grad_value = jnp.einsum(
        "td,ta->da", normed_rows, value_grad, preferred_element_type=jnp.float32
    )
    grad_out = jnp.einsum("ta,td->ad", attended, attn_grad, preferred_element_type=jnp.float32)
    grad_router = jnp.einsum(
        "td,te->de", own_rows, own_logits_grad, preferred_element_type=jnp.float32
    )
    grad_shared_in = jnp.einsum(
        "td,tkf->dkf", ffn_rows, shared_in_grad, preferred_element_type=jnp.float32
    )
    grad_shared_down = jnp.einsum(
        "tf,td->fd", shared_hidden, ffn_grad, preferred_element_type=jnp.float32
    )
    grad_expert_in = jnp.einsum(
        "ecd,eckf->dekf", expert_inputs, gate_up_grad, preferred_element_type=jnp.float32
    )
    grad_expert_down = jnp.einsum(
        "ecf,ecd->efd", expert_hidden, expert_grad_in, preferred_element_type=jnp.float32
    )
    return (
        grad_gain_attn,
        grad_query,
        grad_key,
        grad_value,
        grad_out,
        grad_gain_ffn,
        grad_router,
        grad_shared_in,
        grad_shared_down,
        grad_expert_in,
        grad_expert_down,
    )


def add_grads(running, addition):
    return addition if running is None else jax.tree.map(jnp.add, running, addition)


def per_device(
    tokens,
    cotangent,
    route_experts,
    route_slots,
    gain_attn,
    w_query,
    w_key,
    w_value,
    w_out,
    gain_ffn,
    w_router,
    w_shared_in,
    w_shared_down,
    w_expert_in,
    w_expert_down,
):
    params = (
        gain_attn,
        w_query,
        w_key,
        w_value,
        w_out,
        gain_ffn,
        w_router,
        w_shared_in,
        w_shared_down,
        w_expert_in,
        w_expert_down,
    )
    first_section = lax.axis_index("section") == 0
    tensor_rank = lax.axis_index("tensor")
    micro_count = tokens.shape[0]
    weights = gather_weights(params)
    received = jnp.zeros(tokens.shape[1:], jnp.bfloat16)
    layer_values = []
    kept_states = []
    for tick_index in range(micro_count + 1):
        early_batch = min(tick_index, micro_count - 1)
        late_batch = max(tick_index - 1, 0)
        inputs = jnp.where(first_section, tokens[early_batch], received).astype(jnp.float32)
        experts = jnp.where(
            first_section, route_experts[0, early_batch], route_experts[0, late_batch]
        )
        slot_ids = jnp.where(first_section, route_slots[0, early_batch], route_slots[0, late_batch])
        result, saved_state = layer_forward(inputs, weights, experts, slot_ids)
        sent_rows = result.astype(jnp.bfloat16)
        layer_values.append(sent_rows)
        kept_states.append(saved_state)
        if tick_index < micro_count:
            received = pass_section(sent_rows, 1)
    params_again = lax.optimization_barrier((params, layer_values[-1]))[0]
    weights = gather_weights(params_again)
    grad_received = jnp.zeros(tokens.shape[1:], jnp.bfloat16)
    in_grads = []
    grad_total = None
    for step_index in range(micro_count + 1):
        if step_index < micro_count:
            out_grad = jnp.where(
                first_section, grad_received, cotangent[micro_count - 1 - step_index]
            )
        else:
            out_grad = jnp.where(first_section, grad_received, jnp.zeros_like(grad_received))
        in_grad, pieces = layer_backward(
            out_grad.astype(jnp.float32),
            kept_states[micro_count - step_index],
            weights,
            tensor_rank,
        )
        sent_grad = in_grad.astype(jnp.bfloat16)
        in_grads.append(sent_grad)
        if step_index < micro_count:
            grad_received = pass_section(sent_grad, -1)
        grad_total = add_grads(grad_total, weight_grads(pieces))
    grad_total = reduce_grads(grad_total)
    values_out = jnp.stack(
        [
            jnp.where(first_section, layer_values[batch_index], layer_values[batch_index + 1])
            for batch_index in range(micro_count)
        ]
    )[None]
    grads_in = jnp.stack(
        [
            jnp.where(
                first_section,
                in_grads[micro_count - batch_index],
                in_grads[micro_count - 1 - batch_index],
            )
            for batch_index in range(micro_count)
        ]
    )[None]
    return (values_out, grads_in) + tuple(grad_total)


def solution(mesh):
    placed = (
        P("dp", "tensor", None),
        P("dp", "tensor", None),
        P("section", "dp", None, None),
        P("section", "dp", None, None),
        P("section", ("dp", "tensor")),
        P("section", "dp", "tensor"),
        P("section", "dp", "tensor"),
        P("section", "dp", "tensor"),
        P("section", "tensor", "dp"),
        P("section", ("dp", "tensor")),
        P("section", ("dp", "tensor"), None),
        P("section", "dp", None, "tensor"),
        P("section", "tensor", "dp"),
        P("section", "dp", None, None, "tensor"),
        P("section", None, "tensor", "dp"),
    )
    return jax.shard_map(
        per_device,
        mesh=mesh,
        in_specs=placed,
        out_specs=(
            P("section", "dp", "tensor", None),
            P("section", "dp", "tensor", None),
            P("section", ("dp", "tensor")),
            P("section", "dp", "tensor"),
            P("section", "dp", "tensor"),
            P("section", "dp", "tensor"),
            P("section", "tensor", "dp"),
            P("section", ("dp", "tensor")),
            P("section", ("dp", "tensor"), None),
            P("section", "dp", None, "tensor"),
            P("section", "tensor", "dp"),
            P("section", "dp", None, None, "tensor"),
            P("section", None, "tensor", "dp"),
        ),
        check_vma=False,
    )
```

profile of v0, /device:TPU:8, one launch (start us, length us, event | category | flops | bytes accessed | tf_op | source)
XLA Modules:
  0.0 3113.9 jit_solution(12142284133512622885)
XLA Ops:
  9.9 26.8 all-gather
  40.4 165.4 %all-reduce.15 = (bf16[1536]{0:T(1024)(128)(2,1)S(1)}, bf16[1536]{0:T(1024)(128)(2,1)S(1)}) all-reduce(bf16[1536]{0:T(1024)(128)(2,1)S(1)} %dynamic-update-slice, bf16[1536]{0:T(1024)(128)(2,1)S(1)} %dynamic-update-slice.1), channel_id=1, replica_groups=mesh['section'=2,'dp'=16,'tensor'=4] {'dp','tensor'}, use_global_device_ids=true, to_apply=%add.6 | all-reduce | flops 3072 | bytes 12288
  206.9 12.1 all_gather.103
  219.3 20.5 all-gather.1
  251.9 168.9 %all_gather.110 = bf16[1,1536,16]{2,0,1:T(2,128)(2,1)S(1)} all-gather(bf16[1,24,16]{2,0,1:T(2,128)(2,1)S(1)} %copy.306), channel_id=1, replica_groups=mesh['section'=2,'dp'=16,'tensor'=4] {'dp','tensor'}, dimensions={1}, use_global_device_ids=true | all-gather | bytes 49920 | tf_op jit(solution)/shard_map/all_gather | solution.py:101
  428.6 26.5 all-gather.6
  457.5 12.9 all_gather.109
  472.2 10.7 gather_fusion
  509.4 14.9 gather_fusion.1
  524.3 11.9 reshape.777
  536.3 10.6 multiply_reduce_fusion.2
  549.8 18.4 reduce-scatter.30.cloned.1.call-done
  577.1 14.3 all_gather.115
  604.3 15.1 reduce-scatter.32.cloned.1.call-done
  622.1 13.8 all_gather.116
  665.1 14.9 gather_fusion.3
  680.0 11.4 reshape.783
  692.3 10.8 multiply_reduce_fusion.1
  707.5 22.3 reduce-scatter.34.cloned.1.call-done
  740.5 14.3 all_gather.117
  767.7 16.4 all-gather.7
  787.7 14.1 all_gather.118
  831.1 14.9 gather_fusion.5
  846.0 11.4 reshape.789
  865.6 11.0 psum.21
  876.9 10.7 multiply_reduce_fusion
  893.3 19.9 reduce-scatter.38.cloned.1.call-done
  934.6 28.5 all-gather.8
  964.4 18.3 all-gather.28.cloned.1.call-done
  999.8 74.7 %all-gather.40.cloned.1.call-done = bf16[1,1536,16,2,128]{4,1,2,3,0:T(8,128)(2,1)} async-done(((bf16[1,96,16,2,128]{4,1,2,3,0:T(8,128)(2,1)}), bf16[1,1536,16,2,128]{4,1,2,3,0:T(8,128)(2,1)}) %all-gather.40.cloned.1.call-update) | async-done | bytes 12582928 | tf_op jit(solution)/shard_map/all_gather | solution.py:104
  1074.5 13.3 fusion.7
  1087.9 14.9 gather_fusion.7
  1102.8 11.4 reshape.791
  1128.6 166.3 %all-reduce.14 = (bf16[1536]{0:T(1024)(128)(2,1)S(1)}, bf16[1536]{0:T(1024)(128)(2,1)}) all-reduce(bf16[1536]{0:T(1024)(128)(2,1)S(1)} %dynamic-update-slice.2, bf16[1536]{0:T(1024)(128)(2,1)S(1)} %dynamic-update-slice.3), channel_id=1, replica_groups=mesh['section'=2,'dp'=16,'tensor'=4] {'dp','tensor'}, use_global_device_ids=true, to_apply=%add.8 | all-reduce | flops 3072 | bytes 12288
  1295.0 167.4 %all_gather.124 = bf16[1,1536,16]{2,0,1:T(2,128)(2,1)S(1)} all-gather(bf16[1,24,16]{2,0,1:T(2,128)(2,1)S(1)} %copy.339), channel_id=1, replica_groups=mesh['section'=2,'dp'=16,'tensor'=4] {'dp','tensor'}, dimensions={1}, use_global_device_ids=true | all-gather | bytes 49920 | tf_op jit(solution)/shard_map/all_gather | solution.py:101
  1462.8 20.1 all-gather.13
  1482.9 21.9 all-gather.14
  1507.9 14.1 all_gather.126
  1530.0 16.9 all-gather.44.cloned.1.call-done
  1552.3 18.4 reduce-scatter.42.cloned.1.call-done
  1582.6 13.8 all_gather.132
  1616.3 13.7 fusion.5
  1630.0 14.9 gather_fusion.9
  1644.9 11.4 reshape.799
  1686.2 10.8 psum.22
  1700.4 13.1 all_gather.133
  1759.3 14.5 all_gather.134
  1775.8 10.7 gather_fusion.10
  1793.7 13.7 fusion.3
  1807.4 14.9 gather_fusion.11
  1822.3 11.4 reshape.807
  1885.7 12.7 all_gather.135
  1964.1 15.4 fusion.34
  1989.8 13.1 fusion.143
  2013.1 23.3 fusion.13
  2036.5 16.9 copy.364
  2055.2 382.2 %all-reduce.18.cloned.1.call-done = f32[1,1536,16]{1,2,0:T(8,128)} async-done(((f32[1,1536,16]{1,2,0:T(8,128)}), f32[1,1536,16]{1,2,0:T(8,128)}) %all-reduce.18.cloned.1.call-update) | async-done | bytes 98320
  2438.8 69.6 %reduce-scatter.66.cloned.1.call-done = bf16[96,256]{1,0:T(8,128)(2,1)} async-done(((bf16[1536,256]{1,0:T(8,128)(2,1)}), bf16[96,256]{1,0:T(8,128)(2,1)}) %reduce-scatter.66.cloned.1.call-update) | async-done | bytes 49168
  2510.2 66.3 %reduce-scatter.54.cloned.1.call-done = bf16[1,1,1,96,128]{4,3,2,1,0:T(8,128)(2,1)} async-done(((bf16[1,1,1,1536,128]{4,3,2,1,0:T(8,128)(2,1)}), bf16[1,1,1,96,128]{4,3,2,1,0:T(8,128)(2,1)}) %reduce-scatter.54.cloned.1.call-update) | async-done | bytes 24592 | tf_op jit(solution)/shard_map/reduce_scatter | solution.py:142
  2577.9 67.4 %reduce-scatter.56.cloned.1.call-done = bf16[1,1,1,96,128]{4,3,2,1,0:T(8,128)(2,1)} async-done(((bf16[1,1,1,1536,128]{4,3,2,1,0:T(8,128)(2,1)}), bf16[1,1,1,96,128]{4,3,2,1,0:T(8,128)(2,1)}) %reduce-scatter.56.cloned.1.call-update) | async-done | bytes 24592 | tf_op jit(solution)/shard_map/reduce_scatter | solution.py:145
  2646.6 71.1 %reduce-scatter.58.cloned.1.call-done = bf16[1,1,1,96,2,256]{5,3,4,2,1,0:T(8,128)(2,1)} async-done(((bf16[1,1,1,1536,2,256]{5,3,4,2,1,0:T(8,128)(2,1)}), bf16[1,1,1,96,2,256]{5,3,4,2,1,0:T(8,128)(2,1)}) %reduce-scatter.58.cloned.1.call-update) | async-done | bytes 98320 | tf_op jit(solution)/shard_map/reduce_scatter | solution.py:148
  2719.5 20.4 reduce-scatter.50.cloned.1.call-done
  2741.1 324.2 %all-reduce.13 = (f32[1,1536]{1,0:T(1,128)S(1)}, f32[1,1536]{1,0:T(1,128)S(1)}) all-reduce(f32[1,1536]{1,0:T(1,128)S(1)} %add.542, f32[1,1536]{1,0:T(1,128)S(1)} %add.553), channel_id=29, replica_groups=mesh['section'=2,'dp'=16,'tensor'=4] {'dp','tensor'}, use_global_device_ids=true, to_apply=%region_66.67.clone | all-reduce | flops 3072 | bytes 24576
  3074.0 29.5 reduce-scatter.60.cloned.1.call-done
  (836 shorter events, 538.0 us)
Async XLA Ops:
  7.2 233.0 %all-gather.30.cloned.1.call-start = ((), (), s32[]{:S(2)}) async-start(), calls=%async_computation.40 | async-start | bytes 1253376 | tf_op jit(solution)/shard_map/all_gather | solution.py:91
  7.9 235.9 %all-gather.32.cloned.1.call-start = ((), (), s32[]{:S(2)}) async-start(), calls=%async_computation.41 | async-start | bytes 1253376 | tf_op jit(solution)/shard_map/all_gather | solution.py:95
  8.7 446.5 %reduce-scatter.28.cloned.1.call-start = ((), (), s32[]{:S(2)}) async-start(), calls=%async_computation.20 | async-start | bytes 983040 | tf_op jit(solution)/shard_map/reduce_scatter | solution.py:67
  8.8 237.9 %copy-start.102 = (pred[256,256]{0,1:T(8,128)(4,1)}, pred[256,256]{0,1:T(8,128)(4,1)S(1)}, u32[]{:S(2)}) copy-start(pred[256,256]{0,1:T(8,128)(4,1)S(1)} %iota_compare_fusion) | copy-start | bytes 196612
  9.9 232.7 %copy-start.223 = (f32[64]{0:T(128)}, f32[64]{0:T(128)S(1)}, u32[]{:S(2)}) copy-start(f32[64]{0:T(128)S(1)} %add_rsqrt_fusion.5) | copy-start | bytes 772
  36.7 554.7 %copy-start.44 = (bf16[1,1536,128]{2,1,0:T(8,128)(2,1)}, bf16[1,1536,128]{2,1,0:T(8,128)(2,1)S(1)}, u32[]{:S(2)}) copy-start(bf16[1,1536,128]{2,1,0:T(8,128)(2,1)S(1)} %all-gather) | copy-start | bytes 1179652
  243.5 211.6 %copy-start.30 = (bf16[2,64,1536]{2,1,0:T(8,128)(2,1)S(1)}, bf16[2,64,1536]{2,1,0:T(8,128)(2,1)}, u32[]{:S(2)}) copy-start(bf16[2,64,1536]{2,1,0:T(8,128)(2,1)} %param.15) | copy-start | bytes 1179652
  243.8 226.7 %copy-start.105 = (bf16[128,3,256]{2,0,1:T(8,128)(2,1)}, bf16[128,3,256]{2,0,1:T(8,128)(2,1)S(1)}, u32[]{:S(2)}) copy-start(bf16[128,3,256]{2,0,1:T(8,128)(2,1)S(1)} %convolution_convert_fusion.8) | copy-start | bytes 589828
  246.7 236.2 %all-gather.36.cloned.1.call-start = ((), (), s32[]{:S(2)}) async-start(), calls=%async_computation.43 | async-start | bytes 1671168 | tf_op jit(solution)/shard_map/all_gather | solution.py:94
  247.4 237.4 %all-gather.26.cloned.1.call-start = ((), (), s32[]{:S(2)}) async-start(), calls=%async_computation.21 | async-start | bytes 6684672 | tf_op jit(solution)/shard_map/all_gather | solution.py:105
  249.4 244.6 %all-gather.34.cloned.1.call-start = ((), (), s32[]{:S(2)}) async-start(), calls=%async_computation.42 | async-start | bytes 13369344 | tf_op jit(solution)/shard_map/all_gather | solution.py:104
  250.7 317.4 %reduce-scatter.30.cloned.1.call-start = ((), (), s32[]{:S(2)}) async-start(), calls=%async_computation.22 | async-start | bytes 983040 | tf_op jit(solution)/shard_map/reduce_scatter | solution.py:67
  250.8 219.6 %copy-start.171 = (s32[1,1,256,6]{2,1,3,0:T(1,128)}, s32[1,1,256,6]{2,1,3,0:T(1,128)S(1)}, u32[]{:S(2)}) copy-start(s32[1,1,256,6]{2,1,3,0:T(1,128)S(1)} %get-tuple-element.145) | copy-start | bytes 18436
  250.8 219.6 %copy-start.173 = (s32[1,1,256,6]{2,1,3,0:T(1,128)}, s32[1,1,256,6]{2,1,3,0:T(1,128)S(1)}, u32[]{:S(2)}) copy-start(s32[1,1,256,6]{2,1,3,0:T(1,128)S(1)} %get-tuple-element.146) | copy-start | bytes 18436
  251.5 219.5 %copy-start.163 = (s32[256,6]{0,1:T(8,128)}, s32[256,6]{0,1:T(8,128)S(1)}, u32[]{:S(2)}) copy-start(s32[256,6]{0,1:T(8,128)S(1)} %get-tuple-element.149) | copy-start | bytes 18436
  549.7 69.6 %reduce-scatter.32.cloned.1.call-start = ((), (), s32[]{:S(2)}) async-start(), calls=%async_computation.23 | async-start | bytes 983040 | tf_op jit(solution)/shard_map/reduce_scatter | solution.py:67
  569.2 6.8 collective-permute-start
  597.4 132.4 %reduce-scatter.34.cloned.1.call-start = ((), (), s32[]{:S(2)}) async-start(), calls=%async_computation.24 | async-start | bytes 983040 | tf_op jit(solution)/shard_map/reduce_scatter | solution.py:67
  707.3 77.7 %reduce-scatter.36.cloned.1.call-start = ((), (), s32[]{:S(2)}) async-start(), calls=%async_computation.25 | async-start | bytes 983040 | tf_op jit(solution)/shard_map/reduce_scatter | solution.py:67
  731.7 6.9 collective-permute-start.1
  760.8 152.4 %reduce-scatter.38.cloned.1.call-start = ((), (), s32[]{:S(2)}) async-start(), calls=%async_computation.26 | async-start | bytes 983040 | tf_op jit(solution)/shard_map/reduce_scatter | solution.py:67
  893.2 89.5 %all-gather.28.cloned.1.call-start = ((), (), s32[]{:S(2)}) async-start(), calls=%async_computation.27 | async-start | bytes 6684672 | tf_op jit(solution)/shard_map/all_gather | solution.py:105
  915.8 158.7 %all-gather.40.cloned.1.call-start = ((), (), s32[]{:S(2)}) async-start(), calls=%async_computation.45 | async-start | bytes 13369344 | tf_op jit(solution)/shard_map/all_gather | solution.py:104
  917.1 206.8 %all-gather.38.cloned.1.call-start = ((), (), s32[]{:S(2)}) async-start(), calls=%async_computation.44 | async-start | bytes 1671168 | tf_op jit(solution)/shard_map/all_gather | solution.py:94
  934.6 570.3 %reduce-scatter.40.cloned.1.call-start = ((), (), s32[]{:S(2)}) async-start(), calls=%async_computation.28 | async-start | bytes 983040 | tf_op jit(solution)/shard_map/reduce_scatter | solution.py:67
  1114.2 180.7 %copy-start.211 = (bf16[1,24,16]{1,2,0:T(8,128)(2,1)S(1)}, bf16[1,24,16]{1,2,0:T(8,128)(2,1)}, u32[]{:S(2)}) copy-start(bf16[1,24,16]{1,2,0:T(8,128)(2,1)} %param.25) | copy-start | bytes 2308
  1123.8 338.9 %copy-start.153 = (bf16[1,96,128]{2,1,0:T(8,128)(2,1)S(1)}, bf16[1,96,128]{2,1,0:T(8,128)(2,1)}, u32[]{:S(2)}) copy-start(bf16[1,96,128]{2,1,0:T(8,128)(2,1)} %param.21) | copy-start | bytes 73732
  1123.8 359.0 %copy-start.154 = (bf16[1,96,128]{2,1,0:T(8,128)(2,1)S(1)}, bf16[1,96,128]{2,1,0:T(8,128)(2,1)}, u32[]{:S(2)}) copy-start(bf16[1,96,128]{2,1,0:T(8,128)(2,1)} %param.22) | copy-start | bytes 73732
  1123.8 381.0 %copy-start.215 = (f32[64]{0:T(128)S(1)}, f32[64]{0:T(128)}, u32[]{:S(2)}) copy-start(f32[64]{0:T(128)} %copy-done.214) | copy-start | bytes 772
  1123.9 402.0 %copy-start.19 = (f32[1,3,256,256]{2,3,1,0:T(8,128)S(1)}, f32[1,3,256,256]{2,3,1,0:T(8,128)}, u32[]{:S(2)}) copy-start(f32[1,3,256,256]{2,3,1,0:T(8,128)} %copy-done.18) | copy-start | bytes 2359300
  1123.9 402.0 %copy-start.150 = (bf16[256,128,1]{1,0,2:T(8,128)(2,1)S(1)}, bf16[256,128,1]{1,0,2:T(8,128)(2,1)}, u32[]{:S(2)}) copy-start(bf16[256,128,1]{1,0,2:T(8,128)(2,1)} %copy-done.149) | copy-start | bytes 196612
  1127.4 398.9 %copy-start.123 = (bf16[256,128,1]{1,0,2:T(8,128)(2,1)S(1)}, bf16[256,128,1]{1,0,2:T(8,128)(2,1)}, u32[]{:S(2)}) copy-start(bf16[256,128,1]{1,0,2:T(8,128)(2,1)} %copy-done.122) | copy-start | bytes 196612
  1127.4 394.6 %all-gather.42.cloned.1.call-start = ((), (), s32[]{:S(2)}) async-start(), calls=%async_computation.46 | async-start | bytes 1253376 | tf_op jit(solution)/shard_map/all_gather | solution.py:95
  1127.9 419.0 %all-gather.44.cloned.1.call-start = ((), (), s32[]{:S(2)}) async-start(), calls=%async_computation.47 | async-start | bytes 1253376 | tf_op jit(solution)/shard_map/all_gather | solution.py:91
  1128.1 399.2 %copy-start.181 = (bf16[256,16]{0,1:T(8,128)(2,1)}, bf16[256,16]{0,1:T(8,128)(2,1)S(1)}, u32[]{:S(2)}) copy-start(bf16[256,16]{0,1:T(8,128)(2,1)S(1)} %select_reduce_fusion.2) | copy-start | bytes 24580
  1504.8 65.9 %reduce-scatter.42.cloned.1.call-start = ((), (), s32[]{:S(2)}) async-start(), calls=%async_computation.29 | async-start | bytes 983040 | tf_op jit(solution)/shard_map/reduce_scatter | solution.py:67
  1551.6 145.5 %reduce-scatter.44.cloned.1.call-start = ((), (), s32[]{:S(2)}) async-start(), calls=%async_computation.30 | async-start | bytes 983040 | tf_op jit(solution)/shard_map/reduce_scatter | solution.py:67
  1573.8 7.8 collective-permute-start.2
  1669.3 77.8 %reduce-scatter.46.cloned.1.call-start = ((), (), s32[]{:S(2)}) async-start(), calls=%async_computation.31 | async-start | bytes 983040 | tf_op jit(solution)/shard_map/reduce_scatter | solution.py:67
  1725.3 156.4 %reduce-scatter.48.cloned.1.call-start = ((), (), s32[]{:S(2)}) async-start(), calls=%async_computation.32 | async-start | bytes 983040 | tf_op jit(solution)/shard_map/reduce_scatter | solution.py:67
  1750.8 7.8 collective-permute-start.3
  1846.9 590.5 %all-reduce.18.cloned.1.call-start = ((), (), s32[]{:S(2)}) async-start(), calls=%async_computation.50 | async-start | bytes 196608
  1871.3 637.1 %reduce-scatter.66.cloned.1.call-start = ((), (), s32[]{:S(2)}) async-start(), calls=%async_computation.49 | async-start | bytes 835584
  1881.6 694.9 %reduce-scatter.54.cloned.1.call-start = ((), (), s32[]{:S(2)}) async-start(), calls=%async_computation.35 | async-start | bytes 417792 | tf_op jit(solution)/shard_map/reduce_scatter | solution.py:142
  1910.7 734.5 %reduce-scatter.56.cloned.1.call-start = ((), (), s32[]{:S(2)}) async-start(), calls=%async_computation.36 | async-start | bytes 417792 | tf_op jit(solution)/shard_map/reduce_scatter | solution.py:145
  1915.1 802.6 %reduce-scatter.58.cloned.1.call-start = ((), (), s32[]{:S(2)}) async-start(), calls=%async_computation.37 | async-start | bytes 1671168 | tf_op jit(solution)/shard_map/reduce_scatter | solution.py:148
  1919.7 820.1 %reduce-scatter.50.cloned.1.call-start = ((), (), s32[]{:S(2)}) async-start(), calls=%async_computation.33 | async-start | bytes 983040 | tf_op jit(solution)/shard_map/reduce_scatter | solution.py:67
  1926.2 1142.4 %reduce-scatter.64.cloned.1.call-start = ((), (), s32[]{:S(2)}) async-start(), calls=%async_computation.48 | async-start | bytes 1253376
  1942.2 1128.3 %reduce-scatter.52.cloned.1.call-start = ((), (), s32[]{:S(2)}) async-start(), calls=%async_computation.34 | async-start | bytes 1253376 | tf_op jit(solution)/shard_map/reduce_scatter | solution.py:139
  1954.7 1117.3 %reduce-scatter.62.cloned.1.call-start = ((), (), s32[]{:S(2)}) async-start(), calls=%async_computation.39 | async-start | bytes 6684672 | tf_op jit(solution)/shard_map/reduce_scatter | solution.py:173
  1988.6 1114.9 %reduce-scatter.60.cloned.1.call-start = ((), (), s32[]{:S(2)}) async-start(), calls=%async_computation.38 | async-start | bytes 13369344 | tf_op jit(solution)/shard_map/reduce_scatter | solution.py:167
  2053.4 456.7 %copy-start.188 = (f32[1536]{0:T(1024)S(1)}, f32[1536]{0:T(1024)}, u32[]{:S(2)}) copy-start(f32[1536]{0:T(1024)} %get-tuple-element.104) | copy-start | bytes 18436
  2053.4 456.7 %copy-start.189 = (f32[1536]{0:T(1024)S(1)}, f32[1536]{0:T(1024)}, u32[]{:S(2)}) copy-start(f32[1536]{0:T(1024)} %get-tuple-element.102) | copy-start | bytes 18436
  2053.4 456.7 %copy-start.218 = (f32[1536]{0:T(1024)S(1)}, f32[1536]{0:T(1024)}, u32[]{:S(2)}) copy-start(f32[1536]{0:T(1024)} %get-tuple-element.100) | copy-start | bytes 18436
  2053.4 686.4 %copy-start.31 = (bf16[2,64,1536]{2,1,0:T(8,128)(2,1)S(1)}, bf16[2,64,1536]{2,1,0:T(8,128)(2,1)}, u32[]{:S(2)}) copy-start(bf16[2,64,1536]{2,1,0:T(8,128)(2,1)} %param.15) | copy-start | bytes 1179652
  2053.4 686.4 %copy-start.138 = (f32[1536]{0:T(1024)S(1)}, f32[1536]{0:T(1024)}, u32[]{:S(2)}) copy-start(f32[1536]{0:T(1024)} %copy-done.136) | copy-start | bytes 18436
  2053.4 686.4 %copy-start.224 = (f32[64]{0:T(128)S(1)}, f32[64]{0:T(128)}, u32[]{:S(2)}) copy-start(f32[64]{0:T(128)} %copy-done.223) | copy-start | bytes 772
  2053.5 687.6 %copy-start.193 = (f32[1536]{0:T(1024)S(1)}, f32[1536]{0:T(1024)}, u32[]{:S(2)}) copy-start(f32[1536]{0:T(1024)} %get-tuple-element.110) | copy-start | bytes 18436
  2053.5 687.6 %copy-start.194 = (f32[1536]{0:T(1024)S(1)}, f32[1536]{0:T(1024)}, u32[]{:S(2)}) copy-start(f32[1536]{0:T(1024)} %get-tuple-element.108) | copy-start | bytes 18436
  2053.5 1013.0 %copy-start.90 = (bf16[64,1536]{1,0:T(8,128)(2,1)S(1)}, bf16[64,1536]{1,0:T(8,128)(2,1)}, u32[]{:S(2)}) copy-start(bf16[64,1536]{1,0:T(8,128)(2,1)} %copy-done.89) | copy-start | bytes 589828
  2053.5 1013.0 %copy-start.97 = (f32[64,1536]{1,0:T(8,128)S(1)}, f32[64,1536]{1,0:T(8,128)}, u32[]{:S(2)}) copy-start(f32[64,1536]{1,0:T(8,128)} %copy-done.96) | copy-start | bytes 1179652
  2053.5 1013.0 %copy-start.114 = (bf16[64,1536]{1,0:T(8,128)(2,1)S(1)}, bf16[64,1536]{1,0:T(8,128)(2,1)}, u32[]{:S(2)}) copy-start(bf16[64,1536]{1,0:T(8,128)(2,1)} %copy-done.113) | copy-start | bytes 589828
  2053.5 1013.0 %copy-start.226 = (f32[64]{0:T(128)S(1)}, f32[64]{0:T(128)}, u32[]{:S(2)}) copy-start(f32[64]{0:T(128)} %copy-done.225) | copy-start | bytes 772
  2053.5 1014.2 %copy-start.112 = (bf16[1,64,1536]{2,1,0:T(8,128)(2,1)S(1)}, bf16[1,64,1536]{2,1,0:T(8,128)(2,1)}, u32[]{:S(2)}) copy-start(bf16[1,64,1536]{2,1,0:T(8,128)(2,1)} %get-tuple-element.118) | copy-start | bytes 589828
  (207 other events, 5128.0 us)
Sparse Core Ops, SparseCore 0:
  10.5 47.6 all-gather.29
  60.7 44.0 all-gather.31
  246.8 19.3 reduce-scatter.27
  269.2 48.0 all-gather.35
  320.1 63.0 all-gather.25
  386.1 92.4 all-gather.33
  549.9 18.2 reduce-scatter.29
  597.5 21.7 reduce-scatter.31
  707.4 22.3 reduce-scatter.33
  760.9 23.9 reduce-scatter.35
  893.4 19.7 reduce-scatter.37
  916.1 66.6 all-gather.27
  985.9 88.6 all-gather.39
  1077.5 44.0 all-gather.37
  1127.5 18.1 reduce-scatter.39
  1148.0 47.0 all-gather.41
  1504.9 41.9 all-gather.43
  1551.7 18.9 reduce-scatter.41
  1669.4 23.1 reduce-scatter.43
  1725.4 21.6 reduce-scatter.45
  1847.0 21.1 reduce-scatter.47
  1871.4 565.9 all-reduce.17
  2441.7 66.6 reduce-scatter.65
  2512.0 64.4 reduce-scatter.53
  2580.7 64.4 reduce-scatter.55
  2649.6 68.0 reduce-scatter.57
  2720.7 19.1 reduce-scatter.49
  2744.2 69.5 reduce-scatter.63
  2818.2 66.5 reduce-scatter.51
  2889.3 88.7 reduce-scatter.61
  2982.5 121.0 reduce-scatter.59
where the time goes:
time: 3130 us; the launch traced here: 3110 us
  blocking collectives  1330 us (42%)
  waiting for transfers between devices  935 us (30%)
  local copies, waits for them, and re-layouts  362 us (12%)
  matrix products  343 us (11%)
  other arithmetic  108 us (3%)
    unnamed x3, blocking collectives  656 us
    unnamed x34, waiting for transfers between devices  454 us
    all_gather x2, blocking collectives, gather_weights(): lax.all_gather(w_router, ('dp', 'tensor'), axis=1, tiled=True)  336 us
    all_gather x12, blocking collectives, gather_tokens(): return lax.all_gather(rows_in, 'tensor', axis=0, tiled=True)  166 us
    reduce_scatter x12, waiting for transfers between devices, sum_branch(): lax.psum_scatter(partial_rows.astype(jnp.bfloat16), 'tensor', scatter_dim...  125 us
    all_gather x2, waiting for transfers between devices, gather_weights(): lax.all_gather(w_expert_in[:, None, None], 'dp', axis=3, tiled=True)  74.7 us
    reduce_scatter x1, waiting for transfers between devices, reduce_grads(): lax.psum_scatter(grad_shared_in[None, None, None].astype(jnp.bfloat16), '...  71.1 us
    reduce_scatter x1, waiting for transfers between devices, reduce_grads(): lax.psum_scatter(grad_value[None, None, None].astype(jnp.bfloat16), 'dp',...  67.4 us
  transfers between devices with their start and end apart: 35, of which 21 were waited for; matrix products, arithmetic and copies ran while one was open for 13% of the time, Pallas kernels for 0%

commit v1 on v0

v1 whole, which is shorter than its diff:
```python
import jax
import jax.numpy as jnp
from jax import lax
from jax.sharding import Mesh
from jax.sharding import PartitionSpec as P

D = 1536
HD = 128
E = 16
HALF_E = 8
GROUPS = 3
LEN = 256
ROWS = 64
DBLK = 96
HALF = D // 2

NORM_EPSILON = 1e-05
MASK_VALUE = -1e30
SCALE = HD**-0.5

BF = jnp.bfloat16
F32 = jnp.float32

QKV = 640
ATT = 1024
ATT_PAD = 1152
BLOCKS = 9
UP = BLOCKS * 256
DOWN = BLOCKS * 128

SECTION = ("section",)
TENSOR = ("tensor",)
GROUP = ("section", "tensor")
CORE = ("core",)
ROW = ("z",)
SIDE = ("section", "xhi")


def dot(a, b, contract):
    return lax.dot_general(a, b, ((contract[:1], contract[1:]), ((), ())), preferred_element_type=F32)


def nn(a, b):
    return dot(a, b, (1, 0))


def nt(a, b):
    return dot(a, b, (1, 1))


def tn(a, b):
    return dot(a, b, (0, 0))


def move(block, axes, target, only=None):
    sizes = [lax.axis_size(axis) for axis in axes]
    pairs = []

    def flat(place):
        index = 0
        for size, at in zip(sizes, place):
            index = index * size + at % size
        return index

    def walk(place):
        if len(place) == len(sizes):
            if only is None or only(*place):
                pairs.append((flat(place), flat(target(*place))))
            return
        for at in range(sizes[len(place)]):
            walk(place + (at,))

    walk(())
    return lax.ppermute(block, axes, pairs)


def tensor_gather(rows):
    return [rows] + [move(rows, TENSOR, lambda t, k=k: (t - k,)) for k in (1, 2, 3)]


def tensor_sum(parts):
    parts = parts.reshape(4, ROWS, -1)
    low = parts.astype(BF)
    total = parts[0].astype(F32)
    for k in (1, 2, 3):
        total = total + move(low[k], TENSOR, lambda t, k=k: (t + k,)).astype(F32)
    return total


def group_gather(rows):
    blocks = []
    for a in (0, 1):
        for k in range(4):
            if a or k:
                blocks.append(move(rows, GROUP, lambda s, t, a=a, k=k: (s - a, t - k)))
            else:
                blocks.append(rows)
    return jnp.concatenate(blocks, axis=0)


def group_sum(parts):
    parts = parts.reshape(8, ROWS, -1)
    low = parts.astype(BF)
    total = parts[0].astype(F32)
    for a in (1, 0):
        for k in range(4):
            if a or k:
                got = move(low[4 * a + k], GROUP, lambda s, t, a=a, k=k: (s + a, t + k))
                total = total + got.astype(F32)
    return total


def rolled(stacked, shift):
    n = stacked.shape[0]
    return lax.dynamic_slice_in_dim(jnp.concatenate([stacked, stacked], axis=0), shift, n, 0)


def rms_factor(rows):
    return lax.rsqrt(jnp.mean(rows * rows, axis=-1, keepdims=True) + NORM_EPSILON)


def norm_backward(rows, factor, gain, upstream):
    unit = rows * factor
    scaled = upstream * gain
    grad = factor * (scaled - unit * jnp.mean(scaled * unit, axis=-1, keepdims=True))
    return grad, jnp.sum(upstream * unit, axis=0)


def by_halves(fn, rows, halves):
    return fn(rows[:, :HALF], halves[0]) + fn(rows[:, HALF:], halves[1])


def to_halves(rows, halves):
    return jnp.concatenate([nt(rows, halves[0]), nt(rows, halves[1])], axis=1)


def swap_core(block):
    return (block, move(block, CORE, lambda c: (1 - c,)))


def attention_forward(hidden_rows, weights, gain, causal):
    hidden = hidden_rows.astype(F32)
    factor = rms_factor(hidden)
    normed = (hidden * factor * gain).astype(BF)
    qkv = by_halves(nn, normed, [w[:, :QKV] for w in weights]).astype(BF)
    queries = qkv[:, : GROUPS * HD].reshape(LEN, GROUPS, HD)
    keys = qkv[:, GROUPS * HD : GROUPS * HD + HD]
    values = qkv[:, GROUPS * HD + HD :]
    scores = jnp.einsum("qgd,kd->gqk", queries, keys, preferred_element_type=F32) * SCALE
    scores = jnp.where(causal[None], scores, MASK_VALUE)
    shifted = jnp.exp(scores - jnp.max(scores, axis=-1, keepdims=True))
    probs = shifted / jnp.sum(shifted, axis=-1, keepdims=True)
    attended = jnp.einsum("gqk,kd->qgd", probs.astype(BF), values, preferred_element_type=F32)
    attended = attended.astype(BF).reshape(LEN, GROUPS * HD)
    part = to_halves(attended, [w[:, QKV:ATT] for w in weights])
    return part, (normed, queries, keys, values, probs, attended)


def attention_backward(grad_rows, weights, saved):
    normed, queries, keys, values, probs, attended = saved
    attended_grad = by_halves(nn, grad_rows, [w[:, QKV:ATT] for w in weights]).astype(BF)
    attended_grad = attended_grad.reshape(LEN, GROUPS, HD)
    value_grad = jnp.einsum("gqk,qgd->kd", probs.astype(BF), attended_grad, preferred_element_type=F32)
    prob_grad = jnp.einsum("qgd,kd->gqk", attended_grad, values, preferred_element_type=F32)
    score_grad = probs * (prob_grad - jnp.sum(probs * prob_grad, axis=-1, keepdims=True))
    score_grad = (score_grad * SCALE).astype(BF)
    query_grad = jnp.einsum("gqk,kd->qgd", score_grad, keys, preferred_element_type=F32)
    key_grad = jnp.einsum("gqk,qgd->kd", score_grad, queries, preferred_element_type=F32)
    qkv_grad = jnp.concatenate(
        [query_grad.reshape(LEN, GROUPS * HD), key_grad, value_grad], axis=1
    ).astype(BF)
    part = to_halves(qkv_grad, [w[:, :QKV] for w in weights])
    return part, qkv_grad


def masked_softmax(logits, mask):
    top = jnp.max(jnp.where(mask, logits, MASK_VALUE), axis=-1, keepdims=True)
    shifted = jnp.where(mask, jnp.exp(jnp.where(mask, logits - top, 0.0)), 0.0)
    return shifted / jnp.sum(shifted, axis=-1, keepdims=True)


def spread(gates):
    return jnp.concatenate([gates, jnp.ones((gates.shape[0], 1), F32)], axis=1)[:, :, None]


def ffn_forward(rows, weights, gates):
    gate_up = by_halves(nn, rows, [w[:, :UP] for w in weights])
    parts = gate_up.reshape(-1, BLOCKS, 2, HD)
    hidden = jax.nn.silu(parts[:, :, 0]) * parts[:, :, 1]
    gated = (hidden * spread(gates)).astype(BF).reshape(-1, DOWN)
    out = to_halves(gated, [w[:, UP:] for w in weights])
    return out, (gate_up, gated)


def ffn_backward(grad_rows, weights, saved, gates):
    gate_up, gated = saved
    hidden_grad = by_halves(nn, grad_rows, [w[:, UP:] for w in weights]).reshape(-1, BLOCKS, HD)
    parts = gate_up.reshape(-1, BLOCKS, 2, HD)
    gate_part, up_part = parts[:, :, 0], parts[:, :, 1]
    sigmoid = jax.nn.sigmoid(gate_part)
    silu = gate_part * sigmoid
    products = jnp.sum((silu * up_part * hidden_grad)[:, :HALF_E], axis=-1)
    hidden_grad = hidden_grad * spread(gates)
    gate_grad = hidden_grad * up_part * sigmoid * (1.0 + gate_part * (1.0 - sigmoid))
    up_grad = hidden_grad * silu
    gate_up_grad = jnp.stack([gate_grad, up_grad], axis=2).astype(BF).reshape(-1, UP)
    part = to_halves(gate_up_grad, [w[:, :UP] for w in weights])
    return part, products, gate_up_grad


def weight_halves(lefts, rights):
    halves = []
    for at in (0, 1):
        cut = slice(at * HALF, (at + 1) * HALF)
        halves.append(
            jnp.concatenate([tn(left[:, cut], right) for left, right in zip(lefts, rights)], axis=1)
        )
    return halves


def reduce_rows(halves):
    other = move(halves[1].astype(BF), CORE, lambda c: (1 - c,))
    own = (halves[0] + other.astype(F32)).astype(BF)
    return lax.psum_scatter(own, "z", scatter_dimension=0, tiled=True).reshape(2, DBLK, -1)


def send_home(blocks, home):
    beside = move(blocks[1], SIDE, lambda s, x: (s, x + 1), lambda s, x: s == home)
    straight = move(blocks[0], SIDE, lambda s, x: (s + 1, x), lambda s, x: s != home)
    across = move(blocks[1], SIDE, lambda s, x: (s + 1, x + 1), lambda s, x: s != home)
    own = blocks[0].astype(F32) + beside.astype(F32)
    return own, straight.astype(F32) + across.astype(F32)


def per_device(
    tokens,
    cotangent,
    route_experts,
    route_slots,
    gain_attn,
    w_query,
    w_key,
    w_value,
    w_out,
    gain_ffn,
    w_router,
    w_shared_in,
    w_shared_down,
    w_expert_in,
    w_expert_down,
):
    s = lax.axis_index("section")
    xhi = lax.axis_index("xhi")
    core = lax.axis_index("core")
    z = lax.axis_index("z")
    t = lax.axis_index("tensor")
    first = s == 0

    own_tokens = lax.dynamic_index_in_dim(tokens, s, 0, keepdims=False)
    own_cotangent = lax.dynamic_index_in_dim(cotangent, s, 0, keepdims=False)
    token_blocks = tensor_gather(own_tokens)

    small = jnp.concatenate(
        [gain_attn[0][:, None], gain_ffn[0][:, None], w_router[0], jnp.zeros((24, 110), BF)], axis=1
    )
    small = lax.all_gather(small, "tensor", axis=0, tiled=True)
    att_piece = jnp.concatenate([w_query[0], w_key[0], w_value[0], w_out[0].T, small], axis=1)

    expert_in = w_expert_in[0].reshape(DBLK, 2, HALF_E * 256)
    shared_in = w_shared_in[0].reshape(DBLK, 2, 2, HD)
    expert_down = w_expert_down[0].transpose(2, 0, 1).reshape(DBLK, 2, HALF_E * HD)
    shared_down = w_shared_down[0].T.reshape(DBLK, 2, HD)

    def ffn_piece(part):
        return jnp.concatenate(
            [
                expert_in[:, part],
                shared_in[:, :, part].reshape(DBLK, 2 * HD),
                expert_down[:, part],
                shared_down[:, part],
            ],
            axis=1,
        )

    ffn_own = jnp.where(first, ffn_piece(0), ffn_piece(1))
    ffn_other = jnp.where(first, ffn_piece(1), ffn_piece(0))

    att_beside = move(att_piece, SIDE, lambda s, x: (s, x + 1))
    att_straight = move(att_piece, SIDE, lambda s, x: (s + 1, x))
    att_across = move(att_piece, SIDE, lambda s, x: (s + 1, x + 1))
    att_same = jnp.concatenate([att_piece, att_beside], axis=0)
    att_else = jnp.concatenate([att_straight, att_across], axis=0)
    att_pairs = [jnp.where(first, att_same, att_else), jnp.where(first, att_else, att_same)]

    ffn_straight = move(ffn_other, SIDE, lambda s, x: (s + 1, x))
    ffn_across = move(ffn_other, SIDE, lambda s, x: (s + 1, x + 1))
    ffn_beside0 = move(ffn_own, SIDE, lambda s, x: (s, x + 1), lambda s, x: s == 0)
    ffn_else = jnp.concatenate([ffn_straight, ffn_across], axis=0)
    ffn_pair0 = jnp.where(first, jnp.concatenate([ffn_own, ffn_beside0], axis=0), ffn_else)
    ffn_beside1 = move(ffn_own, SIDE, lambda s, x: (s, x + 1), lambda s, x: s == 1)
    ffn_pair1 = jnp.where(first, ffn_else, jnp.concatenate([ffn_own, ffn_beside1], axis=0))

    att_z = [att_pairs[0]] + [move(att_pairs[0], ROW, lambda at, k=k: (at - k,)) for k in (1, 2, 3)]
    att_rows = rolled(jnp.stack(att_z), (4 - z) % 4).reshape(HALF, ATT_PAD)
    att_w = [swap_core(att_rows)]
    ffn_w = [swap_core(lax.all_gather(ffn_pair0, "z", axis=0, tiled=True))]
    att_w.append(swap_core(lax.all_gather(att_pairs[1], "z", axis=0, tiled=True)))
    ffn_w.append(swap_core(lax.all_gather(ffn_pair1, "z", axis=0, tiled=True)))

    place = jnp.arange(D, dtype=jnp.int32)
    at_core = (place // HALF + core) % 2
    at_z = (place // (2 * DBLK)) % 4
    at_x = (place // DBLK + xhi) % 2
    column = at_x * HALF + at_z * (2 * DBLK) + at_core * DBLK + place % DBLK
    order = (place[:, None] == column[None, :]).astype(BF)

    def reorder(rows):
        return nn(rows, order).astype(BF)

    def restore(rows):
        return nt(rows, order).astype(BF)

    position = (t * ROWS + jnp.arange(LEN, dtype=jnp.int32)) % LEN
    causal = position[None, :] <= position[:, None]

    named = jnp.sum((route_experts[0][:, :, :, None] == jnp.arange(E)).astype(F32), axis=2)
    named = named.astype(BF).reshape(2 * LEN, E)
    named_else = move(named, SECTION, lambda s: (s + 1,))

    def layer_mask(layer):
        mask = jnp.where(s == layer, named, named_else).reshape(2, 4, ROWS, E)
        mask = rolled(rolled(mask, s).swapaxes(0, 1), t).swapaxes(0, 1)
        return mask.reshape(2 * LEN, E) > 0.5

    masks = [layer_mask(0), layer_mask(1)]

    def small_of(layer):
        low = jnp.concatenate([w[:, ATT:] for w in att_w[layer]], axis=0)
        return low[:, 0].astype(F32), low[:, 1].astype(F32), low[:, 2 : 2 + E]

    hidden_blocks = reorder(jnp.concatenate(token_blocks, axis=0))
    own_hidden = hidden_blocks[:ROWS]
    layer_values = []
    kept = []
    for layer in (0, 1):
        attn_gain, ffn_gain, router = small_of(layer)
        hidden = own_hidden.astype(F32)
        part, att_saved = attention_forward(hidden_blocks, att_w[layer], attn_gain, causal)
        mid = hidden + tensor_sum(part)
        factor_ffn = rms_factor(mid)
        normed_ffn = (mid * factor_ffn * ffn_gain).astype(BF)
        rows = group_gather(normed_ffn)
        gates = masked_softmax(nn(rows, router), masks[layer])
        own_gates = lax.dynamic_slice_in_dim(gates, s * HALF_E, HALF_E, 1)
        out, ffn_saved = ffn_forward(rows, ffn_w[layer], own_gates)
        result = (mid + group_sum(out)).astype(BF)
        layer_values.append(result)
        kept.append((hidden, mid, factor_ffn, rows, gates, own_gates, att_saved, ffn_saved))
        own_hidden = result
        if layer == 0:
            hidden_blocks = jnp.concatenate(tensor_gather(result), axis=0)

    out_low = reorder(own_cotangent)
    in_grads = [None, None]
    small_grads = [None, None]
    att_sums = [None, None]
    ffn_sums = [None, None]
    for layer in (1, 0):
        attn_gain, ffn_gain, router = small_of(layer)
        hidden, mid, factor_ffn, rows, gates, own_gates, att_saved, ffn_saved = kept[layer]
        out_grad = out_low.astype(F32)
        grad_rows = group_gather(out_low)
        part, products, gate_up_grad = ffn_backward(grad_rows, ffn_w[layer], ffn_saved, own_gates)
        empty = jnp.zeros_like(products)
        products = jnp.where(
            first,
            jnp.concatenate([products, empty], axis=1),
            jnp.concatenate([empty, products], axis=1),
        )
        high = products.astype(BF)
        rest = (products - high.astype(F32)).astype(BF)
        extra = jnp.concatenate([high, rest, jnp.zeros((2 * LEN, HD - 2 * E), BF)], axis=1)
        summed = group_sum(jnp.concatenate([part.astype(BF), extra], axis=1))
        ffn_sums[layer] = reduce_rows(weight_halves([rows, grad_rows], [gate_up_grad, ffn_saved[1]]))
        gate_grad = summed[:, D : D + E] + summed[:, D + E : D + 2 * E]
        own = gates[:ROWS]
        logits_grad = own * (gate_grad - jnp.sum(own * gate_grad, axis=1, keepdims=True))
        logits_grad = logits_grad.astype(BF)
        ffn_in_grad = summed[:, :D] + nt(logits_grad, router)
        mid_norm_grad, grad_gain_ffn = norm_backward(mid, factor_ffn, ffn_gain, ffn_in_grad)
        mid_grad = out_grad + mid_norm_grad
        mid_rows = jnp.concatenate(tensor_gather(mid_grad.astype(BF)), axis=0)
        part, qkv_grad = attention_backward(mid_rows, att_w[layer], att_saved)
        normed_grad = tensor_sum(part)
        att_sums[layer] = reduce_rows(
            weight_halves([att_saved[0], mid_rows], [qkv_grad, att_saved[5]])
        )
        hidden_norm_grad, grad_gain_attn = norm_backward(
            hidden, rms_factor(hidden), attn_gain, normed_grad
        )
        out_low = (mid_grad + hidden_norm_grad).astype(BF)
        in_grads[layer] = out_low
        grad_router = tn(rows[:ROWS], logits_grad)
        small_grads[layer] = jnp.concatenate(
            [grad_gain_attn[:, None], grad_gain_ffn[:, None], grad_router], axis=1
        )

    def both_sequences(values):
        low = restore(jnp.concatenate(values, axis=0)).reshape(2, ROWS, D)
        mine = jnp.where(first, low[0], low[1])
        got = move(jnp.where(first, low[1], low[0]), SECTION, lambda s: (s + 1,))
        return jnp.where(first, jnp.stack([mine, got]), jnp.stack([got, mine]))[None]

    values_out = both_sequences(layer_values)
    grads_in = both_sequences(in_grads)

    att_home = [send_home(att_sums[layer], layer) for layer in (0, 1)]
    ffn_home = [send_home(ffn_sums[layer], layer) for layer in (0, 1)]
    att = jnp.where(first, att_home[0][0] + att_home[0][1], att_home[1][0] + att_home[1][1])
    ffn_mine = jnp.where(first, ffn_home[0][0], ffn_home[1][0])
    ffn_got = jnp.where(first, ffn_home[0][1], ffn_home[1][1])
    low_part = jnp.where(first, ffn_mine, ffn_got)
    high_part = jnp.where(first, ffn_got, ffn_mine)

    def reduce_small(values):
        values = values.reshape(2, 4, 2, DBLK, 2, 2 + E)
        values = values[0] + move(values[1], CORE, lambda c: (1 - c,))
        values = rolled(values, z)
        total = values[0]
        for k in (1, 2, 3):
            total = total + move(values[k], ROW, lambda at, k=k: (at + k,))
        total = total[0] + move(total[1], ("xhi",), lambda x: (x + 1,))
        mine = jnp.where(first, total[:, 0], total[:, 1])
        total = mine + move(jnp.where(first, total[:, 1], total[:, 0]), SECTION, lambda s: (s + 1,))
        total = lax.psum(total, "tensor")
        return lax.dynamic_slice_in_dim(total, t * 24, 24, 0)

    small_sum = reduce_small(jnp.stack(small_grads, axis=1))

    def blocks_of(at, count):
        return [part[:, at : at + count] for part in (low_part, high_part)]

    grad_expert_in = jnp.stack(blocks_of(0, HALF_E * 256), axis=1).reshape(DBLK, E, 2, HD)
    grad_shared_in = jnp.concatenate(
        [part.reshape(DBLK, 2, HD) for part in blocks_of(HALF_E * 256, 256)], axis=2
    )
    grad_expert_down = jnp.concatenate(blocks_of(UP, HALF_E * HD), axis=1)
    grad_expert_down = grad_expert_down.reshape(DBLK, E, HD).transpose(1, 2, 0)
    grad_shared_down = jnp.concatenate(blocks_of(UP + HALF_E * HD, HD), axis=1).T
    return (
        values_out,
        grads_in,
        small_sum[:, 0][None],
        att[:, : GROUPS * HD][None],
        att[:, GROUPS * HD : GROUPS * HD + HD][None],
        att[:, GROUPS * HD + HD : QKV][None],
        att[:, QKV:].T[None],
        small_sum[:, 1][None],
        small_sum[:, 2:][None],
        grad_shared_in[None],
        grad_shared_down[None],
        grad_expert_in[None],
        grad_expert_down[None],
    )


def solution(mesh):
    split = Mesh(
        mesh.devices.reshape(2, 2, 4, 2, 4), ("section", "xhi", "z", "core", "tensor")
    )
    dp = ("xhi", "z", "core")
    both = dp + ("tensor",)
    placed = (
        P(dp, "tensor", None),
        P(dp, "tensor", None),
        P("section", dp, None, None),
        P("section", dp, None, None),
        P("section", both),
        P("section", dp, "tensor"),
        P("section", dp, "tensor"),
        P("section", dp, "tensor"),
        P("section", "tensor", dp),
        P("section", both),
        P("section", both, None),
        P("section", dp, None, "tensor"),
        P("section", "tensor", dp),
        P("section", dp, None, None, "tensor"),
        P("section", None, "tensor", dp),
    )
    return jax.shard_map(
        per_device,
        mesh=split,
        in_specs=placed,
        out_specs=(
            P("section", dp, "tensor", None),
            P("section", dp, "tensor", None),
            P("section", both),
            P("section", dp, "tensor"),
            P("section", dp, "tensor"),
            P("section", dp, "tensor"),
            P("section", "tensor", dp),
            P("section", both),
            P("section", both, None),
            P("section", dp, None, "tensor"),
            P("section", "tensor", dp),
            P("section", dp, None, None, "tensor"),
            P("section", None, "tensor", dp),
        ),
        check_vma=False,
    )
```

time: 3130 us -> 888 us (0.28)
  blocking collectives: 1330 us -> 28.2 us
  waiting for transfers between devices: 935 us -> 270 us
  local copies, waits for them, and re-layouts: 362 us -> 138 us
  matrix products: 343 us -> 157 us
  starting transfers between devices: 12.2 us -> 187 us
  other arithmetic: 108 us -> 72.9 us
    unnamed x3 -> x0, blocking collectives: 656 us -> none
    all_gather x20 -> x1, blocking collectives: 647 us -> 12.1 us  [per_device(): small = lax.all_gather(small, 'tensor', axis=0, tiled=True)]
    unnamed x34 -> x9, waiting for transfers between devices: 454 us -> 0.14 us
    reduce_scatter x18 -> x2, waiting for transfers between devices: 360 us -> 38.9 us  [reduce_rows(): lax.psum_scatter(own, 'z', scatter_dimension=0, tiled=True)]
    ppermute x4 -> x119, waiting for transfers between devices: 11.7 us -> 230 us  [move(): return lax.ppermute(block, axes, pairs)]
    dot_general x102 -> x68, matrix products: 343 us -> 153 us  [the longest x58 130 us: dot(): lax.dot_general(a, b, ((contract[:1], contract[1:]), ((), ())), preferred...]
    ppermute x4 -> x119, starting transfers between devices: 9.34 us -> 186 us  [move(): return lax.ppermute(block, axes, pairs)]
    gather x12 -> x0, local copies, waits for them, and re-layouts: 152 us -> none  [the longest x3 44.7 us: layer_backward(): dispatched_grad[flat_slots].reshape(length, TOPK, -1)]
  transfers between devices with their start and end apart: 35 -> 126, of which waited for: 21 -> 60; matrix products, arithmetic and copies ran while one was open for 13% -> 23% of each run, Pallas kernels for 0% -> 0%
where the time goes in v1:
time: 888 us; the launch traced here: 870 us
  waiting for transfers between devices  270 us (30%)
  starting transfers between devices  187 us (21%)
  matrix products  157 us (18%)
  local copies, waits for them, and re-layouts  138 us (16%)
  other arithmetic  72.9 us (8%)
  blocking collectives  28.2 us (3%)
  between operations  17.5 us (2%)
    ppermute x119, waiting for transfers between devices, move(): return lax.ppermute(block, axes, pairs)  230 us
    ppermute x119, starting transfers between devices, move(): return lax.ppermute(block, axes, pairs)  186 us
    dot_general x58, matrix products, dot(): lax.dot_general(a, b, ((contract[:1], contract[1:]), ((), ())), preferred...  130 us
    unnamed x351, local copies, waits for them, and re-layouts  50.6 us
    reduce_scatter x2, waiting for transfers between devices, reduce_rows(): lax.psum_scatter(own, 'z', scatter_dimension=0, tiled=True)  38.9 us
    slice x2, local copies, waits for them, and re-layouts, ffn_forward(): hidden = jax.nn.silu(parts[:, :, 0]) * parts[:, :, 1]  19.2 us
  transfers between devices with their start and end apart: 126, of which 60 were waited for; matrix products, arithmetic and copies ran while one was open for 23% of the time, Pallas kernels for 0%

profile of v1, /device:TPU:8, one launch (start us, length us, event | category | flops | bytes accessed | tf_op | source)
XLA Modules:
  0.0 870.4 jit_solution(7100809537193428615)
XLA Ops:
  22.7 11.0 %collective-permute-done.21 = bf16[96,3456]{1,0:T(8,128)(2,1)S(1)} collective-permute-done((bf16[96,3456]{1,0:T(8,128)(2,1)S(1)}, bf16[96,3456]{1,0:T(8,128)(2,1)S(1)}, u32[]{:S(2)}, u32[]{:S(2)}) %collective-permute-start.21) | collective-permute-done | bytes 663584 | tf_op jit(solution)/shard_map/ppermute | solution.py:74
  33.7 15.4 %collective-permute-done.22 = bf16[96,3456]{1,0:T(8,128)(2,1)S(1)} collective-permute-done((bf16[96,3456]{1,0:T(8,128)(2,1)S(1)}, bf16[96,3456]{1,0:T(8,128)(2,1)S(1)}, u32[]{:S(2)}, u32[]{:S(2)}) %collective-permute-start.22) | collective-permute-done | bytes 663584 | tf_op jit(solution)/shard_map/ppermute | solution.py:74
  51.9 12.1 %all_gather.12 = bf16[96,128]{1,0:T(8,128)(2,1)S(1)} all-gather(bf16[24,128]{1,0:T(8,128)(2,1)S(1)} %maximum_maximum_fusion), channel_id=1, replica_groups=mesh['section'=2,'xhi'=2,'z'=4,'core'=2,'tensor'=4] {'tensor'}, dimensions={0}, use_global_device_ids=true | all-gather | bytes 30720 | tf_op jit(solution)/shard_map/all_gather | solution.py:266
  78.9 4.0 collective-permute-start.6
  84.0 17.3 %collective-permute-done.6 = bf16[192,1152]{1,0:T(8,128)(2,1)S(1)} collective-permute-done((bf16[192,1152]{1,0:T(8,128)(2,1)S(1)}, bf16[192,1152]{1,0:T(8,128)(2,1)S(1)}, u32[]{:S(2)}, u32[]{:S(2)}) %collective-permute-start.6) | collective-permute-done | bytes 442400 | tf_op jit(solution)/shard_map/ppermute | solution.py:74
  104.8 15.2 %collective-permute-done.7 = bf16[192,1152]{1,0:T(8,128)(2,1)S(1)} collective-permute-done((bf16[192,1152]{1,0:T(8,128)(2,1)S(1)}, bf16[192,1152]{1,0:T(8,128)(2,1)S(1)}, u32[]{:S(2)}, u32[]{:S(2)}) %collective-permute-start.7) | collective-permute-done | bytes 442400 | tf_op jit(solution)/shard_map/ppermute | solution.py:74
  120.0 4.9 collective-permute-start.8
  125.7 7.8 collective-permute-done.8
  142.9 6.9 collective-permute-done.57
  151.6 4.5 collective-permute-done.58
  182.0 3.5 collective-permute-done.11
  185.5 5.1 collective-permute-done.10
  200.2 4.8 collective-permute-done.14
  208.8 5.3 collective-permute-done.17
  214.1 3.6 collective-permute-done.18
  223.3 4.0 fusion.27
  227.3 6.1 convolution_add_fusion.1
  233.5 6.4 reshape.704
  239.9 9.3 %fusion.347 = (f32[512,9,1,128]{3,2,1,0:T(1,128)}, f32[512,9,1,128]{3,2,1,0:T(1,128)S(1)}) fusion(f32[512,9,2,128]{3,2,1,0:T(2,128)} %reshape.704), kind=kLoop, calls=%fused_computation.638 | loop fusion | bytes 9437184 | tf_op jit(solution)/shard_map/slice | solution.py:189
  249.2 4.2 copy.496
  253.4 5.2 copy.495
  275.5 3.9 collective-permute-start.27
  282.2 5.3 collective-permute-start.25
  290.4 4.2 collective-permute-done.26
  301.0 4.4 convolution_add_fusion.3
  330.3 3.9 collective-permute-done.37
  346.2 8.6 collective-permute-done.40
  361.4 4.6 fusion.20
  366.1 4.1 convolution_add_fusion
  370.2 6.4 reshape.708
  376.6 10.0 %fusion.346 = (f32[512,9,1,128]{3,2,1,0:T(1,128)}, f32[512,9,1,128]{3,2,1,0:T(1,128)}) fusion(f32[512,9,2,128]{3,2,1,0:T(2,128)} %reshape.708), kind=kLoop, calls=%fused_computation.637 | loop fusion | bytes 9437184 | tf_op jit(solution)/shard_map/slice | solution.py:189
  386.6 6.3 copy.500
  393.0 6.5 copy.499
  411.7 4.4 fusion.35
  424.0 5.8 fusion.82
  429.8 4.9 fusion.85
  435.4 3.9 concatenate.277
  462.3 3.8 convolution_convert_fusion
  466.2 5.4 collective-permute-start.53
  478.5 3.6 collective-permute-done.54
  491.8 4.0 collective-permute-start.72
  498.4 3.6 convolution_convert_fusion.2
  530.8 6.3 collective-permute-done.74
  538.2 4.7 collective-permute-start.76
  562.2 4.1 convolution_add_fusion.2
  569.4 4.0 fusion.44
  575.9 5.5 fusion.76
  581.4 5.0 fusion.79
  595.3 4.1 collective-permute-start.85
  599.9 3.8 collective-permute-done.88
  612.6 4.1 collective-permute-start.91
  654.8 6.3 fusion.5
  661.6 4.2 convolution_convert_fusion.3
  673.5 5.3 collective-permute-done.111
  688.4 4.1 collective-permute-done.55
  702.5 4.3 collective-permute-done.94
  715.2 3.7 collective-permute-done.99
  728.3 16.0 %psum.7 = f32[96,18]{0,1:T(8,128)S(1)} all-reduce(f32[96,18]{0,1:T(8,128)S(1)} %fusion.299), channel_id=1, replica_groups=mesh['section'=2,'xhi'=2,'z'=4,'core'=2,'tensor'=4] {'tensor'}, use_global_device_ids=true, to_apply=%region_29.30 | all-reduce | flops 1728 | bytes 13824 | tf_op jit(solution)/shard_map/psum | solution.py:435
  747.7 4.6 collective-permute-start.110
  759.0 4.1 collective-permute-start.104
  767.8 38.9 %reduce-scatter.9.cloned.1.call-done = bf16[192,3456]{1,0:T(8,128)(2,1)} async-done(((bf16[768,3456]{1,0:T(8,128)(2,1)}), bf16[192,3456]{1,0:T(8,128)(2,1)}) %reduce-scatter.9.cloned.1.call-update) | async-done | bytes 1327120 | tf_op jit(solution)/shard_map/reduce_scatter | solution.py:224
  809.2 5.4 collective-permute-start.118
  831.6 14.5 %collective-permute-done.112 = bf16[96,3456]{1,0:T(8,128)(2,1)} collective-permute-done((bf16[96,3456]{1,0:T(8,128)(2,1)}, bf16[96,3456]{1,0:T(8,128)(2,1)}, u32[]{:S(2)}, u32[]{:S(2)}) %collective-permute-start.112) | collective-permute-done | bytes 663584 | tf_op jit(solution)/shard_map/ppermute | solution.py:74
  846.1 7.3 collective-permute-done.116
  (820 shorter events, 428.1 us)
Async XLA Ops:
  7.2 160.6 %all-gather.4.cloned.1.call-start = ((), (), s32[]{:S(2)}) async-start(), calls=%async_computation.4 | async-start | bytes 6635520 | tf_op jit(solution)/shard_map/all_gather | solution.py:306
  15.8 17.9 %collective-permute-start.21 = (bf16[96,3456]{1,0:T(8,128)(2,1)S(1)}, bf16[96,3456]{1,0:T(8,128)(2,1)S(1)}, u32[]{:S(2)}, u32[]{:S(2)}) collective-permute-start(bf16[96,3456]{1,0:T(8,128)(2,1)S(1)} %get-tuple-element.164), channel_id=1, source_target_pairs={{0,64},{32,96},{64,0},{96,32},{1,65},{33,97},{65,1},{97,33},{2,66}... | collective-permute-start | bytes 1990664 | tf_op jit(solution)/shard_map/ppermute | solution.py:74
  17.4 31.8 %collective-permute-start.22 = (bf16[96,3456]{1,0:T(8,128)(2,1)S(1)}, bf16[96,3456]{1,0:T(8,128)(2,1)S(1)}, u32[]{:S(2)}, u32[]{:S(2)}) collective-permute-start(bf16[96,3456]{1,0:T(8,128)(2,1)S(1)} %get-tuple-element.164), channel_id=1, source_target_pairs={{0,96},{32,64},{64,32},{96,0},{1,97},{33,65},{65,33},{97,1},{2,98}... | collective-permute-start | bytes 1990664 | tf_op jit(solution)/shard_map/ppermute | solution.py:74
  19.5 29.9 %collective-permute-start.46 = (bf16[96,3456]{1,0:T(8,128)(2,1)S(1)}, bf16[96,3456]{1,0:T(8,128)(2,1)S(1)}, u32[]{:S(2)}, u32[]{:S(2)}) collective-permute-start(bf16[96,3456]{1,0:T(8,128)(2,1)S(1)} %get-tuple-element.163), channel_id=1, source_target_pairs={{64,96},{96,64},{65,97},{97,65},{66,98},{98,66},{67,99},{99,67},{6... | collective-permute-start | bytes 1990664 | tf_op jit(solution)/shard_map/ppermute | solution.py:74
  20.2 29.2 %collective-permute-start.20 = (bf16[96,3456]{1,0:T(8,128)(2,1)S(1)}, bf16[96,3456]{1,0:T(8,128)(2,1)S(1)}, u32[]{:S(2)}, u32[]{:S(2)}) collective-permute-start(bf16[96,3456]{1,0:T(8,128)(2,1)S(1)} %get-tuple-element.163), channel_id=1, source_target_pairs={{0,32},{32,0},{1,33},{33,1},{2,34},{34,2},{3,35},{35,3},{4,36},{36... | collective-permute-start | bytes 1990664 | tf_op jit(solution)/shard_map/ppermute | solution.py:74
  51.4 157.2 %all-gather.8.cloned.1.call-start = ((), (), s32[]{:S(2)}) async-start(), calls=%async_computation.6 | async-start | bytes 6635520 | tf_op jit(solution)/shard_map/all_gather | solution.py:308
  64.3 13.1 %collective-permute-start.5 = (bf16[96,1152]{1,0:T(8,128)(2,1)S(1)}, bf16[96,1152]{1,0:T(8,128)(2,1)S(1)}, u32[]{:S(2)}, u32[]{:S(2)}) collective-permute-start(bf16[96,1152]{1,0:T(8,128)(2,1)S(1)} %constant_dynamic-update-slice_fusion), channel_id=1, source_target_pairs={{0,96},{32,64},{64,32},{96,0},{1,97},{33,65},{65,33},{97,1},{2,98}... | collective-permute-start | bytes 663560 | tf_op jit(solution)/shard_map/ppermute | solution.py:74
  68.4 90.3 %collective-permute-start.2 = (bf16[64,1536]{1,0:T(8,128)(2,1)S(1)}, bf16[64,1536]{1,0:T(8,128)(2,1)}, u32[]{:S(2)}, u32[]{:S(2)}) collective-permute-start(bf16[64,1536]{1,0:T(8,128)(2,1)S(1)} %dynamic-slice_bitcast_fusion), channel_id=1, source_target_pairs={{0,1},{1,2},{2,3},{3,0},{4,5},{5,6},{6,7},{7,4},{8,9},{9,10},{10,1... | collective-permute-start | bytes 589832 | tf_op jit(solution)/shard_map/ppermute | solution.py:74
  72.8 87.3 %collective-permute-start.1 = (bf16[64,1536]{1,0:T(8,128)(2,1)S(1)}, bf16[64,1536]{1,0:T(8,128)(2,1)}, u32[]{:S(2)}, u32[]{:S(2)}) collective-permute-start(bf16[64,1536]{1,0:T(8,128)(2,1)S(1)} %dynamic-slice_bitcast_fusion), channel_id=1, source_target_pairs={{0,2},{1,3},{2,0},{3,1},{4,6},{5,7},{6,4},{7,5},{8,10},{9,11},{10,... | collective-permute-start | bytes 589832 | tf_op jit(solution)/shard_map/ppermute | solution.py:74
  75.4 86.1 %collective-permute-start = (bf16[64,1536]{1,0:T(8,128)(2,1)S(1)}, bf16[64,1536]{1,0:T(8,128)(2,1)}, u32[]{:S(2)}, u32[]{:S(2)}) collective-permute-start(bf16[64,1536]{1,0:T(8,128)(2,1)S(1)} %dynamic-slice_bitcast_fusion), channel_id=1, source_target_pairs={{0,3},{1,0},{2,1},{3,2},{4,7},{5,4},{6,5},{7,6},{8,11},{9,8},{10,9... | collective-permute-start | bytes 589832 | tf_op jit(solution)/shard_map/ppermute | solution.py:74
  77.4 63.8 %collective-permute-start.56 = (bf16[64,1536]{1,0:T(8,128)(2,1)S(1)}, bf16[64,1536]{1,0:T(8,128)(2,1)S(1)}, u32[]{:S(2)}, u32[]{:S(2)}) collective-permute-start(bf16[64,1536]{1,0:T(8,128)(2,1)S(1)} %get-tuple-element.223), channel_id=1, source_target_pairs={{0,3},{1,0},{2,1},{3,2},{64,67},{65,64},{66,65},{67,66},{4,7},{5,4... | collective-permute-start | bytes 589832 | tf_op jit(solution)/shard_map/ppermute | solution.py:74
  78.9 22.4 %collective-permute-start.6 = (bf16[192,1152]{1,0:T(8,128)(2,1)S(1)}, bf16[192,1152]{1,0:T(8,128)(2,1)S(1)}, u32[]{:S(2)}, u32[]{:S(2)}) collective-permute-start(bf16[192,1152]{1,0:T(8,128)(2,1)S(1)} %get-tuple-element.165), channel_id=1, source_target_pairs={{0,24},{8,0},{16,8},{24,16},{1,25},{9,1},{17,9},{25,17},{2,26},{10... | collective-permute-start | bytes 1327112 | tf_op jit(solution)/shard_map/ppermute | solution.py:74
  84.0 139.1 %all-gather.6.cloned.1.call-start = ((), (), s32[]{:S(2)}) async-start(), calls=%async_computation.5 | async-start | bytes 2211840 | tf_op jit(solution)/shard_map/all_gather | solution.py:307
  101.3 18.7 %collective-permute-start.7 = (bf16[192,1152]{1,0:T(8,128)(2,1)S(1)}, bf16[192,1152]{1,0:T(8,128)(2,1)S(1)}, u32[]{:S(2)}, u32[]{:S(2)}) collective-permute-start(bf16[192,1152]{1,0:T(8,128)(2,1)S(1)} %get-tuple-element.165), channel_id=1, source_target_pairs={{0,16},{8,24},{16,0},{24,8},{1,17},{9,25},{17,1},{25,9},{2,18},{10... | collective-permute-start | bytes 1327112 | tf_op jit(solution)/shard_map/ppermute | solution.py:74
  120.0 13.5 %collective-permute-start.8 = (bf16[192,1152]{1,0:T(8,128)(2,1)S(1)}, bf16[192,1152]{1,0:T(8,128)(2,1)S(1)}, u32[]{:S(2)}, u32[]{:S(2)}) collective-permute-start(bf16[192,1152]{1,0:T(8,128)(2,1)S(1)} %get-tuple-element.165), channel_id=1, source_target_pairs={{0,8},{8,16},{16,24},{24,0},{1,9},{9,17},{17,25},{25,1},{2,10},{10... | collective-permute-start | bytes 1327112 | tf_op jit(solution)/shard_map/ppermute | solution.py:74
  139.3 26.4 %collective-permute-start.9 = (bf16[768,1152]{1,0:T(8,128)(2,1)S(1)}, bf16[768,1152]{1,0:T(8,128)(2,1)S(1)}, u32[]{:S(2)}, u32[]{:S(2)}) collective-permute-start(bf16[768,1152]{1,0:T(8,128)(2,1)S(1)} %bitcast.403), channel_id=1, source_target_pairs={{0,4},{4,0},{1,5},{5,1},{2,6},{6,2},{3,7},{7,3},{8,12},{12,8},{9,1... | collective-permute-start | bytes 5308424 | tf_op jit(solution)/shard_map/ppermute | solution.py:74
  158.7 17.2 %collective-permute-start.60 = (bf16[64,1536]{1,0:T(8,128)(2,1)S(1)}, bf16[64,1536]{1,0:T(8,128)(2,1)}, u32[]{:S(2)}, u32[]{:S(2)}) collective-permute-start(bf16[64,1536]{1,0:T(8,128)(2,1)S(1)} %get-tuple-element.223), channel_id=1, source_target_pairs={{0,67},{1,64},{2,65},{3,66},{64,3},{65,0},{66,1},{67,2},{4,71},{5,... | collective-permute-start | bytes 589832 | tf_op jit(solution)/shard_map/ppermute | solution.py:74
  160.1 33.1 %collective-permute-start.61 = (bf16[64,1536]{1,0:T(8,128)(2,1)S(1)}, bf16[64,1536]{1,0:T(8,128)(2,1)}, u32[]{:S(2)}, u32[]{:S(2)}) collective-permute-start(bf16[64,1536]{1,0:T(8,128)(2,1)S(1)} %get-tuple-element.223), channel_id=1, source_target_pairs={{0,66},{1,67},{2,64},{3,65},{64,2},{65,3},{66,0},{67,1},{4,70},{5,... | collective-permute-start | bytes 589832 | tf_op jit(solution)/shard_map/ppermute | solution.py:74
  167.8 55.5 %collective-permute-start.23 = (bf16[768,3456]{1,0:T(8,128)(2,1)}, bf16[768,3456]{1,0:T(8,128)(2,1)}, u32[]{:S(2)}, u32[]{:S(2)}) collective-permute-start(bf16[768,3456]{1,0:T(8,128)(2,1)} %all-gather.4.cloned.1.call-done), channel_id=1, source_target_pairs={{0,4},{4,0},{1,5},{5,1},{2,6},{6,2},{3,7},{7,3},{8,12},{12,8},{9,1... | collective-permute-start | bytes 15925256 | tf_op jit(solution)/shard_map/ppermute | solution.py:74
  175.8 14.8 %collective-permute-start.10 = (bf16[64,1536]{1,0:T(8,128)(2,1)S(1)}, bf16[64,1536]{1,0:T(8,128)(2,1)S(1)}, u32[]{:S(2)}, u32[]{:S(2)}) collective-permute-start(bf16[64,1536]{1,0:T(8,128)(2,1)S(1)} %get-tuple-element.179), channel_id=1, source_target_pairs={{0,1},{1,2},{2,3},{3,0},{4,5},{5,6},{6,7},{7,4},{8,9},{9,10},{10,1... | collective-permute-start | bytes 589832 | tf_op jit(solution)/shard_map/ppermute | solution.py:74
  180.0 566.4 %reduce-scatter.15.cloned.1.call-start = ((), (), s32[]{:S(2)}) async-start(), calls=%async_computation.10 | async-start | bytes 1966080
  180.1 89.2 %collective-permute-start.62 = (bf16[64,1536]{1,0:T(8,128)(2,1)S(1)}, bf16[64,1536]{1,0:T(8,128)(2,1)}, u32[]{:S(2)}, u32[]{:S(2)}) collective-permute-start(bf16[64,1536]{1,0:T(8,128)(2,1)S(1)} %get-tuple-element.223), channel_id=1, source_target_pairs={{0,65},{1,66},{2,67},{3,64},{64,1},{65,2},{66,3},{67,0},{4,69},{5,... | collective-permute-start | bytes 589832 | tf_op jit(solution)/shard_map/ppermute | solution.py:74
  208.6 66.9 %collective-permute-start.47 = (bf16[768,3456]{1,0:T(8,128)(2,1)}, bf16[768,3456]{1,0:T(8,128)(2,1)}, u32[]{:S(2)}, u32[]{:S(2)}) collective-permute-start(bf16[768,3456]{1,0:T(8,128)(2,1)} %all-gather.8.cloned.1.call-done), channel_id=1, source_target_pairs={{0,4},{4,0},{1,5},{5,1},{2,6},{6,2},{3,7},{7,3},{8,12},{12,8},{9,1... | collective-permute-start | bytes 15925256 | tf_op jit(solution)/shard_map/ppermute | solution.py:74
  223.0 48.8 %collective-permute-start.35 = (bf16[768,1152]{1,0:T(8,128)(2,1)}, bf16[768,1152]{1,0:T(8,128)(2,1)}, u32[]{:S(2)}, u32[]{:S(2)}) collective-permute-start(bf16[768,1152]{1,0:T(8,128)(2,1)} %all-gather.6.cloned.1.call-done), channel_id=1, source_target_pairs={{0,4},{4,0},{1,5},{5,1},{2,6},{6,2},{3,7},{7,3},{8,12},{12,8},{9,1... | collective-permute-start | bytes 5308424 | tf_op jit(solution)/shard_map/ppermute | solution.py:74
  267.2 15.0 %collective-permute-start.31 = (bf16[64,1536]{1,0:T(8,128)(2,1)S(1)}, bf16[64,1536]{1,0:T(8,128)(2,1)S(1)}, u32[]{:S(2)}, u32[]{:S(2)}) collective-permute-start(bf16[64,1536]{1,0:T(8,128)(2,1)S(1)} %get-tuple-element.153), channel_id=1, source_target_pairs={{0,3},{1,0},{2,1},{3,2},{64,67},{65,64},{66,65},{67,66},{4,7},{5,4... | collective-permute-start | bytes 589832 | tf_op jit(solution)/shard_map/ppermute | solution.py:74
  268.3 13.8 %collective-permute-start.30 = (bf16[64,1536]{1,0:T(8,128)(2,1)S(1)}, bf16[64,1536]{1,0:T(8,128)(2,1)S(1)}, u32[]{:S(2)}, u32[]{:S(2)}) collective-permute-start(bf16[64,1536]{1,0:T(8,128)(2,1)S(1)} %get-tuple-element.154), channel_id=1, source_target_pairs={{0,2},{1,3},{2,0},{3,1},{64,66},{65,67},{66,64},{67,65},{4,6},{5,7... | collective-permute-start | bytes 589832 | tf_op jit(solution)/shard_map/ppermute | solution.py:74
  273.9 16.5 %collective-permute-start.29 = (bf16[64,1536]{1,0:T(8,128)(2,1)S(1)}, bf16[64,1536]{1,0:T(8,128)(2,1)S(1)}, u32[]{:S(2)}, u32[]{:S(2)}) collective-permute-start(bf16[64,1536]{1,0:T(8,128)(2,1)S(1)} %get-tuple-element.155), channel_id=1, source_target_pairs={{0,1},{1,2},{2,3},{3,0},{64,65},{65,66},{66,67},{67,64},{4,5},{5,6... | collective-permute-start | bytes 589832 | tf_op jit(solution)/shard_map/ppermute | solution.py:74
  275.0 15.4 %collective-permute-start.28 = (bf16[64,1536]{1,0:T(8,128)(2,1)S(1)}, bf16[64,1536]{1,0:T(8,128)(2,1)S(1)}, u32[]{:S(2)}, u32[]{:S(2)}) collective-permute-start(bf16[64,1536]{1,0:T(8,128)(2,1)S(1)} %get-tuple-element.156), channel_id=1, source_target_pairs={{0,67},{1,64},{2,65},{3,66},{64,3},{65,0},{66,1},{67,2},{4,71},{5,... | collective-permute-start | bytes 589832 | tf_op jit(solution)/shard_map/ppermute | solution.py:74
  275.5 14.9 %collective-permute-start.27 = (bf16[64,1536]{1,0:T(8,128)(2,1)S(1)}, bf16[64,1536]{1,0:T(8,128)(2,1)S(1)}, u32[]{:S(2)}, u32[]{:S(2)}) collective-permute-start(bf16[64,1536]{1,0:T(8,128)(2,1)S(1)} %get-tuple-element.157), channel_id=1, source_target_pairs={{0,66},{1,67},{2,64},{3,65},{64,2},{65,3},{66,0},{67,1},{4,70},{5,... | collective-permute-start | bytes 589832 | tf_op jit(solution)/shard_map/ppermute | solution.py:74
  282.2 15.0 %collective-permute-start.25 = (bf16[64,1536]{1,0:T(8,128)(2,1)S(1)}, bf16[64,1536]{1,0:T(8,128)(2,1)S(1)}, u32[]{:S(2)}, u32[]{:S(2)}) collective-permute-start(bf16[64,1536]{1,0:T(8,128)(2,1)S(1)} %get-tuple-element.152), channel_id=1, source_target_pairs={{0,64},{1,65},{2,66},{3,67},{64,0},{65,1},{66,2},{67,3},{4,68},{5,... | collective-permute-start | bytes 589832 | tf_op jit(solution)/shard_map/ppermute | solution.py:74
  339.4 15.4 %collective-permute-start.40 = (bf16[64,1536]{1,0:T(8,128)(2,1)S(1)}, bf16[64,1536]{1,0:T(8,128)(2,1)S(1)}, u32[]{:S(2)}, u32[]{:S(2)}) collective-permute-start(bf16[64,1536]{1,0:T(8,128)(2,1)S(1)} %get-tuple-element.112), channel_id=1, source_target_pairs={{0,2},{1,3},{2,0},{3,1},{64,66},{65,67},{66,64},{67,65},{4,6},{5,7... | collective-permute-start | bytes 589832 | tf_op jit(solution)/shard_map/ppermute | solution.py:74
  339.5 15.4 %collective-permute-start.41 = (bf16[64,1536]{1,0:T(8,128)(2,1)S(1)}, bf16[64,1536]{1,0:T(8,128)(2,1)S(1)}, u32[]{:S(2)}, u32[]{:S(2)}) collective-permute-start(bf16[64,1536]{1,0:T(8,128)(2,1)S(1)} %get-tuple-element.112), channel_id=1, source_target_pairs={{0,1},{1,2},{2,3},{3,0},{64,65},{65,66},{66,67},{67,64},{4,5},{5,6... | collective-permute-start | bytes 589832 | tf_op jit(solution)/shard_map/ppermute | solution.py:74
  341.4 13.4 %collective-permute-start.42 = (bf16[64,1536]{1,0:T(8,128)(2,1)S(1)}, bf16[64,1536]{1,0:T(8,128)(2,1)S(1)}, u32[]{:S(2)}, u32[]{:S(2)}) collective-permute-start(bf16[64,1536]{1,0:T(8,128)(2,1)S(1)} %get-tuple-element.112), channel_id=1, source_target_pairs={{0,64},{1,65},{2,66},{3,67},{64,0},{65,1},{66,2},{67,3},{4,68},{5,... | collective-permute-start | bytes 589832 | tf_op jit(solution)/shard_map/ppermute | solution.py:74
  341.4 13.8 %collective-permute-start.43 = (bf16[64,1536]{1,0:T(8,128)(2,1)S(1)}, bf16[64,1536]{1,0:T(8,128)(2,1)S(1)}, u32[]{:S(2)}, u32[]{:S(2)}) collective-permute-start(bf16[64,1536]{1,0:T(8,128)(2,1)S(1)} %get-tuple-element.112), channel_id=1, source_target_pairs={{0,67},{1,64},{2,65},{3,66},{64,3},{65,0},{66,1},{67,2},{4,71},{5,... | collective-permute-start | bytes 589832 | tf_op jit(solution)/shard_map/ppermute | solution.py:74
  344.2 14.4 %collective-permute-start.44 = (bf16[64,1536]{1,0:T(8,128)(2,1)S(1)}, bf16[64,1536]{1,0:T(8,128)(2,1)S(1)}, u32[]{:S(2)}, u32[]{:S(2)}) collective-permute-start(bf16[64,1536]{1,0:T(8,128)(2,1)S(1)} %get-tuple-element.112), channel_id=1, source_target_pairs={{0,66},{1,67},{2,64},{3,65},{64,2},{65,3},{66,0},{67,1},{4,70},{5,... | collective-permute-start | bytes 589832 | tf_op jit(solution)/shard_map/ppermute | solution.py:74
  440.9 17.3 %collective-permute-start.69 = (bf16[64,1664]{1,0:T(8,128)(2,1)S(1)}, bf16[64,1664]{1,0:T(8,128)(2,1)S(1)}, u32[]{:S(2)}, u32[]{:S(2)}) collective-permute-start(bf16[64,1664]{1,0:T(8,128)(2,1)S(1)} %get-tuple-element.139), channel_id=1, source_target_pairs={{0,3},{1,0},{2,1},{3,2},{64,67},{65,64},{66,65},{67,66},{4,7},{5,4... | collective-permute-start | bytes 638984 | tf_op jit(solution)/shard_map/ppermute | solution.py:74
  443.5 18.2 %collective-permute-start.68 = (bf16[64,1664]{1,0:T(8,128)(2,1)S(1)}, bf16[64,1664]{1,0:T(8,128)(2,1)S(1)}, u32[]{:S(2)}, u32[]{:S(2)}) collective-permute-start(bf16[64,1664]{1,0:T(8,128)(2,1)S(1)} %get-tuple-element.140), channel_id=1, source_target_pairs={{0,2},{1,3},{2,0},{3,1},{64,66},{65,67},{66,64},{67,65},{4,6},{5,7... | collective-permute-start | bytes 638984 | tf_op jit(solution)/shard_map/ppermute | solution.py:74
  445.2 20.9 %collective-permute-start.67 = (bf16[64,1664]{1,0:T(8,128)(2,1)S(1)}, bf16[64,1664]{1,0:T(8,128)(2,1)S(1)}, u32[]{:S(2)}, u32[]{:S(2)}) collective-permute-start(bf16[64,1664]{1,0:T(8,128)(2,1)S(1)} %get-tuple-element.141), channel_id=1, source_target_pairs={{0,1},{1,2},{2,3},{3,0},{64,65},{65,66},{66,67},{67,64},{4,5},{5,6... | collective-permute-start | bytes 638984 | tf_op jit(solution)/shard_map/ppermute | solution.py:74
  447.7 18.5 %collective-permute-start.66 = (bf16[64,1664]{1,0:T(8,128)(2,1)S(1)}, bf16[64,1664]{1,0:T(8,128)(2,1)S(1)}, u32[]{:S(2)}, u32[]{:S(2)}) collective-permute-start(bf16[64,1664]{1,0:T(8,128)(2,1)S(1)} %get-tuple-element.142), channel_id=1, source_target_pairs={{0,67},{1,64},{2,65},{3,66},{64,3},{65,0},{66,1},{67,2},{4,71},{5,... | collective-permute-start | bytes 638984 | tf_op jit(solution)/shard_map/ppermute | solution.py:74
  447.7 23.9 %collective-permute-start.65 = (bf16[64,1664]{1,0:T(8,128)(2,1)S(1)}, bf16[64,1664]{1,0:T(8,128)(2,1)S(1)}, u32[]{:S(2)}, u32[]{:S(2)}) collective-permute-start(bf16[64,1664]{1,0:T(8,128)(2,1)S(1)} %get-tuple-element.143), channel_id=1, source_target_pairs={{0,66},{1,67},{2,64},{3,65},{64,2},{65,3},{66,0},{67,1},{4,70},{5,... | collective-permute-start | bytes 638984 | tf_op jit(solution)/shard_map/ppermute | solution.py:74
  458.2 13.9 %collective-permute-start.64 = (bf16[64,1664]{1,0:T(8,128)(2,1)S(1)}, bf16[64,1664]{1,0:T(8,128)(2,1)S(1)}, u32[]{:S(2)}, u32[]{:S(2)}) collective-permute-start(bf16[64,1664]{1,0:T(8,128)(2,1)S(1)} %get-tuple-element.144), channel_id=1, source_target_pairs={{0,65},{1,66},{2,67},{3,64},{64,1},{65,2},{66,3},{67,0},{4,69},{5,... | collective-permute-start | bytes 638984 | tf_op jit(solution)/shard_map/ppermute | solution.py:74
  466.1 16.0 %collective-permute-start.54 = (bf16[64,1536]{1,0:T(8,128)(2,1)S(1)}, bf16[64,1536]{1,0:T(8,128)(2,1)S(1)}, u32[]{:S(2)}, u32[]{:S(2)}) collective-permute-start(bf16[64,1536]{1,0:T(8,128)(2,1)S(1)} %get-tuple-element.146), channel_id=1, source_target_pairs={{0,3},{1,0},{2,1},{3,2},{64,67},{65,64},{66,65},{67,66},{4,7},{5,4... | collective-permute-start | bytes 589832 | tf_op jit(solution)/shard_map/ppermute | solution.py:74
  466.2 18.9 %collective-permute-start.53 = (bf16[64,1536]{1,0:T(8,128)(2,1)S(1)}, bf16[64,1536]{1,0:T(8,128)(2,1)S(1)}, u32[]{:S(2)}, u32[]{:S(2)}) collective-permute-start(bf16[64,1536]{1,0:T(8,128)(2,1)S(1)} %get-tuple-element.147), channel_id=1, source_target_pairs={{0,2},{1,3},{2,0},{3,1},{64,66},{65,67},{66,64},{67,65},{4,6},{5,7... | collective-permute-start | bytes 589832 | tf_op jit(solution)/shard_map/ppermute | solution.py:74
  471.6 13.6 %collective-permute-start.52 = (bf16[64,1536]{1,0:T(8,128)(2,1)S(1)}, bf16[64,1536]{1,0:T(8,128)(2,1)S(1)}, u32[]{:S(2)}, u32[]{:S(2)}) collective-permute-start(bf16[64,1536]{1,0:T(8,128)(2,1)S(1)} %get-tuple-element.148), channel_id=1, source_target_pairs={{0,1},{1,2},{2,3},{3,0},{64,65},{65,66},{66,67},{67,64},{4,5},{5,6... | collective-permute-start | bytes 589832 | tf_op jit(solution)/shard_map/ppermute | solution.py:74
  472.1 13.1 %collective-permute-start.51 = (bf16[64,1536]{1,0:T(8,128)(2,1)S(1)}, bf16[64,1536]{1,0:T(8,128)(2,1)S(1)}, u32[]{:S(2)}, u32[]{:S(2)}) collective-permute-start(bf16[64,1536]{1,0:T(8,128)(2,1)S(1)} %get-tuple-element.149), channel_id=1, source_target_pairs={{0,67},{1,64},{2,65},{3,66},{64,3},{65,0},{66,1},{67,2},{4,71},{5,... | collective-permute-start | bytes 589832 | tf_op jit(solution)/shard_map/ppermute | solution.py:74
  523.4 13.7 %collective-permute-start.74 = (bf16[64,1536]{1,0:T(8,128)(2,1)S(1)}, bf16[64,1536]{1,0:T(8,128)(2,1)S(1)}, u32[]{:S(2)}, u32[]{:S(2)}) collective-permute-start(bf16[64,1536]{1,0:T(8,128)(2,1)S(1)} %get-tuple-element.173), channel_id=1, source_target_pairs={{0,2},{1,3},{2,0},{3,1},{4,6},{5,7},{6,4},{7,5},{8,10},{9,11},{10,... | collective-permute-start | bytes 589832 | tf_op jit(solution)/shard_map/ppermute | solution.py:74
  605.6 49.1 %collective-permute-start.113 = (bf16[768,3456]{1,0:T(8,128)(2,1)}, bf16[768,3456]{1,0:T(8,128)(2,1)}, u32[]{:S(2)}, u32[]{:S(2)}) collective-permute-start(bf16[768,3456]{1,0:T(8,128)(2,1)} %pad_maximum_fusion.1), channel_id=1, source_target_pairs={{0,4},{4,0},{1,5},{5,1},{2,6},{6,2},{3,7},{7,3},{8,12},{12,8},{9,1... | collective-permute-start | bytes 15925256 | tf_op jit(solution)/shard_map/ppermute | solution.py:74
  605.7 22.3 %collective-permute-start.107 = (bf16[768,1024]{0,1:T(8,128)(2,1)}, bf16[768,1024]{0,1:T(8,128)(2,1)}, u32[]{:S(2)}, u32[]{:S(2)}) collective-permute-start(bf16[768,1024]{0,1:T(8,128)(2,1)} %pad_maximum_fusion.11), channel_id=1, source_target_pairs={{0,4},{4,0},{1,5},{5,1},{2,6},{6,2},{3,7},{7,3},{8,12},{12,8},{9,1... | collective-permute-start | bytes 4718600 | tf_op jit(solution)/shard_map/ppermute | solution.py:74
  633.9 122.6 %reduce-scatter.13.cloned.1.call-start = ((), (), s32[]{:S(2)}) async-start(), calls=%async_computation.9 | async-start | bytes 1966080
  649.7 113.6 %reduce-scatter.11.cloned.1.call-start = ((), (), s32[]{:S(2)}) async-start(), calls=%async_computation.8 | async-start | bytes 6635520 | tf_op jit(solution)/shard_map/reduce_scatter | solution.py:224
  661.1 145.6 %reduce-scatter.9.cloned.1.call-start = ((), (), s32[]{:S(2)}) async-start(), calls=%async_computation.7 | async-start | bytes 6635520 | tf_op jit(solution)/shard_map/reduce_scatter | solution.py:224
  726.2 19.4 %collective-permute-start.96 = (bf16[64,1536]{1,0:T(8,128)(2,1)S(1)}, bf16[64,1536]{1,0:T(8,128)(2,1)S(1)}, u32[]{:S(2)}, u32[]{:S(2)}) collective-permute-start(bf16[64,1536]{1,0:T(8,128)(2,1)S(1)} %get-tuple-element.191), channel_id=1, source_target_pairs={{0,64},{64,0},{1,65},{65,1},{2,66},{66,2},{3,67},{67,3},{4,68},{68... | collective-permute-start | bytes 589832 | tf_op jit(solution)/shard_map/ppermute | solution.py:74
  747.7 18.1 %collective-permute-start.110 = (bf16[96,1024]{0,1:T(8,128)(2,1)S(1)}, bf16[96,1024]{0,1:T(8,128)(2,1)S(1)}, u32[]{:S(2)}, u32[]{:S(2)}) collective-permute-start(bf16[96,1024]{0,1:T(8,128)(2,1)S(1)} %copy.509), channel_id=1, source_target_pairs={{0,96},{32,64},{1,97},{33,65},{2,98},{34,66},{3,99},{35,67},{4,100... | collective-permute-start | bytes 589832 | tf_op jit(solution)/shard_map/ppermute | solution.py:74
  752.2 57.0 %collective-permute-start.108 = (bf16[96,1024]{0,1:T(8,128)(2,1)S(1)}, bf16[96,1024]{0,1:T(8,128)(2,1)S(1)}, u32[]{:S(2)}, u32[]{:S(2)}) collective-permute-start(bf16[96,1024]{0,1:T(8,128)(2,1)S(1)} %copy.509), channel_id=1, source_target_pairs={{64,96},{96,64},{65,97},{97,65},{66,98},{98,66},{67,99},{99,67},{6... | collective-permute-start | bytes 589832 | tf_op jit(solution)/shard_map/ppermute | solution.py:74
  753.1 14.0 %collective-permute-start.109 = (bf16[96,1024]{0,1:T(8,128)(2,1)S(1)}, bf16[96,1024]{0,1:T(8,128)(2,1)S(1)}, u32[]{:S(2)}, u32[]{:S(2)}) collective-permute-start(bf16[96,1024]{0,1:T(8,128)(2,1)S(1)} %copy.508), channel_id=1, source_target_pairs={{0,64},{32,96},{1,65},{33,97},{2,66},{34,98},{3,67},{35,99},{4,68}... | collective-permute-start | bytes 589832 | tf_op jit(solution)/shard_map/ppermute | solution.py:74
  757.7 56.9 %collective-permute-start.106 = (bf16[96,1024]{0,1:T(8,128)(2,1)S(1)}, bf16[96,1024]{0,1:T(8,128)(2,1)S(1)}, u32[]{:S(2)}, u32[]{:S(2)}) collective-permute-start(bf16[96,1024]{0,1:T(8,128)(2,1)S(1)} %copy.507), channel_id=1, source_target_pairs={{64,32},{96,0},{65,33},{97,1},{66,34},{98,2},{67,35},{99,3},{68,36... | collective-permute-start | bytes 589832 | tf_op jit(solution)/shard_map/ppermute | solution.py:74
  759.0 60.6 %collective-permute-start.104 = (bf16[96,1024]{0,1:T(8,128)(2,1)S(1)}, bf16[96,1024]{0,1:T(8,128)(2,1)S(1)}, u32[]{:S(2)}, u32[]{:S(2)}) collective-permute-start(bf16[96,1024]{0,1:T(8,128)(2,1)S(1)} %copy.507), channel_id=1, source_target_pairs={{0,32},{32,0},{1,33},{33,1},{2,34},{34,2},{3,35},{35,3},{4,36},{36... | collective-permute-start | bytes 589832 | tf_op jit(solution)/shard_map/ppermute | solution.py:74
  765.8 51.1 %collective-permute-start.105 = (bf16[96,1024]{0,1:T(8,128)(2,1)S(1)}, bf16[96,1024]{0,1:T(8,128)(2,1)S(1)}, u32[]{:S(2)}, u32[]{:S(2)}) collective-permute-start(bf16[96,1024]{0,1:T(8,128)(2,1)S(1)} %copy.506), channel_id=1, source_target_pairs={{64,0},{96,32},{65,1},{97,33},{66,2},{98,34},{67,3},{99,35},{68,4}... | collective-permute-start | bytes 589832 | tf_op jit(solution)/shard_map/ppermute | solution.py:74
  767.1 53.8 %collective-permute-start.114 = (bf16[96,3456]{1,0:T(8,128)(2,1)}, bf16[96,3456]{1,0:T(8,128)(2,1)S(1)}, u32[]{:S(2)}, u32[]{:S(2)}) collective-permute-start(bf16[96,3456]{1,0:T(8,128)(2,1)} %get-tuple-element.162), channel_id=1, source_target_pairs={{64,96},{96,64},{65,97},{97,65},{66,98},{98,66},{67,99},{99,67},{6... | collective-permute-start | bytes 1990664 | tf_op jit(solution)/shard_map/ppermute | solution.py:74
  809.2 20.7 %collective-permute-start.118 = (bf16[96,3456]{1,0:T(8,128)(2,1)}, bf16[96,3456]{1,0:T(8,128)(2,1)}, u32[]{:S(2)}, u32[]{:S(2)}) collective-permute-start(bf16[96,3456]{1,0:T(8,128)(2,1)} %get-tuple-element.162), channel_id=1, source_target_pairs={{0,96},{32,64},{1,97},{33,65},{2,98},{34,66},{3,99},{35,67},{4,100... | collective-permute-start | bytes 1990664 | tf_op jit(solution)/shard_map/ppermute | solution.py:74
  814.7 16.9 %collective-permute-start.117 = (bf16[96,3456]{1,0:T(8,128)(2,1)}, bf16[96,3456]{1,0:T(8,128)(2,1)}, u32[]{:S(2)}, u32[]{:S(2)}) collective-permute-start(bf16[96,3456]{1,0:T(8,128)(2,1)} %get-tuple-element.161), channel_id=1, source_target_pairs={{0,64},{32,96},{1,65},{33,97},{2,66},{34,98},{3,67},{35,99},{4,68}... | collective-permute-start | bytes 1990664 | tf_op jit(solution)/shard_map/ppermute | solution.py:74
  816.8 29.3 %collective-permute-start.112 = (bf16[96,3456]{1,0:T(8,128)(2,1)}, bf16[96,3456]{1,0:T(8,128)(2,1)}, u32[]{:S(2)}, u32[]{:S(2)}) collective-permute-start(bf16[96,3456]{1,0:T(8,128)(2,1)} %get-tuple-element.160), channel_id=1, source_target_pairs={{0,32},{32,0},{1,33},{33,1},{2,34},{34,2},{3,35},{35,3},{4,36},{36... | collective-permute-start | bytes 1990664 | tf_op jit(solution)/shard_map/ppermute | solution.py:74
  819.6 33.8 %collective-permute-start.116 = (bf16[96,3456]{1,0:T(8,128)(2,1)}, bf16[96,3456]{1,0:T(8,128)(2,1)}, u32[]{:S(2)}, u32[]{:S(2)}) collective-permute-start(bf16[96,3456]{1,0:T(8,128)(2,1)} %get-tuple-element.160), channel_id=1, source_target_pairs={{64,32},{96,0},{65,33},{97,1},{66,34},{98,2},{67,35},{99,3},{68,36... | collective-permute-start | bytes 1990664 | tf_op jit(solution)/shard_map/ppermute | solution.py:74
  821.8 31.6 %collective-permute-start.115 = (bf16[96,3456]{1,0:T(8,128)(2,1)}, bf16[96,3456]{1,0:T(8,128)(2,1)}, u32[]{:S(2)}, u32[]{:S(2)}) collective-permute-start(bf16[96,3456]{1,0:T(8,128)(2,1)} %get-tuple-element.159), channel_id=1, source_target_pairs={{64,0},{96,32},{65,1},{97,33},{66,2},{98,34},{67,3},{99,35},{68,4}... | collective-permute-start | bytes 1990664 | tf_op jit(solution)/shard_map/ppermute | solution.py:74
  (211 other events, 2055.5 us)
Sparse Core Ops, SparseCore 0:
  51.5 77.3 all-gather.3
  130.6 58.7 all-gather.7
  191.1 28.7 all-gather.5
  634.0 26.9 reduce-scatter.14
  663.3 25.4 reduce-scatter.12
  691.1 57.2 reduce-scatter.10
  751.0 55.6 reduce-scatter.8

commit v2 on v1

v2 whole, which is shorter than its diff:
```python
import jax
import jax.numpy as jnp
from jax import lax
from jax.experimental import pallas as pl
from jax.experimental.pallas import tpu as pltpu
from jax.sharding import Mesh
from jax.sharding import PartitionSpec as P

D = 1536
HD = 128
E = 16
HALF_E = 8
GROUPS = 3
LEN = 256
ROWS = 64
DBLK = 96
HALF = D // 2
ROUTES = 2 * LEN

NORM_EPSILON = 1e-05
MASK_VALUE = -1e30
SCALE = HD**-0.5

BF = jnp.bfloat16
F32 = jnp.float32

QKV = 640
ATT = 1024
ATT_PAD = 1152
BLOCKS = 9
STEPS = 3
STEP = 3 * HD
UP = BLOCKS * 256
DOWN = BLOCKS * 128
PIECE = UP + DOWN
WIDE = D + HD
SMALL = 24

SECTION = ("section",)
TENSOR = ("tensor",)
GROUP = ("section", "tensor")
CORE = ("core",)
ROW = ("z",)
SIDE = ("section", "xhi")


def dot(a, b, contract):
    return lax.dot_general(a, b, ((contract[:1], contract[1:]), ((), ())), preferred_element_type=F32)


def nn(a, b):
    return dot(a, b, (1, 0))


def nt(a, b):
    return dot(a, b, (1, 1))


def tn(a, b):
    return dot(a, b, (0, 0))


def move(block, axes, target, only=None):
    sizes = [lax.axis_size(axis) for axis in axes]
    pairs = []

    def flat(place):
        index = 0
        for size, at in zip(sizes, place):
            index = index * size + at % size
        return index

    def walk(place):
        if len(place) == len(sizes):
            if only is None or only(*place):
                pairs.append((flat(place), flat(target(*place))))
            return
        for at in range(sizes[len(place)]):
            walk(place + (at,))

    walk(())
    return lax.ppermute(block, axes, pairs)

VMEM = pl.BlockSpec(memory_space=pltpu.VMEM)
SMEM = pl.BlockSpec(memory_space=pltpu.SMEM)


def shaped(shape, dtype=BF):
    return jax.ShapeDtypeStruct(shape, dtype)


def run(kernel, outs, operands, scalars=0, flops=0, in_specs=None, out_specs=None, grid=(), scratch=()):
    if in_specs is None:
        in_specs = [SMEM] * scalars + [VMEM] * (len(operands) - scalars)
    if out_specs is None:
        out_specs = [VMEM] * len(outs)
    moved = sum(x.size * x.dtype.itemsize for x in list(operands) + list(outs))
    return pl.pallas_call(
        kernel,
        out_shape=list(outs),
        in_specs=in_specs,
        out_specs=out_specs,
        grid=grid,
        scratch_shapes=list(scratch),
        compiler_params=pltpu.CompilerParams(vmem_limit_bytes=48 * 1024 * 1024),
        cost_estimate=pl.CostEstimate(flops=flops, bytes_accessed=moved, transcendentals=0),
    )(*operands)


def together(*values):
    return lax.optimization_barrier(values)


def tensor_gather(rows):
    return [rows] + [move(rows, TENSOR, lambda t, k=k: (t - k,)) for k in (1, 2, 3)]


def tensor_send(parts):
    return [move(parts[k], TENSOR, lambda t, k=k: (t + k,)) for k in (1, 2, 3)]


def group_exchange(rows):
    return lax.all_to_all(rows, GROUP, 0, 0, tiled=True)


def rolled(stacked, shift):
    n = stacked.shape[0]
    return lax.dynamic_slice_in_dim(jnp.concatenate([stacked, stacked], axis=0), shift, n, 0)


def rms_factor(rows):
    return lax.rsqrt(jnp.mean(rows * rows, axis=-1, keepdims=True) + NORM_EPSILON)


def norm_backward(rows, gain, upstream):
    factor = rms_factor(rows)
    unit = rows * factor
    scaled = upstream * gain
    grad = factor * (scaled - unit * jnp.mean(scaled * unit, axis=-1, keepdims=True))
    return grad, jnp.sum(upstream * unit, axis=0, keepdims=True)


def add_up(refs):
    total = refs[0][...].astype(F32)
    for ref in refs[1:]:
        total = total + ref[...].astype(F32)
    return total


def block(index):
    return slice(index * ROWS, (index + 1) * ROWS)


def add_blocks(ref):
    total = ref[block(0), :].astype(F32)
    for index in range(1, 8):
        total = total + ref[block(index), :].astype(F32)
    return total


def head(index):
    return slice(index * HD, (index + 1) * HD)


KEYS = head(GROUPS)
VALUES = head(GROUPS + 1)


def attention_forward_kernel(t_ref, *refs):
    hidden, (w0, w1) = refs[:4], refs[4:6]
    parts, (normed_ref, qkv_ref, probs_ref, attended_ref, small_ref) = refs[6:10], refs[10:]
    for at, w in ((0, w0), (HALF, w1)):
        small_ref[:, at : at + HALF] = w[:, ATT:].astype(F32).T[:SMALL]
    for index, ref in enumerate(hidden):
        rows = ref[...].astype(F32)
        normed_ref[block(index), :] = (rows * rms_factor(rows) * small_ref[0:1, :]).astype(BF)
    normed = normed_ref[...]
    qkv = nn(normed[:, :HALF], w0[:, :QKV]) + nn(normed[:, HALF:], w1[:, :QKV])
    qkv = qkv.astype(BF)
    qkv_ref[...] = qkv

    def position(axis):
        return (t_ref[0] * ROWS + lax.broadcasted_iota(jnp.int32, (LEN, LEN), axis)) & (LEN - 1)

    causal = position(1) <= position(0)
    for g in range(GROUPS):
        scores = jnp.where(causal, nt(qkv[:, head(g)], qkv[:, KEYS]) * SCALE, MASK_VALUE)
        shifted = jnp.exp(scores - jnp.max(scores, axis=-1, keepdims=True))
        probs = (shifted / jnp.sum(shifted, axis=-1, keepdims=True)).astype(BF)
        probs_ref[g] = probs
        attended_ref[:, head(g)] = nn(probs, qkv[:, VALUES]).astype(BF)
    attended = attended_ref[...]
    for at, w in ((0, w0), (HALF, w1)):
        out = nt(attended, w[:, QKV:ATT]).astype(BF)
        for index, part in enumerate(parts):
            part[:, at : at + HALF] = out[block(index)]


def attention_forward(t, hidden_blocks, weights):
    outs = [shaped((ROWS, D))] * 4
    outs += [shaped((LEN, D)), shaped((LEN, QKV)), shaped((GROUPS, LEN, LEN)), shaped((LEN, STEP))]
    outs += [shaped((SMALL, D), F32)]
    flops = 2 * LEN * D * ATT + 4 * GROUPS * LEN * LEN * HD
    got = run(attention_forward_kernel, outs, [t, *hidden_blocks, *weights], 1, flops)
    return got[:4], got[4:]


def attention_backward_kernel(*refs):
    grads, (w0, w1, qkv_ref, probs_ref) = refs[:4], refs[4:8]
    parts, (rows_ref, qkv_grad_ref) = refs[8:12], refs[12:]
    for index, ref in enumerate(grads):
        rows_ref[block(index), :] = ref[...]
    rows = rows_ref[...]
    attended_grad = nn(rows[:, :HALF], w0[:, QKV:ATT]) + nn(rows[:, HALF:], w1[:, QKV:ATT])
    attended_grad = attended_grad.astype(BF)
    qkv = qkv_ref[...]
    key_grad = jnp.zeros((LEN, HD), F32)
    value_grad = jnp.zeros((LEN, HD), F32)
    for g in range(GROUPS):
        probs = probs_ref[g]
        upstream = attended_grad[:, head(g)]
        value_grad = value_grad + tn(probs, upstream)
        prob_grad = nt(upstream, qkv[:, VALUES])
        wide = probs.astype(F32)
        score_grad = wide * (prob_grad - jnp.sum(wide * prob_grad, axis=-1, keepdims=True))
        score_grad = (score_grad * SCALE).astype(BF)
        qkv_grad_ref[:, head(g)] = nn(score_grad, qkv[:, KEYS]).astype(BF)
        key_grad = key_grad + tn(score_grad, qkv[:, head(g)])
    qkv_grad_ref[:, KEYS] = key_grad.astype(BF)
    qkv_grad_ref[:, VALUES] = value_grad.astype(BF)
    qkv_grad = qkv_grad_ref[...]
    for at, w in ((0, w0), (HALF, w1)):
        out = nt(qkv_grad, w[:, :QKV]).astype(BF)
        for index, part in enumerate(parts):
            part[:, at : at + HALF] = out[block(index)]


def attention_backward(grad_blocks, weights, qkv, probs):
    outs = [shaped((ROWS, D))] * 4 + [shaped((LEN, D)), shaped((LEN, QKV))]
    flops = 2 * LEN * D * ATT + 10 * GROUPS * LEN * LEN * HD
    got = run(attention_backward_kernel, outs, [*grad_blocks, *weights, qkv, probs], 0, flops)
    return got[:4], got[4], got[5]


def attention_weights_kernel(normed, rows, qkv_grad, attended, *refs):
    out = refs[-1]
    for columns, left, right in (
        (slice(0, QKV), normed, qkv_grad),
        (slice(QKV, ATT), rows, attended),
    ):
        total = tn(left[...], right[...])
        if len(refs) > 1:
            total = total + refs[0][:, columns].astype(F32)
        out[:, columns] = total.astype(BF)


def attention_weights(half, normed, rows, qkv_grad, attended, *other):
    def full(*shape):
        return pl.BlockSpec(shape, lambda i: (0, 0))

    cut = pl.BlockSpec((LEN, HALF), lambda i: (0, half))
    in_specs = [cut, cut, full(LEN, QKV), full(LEN, STEP)] + [full(HALF, ATT)] * len(other)
    return run(
        attention_weights_kernel,
        [shaped((HALF, ATT))],
        [normed, rows, qkv_grad, attended, *other],
        flops=2 * HALF * LEN * ATT,
        in_specs=in_specs,
        out_specs=[full(HALF, ATT)],
        grid=(1,),
    )[0]


def gate_column(gates, section, number):
    lane = lax.broadcasted_iota(jnp.int32, gates.shape, 1)
    picked = jnp.where(lane == section * HALF_E + number, gates, 0.0)
    return jnp.where(number == HALF_E, 1.0, jnp.sum(picked, axis=1, keepdims=True))


def ffn_forward_kernel(s_ref, t_ref, rows_ref, router, mask_ref, up0, up1, down0, down1, *refs):
    step = pl.program_id(0)
    part, gates_ref, own_ref, gate_up_ref, gated_ref, total = refs

    @pl.when(step == 0)
    def _():
        logits = nt(rows_ref[...], router[...])
        named = mask_ref[...] > 0.5
        top = jnp.max(jnp.where(named, logits, MASK_VALUE), axis=-1, keepdims=True)
        shifted = jnp.where(named, jnp.exp(jnp.where(named, logits - top, 0.0)), 0.0)
        gates_ref[...] = shifted / jnp.sum(shifted, axis=-1, keepdims=True)
        own_ref[...] = gates_ref[pl.ds((4 * s_ref[0] + t_ref[0]) * ROWS, ROWS), :]
        total[...] = jnp.zeros_like(total)

    gate_up = nn(rows_ref[:, :HALF], up0[...]) + nn(rows_ref[:, HALF:], up1[...])
    gate_up_ref[...] = gate_up.astype(BF)
    gates = gates_ref[...]
    for i in range(3):
        gate_part, up_part = gate_up[:, head(i)], gate_up[:, head(3 + i)]
        hidden = gate_part * jax.nn.sigmoid(gate_part) * up_part
        gated_ref[:, head(i)] = (hidden * gate_column(gates, s_ref[0], 3 * step + i)).astype(BF)
    gated = gated_ref[...]
    total[:, :HALF] += nt(gated, down0[...])
    total[:, HALF:] += nt(gated, down1[...])

    @pl.when(step == STEPS - 1)
    def _():
        part[...] = total[...].astype(BF)


def fixed(*shape):
    return pl.BlockSpec(shape, lambda j: (0,) * len(shape))


def by_step(rows, columns, first=0):
    return pl.BlockSpec((rows, columns), lambda j: (0, first + j))


def ffn_weight_specs():
    return [by_step(HALF, 2 * STEP)] * 2 + [by_step(HALF, STEP, UP // STEP)] * 2


def ffn_forward(s, t, rows, router, mask, weights):
    return run(
        ffn_forward_kernel,
        [
            shaped((ROUTES, D)),
            shaped((ROUTES, E), F32),
            shaped((ROWS, E), F32),
            shaped((ROUTES, UP)),
            shaped((ROUTES, DOWN)),
        ],
        [s, t, rows, router, mask, weights[0], weights[1], weights[0], weights[1]],
        flops=2 * ROUTES * D * PIECE,
        in_specs=[SMEM, SMEM, fixed(ROUTES, D), fixed(E, D), fixed(ROUTES, E)] + ffn_weight_specs(),
        out_specs=[fixed(ROUTES, D), fixed(ROUTES, E), fixed(ROWS, E)]
        + [by_step(ROUTES, 2 * STEP), by_step(ROUTES, STEP)],
        grid=(STEPS,),
        scratch=[pltpu.VMEM((ROUTES, D), F32)],
    )


def ffn_backward_kernel(s_ref, rows_ref, gates_ref, gate_up_ref, up0, up1, down0, down1, *refs):
    step = pl.program_id(0)
    part, grad_ref, total, products = refs

    @pl.when(step == 0)
    def _():
        total[...] = jnp.zeros_like(total)
        products[...] = jnp.zeros_like(products)

    hidden_grad = nn(rows_ref[:, :HALF], down0[...]) + nn(rows_ref[:, HALF:], down1[...])
    gates = gates_ref[...]
    lane = lax.broadcasted_iota(jnp.int32, (ROUTES, HD), 1)
    for i in range(3):
        number = 3 * step + i
        gate_part = gate_up_ref[:, head(i)].astype(F32)
        up_part = gate_up_ref[:, head(3 + i)].astype(F32)
        sigmoid = jax.nn.sigmoid(gate_part)
        silu = gate_part * sigmoid
        upstream = hidden_grad[:, head(i)]
        product = jnp.sum(silu * up_part * upstream, axis=1, keepdims=True)
        at = jnp.where(number < HALF_E, s_ref[0] * HALF_E + number, -1)
        products[...] = jnp.where(lane == at, product, products[...])
        upstream = upstream * gate_column(gates, s_ref[0], number)
        gate_grad = upstream * up_part * sigmoid * (1.0 + gate_part * (1.0 - sigmoid))
        grad_ref[:, head(i)] = gate_grad.astype(BF)
        grad_ref[:, head(3 + i)] = (upstream * silu).astype(BF)
    grad = grad_ref[...]
    total[:, :HALF] += nt(grad, up0[...])
    total[:, HALF:] += nt(grad, up1[...])

    @pl.when(step == STEPS - 1)
    def _():
        whole = products[...]
        high = whole.astype(BF).astype(F32)
        extra = high + pltpu.roll(whole - high, E, 1)
        part[:, :D] = total[...].astype(BF)
        part[:, D:] = extra.astype(BF)


def ffn_backward(s, rows, gates, gate_up, weights):
    return run(
        ffn_backward_kernel,
        [shaped((ROUTES, WIDE)), shaped((ROUTES, UP))],
        [s, rows, gates, gate_up, weights[0], weights[1], weights[0], weights[1]],
        flops=2 * ROUTES * D * PIECE,
        in_specs=[SMEM, fixed(ROUTES, D), fixed(ROUTES, E), by_step(ROUTES, 2 * STEP)]
        + ffn_weight_specs(),
        out_specs=[fixed(ROUTES, WIDE), by_step(ROUTES, 2 * STEP)],
        grid=(STEPS,),
        scratch=[pltpu.VMEM((ROUTES, D), F32), pltpu.VMEM((ROUTES, HD), F32)],
    )


def ffn_weights_kernel(rows, grad_rows, gate_up_grad, gated, *refs):
    step = pl.program_id(0)
    out = refs[-1]

    def store(total):
        if len(refs) > 1:
            total = total + refs[0][...].astype(F32)
        out[...] = total.astype(BF)

    @pl.when(step < 2)
    def _():
        store(tn(rows[...], gate_up_grad[...]))

    @pl.when(step == 2)
    def _():
        store(tn(grad_rows[...], gated[...]))


def ffn_weights(half, rows, grad_rows, gate_up_grad, gated, *other):
    cut = pl.BlockSpec((ROUTES, HALF), lambda j: (0, half))
    third = pl.BlockSpec((ROUTES, DOWN), lambda j: (0, jnp.minimum(j, 1)))
    return run(
        ffn_weights_kernel,
        [shaped((HALF, PIECE))],
        [rows, grad_rows, gate_up_grad, gated, *other],
        flops=2 * ROUTES * HALF * PIECE,
        in_specs=[cut, cut, third, fixed(ROUTES, DOWN)] + [by_step(HALF, DOWN)] * len(other),
        out_specs=[by_step(HALF, DOWN)],
        grid=(3,),
    )[0]


def mid_kernel(hidden, gain, *refs):
    mid_ref, normed_ref, copies = refs[-3:]
    mid = hidden[...].astype(F32) + add_up(refs[:-3])
    mid_ref[...] = mid
    normed = (mid * rms_factor(mid) * gain[...]).astype(BF)
    normed_ref[...] = normed
    for index in range(8):
        copies[block(index), :] = normed


def result_kernel(mid, got, out):
    out[...] = (mid[...] + add_blocks(got)).astype(BF)


def mid_backward_kernel(mid, own_gates, out_grad, gain, router, normed, got, *refs):
    mid_grad_ref, low_ref, gain_grad, router_grad = refs
    total = add_blocks(got)
    extra = total[:, D:]
    gate_grad = (extra + pltpu.roll(extra, HD - E, 1))[:, :E]
    own = own_gates[...]
    logits_grad = own * (gate_grad - jnp.sum(own * gate_grad, axis=1, keepdims=True))
    logits_grad = logits_grad.astype(BF)
    upstream = total[:, :D] + nn(logits_grad, router[...])
    grad, gain_grad[...] = norm_backward(mid[...], gain[...], upstream)
    router_grad[...] = tn(logits_grad, normed[...])
    mid_grad = out_grad[...].astype(F32) + grad
    mid_grad_ref[...] = mid_grad
    low_ref[...] = mid_grad.astype(BF)


def hidden_backward_kernel(hidden, gain, mid_grad, *refs):
    out, gain_grad, copies = refs[-3:]
    grad, gain_grad[...] = norm_backward(hidden[...].astype(F32), gain[...], add_up(refs[:-3]))
    low = (mid_grad[...] + grad).astype(BF)
    out[...] = low
    for index in range(8):
        copies[block(index), :] = low


def send_home(blocks, home):
    blocks = blocks.reshape(2, DBLK, -1)
    beside = move(blocks[1], SIDE, lambda s, x: (s, x + 1), lambda s, x: s == home)
    straight = move(blocks[0], SIDE, lambda s, x: (s + 1, x), lambda s, x: s != home)
    across = move(blocks[1], SIDE, lambda s, x: (s + 1, x + 1), lambda s, x: s != home)
    return blocks[0], beside, straight, across


def from_home(sent):
    own, beside, straight, across = [x.astype(F32) for x in sent]
    return own + beside, straight + across


def swap_core(part):
    return move(part, CORE, lambda c: (1 - c,))


def sum_row(part):
    return lax.psum_scatter(part, "z", scatter_dimension=0, tiled=True)


def gather_row(part):
    return lax.all_gather(part, "z", axis=0, tiled=True)


def per_device(
    tokens,
    cotangent,
    route_experts,
    route_slots,
    gain_attn,
    w_query,
    w_key,
    w_value,
    w_out,
    gain_ffn,
    w_router,
    w_shared_in,
    w_shared_down,
    w_expert_in,
    w_expert_down,
):
    s = lax.axis_index("section")
    xhi = lax.axis_index("xhi")
    core = lax.axis_index("core")
    z = lax.axis_index("z")
    t = lax.axis_index("tensor")
    first = s == 0
    s_arg = s.astype(jnp.int32)[None]
    t_arg = t.astype(jnp.int32)[None]

    small = jnp.concatenate(
        [gain_attn[0][:, None], gain_ffn[0][:, None], w_router[0], jnp.zeros((24, 110), BF)], axis=1
    )
    small = rolled(jnp.stack(tensor_gather(small)), (4 - t) % 4).reshape(DBLK, HD)
    att_piece = jnp.concatenate([w_query[0], w_key[0], w_value[0], w_out[0].T, small], axis=1)

    expert_in = w_expert_in[0].reshape(DBLK, 2, HALF_E, 2, HD)
    shared_in = w_shared_in[0].reshape(DBLK, 2, 2, HD)
    expert_down = w_expert_down[0].transpose(2, 0, 1).reshape(DBLK, 2, HALF_E * HD)
    shared_down = w_shared_down[0].T.reshape(DBLK, 2, HD)

    def ffn_piece(part):
        up = jnp.concatenate([expert_in[:, part], shared_in[:, None, :, part]], axis=1)
        up = up.reshape(DBLK, STEPS, 3, 2, HD).swapaxes(2, 3).reshape(DBLK, UP)
        return jnp.concatenate([up, expert_down[:, part], shared_down[:, part]], axis=1)

    ffn_own = jnp.where(first, ffn_piece(0), ffn_piece(1))
    ffn_other = jnp.where(first, ffn_piece(1), ffn_piece(0))

    att_beside = move(att_piece, SIDE, lambda s, x: (s, x + 1))
    att_straight = move(att_piece, SIDE, lambda s, x: (s + 1, x))
    att_across = move(att_piece, SIDE, lambda s, x: (s + 1, x + 1))
    att_beside, att_straight, att_across, ffn_own, ffn_other = together(
        att_beside, att_straight, att_across, ffn_own, ffn_other
    )
    att_same = jnp.concatenate([att_piece, att_beside], axis=0)
    att_else = jnp.concatenate([att_straight, att_across], axis=0)
    att_pairs = [jnp.where(first, att_same, att_else), jnp.where(first, att_else, att_same)]
    ffn_straight = move(ffn_other, SIDE, lambda s, x: (s + 1, x))
    ffn_across = move(ffn_other, SIDE, lambda s, x: (s + 1, x + 1))
    ffn_beside0 = move(ffn_own, SIDE, lambda s, x: (s, x + 1), lambda s, x: s == 0)
    ffn_else = jnp.concatenate([ffn_straight, ffn_across], axis=0)
    ffn_pair0 = jnp.where(first, jnp.concatenate([ffn_own, ffn_beside0], axis=0), ffn_else)

    att_row0 = gather_row(att_pairs[0])
    ffn_row0 = gather_row(ffn_pair0)

    place = jnp.arange(D, dtype=jnp.int32)
    at_core = (place // HALF + core) % 2
    at_z = (place // (2 * DBLK)) % 4
    at_x = (place // DBLK + xhi) % 2
    column = at_x * HALF + at_z * (2 * DBLK) + at_core * DBLK + place % DBLK
    order = (place[:, None] == column[None, :]).astype(BF)

    own_tokens = lax.dynamic_index_in_dim(tokens, s, 0, keepdims=False)
    own_cotangent = lax.dynamic_index_in_dim(cotangent, s, 0, keepdims=False)
    own_rows = nn(jnp.concatenate([own_tokens, own_cotangent], axis=0), order).astype(BF)
    hidden_blocks = tensor_gather(own_rows[:ROWS])
    own_cotangent = own_rows[ROWS:]

    named = jnp.sum((route_experts[0][:, :, :, None] == jnp.arange(E)).astype(F32), axis=2)
    named = named.astype(BF).reshape(ROUTES, E)
    named_else = move(named, SECTION, lambda s: (s + 1,))

    masks = [jnp.where(s == layer, named, named_else).astype(F32) for layer in (0, 1)]

    att_row0, masks[0], masks[1], *hidden_blocks = together(
        att_row0, masks[0], masks[1], *hidden_blocks
    )
    att_w = [(att_row0, swap_core(att_row0)), None]
    ffn_w = [None, None]
    layer_values = []
    kept = []
    for layer in (0, 1):
        parts, att_saved = attention_forward(t_arg, hidden_blocks, att_w[layer])
        normed, *att_saved, small = att_saved
        attn_gain, ffn_gain, router = small[0:1], small[1:2], small[2 : 2 + E].astype(BF)
        mid, normed_ffn, copies = run(
            mid_kernel,
            [shaped((ROWS, D), F32), shaped((ROWS, D)), shaped((ROUTES, D))],
            [hidden_blocks[0], ffn_gain, parts[0], *tensor_send(parts)],
        )
        rows = group_exchange(copies)
        if layer == 0:
            normed, own_cotangent = together(normed, own_cotangent)
            grad_rows = group_exchange(jnp.tile(own_cotangent, (8, 1)))
            ffn_row0, rows, grad_rows, att_pair1, ffn_own, ffn_else = together(
                ffn_row0, rows, grad_rows, att_pairs[1], ffn_own, ffn_else
            )
            ffn_w[0] = (ffn_row0, swap_core(ffn_row0))
            ffn_beside1 = move(ffn_own, SIDE, lambda s, x: (s, x + 1), lambda s, x: s == 1)
            ffn_pair1 = jnp.where(first, ffn_else, jnp.concatenate([ffn_own, ffn_beside1], axis=0))
            att_row1 = gather_row(att_pair1)
            ffn_row1 = gather_row(ffn_pair1)
        else:
            ffn_row1, mid = together(ffn_row1, mid)
            ffn_w[1] = (ffn_row1, swap_core(ffn_row1))
        part, gates, own_gates, gate_up, gated = ffn_forward(
            s_arg, t_arg, rows, router, masks[layer], ffn_w[layer]
        )
        result = run(result_kernel, [shaped((ROWS, D))], [mid, group_exchange(part)])[0]
        layer_values.append(result)
        kept.append((hidden_blocks[0], attn_gain, normed, *att_saved))
        kept.append((mid, ffn_gain, router, normed_ffn, rows, gates, own_gates, gate_up, gated))
        if layer == 0:
            hidden_blocks = tensor_gather(result)
            att_row1, own_gates = together(att_row1, own_gates)
            kept[1] = (*kept[1][:6], own_gates, gate_up, gated)
            att_w[1] = (att_row1, swap_core(att_row1))

    in_grads = [None, None]
    small_grads = [None, None]
    ffn_sums = [None, None]
    att_sums = [None, None]
    out_low = own_cotangent
    for layer in (1, 0):
        hidden, attn_gain, normed, qkv, probs, attended = kept[2 * layer]
        mid, ffn_gain, router, normed_ffn, rows, gates, own_gates, gate_up, gated = kept[2 * layer + 1]
        part, gate_up_grad = ffn_backward(s_arg, grad_rows, gates, gate_up, ffn_w[layer])
        ffn_parts = (rows, grad_rows, gate_up_grad, gated)
        other = None
        if layer == 0:
            part, other = together(part, ffn_weights(1, *ffn_parts))
            other = swap_core(other)
        mid_grad, mid_low, grad_gain_ffn, grad_router = run(
            mid_backward_kernel,
            [
                shaped((ROWS, D), F32),
                shaped((ROWS, D)),
                shaped((1, D), F32),
                shaped((E, D), F32),
            ],
            [mid, own_gates, out_low, ffn_gain, router, normed_ffn, group_exchange(part)],
        )
        mid_blocks = tensor_gather(mid_low)
        if layer == 1:
            *mid_blocks, other = together(*mid_blocks, ffn_weights(1, *ffn_parts))
            other = swap_core(other)
        else:
            gate_up_grad, ffn_sums[1] = together(gate_up_grad, ffn_sums[1])
            own = ffn_weights(0, rows, grad_rows, gate_up_grad, gated, other)
            *mid_blocks, own = together(*mid_blocks, own)
            ffn_sums[0] = sum_row(own)
        parts, mid_rows, qkv_grad = attention_backward(mid_blocks, att_w[layer], qkv, probs)
        got = tensor_send(parts)
        att_parts = (normed, mid_rows, qkv_grad, attended)
        att_other = attention_weights(1, *att_parts)
        if layer == 1:
            own = ffn_weights(0, *ffn_parts, other)
            *got, att_other, own = together(*got, att_other, own)
            ffn_sums[1] = sum_row(own)
        else:
            *got, att_other = together(*got, att_other)
        out_low, grad_gain_attn, copies = run(
            hidden_backward_kernel,
            [shaped((ROWS, D)), shaped((1, D), F32), shaped((ROUTES, D))],
            [hidden, attn_gain, mid_grad, parts[0], *got],
        )
        in_grads[layer] = out_low
        small_grads[layer] = jnp.concatenate([grad_gain_attn, grad_gain_ffn, grad_router], axis=0)
        att_own = attention_weights(0, *att_parts, swap_core(att_other))
        if layer == 1:
            grad_rows, att_own = together(group_exchange(copies), att_own)
            att_sums[1] = sum_row(att_own)
    att_blocks = rolled(att_own.reshape(4, 2 * DBLK, ATT), z)
    total = att_blocks[0].astype(F32)
    for k in (1, 2, 3):
        total = total + move(att_blocks[k], ROW, lambda at, k=k: (at + k,)).astype(F32)
    att_sums[0] = total.astype(BF)
    out_low, ffn_sums[1], att_sums[1] = together(in_grads[0], ffn_sums[1], att_sums[1])
    in_grads[0] = out_low
    ffn_home = [None, send_home(ffn_sums[1], 1)]
    att_home = [None, send_home(att_sums[1], 1)]
    att_home[0] = send_home(att_sums[0], 0)
    ffn_home[0] = send_home(ffn_sums[0], 0)

    def both_sequences(values):
        low = nt(jnp.concatenate(values, axis=0), order).astype(BF).reshape(2, ROWS, D)
        mine = jnp.where(first, low[0], low[1])
        got = move(jnp.where(first, low[1], low[0]), SECTION, lambda s: (s + 1,))
        return jnp.where(first, jnp.stack([mine, got]), jnp.stack([got, mine]))[None]

    values_out = both_sequences(layer_values)
    grads_in = both_sequences(in_grads)

    att_home = [sum(from_home(sent)) for sent in att_home]
    ffn_home = [from_home(sent) for sent in ffn_home]
    att = jnp.where(first, att_home[0], att_home[1])
    ffn_mine = jnp.where(first, ffn_home[0][0], ffn_home[1][0])
    ffn_got = jnp.where(first, ffn_home[0][1], ffn_home[1][1])
    ffn_parts = (jnp.where(first, ffn_mine, ffn_got), jnp.where(first, ffn_got, ffn_mine))

    values = jnp.concatenate(small_grads, axis=0).T.reshape(2, 4, 2, DBLK, 2 * (2 + E))
    values = values[0] + move(values[1], CORE, lambda c: (1 - c,))
    values = rolled(values, z)
    total = values[0]
    for k in (1, 2, 3):
        total = total + move(values[k], ROW, lambda at, k=k: (at + k,))
    total = total[0] + move(total[1], ("xhi",), lambda x: (x + 1,))
    halves = total.reshape(DBLK, 2, 2 + E).swapaxes(0, 1)
    mine = jnp.where(first, halves[0], halves[1])
    theirs = jnp.where(first, halves[1], halves[0])
    total = mine + move(theirs, SECTION, lambda s: (s + 1,))
    total = rolled(total.reshape(4, DBLK // 4, 2 + E), t)
    small_sum = total[0]
    for got in tensor_send([total[k] for k in range(4)]):
        small_sum = small_sum + got

    ups, downs = [], []
    for part in ffn_parts:
        up = part[:, :UP].reshape(DBLK, STEPS, 2, 3, HD).swapaxes(2, 3)
        ups.append(up.reshape(DBLK, BLOCKS, 2, HD))
        downs.append(part[:, UP:].reshape(DBLK, BLOCKS, HD))
    grad_expert_in = jnp.concatenate([up[:, :HALF_E] for up in ups], axis=1)
    grad_shared_in = jnp.concatenate([up[:, HALF_E] for up in ups], axis=2)
    grad_expert_down = jnp.concatenate([down[:, :HALF_E] for down in downs], axis=1)
    grad_shared_down = jnp.concatenate([down[:, HALF_E] for down in downs], axis=1)
    return (
        values_out,
        grads_in,
        small_sum[:, 0][None],
        att[:, : GROUPS * HD][None],
        att[:, KEYS][None],
        att[:, VALUES][None],
        att[:, QKV:].T[None],
        small_sum[:, 1][None],
        small_sum[:, 2:][None],
        grad_shared_in[None],
        grad_shared_down.T[None],
        grad_expert_in[None],
        grad_expert_down.transpose(1, 2, 0)[None],
    )


def solution(mesh):
    split = Mesh(
        mesh.devices.reshape(2, 2, 4, 2, 4), ("section", "xhi", "z", "core", "tensor")
    )
    dp = ("xhi", "z", "core")
    both = dp + ("tensor",)
    placed = (
        P(dp, "tensor", None),
        P(dp, "tensor", None),
        P("section", dp, None, None),
        P("section", dp, None, None),
        P("section", both),
        P("section", dp, "tensor"),
        P("section", dp, "tensor"),
        P("section", dp, "tensor"),
        P("section", "tensor", dp),
        P("section", both),
        P("section", both, None),
        P("section", dp, None, "tensor"),
        P("section", "tensor", dp),
        P("section", dp, None, None, "tensor"),
        P("section", None, "tensor", dp),
    )
    return jax.shard_map(
        per_device,
        mesh=split,
        in_specs=placed,
        out_specs=(
            P("section", dp, "tensor", None),
            P("section", dp, "tensor", None),
            P("section", both),
            P("section", dp, "tensor"),
            P("section", dp, "tensor"),
            P("section", dp, "tensor"),
            P("section", "tensor", dp),
            P("section", both),
            P("section", both, None),
            P("section", dp, None, "tensor"),
            P("section", "tensor", dp),
            P("section", dp, None, None, "tensor"),
            P("section", None, "tensor", dp),
        ),
        check_vma=False,
    )
```

time: 888 us -> 666 us (0.75)
  matrix products: 157 us -> 7.09 us
  Pallas kernels: 0 us -> 104 us
  blocking collectives: 28.2 us -> 114 us
  waiting for transfers between devices: 270 us -> 190 us
  starting transfers between devices: 187 us -> 122 us
  other arithmetic: 72.9 us -> 18.5 us
  local copies, waits for them, and re-layouts: 138 us -> 83.8 us
    dot_general x58 -> x3, matrix products: 130 us -> 7.09 us  [dot(): lax.dot_general(a, b, ((contract[:1], contract[1:]), ((), ())), preferred...]
    all_to_all x0 -> x4, blocking collectives: none -> 114 us  [group_exchange(): return lax.all_to_all(rows, GROUP, 0, 0, tiled=True)]
    pallas_call x0 -> x24, Pallas kernels: none -> 104 us  [run(): pl.pallas_call(kernel, out_shape=list(outs), in_specs=in_specs, out_specs...]
    ppermute x119 -> x69, waiting for transfers between devices: 230 us -> 139 us  [move(): return lax.ppermute(block, axes, pairs)]
    ppermute x119 -> x69, starting transfers between devices: 186 us -> 96.6 us  [move(): return lax.ppermute(block, axes, pairs)]
    all_to_all x0 -> x4, waiting for transfers between devices: none -> 49.4 us  [group_exchange(): return lax.all_to_all(rows, GROUP, 0, 0, tiled=True)]
    reduce_scatter x2 -> x3, waiting for transfers between devices: 38.9 us -> 0.02 us  [sum_row(): return lax.psum_scatter(part, 'z', scatter_dimension=0, tiled=True)]
    convert_element_type x23 -> x2, other arithmetic: 26.4 us -> 1.1 us  [the longest x1 0.83 us: per_device(): jnp.where(s == layer, named, named_else).astype(F32)]
  transfers between devices with their start and end apart: 126 -> 80, of which waited for: 60 -> 38; matrix products, arithmetic and copies ran while one was open for 23% -> 9% of each run, Pallas kernels for 0% -> 12%
where the time goes in v2:
time: 666 us; the launch traced here: 656 us
  waiting for transfers between devices  190 us (29%)
  starting transfers between devices  122 us (18%)
  blocking collectives  114 us (17%)
  Pallas kernels  104 us (16%)
  local copies, waits for them, and re-layouts  83.8 us (13%)
  other arithmetic  18.5 us (3%)
  between operations  16.1 us (2%)
  matrix products  7.09 us (1%)
    ppermute x69, waiting for transfers between devices, move(): return lax.ppermute(block, axes, pairs)  139 us
    all_to_all x4, blocking collectives, group_exchange(): return lax.all_to_all(rows, GROUP, 0, 0, tiled=True)  114 us
    pallas_call x24, Pallas kernels, run(): pl.pallas_call(kernel, out_shape=list(outs), in_specs=in_specs, out_specs...  104 us
    ppermute x69, starting transfers between devices, move(): return lax.ppermute(block, axes, pairs)  96.6 us
    all_to_all x4, waiting for transfers between devices, group_exchange(): return lax.all_to_all(rows, GROUP, 0, 0, tiled=True)  49.4 us
    unnamed x229, local copies, waits for them, and re-layouts  44.8 us
    all_to_all x4, starting transfers between devices, group_exchange(): return lax.all_to_all(rows, GROUP, 0, 0, tiled=True)  24.7 us
  transfers between devices with their start and end apart: 80, of which 38 were waited for; matrix products, arithmetic and copies ran while one was open for 9% of the time, Pallas kernels for 12%

profile of v2, /device:TPU:8, one launch (start us, length us, event | category | flops | bytes accessed | tf_op | source)
XLA Modules:
  0.0 655.7 jit_solution(15100637418927620935)
XLA Ops:
  10.0 2.7 collective-permute-start.1
  21.6 3.1 collective-permute-start.3
  26.1 5.5 collective-permute-done.3
  31.6 2.8 collective-permute-done.4
  39.2 2.5 collective-permute-start.14
  41.7 10.8 %collective-permute-done.15 = bf16[96,3456]{1,0:T(8,128)(2,1)S(1)} collective-permute-done((bf16[96,3456]{1,0:T(8,128)(2,1)S(1)}, bf16[96,3456]{1,0:T(8,128)(2,1)S(1)}, u32[]{:S(2)}, u32[]{:S(2)}) %collective-permute-start.15) | collective-permute-done | bytes 663584 | tf_op jit(solution)/shard_map/ppermute | solution.py:82
  52.6 2.4 collective-permute-done.16
  55.1 13.6 %collective-permute-done.14 = bf16[96,3456]{1,0:T(8,128)(2,1)S(1)} collective-permute-done((bf16[96,3456]{1,0:T(8,128)(2,1)S(1)}, bf16[96,3456]{1,0:T(8,128)(2,1)S(1)}, u32[]{:S(2)}, u32[]{:S(2)}) %collective-permute-start.14) | collective-permute-done | bytes 663584 | tf_op jit(solution)/shard_map/ppermute | solution.py:82
  78.2 3.0 collective-permute-done.7.refs_1_
  81.2 2.3 collective-permute-done.8.refs_2_
  85.5 3.9 collective-permute-done.10.refs_5_
  92.1 3.5 shard_map.237
  100.0 5.3 all-to-all-start.1
  107.6 2.4 collective-permute-start.13
  110.6 17.5 %collective-permute-done.11.refs_1_ = bf16[64,1536]{1,0:T(8,128)(2,1)S(1)} collective-permute-done((bf16[64,1536]{1,0:T(8,128)(2,1)S(1)}, bf16[64,1536]{1,0:T(8,128)(2,1)S(1)}, u32[]{:S(2)}, u32[]{:S(2)}) %collective-permute-start.11) | collective-permute-done | bytes 196640 | tf_op jit(solution)/shard_map/ppermute | solution.py:82
  130.2 2.8 collective-permute-done.13.refs_3_
  135.9 25.3 %all_to_all.88 = bf16[8,64,1536]{2,1,0:T(8,128)(2,1)S(1)} all-to-all(bf16[8,64,1536]{2,1,0:T(8,128)(2,1)} %bitcast.215), channel_id=1, replica_groups=mesh['section'=2,'xhi'=2,'z'=4,'core'=2,'tensor'=4] {'section','tensor'}, dimensions={0} | all-to-all | bytes 3145728 | tf_op jit(solution)/shard_map/all_to_all | solution.py:123
  162.1 2.9 maximum_select_fusion.1
  165.9 5.2 collective-permute-done.17.up1.down1
  172.1 12.4 %shard_map.239 = (bf16[512,1536]{1,0:T(8,128)(2,1)S(1)}, f32[512,16]{1,0:T(8,128)S(1)}, f32[64,16]{1,0:T(8,128)S(1)}, bf16[512,2304]{1,0:T(8,128)(2,1)}, bf16[512,1152]{1,0:T(8,128)(2,1)S(1)}) custom-call(s32[1]{0:T(128)} %bitcast.33.s_ref, s32[1]{0:T(128)} %bitcast.32.t_ref, bf16[512,1536]{1,0:T(8,128)(2,1)S(1)} %bitcast.193, ...), custom_call_target="tpu_custom_call" | custom-call | flops 5435817984 | bytes 28037128 | tf_op jit(solution)/shard_map/pallas_call | solution.py:98
  189.0 35.6 %all_to_all.89 = bf16[8,64,1536]{2,1,0:T(8,128)(2,1)S(1)} all-to-all(bf16[8,64,1536]{2,1,0:T(8,128)(2,1)S(1)} %bitcast.214), channel_id=1, replica_groups=mesh['section'=2,'xhi'=2,'z'=4,'core'=2,'tensor'=4] {'section','tensor'}, dimensions={0} | all-to-all | bytes 3145728 | tf_op jit(solution)/shard_map/all_to_all | solution.py:123
  229.0 2.7 collective-permute-done.19.refs_1_
  231.6 3.9 collective-permute-done.20.refs_2_
  237.6 3.5 shard_map.241
  245.6 3.3 collective-permute-start.24
  249.7 2.9 collective-permute-done.23.refs_1_
  252.6 2.4 collective-permute-done.24.refs_2_
  255.0 2.6 collective-permute-done.25.refs_3_
  260.5 7.6 %all-to-all-start.3 = ((bf16[8,64,1536]{2,1,0:T(8,128)(2,1)}), bf16[8,64,1536]{2,1,0:T(8,128)(2,1)S(1)}, u32[]{:S(2)}, u32[]{:S(2)}) async-start(bf16[8,64,1536]{2,1,0:T(8,128)(2,1)} %bitcast.213), calls=%async_computation.3 | async-start | bytes 3145728 | tf_op jit(solution)/shard_map/all_to_all | solution.py:123
  269.6 18.4 %all-to-all-done.3 = bf16[8,64,1536]{2,1,0:T(8,128)(2,1)S(1)} async-done(((bf16[8,64,1536]{2,1,0:T(8,128)(2,1)}), bf16[8,64,1536]{2,1,0:T(8,128)(2,1)S(1)}, u32[]{:S(2)}, u32[]{:S(2)}) %all-to-all-start.3) | async-done | bytes 1572896 | tf_op jit(solution)/shard_map/all_to_all | solution.py:123
  289.7 13.1 %shard_map.243 = (bf16[512,1536]{1,0:T(8,128)(2,1)}, f32[512,16]{1,0:T(8,128)S(1)}, f32[64,16]{1,0:T(8,128)S(1)}, bf16[512,2304]{1,0:T(8,128)(2,1)}, bf16[512,1152]{1,0:T(8,128)(2,1)S(1)}) custom-call(s32[1]{0:T(128)} %bitcast.33.s_ref, s32[1]{0:T(128)} %bitcast.32.t_ref, bf16[512,1536]{1,0:T(8,128)(2,1)S(1)} %bitcast.196, bf16[16,1536]{1,0:T(8,128)(2,1)S(1)} %copy-done.44, ...), custom_call_target="tpu_custom_call" | custom-call | flops 5435817984 | bytes 28037128 | tf_op jit(solution)/shard_map/pallas_call | solution.py:98
  302.8 10.7 %shard_map.245 = (bf16[512,1664]{1,0:T(8,128)(2,1)S(1)}, bf16[512,2304]{1,0:T(8,128)(2,1)S(1)}) custom-call(s32[1]{0:T(128)} %bitcast.33.s_ref, bf16[512,1536]{1,0:T(8,128)(2,1)S(1)} %bitcast.199, f32[512,16]{1,0:T(8,128)S(1)} %get-tuple-element.171.gates_ref, bf16[512,2304]{1,0:T(8,128)(2,1)} %get-tuple-element.172.gate_up_ref, ...), custom_call_target="tpu_custom_call" | custom-call | flops 5435817984 | bytes 29261828 | tf_op jit(solution)/shard_map/pallas_call | solution.py:98
  313.5 26.5 %all_to_all.90 = bf16[8,64,1664]{2,1,0:T(8,128)(2,1)S(1)} all-to-all(bf16[8,64,1664]{2,1,0:T(8,128)(2,1)S(1)} %bitcast.211), channel_id=1, replica_groups=mesh['section'=2,'xhi'=2,'z'=4,'core'=2,'tensor'=4] {'section','tensor'}, dimensions={0} | all-to-all | bytes 3407872 | tf_op jit(solution)/shard_map/all_to_all | solution.py:123
  344.8 6.5 shard_map.247
  352.5 4.4 shard_map.248
  358.4 2.7 collective-permute-start.32
  363.0 7.7 %shard_map.250 = bf16[768,3456]{1,0:T(8,128)(2,1)} custom-call(bf16[512,1536]{1,0:T(8,128)(2,1)S(1)} %bitcast.198, bf16[512,1536]{1,0:T(8,128)(2,1)S(1)} %bitcast.201, bf16[512,2304]{1,0:T(8,128)(2,1)} %copy-done.2, bf16[512,1152]{1,0:T(8,128)(2,1)S(1)} %get-tuple-element.177.gated, bf16[768,3456]{1,0:T(8,128)(2,1)} %collective-permute-done.34.refs_0_), custom_call_target="tpu_custom_call" | custom-call | flops 2717908992 | bytes 17301504 | tf_op jit(solution)/shard_map/pallas_call | solution.py:98
  375.2 6.2 all-to-all-start.6
  389.2 11.6 %all-to-all-done.6 = bf16[8,64,1536]{2,1,0:T(8,128)(2,1)S(1)} async-done(((bf16[8,64,1536]{2,1,0:T(8,128)(2,1)}), bf16[8,64,1536]{2,1,0:T(8,128)(2,1)S(1)}, u32[]{:S(2)}, u32[]{:S(2)}) %all-to-all-start.6) | async-done | bytes 1572896 | tf_op jit(solution)/shard_map/all_to_all | solution.py:123
  401.8 10.8 %shard_map.253 = (bf16[512,1664]{1,0:T(8,128)(2,1)S(1)}, bf16[512,2304]{1,0:T(8,128)(2,1)S(1)}) custom-call(s32[1]{0:T(128)} %bitcast.33.s_ref, bf16[512,1536]{1,0:T(8,128)(2,1)S(1)} %bitcast.202, f32[512,16]{1,0:T(8,128)S(1)} %copy-done.59, bf16[512,2304]{1,0:T(8,128)(2,1)} %get-tuple-element.202.gate_up_ref, ...), custom_call_target="tpu_custom_call" | custom-call | flops 5435817984 | bytes 29261828 | tf_op jit(solution)/shard_map/pallas_call | solution.py:98
  414.0 6.9 %shard_map.254 = bf16[768,3456]{1,0:T(8,128)(2,1)} custom-call(bf16[512,1536]{1,0:T(8,128)(2,1)S(1)} %bitcast.194, bf16[512,1536]{1,0:T(8,128)(2,1)S(1)} %bitcast.203, bf16[512,2304]{1,0:T(8,128)(2,1)} %copy-done.3, bf16[512,1152]{1,0:T(8,128)(2,1)S(1)} %copy-done.10), custom_call_target="tpu_custom_call" | custom-call | flops 2717908992 | bytes 11993088 | tf_op jit(solution)/shard_map/pallas_call | solution.py:98
  421.0 27.1 %all_to_all.91 = bf16[8,64,1664]{2,1,0:T(8,128)(2,1)S(1)} all-to-all(bf16[8,64,1664]{2,1,0:T(8,128)(2,1)} %bitcast.210), channel_id=1, replica_groups=mesh['section'=2,'xhi'=2,'z'=4,'core'=2,'tensor'=4] {'section','tensor'}, dimensions={0} | all-to-all | bytes 3407872 | tf_op jit(solution)/shard_map/all_to_all | solution.py:123
  453.2 2.3 collective-permute-start.38
  456.8 7.7 %shard_map.256 = bf16[768,3456]{1,0:T(8,128)(2,1)} custom-call(bf16[512,1536]{1,0:T(8,128)(2,1)S(1)} %bitcast.195, bf16[512,1536]{1,0:T(8,128)(2,1)S(1)} %bitcast.204, bf16[512,2304]{1,0:T(8,128)(2,1)} %copy-done.3, bf16[512,1152]{1,0:T(8,128)(2,1)S(1)} %copy-done.11, bf16[768,3456]{1,0:T(8,128)(2,1)} %collective-permute-done.39.refs_0_), custom_call_target="tpu_custom_call" | custom-call | flops 2717908992 | bytes 17301504 | tf_op jit(solution)/shard_map/pallas_call | solution.py:98
  464.5 5.7 all-to-all-start.4
  470.2 19.4 %all-to-all-done.4 = bf16[8,64,1536]{2,1,0:T(8,128)(2,1)S(1)} async-done(((bf16[8,64,1536]{2,1,0:T(8,128)(2,1)}), bf16[8,64,1536]{2,1,0:T(8,128)(2,1)S(1)}, u32[]{:S(2)}, u32[]{:S(2)}) %all-to-all-start.4) | async-done | bytes 1572896 | tf_op jit(solution)/shard_map/all_to_all | solution.py:123
  492.0 4.1 shard_map.257
  497.1 2.2 collective-permute-start.41
  511.1 6.0 concatenate.117
  527.2 4.1 collective-permute-start.47
  532.4 3.0 fusion.8
  540.2 2.3 collective-permute-done.48
  547.3 2.4 fusion.57
  554.4 2.5 collective-permute-start.50
  558.7 3.3 collective-permute-start.62
  572.8 5.8 collective-permute-done.56
  581.5 4.8 collective-permute-done.54
  593.6 7.1 %collective-permute-start.68 = (bf16[96,3456]{1,0:T(8,128)(2,1)S(1)}, bf16[96,3456]{1,0:T(8,128)(2,1)S(1)}, u32[]{:S(2)}, u32[]{:S(2)}) collective-permute-start(bf16[96,3456]{1,0:T(8,128)(2,1)S(1)} %copy-done.92), channel_id=1, source_target_pairs={{0,96},{32,64},{1,97},{33,65},{2,98},{34,66},{3,99},{35,67},{4,100... | collective-permute-start | bytes 1990664 | tf_op jit(solution)/shard_map/ppermute | solution.py:82
  602.1 3.3 collective-permute-start.63
  610.9 3.6 collective-permute-done.68
  614.5 2.9 collective-permute-done.67
  617.4 14.6 %collective-permute-done.63 = bf16[96,3456]{1,0:T(8,128)(2,1)S(1)} collective-permute-done((bf16[96,3456]{1,0:T(8,128)(2,1)S(1)}, bf16[96,3456]{1,0:T(8,128)(2,1)S(1)}, u32[]{:S(2)}, u32[]{:S(2)}) %collective-permute-start.63) | collective-permute-done | bytes 663584 | tf_op jit(solution)/shard_map/ppermute | solution.py:82
  632.1 6.5 collective-permute-done.66
  644.7 2.4 copy.143
  (463 shorter events, 176.6 us)
Async XLA Ops:
  7.2 78.2 %all-gather.5.cloned.1.call-start = ((), (), s32[]{:S(2)}) async-start(), calls=%async_computation.11 | async-start | bytes 2211840 | tf_op jit(solution)/shard_map/all_gather | solution.py:488
  9.6 11.8 %collective-permute-start = (bf16[24,128]{1,0:T(8,128)(2,1)S(1)}, bf16[24,128]{1,0:T(8,128)(2,1)S(1)}, u32[]{:S(2)}, u32[]{:S(2)}) collective-permute-start(bf16[24,128]{1,0:T(8,128)(2,1)S(1)} %get-tuple-element.296), channel_id=1, source_target_pairs={{0,3},{1,0},{2,1},{3,2},{4,7},{5,4},{6,5},{7,6},{8,11},{9,8},{10,9... | collective-permute-start | bytes 18440 | tf_op jit(solution)/shard_map/ppermute | solution.py:82
  10.0 11.5 %collective-permute-start.1 = (bf16[24,128]{1,0:T(8,128)(2,1)S(1)}, bf16[24,128]{1,0:T(8,128)(2,1)S(1)}, u32[]{:S(2)}, u32[]{:S(2)}) collective-permute-start(bf16[24,128]{1,0:T(8,128)(2,1)S(1)} %get-tuple-element.296), channel_id=1, source_target_pairs={{0,2},{1,3},{2,0},{3,1},{4,6},{5,7},{6,4},{7,5},{8,10},{9,11},{10,... | collective-permute-start | bytes 18440 | tf_op jit(solution)/shard_map/ppermute | solution.py:82
  12.7 8.8 %collective-permute-start.2 = (bf16[24,128]{1,0:T(8,128)(2,1)S(1)}, bf16[24,128]{1,0:T(8,128)(2,1)S(1)}, u32[]{:S(2)}, u32[]{:S(2)}) collective-permute-start(bf16[24,128]{1,0:T(8,128)(2,1)S(1)} %get-tuple-element.296), channel_id=1, source_target_pairs={{0,1},{1,2},{2,3},{3,0},{4,5},{5,6},{6,7},{7,4},{8,9},{9,10},{10,1... | collective-permute-start | bytes 18440 | tf_op jit(solution)/shard_map/ppermute | solution.py:82
  21.6 10.0 %collective-permute-start.3 = (bf16[96,1152]{1,0:T(8,128)(2,1)S(1)}, bf16[96,1152]{1,0:T(8,128)(2,1)S(1)}, u32[]{:S(2)}, u32[]{:S(2)}) collective-permute-start(bf16[96,1152]{1,0:T(8,128)(2,1)S(1)} %constant_dynamic-update-slice_fusion.8), channel_id=1, source_target_pairs={{0,32},{32,0},{64,96},{96,64},{1,33},{33,1},{65,97},{97,65},{2,34}... | collective-permute-start | bytes 663560 | tf_op jit(solution)/shard_map/ppermute | solution.py:82
  24.7 9.7 %collective-permute-start.4 = (bf16[96,1152]{1,0:T(8,128)(2,1)S(1)}, bf16[96,1152]{1,0:T(8,128)(2,1)S(1)}, u32[]{:S(2)}, u32[]{:S(2)}) collective-permute-start(bf16[96,1152]{1,0:T(8,128)(2,1)S(1)} %constant_dynamic-update-slice_fusion.8), channel_id=1, source_target_pairs={{0,64},{32,96},{64,0},{96,32},{1,65},{33,97},{65,1},{97,33},{2,66}... | collective-permute-start | bytes 663560 | tf_op jit(solution)/shard_map/ppermute | solution.py:82
  25.3 9.1 %collective-permute-start.5 = (bf16[96,1152]{1,0:T(8,128)(2,1)S(1)}, bf16[96,1152]{1,0:T(8,128)(2,1)S(1)}, u32[]{:S(2)}, u32[]{:S(2)}) collective-permute-start(bf16[96,1152]{1,0:T(8,128)(2,1)S(1)} %constant_dynamic-update-slice_fusion.8), channel_id=1, source_target_pairs={{0,96},{32,64},{64,32},{96,0},{1,97},{33,65},{65,33},{97,1},{2,98}... | collective-permute-start | bytes 663560 | tf_op jit(solution)/shard_map/ppermute | solution.py:82
  35.6 125.6 %all-gather.7.cloned.1.call-start = ((), (), s32[]{:S(2)}) async-start(), calls=%async_computation.12 | async-start | bytes 6635520 | tf_op jit(solution)/shard_map/all_gather | solution.py:488
  35.6 16.9 %collective-permute-start.15 = (bf16[96,3456]{1,0:T(8,128)(2,1)S(1)}, bf16[96,3456]{1,0:T(8,128)(2,1)S(1)}, u32[]{:S(2)}, u32[]{:S(2)}) collective-permute-start(bf16[96,3456]{1,0:T(8,128)(2,1)S(1)} %get-tuple-element.143), channel_id=1, source_target_pairs={{0,64},{32,96},{64,0},{96,32},{1,65},{33,97},{65,1},{97,33},{2,66}... | collective-permute-start | bytes 1990664 | tf_op jit(solution)/shard_map/ppermute | solution.py:82
  37.1 17.8 %collective-permute-start.16 = (bf16[96,3456]{1,0:T(8,128)(2,1)S(1)}, bf16[96,3456]{1,0:T(8,128)(2,1)S(1)}, u32[]{:S(2)}, u32[]{:S(2)}) collective-permute-start(bf16[96,3456]{1,0:T(8,128)(2,1)S(1)} %get-tuple-element.143), channel_id=1, source_target_pairs={{0,96},{32,64},{64,32},{96,0},{1,97},{33,65},{65,33},{97,1},{2,98}... | collective-permute-start | bytes 1990664 | tf_op jit(solution)/shard_map/ppermute | solution.py:82
  39.2 29.5 %collective-permute-start.14 = (bf16[96,3456]{1,0:T(8,128)(2,1)S(1)}, bf16[96,3456]{1,0:T(8,128)(2,1)S(1)}, u32[]{:S(2)}, u32[]{:S(2)}) collective-permute-start(bf16[96,3456]{1,0:T(8,128)(2,1)S(1)} %get-tuple-element.152), channel_id=1, source_target_pairs={{0,32},{32,0},{1,33},{33,1},{2,34},{34,2},{3,35},{35,3},{4,36},{36... | collective-permute-start | bytes 1990664 | tf_op jit(solution)/shard_map/ppermute | solution.py:82
  73.6 9.9 %collective-permute-start.8 = (bf16[64,1536]{1,0:T(8,128)(2,1)S(1)}, bf16[64,1536]{1,0:T(8,128)(2,1)S(1)}, u32[]{:S(2)}, u32[]{:S(2)}) collective-permute-start(bf16[64,1536]{1,0:T(8,128)(2,1)S(1)} %get-tuple-element.131.refs_0_.hidden), channel_id=1, source_target_pairs={{0,2},{1,3},{2,0},{3,1},{4,6},{5,7},{6,4},{7,5},{8,10},{9,11},{10,... | collective-permute-start | bytes 589832 | tf_op jit(solution)/shard_map/ppermute | solution.py:82
  75.3 10.0 %collective-permute-start.9 = (bf16[64,1536]{1,0:T(8,128)(2,1)S(1)}, bf16[64,1536]{1,0:T(8,128)(2,1)S(1)}, u32[]{:S(2)}, u32[]{:S(2)}) collective-permute-start(bf16[64,1536]{1,0:T(8,128)(2,1)S(1)} %get-tuple-element.131.refs_0_.hidden), channel_id=1, source_target_pairs={{0,1},{1,2},{2,3},{3,0},{4,5},{5,6},{6,7},{7,4},{8,9},{9,10},{10,1... | collective-permute-start | bytes 589832 | tf_op jit(solution)/shard_map/ppermute | solution.py:82
  100.0 35.8 %all-to-all-start.1 = ((bf16[8,64,1536]{2,1,0:T(8,128)(2,1)}), bf16[8,64,1536]{2,1,0:T(8,128)(2,1)S(1)}, u32[]{:S(2)}, u32[]{:S(2)}) async-start(bf16[8,64,1536]{2,1,0:T(8,128)(2,1)} %tile.2), calls=%async_computation.1 | async-start | bytes 3145728 | tf_op jit(solution)/shard_map/all_to_all | solution.py:123
  105.3 83.7 %all-gather.11.cloned.1.call-start = ((), (), s32[]{:S(2)}) async-start(), calls=%async_computation.14 | async-start | bytes 2211840 | tf_op jit(solution)/shard_map/all_gather | solution.py:488
  105.3 22.9 %collective-permute-start.11 = (bf16[64,1536]{1,0:T(8,128)(2,1)S(1)}, bf16[64,1536]{1,0:T(8,128)(2,1)S(1)}, u32[]{:S(2)}, u32[]{:S(2)}) collective-permute-start(bf16[64,1536]{1,0:T(8,128)(2,1)S(1)} %get-tuple-element.138), channel_id=1, source_target_pairs={{0,1},{1,2},{2,3},{3,0},{4,5},{5,6},{6,7},{7,4},{8,9},{9,10},{10,1... | collective-permute-start | bytes 589832 | tf_op jit(solution)/shard_map/ppermute | solution.py:82
  106.8 23.5 %collective-permute-start.12 = (bf16[64,1536]{1,0:T(8,128)(2,1)S(1)}, bf16[64,1536]{1,0:T(8,128)(2,1)S(1)}, u32[]{:S(2)}, u32[]{:S(2)}) collective-permute-start(bf16[64,1536]{1,0:T(8,128)(2,1)S(1)} %get-tuple-element.139), channel_id=1, source_target_pairs={{0,2},{1,3},{2,0},{3,1},{4,6},{5,7},{6,4},{7,5},{8,10},{9,11},{10,... | collective-permute-start | bytes 589832 | tf_op jit(solution)/shard_map/ppermute | solution.py:82
  107.6 25.4 %collective-permute-start.13 = (bf16[64,1536]{1,0:T(8,128)(2,1)S(1)}, bf16[64,1536]{1,0:T(8,128)(2,1)S(1)}, u32[]{:S(2)}, u32[]{:S(2)}) collective-permute-start(bf16[64,1536]{1,0:T(8,128)(2,1)S(1)} %get-tuple-element.140), channel_id=1, source_target_pairs={{0,3},{1,0},{2,1},{3,2},{4,7},{5,4},{6,5},{7,6},{8,11},{9,8},{10,9... | collective-permute-start | bytes 589832 | tf_op jit(solution)/shard_map/ppermute | solution.py:82
  161.2 99.2 %all-gather.9.cloned.1.call-start = ((), (), s32[]{:S(2)}) async-start(), calls=%async_computation.13 | async-start | bytes 6635520 | tf_op jit(solution)/shard_map/all_gather | solution.py:488
  162.0 9.2 %collective-permute-start.17 = (bf16[768,3456]{1,0:T(8,128)(2,1)}, bf16[768,3456]{1,0:T(8,128)(2,1)}, u32[]{:S(2)}, u32[]{:S(2)}) collective-permute-start(bf16[768,3456]{1,0:T(8,128)(2,1)} %all-gather.7.cloned.1.call-done.up0.down0), channel_id=1, source_target_pairs={{0,4},{4,0},{1,5},{5,1},{2,6},{6,2},{3,7},{7,3},{8,12},{12,8},{9,1... | collective-permute-start | bytes 15925256 | tf_op jit(solution)/shard_map/ppermute | solution.py:82
  189.0 47.4 %collective-permute-start.22 = (bf16[768,1152]{1,0:T(8,128)(2,1)}, bf16[768,1152]{1,0:T(8,128)(2,1)S(1)}, u32[]{:S(2)}, u32[]{:S(2)}) collective-permute-start(bf16[768,1152]{1,0:T(8,128)(2,1)} %all-gather.11.cloned.1.call-done.refs_4_), channel_id=1, source_target_pairs={{0,4},{4,0},{1,5},{5,1},{2,6},{6,2},{3,7},{7,3},{8,12},{12,8},{9,1... | collective-permute-start | bytes 5308424 | tf_op jit(solution)/shard_map/ppermute | solution.py:82
  226.6 9.0 %collective-permute-start.20 = (bf16[64,1536]{1,0:T(8,128)(2,1)S(1)}, bf16[64,1536]{1,0:T(8,128)(2,1)S(1)}, u32[]{:S(2)}, u32[]{:S(2)}) collective-permute-start(bf16[64,1536]{1,0:T(8,128)(2,1)S(1)} %shard_map.240.refs_0_.hidden), channel_id=1, source_target_pairs={{0,2},{1,3},{2,0},{3,1},{4,6},{5,7},{6,4},{7,5},{8,10},{9,11},{10,... | collective-permute-start | bytes 589832 | tf_op jit(solution)/shard_map/ppermute | solution.py:82
  227.0 9.4 %collective-permute-start.21 = (bf16[64,1536]{1,0:T(8,128)(2,1)S(1)}, bf16[64,1536]{1,0:T(8,128)(2,1)S(1)}, u32[]{:S(2)}, u32[]{:S(2)}) collective-permute-start(bf16[64,1536]{1,0:T(8,128)(2,1)S(1)} %shard_map.240.refs_0_.hidden), channel_id=1, source_target_pairs={{0,1},{1,2},{2,3},{3,0},{4,5},{5,6},{6,7},{7,4},{8,9},{9,10},{10,1... | collective-permute-start | bytes 589832 | tf_op jit(solution)/shard_map/ppermute | solution.py:82
  245.6 9.3 %collective-permute-start.24 = (bf16[64,1536]{1,0:T(8,128)(2,1)S(1)}, bf16[64,1536]{1,0:T(8,128)(2,1)S(1)}, u32[]{:S(2)}, u32[]{:S(2)}) collective-permute-start(bf16[64,1536]{1,0:T(8,128)(2,1)S(1)} %get-tuple-element.159), channel_id=1, source_target_pairs={{0,2},{1,3},{2,0},{3,1},{4,6},{5,7},{6,4},{7,5},{8,10},{9,11},{10,... | collective-permute-start | bytes 589832 | tf_op jit(solution)/shard_map/ppermute | solution.py:82
  260.5 27.5 %collective-permute-start.26 = (bf16[768,3456]{1,0:T(8,128)(2,1)}, bf16[768,3456]{1,0:T(8,128)(2,1)}, u32[]{:S(2)}, u32[]{:S(2)}) collective-permute-start(bf16[768,3456]{1,0:T(8,128)(2,1)} %all-gather.9.cloned.1.call-done.up0.down0), channel_id=1, source_target_pairs={{0,4},{4,0},{1,5},{5,1},{2,6},{6,2},{3,7},{7,3},{8,12},{12,8},{9,1... | collective-permute-start | bytes 15925256 | tf_op jit(solution)/shard_map/ppermute | solution.py:82
  260.5 27.5 %all-to-all-start.3 = ((bf16[8,64,1536]{2,1,0:T(8,128)(2,1)}), bf16[8,64,1536]{2,1,0:T(8,128)(2,1)S(1)}, u32[]{:S(2)}, u32[]{:S(2)}) async-start(bf16[8,64,1536]{2,1,0:T(8,128)(2,1)} %bitcast.213), calls=%async_computation.3 | async-start | bytes 3145728 | tf_op jit(solution)/shard_map/all_to_all | solution.py:123
  268.0 187.5 %reduce-scatter.4.cloned.1.call-start = ((), (), s32[]{:S(2)}) async-start(), calls=%async_computation.15 | async-start | bytes 6635520 | tf_op jit(solution)/shard_map/reduce_scatter | solution.py:484
  340.7 10.7 %collective-permute-start.28 = (bf16[64,1536]{1,0:T(8,128)(2,1)S(1)}, bf16[64,1536]{1,0:T(8,128)(2,1)S(1)}, u32[]{:S(2)}, u32[]{:S(2)}) collective-permute-start(bf16[64,1536]{1,0:T(8,128)(2,1)S(1)} %get-tuple-element.178.refs_0_), channel_id=1, source_target_pairs={{0,3},{1,0},{2,1},{3,2},{4,7},{5,4},{6,5},{7,6},{8,11},{9,8},{10,9... | collective-permute-start | bytes 589832 | tf_op jit(solution)/shard_map/ppermute | solution.py:82
  342.3 9.1 %collective-permute-start.29 = (bf16[64,1536]{1,0:T(8,128)(2,1)S(1)}, bf16[64,1536]{1,0:T(8,128)(2,1)S(1)}, u32[]{:S(2)}, u32[]{:S(2)}) collective-permute-start(bf16[64,1536]{1,0:T(8,128)(2,1)S(1)} %get-tuple-element.178.refs_0_), channel_id=1, source_target_pairs={{0,2},{1,3},{2,0},{3,1},{4,6},{5,7},{6,4},{7,5},{8,10},{9,11},{10,... | collective-permute-start | bytes 589832 | tf_op jit(solution)/shard_map/ppermute | solution.py:82
  342.6 9.5 %collective-permute-start.30 = (bf16[64,1536]{1,0:T(8,128)(2,1)S(1)}, bf16[64,1536]{1,0:T(8,128)(2,1)S(1)}, u32[]{:S(2)}, u32[]{:S(2)}) collective-permute-start(bf16[64,1536]{1,0:T(8,128)(2,1)S(1)} %get-tuple-element.178.refs_0_), channel_id=1, source_target_pairs={{0,1},{1,2},{2,3},{3,0},{4,5},{5,6},{6,7},{7,4},{8,9},{9,10},{10,1... | collective-permute-start | bytes 589832 | tf_op jit(solution)/shard_map/ppermute | solution.py:82
  352.1 10.9 %collective-permute-start.34 = (bf16[768,3456]{1,0:T(8,128)(2,1)}, bf16[768,3456]{1,0:T(8,128)(2,1)}, u32[]{:S(2)}, u32[]{:S(2)}) collective-permute-start(bf16[768,3456]{1,0:T(8,128)(2,1)} %shard_map.247), channel_id=1, source_target_pairs={{0,4},{4,0},{1,5},{5,1},{2,6},{6,2},{3,7},{7,3},{8,12},{12,8},{9,1... | collective-permute-start | bytes 15925256 | tf_op jit(solution)/shard_map/ppermute | solution.py:82
  357.0 13.8 %collective-permute-start.31 = (bf16[64,1536]{1,0:T(8,128)(2,1)}, bf16[64,1536]{1,0:T(8,128)(2,1)}, u32[]{:S(2)}, u32[]{:S(2)}) collective-permute-start(bf16[64,1536]{1,0:T(8,128)(2,1)} %get-tuple-element.185), channel_id=1, source_target_pairs={{0,1},{1,2},{2,3},{3,0},{4,5},{5,6},{6,7},{7,4},{8,9},{9,10},{10,1... | collective-permute-start | bytes 589832 | tf_op jit(solution)/shard_map/ppermute | solution.py:82
  358.4 12.3 %collective-permute-start.32 = (bf16[64,1536]{1,0:T(8,128)(2,1)}, bf16[64,1536]{1,0:T(8,128)(2,1)}, u32[]{:S(2)}, u32[]{:S(2)}) collective-permute-start(bf16[64,1536]{1,0:T(8,128)(2,1)} %get-tuple-element.186), channel_id=1, source_target_pairs={{0,2},{1,3},{2,0},{3,1},{4,6},{5,7},{6,4},{7,5},{8,10},{9,11},{10,... | collective-permute-start | bytes 589832 | tf_op jit(solution)/shard_map/ppermute | solution.py:82
  361.1 10.4 %collective-permute-start.33 = (bf16[64,1536]{1,0:T(8,128)(2,1)}, bf16[64,1536]{1,0:T(8,128)(2,1)}, u32[]{:S(2)}, u32[]{:S(2)}) collective-permute-start(bf16[64,1536]{1,0:T(8,128)(2,1)} %get-tuple-element.187), channel_id=1, source_target_pairs={{0,3},{1,0},{2,1},{3,2},{4,7},{5,4},{6,5},{7,6},{8,11},{9,8},{10,9... | collective-permute-start | bytes 589832 | tf_op jit(solution)/shard_map/ppermute | solution.py:82
  371.5 10.0 %collective-permute-start.35 = (bf16[768,1024]{1,0:T(8,128)(2,1)}, bf16[768,1024]{1,0:T(8,128)(2,1)}, u32[]{:S(2)}, u32[]{:S(2)}) collective-permute-start(bf16[768,1024]{1,0:T(8,128)(2,1)} %shard_map.249), channel_id=1, source_target_pairs={{0,4},{4,0},{1,5},{5,1},{2,6},{6,2},{3,7},{7,3},{8,12},{12,8},{9,1... | collective-permute-start | bytes 4718600 | tf_op jit(solution)/shard_map/ppermute | solution.py:82
  375.2 25.7 %all-to-all-start.6 = ((bf16[8,64,1536]{2,1,0:T(8,128)(2,1)}), bf16[8,64,1536]{2,1,0:T(8,128)(2,1)S(1)}, u32[]{:S(2)}, u32[]{:S(2)}) async-start(bf16[8,64,1536]{2,1,0:T(8,128)(2,1)} %bitcast.212), calls=%async_computation.6 | async-start | bytes 3145728 | tf_op jit(solution)/shard_map/all_to_all | solution.py:123
  381.3 142.9 %reduce-scatter.6.cloned.1.call-start = ((), (), s32[]{:S(2)}) async-start(), calls=%async_computation.16 | async-start | bytes 1966080 | tf_op jit(solution)/shard_map/reduce_scatter | solution.py:484
  420.9 34.6 %collective-permute-start.39 = (bf16[768,3456]{1,0:T(8,128)(2,1)}, bf16[768,3456]{1,0:T(8,128)(2,1)}, u32[]{:S(2)}, u32[]{:S(2)}) collective-permute-start(bf16[768,3456]{1,0:T(8,128)(2,1)} %shard_map.254), channel_id=1, source_target_pairs={{0,4},{4,0},{1,5},{5,1},{2,6},{6,2},{3,7},{7,3},{8,12},{12,8},{9,1... | collective-permute-start | bytes 15925256 | tf_op jit(solution)/shard_map/ppermute | solution.py:82
  420.9 171.3 %reduce-scatter.8.cloned.1.call-start = ((), (), s32[]{:S(2)}) async-start(), calls=%async_computation.17 | async-start | bytes 6635520 | tf_op jit(solution)/shard_map/reduce_scatter | solution.py:484
  451.4 13.0 %collective-permute-start.36 = (bf16[64,1536]{1,0:T(8,128)(2,1)}, bf16[64,1536]{1,0:T(8,128)(2,1)}, u32[]{:S(2)}, u32[]{:S(2)}) collective-permute-start(bf16[64,1536]{1,0:T(8,128)(2,1)} %get-tuple-element.212.refs_0_), channel_id=1, source_target_pairs={{0,3},{1,0},{2,1},{3,2},{4,7},{5,4},{6,5},{7,6},{8,11},{9,8},{10,9... | collective-permute-start | bytes 589832 | tf_op jit(solution)/shard_map/ppermute | solution.py:82
  452.9 11.5 %collective-permute-start.37 = (bf16[64,1536]{1,0:T(8,128)(2,1)}, bf16[64,1536]{1,0:T(8,128)(2,1)}, u32[]{:S(2)}, u32[]{:S(2)}) collective-permute-start(bf16[64,1536]{1,0:T(8,128)(2,1)} %get-tuple-element.212.refs_0_), channel_id=1, source_target_pairs={{0,2},{1,3},{2,0},{3,1},{4,6},{5,7},{6,4},{7,5},{8,10},{9,11},{10,... | collective-permute-start | bytes 589832 | tf_op jit(solution)/shard_map/ppermute | solution.py:82
  453.2 11.3 %collective-permute-start.38 = (bf16[64,1536]{1,0:T(8,128)(2,1)}, bf16[64,1536]{1,0:T(8,128)(2,1)}, u32[]{:S(2)}, u32[]{:S(2)}) collective-permute-start(bf16[64,1536]{1,0:T(8,128)(2,1)} %get-tuple-element.212.refs_0_), channel_id=1, source_target_pairs={{0,1},{1,2},{2,3},{3,0},{4,5},{5,6},{6,7},{7,4},{8,9},{9,10},{10,1... | collective-permute-start | bytes 589832 | tf_op jit(solution)/shard_map/ppermute | solution.py:82
  464.5 25.1 %all-to-all-start.4 = ((bf16[8,64,1536]{2,1,0:T(8,128)(2,1)}), bf16[8,64,1536]{2,1,0:T(8,128)(2,1)S(1)}, u32[]{:S(2)}, u32[]{:S(2)}) async-start(bf16[8,64,1536]{2,1,0:T(8,128)(2,1)} %bitcast.41), calls=%async_computation.4 | async-start | bytes 3145728 | tf_op jit(solution)/shard_map/all_to_all | solution.py:123
  497.1 9.1 %collective-permute-start.41 = (bf16[64,1536]{1,0:T(8,128)(2,1)S(1)}, bf16[64,1536]{1,0:T(8,128)(2,1)S(1)}, u32[]{:S(2)}, u32[]{:S(2)}) collective-permute-start(bf16[64,1536]{1,0:T(8,128)(2,1)S(1)} %get-tuple-element.220), channel_id=1, source_target_pairs={{0,2},{1,3},{2,0},{3,1},{4,6},{5,7},{6,4},{7,5},{8,10},{9,11},{10,... | collective-permute-start | bytes 589832 | tf_op jit(solution)/shard_map/ppermute | solution.py:82
  499.4 8.9 %collective-permute-start.42 = (bf16[64,1536]{1,0:T(8,128)(2,1)S(1)}, bf16[64,1536]{1,0:T(8,128)(2,1)S(1)}, u32[]{:S(2)}, u32[]{:S(2)}) collective-permute-start(bf16[64,1536]{1,0:T(8,128)(2,1)S(1)} %get-tuple-element.221), channel_id=1, source_target_pairs={{0,3},{1,0},{2,1},{3,2},{4,7},{5,4},{6,5},{7,6},{8,11},{9,8},{10,9... | collective-permute-start | bytes 589832 | tf_op jit(solution)/shard_map/ppermute | solution.py:82
  501.5 20.8 %collective-permute-start.27 = (bf16[64,1536]{1,0:T(8,128)(2,1)}, bf16[64,1536]{1,0:T(8,128)(2,1)}, u32[]{:S(2)}, u32[]{:S(2)}) collective-permute-start(bf16[64,1536]{1,0:T(8,128)(2,1)} %get-tuple-element.323), channel_id=1, source_target_pairs={{0,64},{64,0},{1,65},{65,1},{2,66},{66,2},{3,67},{67,3},{4,68},{68... | collective-permute-start | bytes 589832 | tf_op jit(solution)/shard_map/ppermute | solution.py:82
  538.7 31.6 %collective-permute-start.43 = (bf16[64,1536]{1,0:T(8,128)(2,1)}, bf16[64,1536]{1,0:T(8,128)(2,1)}, u32[]{:S(2)}, u32[]{:S(2)}) collective-permute-start(bf16[64,1536]{1,0:T(8,128)(2,1)} %get-tuple-element.321), channel_id=1, source_target_pairs={{0,64},{64,0},{1,65},{65,1},{2,66},{66,2},{3,67},{67,3},{4,68},{68... | collective-permute-start | bytes 589832 | tf_op jit(solution)/shard_map/ppermute | solution.py:82
  540.1 22.5 %collective-permute-start.53 = (bf16[768,1024]{1,0:T(8,128)(2,1)S(1)}, bf16[768,1024]{1,0:T(8,128)(2,1)}, u32[]{:S(2)}, u32[]{:S(2)}) collective-permute-start(bf16[768,1024]{1,0:T(8,128)(2,1)S(1)} %shard_map.258), channel_id=1, source_target_pairs={{0,4},{4,0},{1,5},{5,1},{2,6},{6,2},{3,7},{7,3},{8,12},{12,8},{9,1... | collective-permute-start | bytes 4718600 | tf_op jit(solution)/shard_map/ppermute | solution.py:82
  552.8 9.2 %collective-permute-start.51 = (f32[24,18]{0,1:T(8,128)S(1)}, f32[24,18]{0,1:T(8,128)S(1)}, u32[]{:S(2)}, u32[]{:S(2)}) collective-permute-start(f32[24,18]{0,1:T(8,128)S(1)} %bitcast.237), channel_id=1, source_target_pairs={{0,2},{1,3},{2,0},{3,1},{4,6},{5,7},{6,4},{7,5},{8,10},{9,11},{10,... | collective-permute-start | bytes 5192 | tf_op jit(solution)/shard_map/ppermute | solution.py:82
  558.7 30.0 %collective-permute-start.62 = (bf16[96,1024]{1,0:T(8,128)(2,1)}, bf16[96,1024]{1,0:T(8,128)(2,1)}, u32[]{:S(2)}, u32[]{:S(2)}) collective-permute-start(bf16[96,1024]{1,0:T(8,128)(2,1)} %get-tuple-element.319), channel_id=1, source_target_pairs={{0,96},{32,64},{1,97},{33,65},{2,98},{34,66},{3,99},{35,67},{4,100... | collective-permute-start | bytes 589832 | tf_op jit(solution)/shard_map/ppermute | solution.py:82
  566.4 12.1 %collective-permute-start.56 = (bf16[192,1024]{1,0:T(8,128)(2,1)S(1)}, bf16[192,1024]{1,0:T(8,128)(2,1)S(1)}, u32[]{:S(2)}, u32[]{:S(2)}) collective-permute-start(bf16[192,1024]{1,0:T(8,128)(2,1)S(1)} %get-tuple-element.301), channel_id=1, source_target_pairs={{0,24},{8,0},{16,8},{24,16},{1,25},{9,1},{17,9},{25,17},{2,26},{10... | collective-permute-start | bytes 1179656 | tf_op jit(solution)/shard_map/ppermute | solution.py:82
  567.2 13.6 %collective-permute-start.55 = (bf16[192,1024]{1,0:T(8,128)(2,1)S(1)}, bf16[192,1024]{1,0:T(8,128)(2,1)S(1)}, u32[]{:S(2)}, u32[]{:S(2)}) collective-permute-start(bf16[192,1024]{1,0:T(8,128)(2,1)S(1)} %get-tuple-element.300), channel_id=1, source_target_pairs={{0,16},{8,24},{16,0},{24,8},{1,17},{9,25},{17,1},{25,9},{2,18},{10... | collective-permute-start | bytes 1179656 | tf_op jit(solution)/shard_map/ppermute | solution.py:82
  569.3 17.0 %collective-permute-start.54 = (bf16[192,1024]{1,0:T(8,128)(2,1)S(1)}, bf16[192,1024]{1,0:T(8,128)(2,1)S(1)}, u32[]{:S(2)}, u32[]{:S(2)}) collective-permute-start(bf16[192,1024]{1,0:T(8,128)(2,1)S(1)} %get-tuple-element.299), channel_id=1, source_target_pairs={{0,8},{8,16},{16,24},{24,0},{1,9},{9,17},{17,25},{25,1},{2,10},{10... | collective-permute-start | bytes 1179656 | tf_op jit(solution)/shard_map/ppermute | solution.py:82
  570.3 23.4 %collective-permute-start.60 = (bf16[96,1024]{1,0:T(8,128)(2,1)}, bf16[96,1024]{1,0:T(8,128)(2,1)S(1)}, u32[]{:S(2)}, u32[]{:S(2)}) collective-permute-start(bf16[96,1024]{1,0:T(8,128)(2,1)} %get-tuple-element.319), channel_id=1, source_target_pairs={{64,96},{96,64},{65,97},{97,65},{66,98},{98,66},{67,99},{99,67},{6... | collective-permute-start | bytes 589832 | tf_op jit(solution)/shard_map/ppermute | solution.py:82
  578.6 12.3 %collective-permute-start.61 = (bf16[96,1024]{1,0:T(8,128)(2,1)S(1)}, bf16[96,1024]{1,0:T(8,128)(2,1)S(1)}, u32[]{:S(2)}, u32[]{:S(2)}) collective-permute-start(bf16[96,1024]{1,0:T(8,128)(2,1)S(1)} %get-tuple-element.318), channel_id=1, source_target_pairs={{0,64},{32,96},{1,65},{33,97},{2,66},{34,98},{3,67},{35,99},{4,68}... | collective-permute-start | bytes 589832 | tf_op jit(solution)/shard_map/ppermute | solution.py:82
  580.8 20.0 %collective-permute-start.64 = (bf16[96,3456]{1,0:T(8,128)(2,1)S(1)}, bf16[96,3456]{1,0:T(8,128)(2,1)S(1)}, u32[]{:S(2)}, u32[]{:S(2)}) collective-permute-start(bf16[96,3456]{1,0:T(8,128)(2,1)S(1)} %copy-done.92), channel_id=1, source_target_pairs={{64,96},{96,64},{65,97},{97,65},{66,98},{98,66},{67,99},{99,67},{6... | collective-permute-start | bytes 1990664 | tf_op jit(solution)/shard_map/ppermute | solution.py:82
  587.3 14.8 %collective-permute-start.59 = (bf16[96,1024]{1,0:T(8,128)(2,1)}, bf16[96,1024]{1,0:T(8,128)(2,1)S(1)}, u32[]{:S(2)}, u32[]{:S(2)}) collective-permute-start(bf16[96,1024]{1,0:T(8,128)(2,1)} %get-tuple-element.317), channel_id=1, source_target_pairs={{64,32},{96,0},{65,33},{97,1},{66,34},{98,2},{67,35},{99,3},{68,36... | collective-permute-start | bytes 589832 | tf_op jit(solution)/shard_map/ppermute | solution.py:82
  588.6 18.1 %collective-permute-start.57 = (bf16[96,1024]{1,0:T(8,128)(2,1)}, bf16[96,1024]{1,0:T(8,128)(2,1)}, u32[]{:S(2)}, u32[]{:S(2)}) collective-permute-start(bf16[96,1024]{1,0:T(8,128)(2,1)} %get-tuple-element.317), channel_id=1, source_target_pairs={{0,32},{32,0},{1,33},{33,1},{2,34},{34,2},{3,35},{35,3},{4,36},{36... | collective-permute-start | bytes 589832 | tf_op jit(solution)/shard_map/ppermute | solution.py:82
  590.9 14.6 %collective-permute-start.58 = (bf16[96,1024]{1,0:T(8,128)(2,1)}, bf16[96,1024]{1,0:T(8,128)(2,1)}, u32[]{:S(2)}, u32[]{:S(2)}) collective-permute-start(bf16[96,1024]{1,0:T(8,128)(2,1)} %get-tuple-element.316), channel_id=1, source_target_pairs={{64,0},{96,32},{65,1},{97,33},{66,2},{98,34},{67,3},{99,35},{68,4}... | collective-permute-start | bytes 589832 | tf_op jit(solution)/shard_map/ppermute | solution.py:82
  593.6 20.9 %collective-permute-start.68 = (bf16[96,3456]{1,0:T(8,128)(2,1)S(1)}, bf16[96,3456]{1,0:T(8,128)(2,1)S(1)}, u32[]{:S(2)}, u32[]{:S(2)}) collective-permute-start(bf16[96,3456]{1,0:T(8,128)(2,1)S(1)} %copy-done.92), channel_id=1, source_target_pairs={{0,96},{32,64},{1,97},{33,65},{2,98},{34,66},{3,99},{35,67},{4,100... | collective-permute-start | bytes 1990664 | tf_op jit(solution)/shard_map/ppermute | solution.py:82
  600.8 16.6 %collective-permute-start.67 = (bf16[96,3456]{1,0:T(8,128)(2,1)S(1)}, bf16[96,3456]{1,0:T(8,128)(2,1)S(1)}, u32[]{:S(2)}, u32[]{:S(2)}) collective-permute-start(bf16[96,3456]{1,0:T(8,128)(2,1)S(1)} %copy-done.91), channel_id=1, source_target_pairs={{0,64},{32,96},{1,65},{33,97},{2,66},{34,98},{3,67},{35,99},{4,68}... | collective-permute-start | bytes 1990664 | tf_op jit(solution)/shard_map/ppermute | solution.py:82
  602.1 29.9 %collective-permute-start.63 = (bf16[96,3456]{1,0:T(8,128)(2,1)S(1)}, bf16[96,3456]{1,0:T(8,128)(2,1)S(1)}, u32[]{:S(2)}, u32[]{:S(2)}) collective-permute-start(bf16[96,3456]{1,0:T(8,128)(2,1)S(1)} %get-tuple-element.303), channel_id=1, source_target_pairs={{0,32},{32,0},{1,33},{33,1},{2,34},{34,2},{3,35},{35,3},{4,36},{36... | collective-permute-start | bytes 1990664 | tf_op jit(solution)/shard_map/ppermute | solution.py:82
  605.5 33.0 %collective-permute-start.66 = (bf16[96,3456]{1,0:T(8,128)(2,1)S(1)}, bf16[96,3456]{1,0:T(8,128)(2,1)S(1)}, u32[]{:S(2)}, u32[]{:S(2)}) collective-permute-start(bf16[96,3456]{1,0:T(8,128)(2,1)S(1)} %get-tuple-element.303), channel_id=1, source_target_pairs={{64,32},{96,0},{65,33},{97,1},{66,34},{98,2},{67,35},{99,3},{68,36... | collective-permute-start | bytes 1990664 | tf_op jit(solution)/shard_map/ppermute | solution.py:82
  606.8 31.7 %collective-permute-start.65 = (bf16[96,3456]{1,0:T(8,128)(2,1)S(1)}, bf16[96,3456]{1,0:T(8,128)(2,1)S(1)}, u32[]{:S(2)}, u32[]{:S(2)}) collective-permute-start(bf16[96,3456]{1,0:T(8,128)(2,1)S(1)} %get-tuple-element.302), channel_id=1, source_target_pairs={{64,0},{96,32},{65,1},{97,33},{66,2},{98,34},{67,3},{99,35},{68,4}... | collective-permute-start | bytes 1990664 | tf_op jit(solution)/shard_map/ppermute | solution.py:82
  (120 other events, 1010.9 us)
Sparse Core Ops, SparseCore 0:
  35.7 29.2 all-gather.4
  70.3 58.7 all-gather.6
  161.3 27.6 all-gather.10
  190.5 57.5 all-gather.8
  371.6 56.9 reduce-scatter.3
  431.1 25.4 reduce-scatter.5
  464.6 56.2 reduce-scatter.7

commit v3 on v2

--- a/solution.py
+++ b/solution.py
@@ -167,13 +167,11 @@
 
 
 def attention_forward_kernel(t_ref, *refs):
-    hidden, (w0, w1) = refs[:4], refs[4:6]
-    parts, (normed_ref, qkv_ref, probs_ref, attended_ref, small_ref) = refs[6:10], refs[10:]
-    for at, w in ((0, w0), (HALF, w1)):
-        small_ref[:, at : at + HALF] = w[:, ATT:].astype(F32).T[:SMALL]
+    hidden, (gain, w0, w1) = refs[:4], refs[4:7]
+    parts, (normed_ref, qkv_ref, probs_ref, attended_ref) = refs[7:11], refs[11:]
     for index, ref in enumerate(hidden):
         rows = ref[...].astype(F32)
-        normed_ref[block(index), :] = (rows * rms_factor(rows) * small_ref[0:1, :]).astype(BF)
+        normed_ref[block(index), :] = (rows * rms_factor(rows) * gain[...]).astype(BF)
     normed = normed_ref[...]
     qkv = nn(normed[:, :HALF], w0[:, :QKV]) + nn(normed[:, HALF:], w1[:, :QKV])
     qkv = qkv.astype(BF)
@@ -196,12 +194,11 @@
             part[:, at : at + HALF] = out[block(index)]
 
 
-def attention_forward(t, hidden_blocks, weights):
+def attention_forward(t, hidden_blocks, gain, weights):
     outs = [shaped((ROWS, D))] * 4
     outs += [shaped((LEN, D)), shaped((LEN, QKV)), shaped((GROUPS, LEN, LEN)), shaped((LEN, STEP))]
-    outs += [shaped((SMALL, D), F32)]
     flops = 2 * LEN * D * ATT + 4 * GROUPS * LEN * LEN * HD
-    got = run(attention_forward_kernel, outs, [t, *hidden_blocks, *weights], 1, flops)
+    got = run(attention_forward_kernel, outs, [t, *hidden_blocks, gain, *weights], 1, flops)
     return got[:4], got[4:]
 
 
@@ -434,12 +431,18 @@
         copies[block(index), :] = normed
 
 
-def result_kernel(mid, got, out):
-    out[...] = (mid[...] + add_blocks(got)).astype(BF)
+def last_kernel(mid, total, out):
+    out[...] = (mid[...] + total[...].astype(F32)).astype(BF)
+
+
+def result_kernel(mid, got, *outs):
+    result = (mid[...] + add_blocks(got)).astype(BF)
+    for out in outs:
+        out[...] = result
 
 
 def mid_backward_kernel(mid, own_gates, out_grad, gain, router, normed, got, *refs):
-    mid_grad_ref, low_ref, gain_grad, router_grad = refs
+    mid_grad_ref, low_ref, small = refs
     total = add_blocks(got)
     extra = total[:, D:]
     gate_grad = (extra + pltpu.roll(extra, HD - E, 1))[:, :E]
@@ -447,33 +450,62 @@
     logits_grad = own * (gate_grad - jnp.sum(own * gate_grad, axis=1, keepdims=True))
     logits_grad = logits_grad.astype(BF)
     upstream = total[:, :D] + nn(logits_grad, router[...])
-    grad, gain_grad[...] = norm_backward(mid[...], gain[...], upstream)
-    router_grad[...] = tn(logits_grad, normed[...])
+    small[...] = jnp.zeros_like(small)
+    grad, small[1:2, :] = norm_backward(mid[...], gain[...], upstream)
+    small[2 : 2 + E, :] = tn(logits_grad, normed[...])
     mid_grad = out_grad[...].astype(F32) + grad
     mid_grad_ref[...] = mid_grad
     low_ref[...] = mid_grad.astype(BF)
 
 
-def hidden_backward_kernel(hidden, gain, mid_grad, *refs):
-    out, gain_grad, copies = refs[-3:]
-    grad, gain_grad[...] = norm_backward(hidden[...].astype(F32), gain[...], add_up(refs[:-3]))
+def hidden_backward_kernel(hidden, gain, mid_grad, small_in, *refs):
+    out, small, copies = refs[-3:]
+    small[...] = small_in[...]
+    grad, small[0:1, :] = norm_backward(hidden[...].astype(F32), gain[...], add_up(refs[:-3]))
     low = (mid_grad[...] + grad).astype(BF)
     out[...] = low
     for index in range(8):
         copies[block(index), :] = low
 
 
-def send_home(blocks, home):
-    blocks = blocks.reshape(2, DBLK, -1)
-    beside = move(blocks[1], SIDE, lambda s, x: (s, x + 1), lambda s, x: s == home)
-    straight = move(blocks[0], SIDE, lambda s, x: (s + 1, x), lambda s, x: s != home)
-    across = move(blocks[1], SIDE, lambda s, x: (s + 1, x + 1), lambda s, x: s != home)
-    return blocks[0], beside, straight, across
-
-
-def from_home(sent):
-    own, beside, straight, across = [x.astype(F32) for x in sent]
-    return own + beside, straight + across
+def small_forward_kernel(own, other, out):
+    out[:, :HALF] = own[...].astype(F32).T[:64]
+    out[:, HALF:] = other[...].astype(F32).T[:64]
+
+
+def small_backward_kernel(first, second, own, other, both):
+    both[...] = jnp.zeros_like(both)
+    both[:SMALL, :] = first[...]
+    both[32 : 32 + SMALL, :] = second[...]
+    own[...] = both[:, :HALF].T.astype(BF)
+    other[...] = both[:, HALF:].T.astype(BF)
+
+
+def final_kernel(s_ref, own, beside, straight, across, *outs):
+    query, key, value, out, shared_in, shared_down, expert_in, expert_down, small = outs
+    mine = own[...].astype(F32) + beside[...].astype(F32)
+    theirs = straight[...].astype(F32) + across[...].astype(F32)
+    att = mine[:, PIECE:] + theirs[:, PIECE:]
+    query[...] = att[:, : GROUPS * HD]
+    key[...] = att[:, KEYS]
+    value[...] = att[:, VALUES]
+    out[...] = att[:, QKV:ATT]
+    small[...] = att[:, ATT:]
+    for half in (0, 1):
+        part = jnp.where(s_ref[0] == half, mine, theirs)
+        for number in range(BLOCKS):
+            at = number // 3 * 2 * STEP + number % 3 * HD
+            gate_part, up_part = part[:, at : at + HD], part[:, at + STEP : at + STEP + HD]
+            down = part[:, UP + number * HD : UP + (number + 1) * HD]
+            if number < HALF_E:
+                expert = half * HALF_E + number
+                expert_in[:, head(2 * expert)] = gate_part
+                expert_in[:, head(2 * expert + 1)] = up_part
+                expert_down[expert] = down
+            else:
+                shared_in[:, head(half)] = gate_part
+                shared_in[:, head(2 + half)] = up_part
+                shared_down[:, head(half)] = down
 
 
 def swap_core(part):
@@ -514,9 +546,8 @@
     s_arg = s.astype(jnp.int32)[None]
     t_arg = t.astype(jnp.int32)[None]
 
-    small = jnp.concatenate(
-        [gain_attn[0][:, None], gain_ffn[0][:, None], w_router[0], jnp.zeros((24, 110), BF)], axis=1
-    )
+    small = jnp.concatenate([gain_attn[0][:, None], gain_ffn[0][:, None], w_router[0]], axis=1)
+    small = jnp.pad(small, ((0, 0), (0, HD - 2 - E)))
     small = rolled(jnp.stack(tensor_gather(small)), (4 - t) % 4).reshape(DBLK, HD)
     att_piece = jnp.concatenate([w_query[0], w_key[0], w_value[0], w_out[0].T, small], axis=1)
 
@@ -533,23 +564,29 @@
     ffn_own = jnp.where(first, ffn_piece(0), ffn_piece(1))
     ffn_other = jnp.where(first, ffn_piece(1), ffn_piece(0))
 
+    named = jnp.sum((route_experts[0][:, :, :, None] == jnp.arange(E)).astype(F32), axis=2)
+    named = named.astype(BF).reshape(ROUTES, E)
+    named_else = move(named, SECTION, lambda s: (s + 1,))
+    att_piece, named_else = together(att_piece, named_else)
+    masks = [jnp.where(s == layer, named, named_else).astype(F32) for layer in (0, 1)]
+
     att_beside = move(att_piece, SIDE, lambda s, x: (s, x + 1))
     att_straight = move(att_piece, SIDE, lambda s, x: (s + 1, x))
     att_across = move(att_piece, SIDE, lambda s, x: (s + 1, x + 1))
-    att_beside, att_straight, att_across, ffn_own, ffn_other = together(
-        att_beside, att_straight, att_across, ffn_own, ffn_other
-    )
+    att_straight, ffn_own, ffn_other = together(att_straight, ffn_own, ffn_other)
     att_same = jnp.concatenate([att_piece, att_beside], axis=0)
     att_else = jnp.concatenate([att_straight, att_across], axis=0)
     att_pairs = [jnp.where(first, att_same, att_else), jnp.where(first, att_else, att_same)]
     ffn_straight = move(ffn_other, SIDE, lambda s, x: (s + 1, x))
     ffn_across = move(ffn_other, SIDE, lambda s, x: (s + 1, x + 1))
     ffn_beside0 = move(ffn_own, SIDE, lambda s, x: (s, x + 1), lambda s, x: s == 0)
-    ffn_else = jnp.concatenate([ffn_straight, ffn_across], axis=0)
-    ffn_pair0 = jnp.where(first, jnp.concatenate([ffn_own, ffn_beside0], axis=0), ffn_else)
-
-    att_row0 = gather_row(att_pairs[0])
-    ffn_row0 = gather_row(ffn_pair0)
+
+    smalls = [pair[:, ATT : ATT + 32] for pair in att_pairs]
+    att_pair0 = jnp.concatenate(
+        [att_pairs[0][:, :ATT], *smalls, jnp.zeros((2 * DBLK, HD - 64), BF)], axis=1
+    )
+    att_pair1 = att_pairs[1][:, :ATT]
+    att_row0 = gather_row(att_pair0)
 
     place = jnp.arange(D, dtype=jnp.int32)
     at_core = (place // HALF + core) % 2
@@ -559,28 +596,40 @@
     order = (place[:, None] == column[None, :]).astype(BF)
 
     own_tokens = lax.dynamic_index_in_dim(tokens, s, 0, keepdims=False)
-    own_cotangent = lax.dynamic_index_in_dim(cotangent, s, 0, keepdims=False)
-    own_rows = nn(jnp.concatenate([own_tokens, own_cotangent], axis=0), order).astype(BF)
+    own_rows = jnp.concatenate([own_tokens, cotangent.reshape(2 * ROWS, D)], axis=0)
+    own_rows = nn(own_rows, order).astype(BF)
     hidden_blocks = tensor_gather(own_rows[:ROWS])
-    own_cotangent = own_rows[ROWS:]
-
-    named = jnp.sum((route_experts[0][:, :, :, None] == jnp.arange(E)).astype(F32), axis=2)
-    named = named.astype(BF).reshape(ROUTES, E)
-    named_else = move(named, SECTION, lambda s: (s + 1,))
-
-    masks = [jnp.where(s == layer, named, named_else).astype(F32) for layer in (0, 1)]
-
-    att_row0, masks[0], masks[1], *hidden_blocks = together(
-        att_row0, masks[0], masks[1], *hidden_blocks
-    )
+    both_cotangents = own_rows[ROWS:]
+    own_cotangent = lax.dynamic_slice_in_dim(both_cotangents, s * ROWS, ROWS, 0)
+    grad_rows = lax.all_to_all(jnp.tile(both_cotangents, (4, 1)), "tensor", 0, 0, tiled=True)
+
+    from_x = (ffn_straight, ffn_across, ffn_beside0)
+    from_x, hidden_blocks, grad_rows, att_row0 = together(
+        from_x, hidden_blocks, grad_rows, att_row0
+    )
+    ffn_straight, ffn_across, ffn_beside0 = from_x
+    ffn_else = jnp.concatenate([ffn_straight, ffn_across], axis=0)
+    ffn_pair0 = jnp.where(first, jnp.concatenate([ffn_own, ffn_beside0], axis=0), ffn_else)
+    ffn_pair0, hidden_blocks = together(ffn_pair0, hidden_blocks)
+    ffn_row0 = gather_row(ffn_pair0)
+    grad_rows = grad_rows.reshape(4, 2, ROWS, D).swapaxes(0, 1).reshape(ROUTES, D)
     att_w = [(att_row0, swap_core(att_row0)), None]
+    small = run(
+        small_forward_kernel,
+        [shaped((64, D), F32)],
+        att_w[0],
+        in_specs=[pl.BlockSpec((HALF, HD), lambda i: (0, ATT // HD))] * 2,
+        out_specs=[pl.BlockSpec((64, D), lambda i: (0, 0))],
+        grid=(1,),
+    )[0]
     ffn_w = [None, None]
-    layer_values = []
     kept = []
     for layer in (0, 1):
-        parts, att_saved = attention_forward(t_arg, hidden_blocks, att_w[layer])
-        normed, *att_saved, small = att_saved
-        attn_gain, ffn_gain, router = small[0:1], small[1:2], small[2 : 2 + E].astype(BF)
+        at = 32 * layer
+        attn_gain, ffn_gain = small[at : at + 1], small[at + 1 : at + 2]
+        router = small[at + 2 : at + 2 + E].astype(BF)
+        parts, att_saved = attention_forward(t_arg, hidden_blocks, attn_gain, att_w[layer])
+        normed, *att_saved = att_saved
         mid, normed_ffn, copies = run(
             mid_kernel,
             [shaped((ROWS, D), F32), shaped((ROWS, D)), shaped((ROUTES, D))],
@@ -588,14 +637,11 @@
         )
         rows = group_exchange(copies)
         if layer == 0:
-            normed, own_cotangent = together(normed, own_cotangent)
-            grad_rows = group_exchange(jnp.tile(own_cotangent, (8, 1)))
-            ffn_row0, rows, grad_rows, att_pair1, ffn_own, ffn_else = together(
-                ffn_row0, rows, grad_rows, att_pairs[1], ffn_own, ffn_else
-            )
-            ffn_w[0] = (ffn_row0, swap_core(ffn_row0))
+            normed, ffn_own = together(normed, ffn_own)
             ffn_beside1 = move(ffn_own, SIDE, lambda s, x: (s, x + 1), lambda s, x: s == 1)
             ffn_pair1 = jnp.where(first, ffn_else, jnp.concatenate([ffn_own, ffn_beside1], axis=0))
+            ffn_row0, rows, att_pair1, ffn_pair1 = together(ffn_row0, rows, att_pair1, ffn_pair1)
+            ffn_w[0] = (ffn_row0, swap_core(ffn_row0))
             att_row1 = gather_row(att_pair1)
             ffn_row1 = gather_row(ffn_pair1)
         else:
@@ -604,14 +650,15 @@
         part, gates, own_gates, gate_up, gated = ffn_forward(
             s_arg, t_arg, rows, router, masks[layer], ffn_w[layer]
         )
-        result = run(result_kernel, [shaped((ROWS, D))], [mid, group_exchange(part)])[0]
-        layer_values.append(result)
+        if layer == 1:
+            sum1 = lax.psum_scatter(part, GROUP, scatter_dimension=0, tiled=True)
         kept.append((hidden_blocks[0], attn_gain, normed, *att_saved))
         kept.append((mid, ffn_gain, router, normed_ffn, rows, gates, own_gates, gate_up, gated))
         if layer == 0:
-            hidden_blocks = tensor_gather(result)
-            att_row1, own_gates = together(att_row1, own_gates)
-            kept[1] = (*kept[1][:6], own_gates, gate_up, gated)
+            outs = [shaped((ROWS, D))] * 2
+            own_result, result = run(result_kernel, outs, [mid, group_exchange(part)])
+            hidden_blocks = tensor_gather(own_result)
+            att_row1, result = together(att_row1, result)
             att_w[1] = (att_row1, swap_core(att_row1))
 
     in_grads = [None, None]
@@ -622,63 +669,90 @@
     for layer in (1, 0):
         hidden, attn_gain, normed, qkv, probs, attended = kept[2 * layer]
         mid, ffn_gain, router, normed_ffn, rows, gates, own_gates, gate_up, gated = kept[2 * layer + 1]
-        part, gate_up_grad = ffn_backward(s_arg, grad_rows, gates, gate_up, ffn_w[layer])
+        if layer == 0:
+            gated, sum1 = together(gated, sum1)
+        part_grad, gate_up_grad = ffn_backward(s_arg, grad_rows, gates, gate_up, ffn_w[layer])
         ffn_parts = (rows, grad_rows, gate_up_grad, gated)
-        other = None
+        got = group_exchange(part_grad)
+        own = ffn_weights(0, *ffn_parts, swap_core(ffn_weights(1, *ffn_parts)))
+        got, own = together(got, own)
         if layer == 0:
-            part, other = together(part, ffn_weights(1, *ffn_parts))
-            other = swap_core(other)
-        mid_grad, mid_low, grad_gain_ffn, grad_router = run(
+            own, ffn_sums[1] = together(own, ffn_sums[1])
+        ffn_sums[layer] = sum_row(own)
+        mid_grad, mid_low, small = run(
             mid_backward_kernel,
-            [
-                shaped((ROWS, D), F32),
-                shaped((ROWS, D)),
-                shaped((1, D), F32),
-                shaped((E, D), F32),
-            ],
-            [mid, own_gates, out_low, ffn_gain, router, normed_ffn, group_exchange(part)],
+            [shaped((ROWS, D), F32), shaped((ROWS, D)), shaped((SMALL, D), F32)],
+            [mid, own_gates, out_low, ffn_gain, router, normed_ffn, got],
         )
         mid_blocks = tensor_gather(mid_low)
-        if layer == 1:
-            *mid_blocks, other = together(*mid_blocks, ffn_weights(1, *ffn_parts))
-            other = swap_core(other)
-        else:
-            gate_up_grad, ffn_sums[1] = together(gate_up_grad, ffn_sums[1])
-            own = ffn_weights(0, rows, grad_rows, gate_up_grad, gated, other)
-            *mid_blocks, own = together(*mid_blocks, own)
-            ffn_sums[0] = sum_row(own)
         parts, mid_rows, qkv_grad = attention_backward(mid_blocks, att_w[layer], qkv, probs)
         got = tensor_send(parts)
         att_parts = (normed, mid_rows, qkv_grad, attended)
         att_other = attention_weights(1, *att_parts)
+        att_own = attention_weights(0, *att_parts, swap_core(att_other))
         if layer == 1:
-            own = ffn_weights(0, *ffn_parts, other)
-            *got, att_other, own = together(*got, att_other, own)
-            ffn_sums[1] = sum_row(own)
+            *got, att_other = together(*got, att_other)
         else:
-            *got, att_other = together(*got, att_other)
-        out_low, grad_gain_attn, copies = run(
+            *got, att_own = together(*got, att_own)
+        out_low, small_grads[layer], copies = run(
             hidden_backward_kernel,
-            [shaped((ROWS, D)), shaped((1, D), F32), shaped((ROUTES, D))],
-            [hidden, attn_gain, mid_grad, parts[0], *got],
+            [shaped((ROWS, D)), shaped((SMALL, D), F32), shaped((ROUTES, D))],
+            [hidden, attn_gain, mid_grad, small, parts[0], *got],
         )
         in_grads[layer] = out_low
-        small_grads[layer] = jnp.concatenate([grad_gain_attn, grad_gain_ffn, grad_router], axis=0)
-        att_own = attention_weights(0, *att_parts, swap_core(att_other))
         if layer == 1:
             grad_rows, att_own = together(group_exchange(copies), att_own)
             att_sums[1] = sum_row(att_own)
-    att_blocks = rolled(att_own.reshape(4, 2 * DBLK, ATT), z)
-    total = att_blocks[0].astype(F32)
-    for k in (1, 2, 3):
-        total = total + move(att_blocks[k], ROW, lambda at, k=k: (at + k,)).astype(F32)
-    att_sums[0] = total.astype(BF)
-    out_low, ffn_sums[1], att_sums[1] = together(in_grads[0], ffn_sums[1], att_sums[1])
-    in_grads[0] = out_low
-    ffn_home = [None, send_home(ffn_sums[1], 1)]
-    att_home = [None, send_home(att_sums[1], 1)]
-    att_home[0] = send_home(att_sums[0], 0)
-    ffn_home[0] = send_home(ffn_sums[0], 0)
+    def sum_z(part):
+        blocks = rolled(part.reshape(4, 2 * DBLK, -1), z)
+        total = blocks[0].astype(F32)
+        for k in (1, 2, 3):
+            total = total + move(blocks[k], ROW, lambda at, k=k: (at + k,)).astype(F32)
+        return total.astype(BF)
+
+    small_own, small_other = run(
+        small_backward_kernel,
+        [shaped((HALF, HD))] * 2,
+        small_grads,
+        scratch=[pltpu.VMEM((HD, D), F32)],
+    )
+    small_own = small_own.astype(F32) + swap_core(small_other).astype(F32)
+    small_sum = sum_z(small_own.astype(BF))
+    att_sums[0] = jnp.concatenate([sum_z(att_own), small_sum[:, :32]], axis=1)
+    att_sums[1] = jnp.concatenate([att_sums[1], small_sum[:, 32:64]], axis=1)
+    result1 = run(last_kernel, [shaped((ROWS, D))], [kept[3][0], sum1])[0]
+    sums = [
+        jnp.concatenate([ffn, att, jnp.zeros((2 * DBLK, HD - 32), BF)], axis=1)
+        for ffn, att in zip(ffn_sums, att_sums)
+    ]
+    sums = together(*sums)
+
+    same = jnp.where(first, sums[0], sums[1]).reshape(2, DBLK, -1)
+    other = jnp.where(first, sums[1], sums[0]).reshape(2, DBLK, -1)
+    beside = move(same[1], SIDE, lambda s, x: (s, x + 1))
+    straight = move(other[0], SIDE, lambda s, x: (s + 1, x))
+    across = move(other[1], SIDE, lambda s, x: (s + 1, x + 1))
+    grads = run(
+        final_kernel,
+        [
+            shaped(shape, F32)
+            for shape in (
+                (DBLK, GROUPS * HD),
+                (DBLK, HD),
+                (DBLK, HD),
+                (DBLK, GROUPS * HD),
+                (DBLK, 4 * HD),
+                (DBLK, 2 * HD),
+                (DBLK, 2 * E * HD),
+                (E, DBLK, HD),
+                (DBLK, HD),
+            )
+        ],
+        [s_arg, same[0], beside, straight, across],
+        1,
+    )
+    grad_query, grad_key, grad_value, grad_out, grad_shared_in, grad_shared_down = grads[:6]
+    grad_expert_in, grad_expert_down, small = grads[6:]
 
     def both_sequences(values):
         low = nt(jnp.concatenate(values, axis=0), order).astype(BF).reshape(2, ROWS, D)
@@ -686,55 +760,28 @@
         got = move(jnp.where(first, low[1], low[0]), SECTION, lambda s: (s + 1,))
         return jnp.where(first, jnp.stack([mine, got]), jnp.stack([got, mine]))[None]
 
-    values_out = both_sequences(layer_values)
+    values_out = both_sequences([result, result1])
     grads_in = both_sequences(in_grads)
 
-    att_home = [sum(from_home(sent)) for sent in att_home]
-    ffn_home = [from_home(sent) for sent in ffn_home]
-    att = jnp.where(first, att_home[0], att_home[1])
-    ffn_mine = jnp.where(first, ffn_home[0][0], ffn_home[1][0])
-    ffn_got = jnp.where(first, ffn_home[0][1], ffn_home[1][1])
-    ffn_parts = (jnp.where(first, ffn_mine, ffn_got), jnp.where(first, ffn_got, ffn_mine))
-
-    values = jnp.concatenate(small_grads, axis=0).T.reshape(2, 4, 2, DBLK, 2 * (2 + E))
-    values = values[0] + move(values[1], CORE, lambda c: (1 - c,))
-    values = rolled(values, z)
-    total = values[0]
-    for k in (1, 2, 3):
-        total = total + move(values[k], ROW, lambda at, k=k: (at + k,))
-    total = total[0] + move(total[1], ("xhi",), lambda x: (x + 1,))
-    halves = total.reshape(DBLK, 2, 2 + E).swapaxes(0, 1)
-    mine = jnp.where(first, halves[0], halves[1])
-    theirs = jnp.where(first, halves[1], halves[0])
-    total = mine + move(theirs, SECTION, lambda s: (s + 1,))
-    total = rolled(total.reshape(4, DBLK // 4, 2 + E), t)
-    small_sum = total[0]
-    for got in tensor_send([total[k] for k in range(4)]):
+    small = rolled(small.reshape(4, DBLK // 4, HD), t)
+    small_sum = small[0]
+    for got in tensor_send([small[k] for k in range(4)]):
         small_sum = small_sum + got
 
-    ups, downs = [], []
-    for part in ffn_parts:
-        up = part[:, :UP].reshape(DBLK, STEPS, 2, 3, HD).swapaxes(2, 3)
-        ups.append(up.reshape(DBLK, BLOCKS, 2, HD))
-        downs.append(part[:, UP:].reshape(DBLK, BLOCKS, HD))
-    grad_expert_in = jnp.concatenate([up[:, :HALF_E] for up in ups], axis=1)
-    grad_shared_in = jnp.concatenate([up[:, HALF_E] for up in ups], axis=2)
-    grad_expert_down = jnp.concatenate([down[:, :HALF_E] for down in downs], axis=1)
-    grad_shared_down = jnp.concatenate([down[:, HALF_E] for down in downs], axis=1)
     return (
         values_out,
         grads_in,
         small_sum[:, 0][None],
-        att[:, : GROUPS * HD][None],
-        att[:, KEYS][None],
-        att[:, VALUES][None],
-        att[:, QKV:].T[None],
+        grad_query[None],
+        grad_key[None],
+        grad_value[None],
+        grad_out.T[None],
         small_sum[:, 1][None],
-        small_sum[:, 2:][None],
-        grad_shared_in[None],
+        small_sum[:, 2 : 2 + E][None],
+        grad_shared_in.reshape(1, DBLK, 2, 2 * HD),
         grad_shared_down.T[None],
-        grad_expert_in[None],
-        grad_expert_down.transpose(1, 2, 0)[None],
+        grad_expert_in.reshape(1, DBLK, E, 2, HD),
+        grad_expert_down.swapaxes(1, 2)[None],
     )
 
 

time: 666 us -> 598 us (0.90)
  blocking collectives: 114 us -> 25.3 us
  waiting for transfers between devices: 190 us -> 233 us
  starting transfers between devices: 122 us -> 111 us
  local copies, waits for them, and re-layouts: 83.8 us -> 73.4 us
    all_to_all x4 -> x1, blocking collectives: 114 us -> 25.3 us  [group_exchange(): return lax.all_to_all(rows, GROUP, 0, 0, tiled=True)]
    ppermute x69 -> x58, waiting for transfers between devices: 139 us -> 160 us  [move(): return lax.ppermute(block, axes, pairs)]
    all_to_all x4 -> x5, waiting for transfers between devices: 49.4 us -> 68 us  [group_exchange(): return lax.all_to_all(rows, GROUP, 0, 0, tiled=True)]
    ppermute x69 -> x58, starting transfers between devices: 96.6 us -> 78.3 us  [move(): return lax.ppermute(block, axes, pairs)]
    slice x21 -> x10, local copies, waits for them, and re-layouts: 13.4 us -> 2.52 us  [the longest x1 0.79 us: per_device(): att_pair1 = att_pairs[1][:, :ATT]]
    all_to_all x4 -> x5, starting transfers between devices: 24.7 us -> 28.4 us  [group_exchange(): return lax.all_to_all(rows, GROUP, 0, 0, tiled=True)]
    pallas_call x24 -> x27, Pallas kernels: 104 us -> 107 us  [run(): pl.pallas_call(kernel, out_shape=list(outs), in_specs=in_specs, out_specs...]
    unnamed x229 -> x237, local copies, waits for them, and re-layouts: 44.8 us -> 47 us
  transfers between devices with their start and end apart: 80 -> 72, of which waited for: 38 -> 44; matrix products, arithmetic and copies ran while one was open for 9% -> 8% of each run, Pallas kernels for 12% -> 13%
where the time goes in v3:
time: 598 us; the launch traced here: 588 us
  waiting for transfers between devices  233 us (39%)
  starting transfers between devices  111 us (19%)
  Pallas kernels  107 us (18%)
  local copies, waits for them, and re-layouts  73.4 us (12%)
  blocking collectives  25.3 us (4%)
  between operations  15.9 us (3%)
  other arithmetic  14.3 us (2%)
  matrix products  7.22 us (1%)
    ppermute x58, waiting for transfers between devices, move(): return lax.ppermute(block, axes, pairs)  160 us
    pallas_call x27, Pallas kernels, run(): pl.pallas_call(kernel, out_shape=list(outs), in_specs=in_specs, out_specs...  107 us
    ppermute x58, starting transfers between devices, move(): return lax.ppermute(block, axes, pairs)  78.3 us
    all_to_all x5, waiting for transfers between devices, group_exchange(): return lax.all_to_all(rows, GROUP, 0, 0, tiled=True)  68 us
    unnamed x237, local copies, waits for them, and re-layouts  47 us
    all_to_all x5, starting transfers between devices, group_exchange(): return lax.all_to_all(rows, GROUP, 0, 0, tiled=True)  28.4 us
    all_to_all x1, blocking collectives, group_exchange(): return lax.all_to_all(rows, GROUP, 0, 0, tiled=True)  25.3 us
  transfers between devices with their start and end apart: 72, of which 44 were waited for; matrix products, arithmetic and copies ran while one was open for 8% of the time, Pallas kernels for 13%

profile of v3, /device:TPU:8, one launch (start us, length us, event | category | flops | bytes accessed | tf_op | source)
XLA Modules:
  0.0 587.5 jit_solution(2626022103216513252)
XLA Ops:
  29.4 2.8 collective-permute-start.12
  33.0 4.3 collective-permute-done.4
  37.3 2.9 collective-permute-done.12
  46.8 3.7 all-to-all-start
  53.2 3.3 collective-permute-start.7
  56.7 2.8 collective-permute-start.9
  59.5 14.4 %collective-permute-done.8.refs_1_ = bf16[64,1536]{1,0:T(8,128)(2,1)S(1)} collective-permute-done((bf16[64,1536]{1,0:T(8,128)(2,1)S(1)}, bf16[64,1536]{1,0:T(8,128)(2,1)S(1)}, u32[]{:S(2)}, u32[]{:S(2)}) %collective-permute-start.8) | collective-permute-done | bytes 196640 | tf_op jit(solution)/shard_map/ppermute | solution.py:82
  76.6 2.9 collective-permute-done.10.refs_3_
  84.8 2.9 maximum_select_fusion
  88.1 3.7 collective-permute-done.13.other.refs_6_.refs_5_
  93.0 3.5 shard_map.238
  105.5 3.4 collective-permute-done.14.refs_1_
  108.9 2.7 collective-permute-done.15.refs_2_
  111.6 3.0 collective-permute-done.16.refs_3_
  116.7 6.2 %all-to-all-start.1 = ((bf16[8,64,1536]{2,1,0:T(8,128)(2,1)}), bf16[8,64,1536]{2,1,0:T(8,128)(2,1)S(1)}, u32[]{:S(2)}, u32[]{:S(2)}) async-start(bf16[8,64,1536]{2,1,0:T(8,128)(2,1)} %bitcast.34), calls=%async_computation.1 | async-start | bytes 3145728 | tf_op jit(solution)/shard_map/all_to_all | solution.py:123
  123.7 3.1 maximum_select_fusion.1
  126.8 15.6 %all-to-all-done.1 = bf16[8,64,1536]{2,1,0:T(8,128)(2,1)S(1)} async-done(((bf16[8,64,1536]{2,1,0:T(8,128)(2,1)}), bf16[8,64,1536]{2,1,0:T(8,128)(2,1)S(1)}, u32[]{:S(2)}, u32[]{:S(2)}) %all-to-all-start.1) | async-done | bytes 1572896 | tf_op jit(solution)/shard_map/all_to_all | solution.py:123
  142.4 2.9 all-gather.7.cloned.1.call-done.up0.down0
  148.3 6.3 %collective-permute-done.18.up1.down1 = bf16[768,3456]{1,0:T(8,128)(2,1)} collective-permute-done((bf16[768,3456]{1,0:T(8,128)(2,1)}, bf16[768,3456]{1,0:T(8,128)(2,1)}, u32[]{:S(2)}, u32[]{:S(2)}) %collective-permute-start.18) | collective-permute-done | bytes 5308448 | tf_op jit(solution)/shard_map/ppermute | solution.py:82
  154.6 12.4 %shard_map.240 = (bf16[512,1536]{1,0:T(8,128)(2,1)S(1)}, f32[512,16]{1,0:T(8,128)S(1)}, f32[64,16]{1,0:T(8,128)S(1)}, bf16[512,2304]{1,0:T(8,128)(2,1)}, bf16[512,1152]{1,0:T(8,128)(2,1)S(1)}) custom-call(s32[1]{0:T(128)} %bitcast.36.s_ref, s32[1]{0:T(128)} %bitcast.33.t_ref, bf16[512,1536]{1,0:T(8,128)(2,1)S(1)} %bitcast.144, ...), custom_call_target="tpu_custom_call" | custom-call | flops 5435817984 | bytes 28037128 | tf_op jit(solution)/shard_map/pallas_call | solution.py:98
  167.1 25.3 %all_to_all.79 = bf16[8,64,1536]{2,1,0:T(8,128)(2,1)S(1)} all-to-all(bf16[8,64,1536]{2,1,0:T(8,128)(2,1)S(1)} %bitcast.162), channel_id=1, replica_groups=mesh['section'=2,'xhi'=2,'z'=4,'core'=2,'tensor'=4] {'section','tensor'}, dimensions={0} | all-to-all | bytes 3145728 | tf_op jit(solution)/shard_map/all_to_all | solution.py:123
  197.4 3.5 collective-permute-done.19.refs_1_
  200.9 4.0 collective-permute-done.20.refs_2_
  209.2 3.5 shard_map.242
  217.1 2.7 collective-permute-start.24
  220.2 3.2 collective-permute-done.23.refs_1_
  223.4 3.0 collective-permute-done.24.refs_2_
  226.4 3.0 collective-permute-done.25.refs_3_
  233.9 5.7 all-to-all-start.3
  239.7 2.7 copy.118
  242.4 17.2 %all-to-all-done.3 = bf16[8,64,1536]{2,1,0:T(8,128)(2,1)S(1)} async-done(((bf16[8,64,1536]{2,1,0:T(8,128)(2,1)}), bf16[8,64,1536]{2,1,0:T(8,128)(2,1)S(1)}, u32[]{:S(2)}, u32[]{:S(2)}) %all-to-all-start.3) | async-done | bytes 1572896 | tf_op jit(solution)/shard_map/all_to_all | solution.py:123
  259.6 12.6 %shard_map.244 = (bf16[512,1536]{1,0:T(8,128)(2,1)S(1)}, f32[512,16]{1,0:T(8,128)S(1)}, f32[64,16]{1,0:T(8,128)S(1)}, bf16[512,2304]{1,0:T(8,128)(2,1)}, bf16[512,1152]{1,0:T(8,128)(2,1)S(1)}) custom-call(s32[1]{0:T(128)} %bitcast.36.s_ref, s32[1]{0:T(128)} %bitcast.33.t_ref, bf16[512,1536]{1,0:T(8,128)(2,1)S(1)} %bitcast.147, ...), custom_call_target="tpu_custom_call" | custom-call | flops 5435817984 | bytes 28037128 | tf_op jit(solution)/shard_map/pallas_call | solution.py:98
  273.3 11.1 %shard_map.246 = (bf16[512,1664]{1,0:T(8,128)(2,1)S(1)}, bf16[512,2304]{1,0:T(8,128)(2,1)S(1)}) custom-call(s32[1]{0:T(128)} %bitcast.36.s_ref, bf16[512,1536]{1,0:T(8,128)(2,1)S(1)} %bitcast.153, f32[512,16]{1,0:T(8,128)S(1)} %get-tuple-element.183.gates_ref, bf16[512,2304]{1,0:T(8,128)(2,1)} %get-tuple-element.184.gate_up_ref, ...), custom_call_target="tpu_custom_call" | custom-call | flops 5435817984 | bytes 29261828 | tf_op jit(solution)/shard_map/pallas_call | solution.py:98
  285.9 6.9 %shard_map.247 = bf16[768,3456]{1,0:T(8,128)(2,1)} custom-call(bf16[512,1536]{1,0:T(8,128)(2,1)S(1)} %bitcast.148, bf16[512,1536]{1,0:T(8,128)(2,1)S(1)} %bitcast.154, bf16[512,2304]{1,0:T(8,128)(2,1)} %copy-done.7, bf16[512,1152]{1,0:T(8,128)(2,1)S(1)} %get-tuple-element.187.gated), custom_call_target="tpu_custom_call" | custom-call | flops 2717908992 | bytes 11993088 | tf_op jit(solution)/shard_map/pallas_call | solution.py:98
  292.8 5.4 all-to-all-start.4
  298.2 3.7 collective-permute-done.28.refs_0_
  304.6 7.7 %shard_map.248 = bf16[768,3456]{1,0:T(8,128)(2,1)} custom-call(bf16[512,1536]{1,0:T(8,128)(2,1)S(1)} %bitcast.149, bf16[512,1536]{1,0:T(8,128)(2,1)S(1)} %bitcast.155, bf16[512,2304]{1,0:T(8,128)(2,1)} %copy-done.7, bf16[512,1152]{1,0:T(8,128)(2,1)S(1)} %copy-done.16, bf16[768,3456]{1,0:T(8,128)(2,1)} %collective-permute-done.28.refs_0_), custom_call_target="tpu_custom_call" | custom-call | flops 2717908992 | bytes 17301504 | tf_op jit(solution)/shard_map/pallas_call | solution.py:98
  312.3 13.5 %all-to-all-done.4 = bf16[8,64,1664]{2,1,0:T(8,128)(2,1)} async-done(((bf16[8,64,1664]{2,1,0:T(8,128)(2,1)}), bf16[8,64,1664]{2,1,0:T(8,128)(2,1)}, u32[]{:S(2)}, u32[]{:S(2)}) %all-to-all-start.4) | async-done | bytes 1703968 | tf_op jit(solution)/shard_map/all_to_all | solution.py:123
  332.6 4.0 collective-permute-start.30
  341.6 5.8 collective-permute-done.30.refs_2_
  348.3 3.6 shard_map.250
  354.7 3.8 collective-permute-start.33
  358.5 3.7 collective-permute-done.32.refs_1_
  364.2 3.7 collective-permute-done.34.refs_3_
  370.8 5.8 all-to-all-start.5
  383.2 12.7 %all-to-all-done.5 = bf16[8,64,1536]{2,1,0:T(8,128)(2,1)S(1)} async-done(((bf16[8,64,1536]{2,1,0:T(8,128)(2,1)}), bf16[8,64,1536]{2,1,0:T(8,128)(2,1)S(1)}, u32[]{:S(2)}, u32[]{:S(2)}) %all-to-all-start.5) | async-done | bytes 1572896 | tf_op jit(solution)/shard_map/all_to_all | solution.py:123
  396.9 10.9 %shard_map.254 = (bf16[512,1664]{1,0:T(8,128)(2,1)S(1)}, bf16[512,2304]{1,0:T(8,128)(2,1)S(1)}) custom-call(s32[1]{0:T(128)} %bitcast.36.s_ref, bf16[512,1536]{1,0:T(8,128)(2,1)S(1)} %bitcast.150, f32[512,16]{1,0:T(8,128)S(1)} %copy-done.64, bf16[512,2304]{1,0:T(8,128)(2,1)} %get-tuple-element.210.gate_up_ref, ...), custom_call_target="tpu_custom_call" | custom-call | flops 5435817984 | bytes 29261828 | tf_op jit(solution)/shard_map/pallas_call | solution.py:98
  409.2 6.9 %shard_map.255 = bf16[768,3456]{1,0:T(8,128)(2,1)} custom-call(bf16[512,1536]{1,0:T(8,128)(2,1)S(1)} %bitcast.145, bf16[512,1536]{1,0:T(8,128)(2,1)S(1)} %bitcast.151, bf16[512,2304]{1,0:T(8,128)(2,1)} %copy-done.8, bf16[512,1152]{1,0:T(8,128)(2,1)S(1)} %copy-done.13), custom_call_target="tpu_custom_call" | custom-call | flops 2717908992 | bytes 11993088 | tf_op jit(solution)/shard_map/pallas_call | solution.py:98
  416.1 5.3 all-to-all-start.6
  421.6 3.6 collective-permute-done.36.refs_0_
  426.5 7.8 %shard_map.256 = bf16[768,3456]{1,0:T(8,128)(2,1)} custom-call(bf16[512,1536]{1,0:T(8,128)(2,1)S(1)} %bitcast.146, bf16[512,1536]{1,0:T(8,128)(2,1)S(1)} %bitcast.152, bf16[512,2304]{1,0:T(8,128)(2,1)} %copy-done.8, bf16[512,1152]{1,0:T(8,128)(2,1)S(1)} %copy-done.14, bf16[768,3456]{1,0:T(8,128)(2,1)} %collective-permute-done.36.refs_0_), custom_call_target="tpu_custom_call" | custom-call | flops 2717908992 | bytes 17301504 | tf_op jit(solution)/shard_map/pallas_call | solution.py:98
  434.2 8.9 %all-to-all-done.6 = bf16[8,64,1664]{2,1,0:T(8,128)(2,1)} async-done(((bf16[8,64,1664]{2,1,0:T(8,128)(2,1)}), bf16[8,64,1664]{2,1,0:T(8,128)(2,1)}, u32[]{:S(2)}, u32[]{:S(2)}) %all-to-all-start.6) | async-done | bytes 1703968 | tf_op jit(solution)/shard_map/all_to_all | solution.py:123
  452.4 2.9 collective-permute-done.37.refs_1_
  455.2 3.7 collective-permute-done.38.refs_2_
  460.4 3.7 shard_map.258
  468.7 3.2 collective-permute-start.41
  471.8 3.0 fusion.7
  478.2 3.4 collective-permute-done.42.refs_3_
  496.1 11.6 %collective-permute-done.47 = bf16[192,1024]{1,0:T(8,128)(2,1)S(1)} collective-permute-done((bf16[192,1024]{1,0:T(8,128)(2,1)S(1)}, bf16[192,1024]{1,0:T(8,128)(2,1)S(1)}, u32[]{:S(2)}, u32[]{:S(2)}) %collective-permute-start.47) | collective-permute-done | bytes 393248 | tf_op jit(solution)/shard_map/ppermute | solution.py:82
  509.7 7.6 %collective-permute-done.45 = bf16[192,1024]{1,0:T(8,128)(2,1)S(1)} collective-permute-done((bf16[192,1024]{1,0:T(8,128)(2,1)S(1)}, bf16[192,1024]{1,0:T(8,128)(2,1)S(1)}, u32[]{:S(2)}, u32[]{:S(2)}) %collective-permute-start.45) | collective-permute-done | bytes 393248 | tf_op jit(solution)/shard_map/ppermute | solution.py:82
  519.9 3.7 concatenate.115
  525.5 3.1 collective-permute-start.52
  534.3 15.3 %collective-permute-done.52.beside = bf16[96,4608]{1,0:T(8,128)(2,1)S(1)} collective-permute-done((bf16[96,4608]{1,0:T(8,128)(2,1)S(1)}, bf16[96,4608]{1,0:T(8,128)(2,1)S(1)}, u32[]{:S(2)}, u32[]{:S(2)}) %collective-permute-start.52) | collective-permute-done | bytes 884768 | tf_op jit(solution)/shard_map/ppermute | solution.py:82
  549.6 19.0 %collective-permute-done.53.straight = bf16[96,4608]{1,0:T(8,128)(2,1)S(1)} collective-permute-done((bf16[96,4608]{1,0:T(8,128)(2,1)S(1)}, bf16[96,4608]{1,0:T(8,128)(2,1)S(1)}, u32[]{:S(2)}, u32[]{:S(2)}) %collective-permute-start.53) | collective-permute-done | bytes 884768 | tf_op jit(solution)/shard_map/ppermute | solution.py:82
  (429 shorter events, 167.7 us)
Async XLA Ops:
  7.2 74.7 %all-gather.5.cloned.1.call-start = ((), (), s32[]{:S(2)}) async-start(), calls=%async_computation.11 | async-start | bytes 2211840 | tf_op jit(solution)/shard_map/all_gather | solution.py:520
  10.2 16.4 %collective-permute-start = (bf16[24,128]{1,0:T(8,128)(2,1)}, bf16[24,128]{1,0:T(8,128)(2,1)S(1)}, u32[]{:S(2)}, u32[]{:S(2)}) collective-permute-start(bf16[24,128]{1,0:T(8,128)(2,1)} %get-tuple-element.295), channel_id=1, source_target_pairs={{0,3},{1,0},{2,1},{3,2},{4,7},{5,4},{6,5},{7,6},{8,11},{9,8},{10,9... | collective-permute-start | bytes 18440 | tf_op jit(solution)/shard_map/ppermute | solution.py:82
  10.6 16.1 %collective-permute-start.1 = (bf16[24,128]{1,0:T(8,128)(2,1)}, bf16[24,128]{1,0:T(8,128)(2,1)S(1)}, u32[]{:S(2)}, u32[]{:S(2)}) collective-permute-start(bf16[24,128]{1,0:T(8,128)(2,1)} %get-tuple-element.295), channel_id=1, source_target_pairs={{0,2},{1,3},{2,0},{3,1},{4,6},{5,7},{6,4},{7,5},{8,10},{9,11},{10,... | collective-permute-start | bytes 18440 | tf_op jit(solution)/shard_map/ppermute | solution.py:82
  13.3 13.4 %collective-permute-start.2 = (bf16[24,128]{1,0:T(8,128)(2,1)}, bf16[24,128]{1,0:T(8,128)(2,1)}, u32[]{:S(2)}, u32[]{:S(2)}) collective-permute-start(bf16[24,128]{1,0:T(8,128)(2,1)} %get-tuple-element.295), channel_id=1, source_target_pairs={{0,1},{1,2},{2,3},{3,0},{4,5},{5,6},{6,7},{7,4},{8,9},{9,10},{10,1... | collective-permute-start | bytes 18440 | tf_op jit(solution)/shard_map/ppermute | solution.py:82
  16.6 12.2 %collective-permute-start.3 = (bf16[512,16]{1,0:T(8,128)(2,1)}, bf16[512,16]{1,0:T(8,128)(2,1)}, u32[]{:S(2)}, u32[]{:S(2)}) collective-permute-start(bf16[512,16]{1,0:T(8,128)(2,1)} %bitcast.14), channel_id=1, source_target_pairs={{0,64},{64,0},{1,65},{65,1},{2,66},{66,2},{3,67},{67,3},{4,68},{68... | collective-permute-start | bytes 49160 | tf_op jit(solution)/shard_map/ppermute | solution.py:82
  28.8 8.4 %collective-permute-start.4 = (bf16[96,1152]{1,0:T(8,128)(2,1)S(1)}, bf16[96,1152]{1,0:T(8,128)(2,1)S(1)}, u32[]{:S(2)}, u32[]{:S(2)}) collective-permute-start(bf16[96,1152]{1,0:T(8,128)(2,1)S(1)} %constant_dynamic-update-slice_fusion.8), channel_id=1, source_target_pairs={{0,64},{32,96},{64,0},{96,32},{1,65},{33,97},{65,1},{97,33},{2,66}... | collective-permute-start | bytes 663560 | tf_op jit(solution)/shard_map/ppermute | solution.py:82
  29.4 10.8 %collective-permute-start.12 = (bf16[96,1152]{1,0:T(8,128)(2,1)S(1)}, bf16[96,1152]{1,0:T(8,128)(2,1)S(1)}, u32[]{:S(2)}, u32[]{:S(2)}) collective-permute-start(bf16[96,1152]{1,0:T(8,128)(2,1)S(1)} %constant_dynamic-update-slice_fusion.8), channel_id=1, source_target_pairs={{0,96},{32,64},{64,32},{96,0},{1,97},{33,65},{65,33},{97,1},{2,98}... | collective-permute-start | bytes 663560 | tf_op jit(solution)/shard_map/ppermute | solution.py:82
  32.2 9.1 %collective-permute-start.11 = (bf16[96,1152]{1,0:T(8,128)(2,1)S(1)}, bf16[96,1152]{1,0:T(8,128)(2,1)S(1)}, u32[]{:S(2)}, u32[]{:S(2)}) collective-permute-start(bf16[96,1152]{1,0:T(8,128)(2,1)S(1)} %constant_dynamic-update-slice_fusion.8), channel_id=1, source_target_pairs={{0,32},{32,0},{64,96},{96,64},{1,33},{33,1},{65,97},{97,65},{2,34}... | collective-permute-start | bytes 663560 | tf_op jit(solution)/shard_map/ppermute | solution.py:82
  46.8 35.1 %all-to-all-start = ((bf16[4,128,1536]{2,1,0:T(8,128)(2,1)}), bf16[4,128,1536]{2,1,0:T(8,128)(2,1)S(1)}, u32[]{:S(2)}, u32[]{:S(2)}) async-start(bf16[4,128,1536]{2,1,0:T(8,128)(2,1)} %tile.2), calls=%async_computation | async-start | bytes 3145728 | tf_op jit(solution)/shard_map/all_to_all | solution.py:604
  50.4 94.9 %all-gather.7.cloned.1.call-start = ((), (), s32[]{:S(2)}) async-start(), calls=%async_computation.12 | async-start | bytes 6635520 | tf_op jit(solution)/shard_map/all_gather | solution.py:520
  50.4 29.1 %collective-permute-start.5 = (bf16[96,3456]{1,0:T(8,128)(2,1)}, bf16[96,3456]{1,0:T(8,128)(2,1)S(1)}, u32[]{:S(2)}, u32[]{:S(2)}) collective-permute-start(bf16[96,3456]{1,0:T(8,128)(2,1)} %get-tuple-element.135), channel_id=1, source_target_pairs={{0,64},{32,96},{64,0},{96,32},{1,65},{33,97},{65,1},{97,33},{2,66}... | collective-permute-start | bytes 1990664 | tf_op jit(solution)/shard_map/ppermute | solution.py:82
  50.9 30.0 %collective-permute-start.6 = (bf16[96,3456]{1,0:T(8,128)(2,1)}, bf16[96,3456]{1,0:T(8,128)(2,1)S(1)}, u32[]{:S(2)}, u32[]{:S(2)}) collective-permute-start(bf16[96,3456]{1,0:T(8,128)(2,1)} %get-tuple-element.135), channel_id=1, source_target_pairs={{0,96},{32,64},{64,32},{96,0},{1,97},{33,65},{65,33},{97,1},{2,98}... | collective-permute-start | bytes 1990664 | tf_op jit(solution)/shard_map/ppermute | solution.py:82
  53.2 28.6 %collective-permute-start.7 = (bf16[96,3456]{1,0:T(8,128)(2,1)}, bf16[96,3456]{1,0:T(8,128)(2,1)}, u32[]{:S(2)}, u32[]{:S(2)}) collective-permute-start(bf16[96,3456]{1,0:T(8,128)(2,1)} %get-tuple-element.156), channel_id=1, source_target_pairs={{0,32},{32,0},{1,33},{33,1},{2,34},{34,2},{3,35},{35,3},{4,36},{36... | collective-permute-start | bytes 1990664 | tf_op jit(solution)/shard_map/ppermute | solution.py:82
  56.5 17.3 %collective-permute-start.8 = (bf16[64,1536]{1,0:T(8,128)(2,1)S(1)}, bf16[64,1536]{1,0:T(8,128)(2,1)S(1)}, u32[]{:S(2)}, u32[]{:S(2)}) collective-permute-start(bf16[64,1536]{1,0:T(8,128)(2,1)S(1)} %slice.208.refs_0_.hidden), channel_id=1, source_target_pairs={{0,3},{1,0},{2,1},{3,2},{4,7},{5,4},{6,5},{7,6},{8,11},{9,8},{10,9... | collective-permute-start | bytes 589832 | tf_op jit(solution)/shard_map/ppermute | solution.py:82
  56.7 19.9 %collective-permute-start.9 = (bf16[64,1536]{1,0:T(8,128)(2,1)S(1)}, bf16[64,1536]{1,0:T(8,128)(2,1)S(1)}, u32[]{:S(2)}, u32[]{:S(2)}) collective-permute-start(bf16[64,1536]{1,0:T(8,128)(2,1)S(1)} %slice.208.refs_0_.hidden), channel_id=1, source_target_pairs={{0,2},{1,3},{2,0},{3,1},{4,6},{5,7},{6,4},{7,5},{8,10},{9,11},{10,... | collective-permute-start | bytes 589832 | tf_op jit(solution)/shard_map/ppermute | solution.py:82
  99.6 24.1 %collective-permute-start.17 = (bf16[96,3456]{1,0:T(8,128)(2,1)}, bf16[96,3456]{1,0:T(8,128)(2,1)}, u32[]{:S(2)}, u32[]{:S(2)}) collective-permute-start(bf16[96,3456]{1,0:T(8,128)(2,1)} %get-tuple-element.156), channel_id=1, source_target_pairs={{64,96},{96,64},{65,97},{97,65},{66,98},{98,66},{67,99},{99,67},{6... | collective-permute-start | bytes 1990664 | tf_op jit(solution)/shard_map/ppermute | solution.py:82
  101.1 7.7 %collective-permute-start.14 = (bf16[64,1536]{1,0:T(8,128)(2,1)S(1)}, bf16[64,1536]{1,0:T(8,128)(2,1)S(1)}, u32[]{:S(2)}, u32[]{:S(2)}) collective-permute-start(bf16[64,1536]{1,0:T(8,128)(2,1)S(1)} %get-tuple-element.151), channel_id=1, source_target_pairs={{0,1},{1,2},{2,3},{3,0},{4,5},{5,6},{6,7},{7,4},{8,9},{9,10},{10,1... | collective-permute-start | bytes 589832 | tf_op jit(solution)/shard_map/ppermute | solution.py:82
  102.2 9.3 %collective-permute-start.15 = (bf16[64,1536]{1,0:T(8,128)(2,1)S(1)}, bf16[64,1536]{1,0:T(8,128)(2,1)S(1)}, u32[]{:S(2)}, u32[]{:S(2)}) collective-permute-start(bf16[64,1536]{1,0:T(8,128)(2,1)S(1)} %get-tuple-element.152), channel_id=1, source_target_pairs={{0,2},{1,3},{2,0},{3,1},{4,6},{5,7},{6,4},{7,5},{8,10},{9,11},{10,... | collective-permute-start | bytes 589832 | tf_op jit(solution)/shard_map/ppermute | solution.py:82
  104.5 10.1 %collective-permute-start.16 = (bf16[64,1536]{1,0:T(8,128)(2,1)S(1)}, bf16[64,1536]{1,0:T(8,128)(2,1)S(1)}, u32[]{:S(2)}, u32[]{:S(2)}) collective-permute-start(bf16[64,1536]{1,0:T(8,128)(2,1)S(1)} %get-tuple-element.153), channel_id=1, source_target_pairs={{0,3},{1,0},{2,1},{3,2},{4,7},{5,4},{6,5},{7,6},{8,11},{9,8},{10,9... | collective-permute-start | bytes 589832 | tf_op jit(solution)/shard_map/ppermute | solution.py:82
  116.7 25.7 %all-to-all-start.1 = ((bf16[8,64,1536]{2,1,0:T(8,128)(2,1)}), bf16[8,64,1536]{2,1,0:T(8,128)(2,1)S(1)}, u32[]{:S(2)}, u32[]{:S(2)}) async-start(bf16[8,64,1536]{2,1,0:T(8,128)(2,1)} %bitcast.34), calls=%async_computation.1 | async-start | bytes 3145728 | tf_op jit(solution)/shard_map/all_to_all | solution.py:123
  122.9 70.4 %all-gather.9.cloned.1.call-start = ((), (), s32[]{:S(2)}) async-start(), calls=%async_computation.13 | async-start | bytes 1966080 | tf_op jit(solution)/shard_map/all_gather | solution.py:520
  145.4 88.6 %all-gather.11.cloned.1.call-start = ((), (), s32[]{:S(2)}) async-start(), calls=%async_computation.14 | async-start | bytes 6635520 | tf_op jit(solution)/shard_map/all_gather | solution.py:520
  145.4 9.2 %collective-permute-start.18 = (bf16[768,3456]{1,0:T(8,128)(2,1)}, bf16[768,3456]{1,0:T(8,128)(2,1)}, u32[]{:S(2)}, u32[]{:S(2)}) collective-permute-start(bf16[768,3456]{1,0:T(8,128)(2,1)} %all-gather.7.cloned.1.call-done.up0.down0), channel_id=1, source_target_pairs={{0,4},{4,0},{1,5},{5,1},{2,6},{6,2},{3,7},{7,3},{8,12},{12,8},{9,1... | collective-permute-start | bytes 15925256 | tf_op jit(solution)/shard_map/ppermute | solution.py:82
  193.3 13.4 %collective-permute-start.22 = (bf16[768,1024]{1,0:T(8,128)(2,1)}, bf16[768,1024]{1,0:T(8,128)(2,1)S(1)}, u32[]{:S(2)}, u32[]{:S(2)}) collective-permute-start(bf16[768,1024]{1,0:T(8,128)(2,1)} %all-gather.9.cloned.1.call-done.refs_5_.refs_4_), channel_id=1, source_target_pairs={{0,4},{4,0},{1,5},{5,1},{2,6},{6,2},{3,7},{7,3},{8,12},{12,8},{9,1... | collective-permute-start | bytes 4718600 | tf_op jit(solution)/shard_map/ppermute | solution.py:82
  193.3 7.6 %collective-permute-start.19 = (bf16[64,1536]{1,0:T(8,128)(2,1)S(1)}, bf16[64,1536]{1,0:T(8,128)(2,1)S(1)}, u32[]{:S(2)}, u32[]{:S(2)}) collective-permute-start(bf16[64,1536]{1,0:T(8,128)(2,1)S(1)} %get-tuple-element.166.refs_0_.hidden), channel_id=1, source_target_pairs={{0,3},{1,0},{2,1},{3,2},{4,7},{5,4},{6,5},{7,6},{8,11},{9,8},{10,9... | collective-permute-start | bytes 589832 | tf_op jit(solution)/shard_map/ppermute | solution.py:82
  195.1 9.8 %collective-permute-start.20 = (bf16[64,1536]{1,0:T(8,128)(2,1)S(1)}, bf16[64,1536]{1,0:T(8,128)(2,1)S(1)}, u32[]{:S(2)}, u32[]{:S(2)}) collective-permute-start(bf16[64,1536]{1,0:T(8,128)(2,1)S(1)} %get-tuple-element.166.refs_0_.hidden), channel_id=1, source_target_pairs={{0,2},{1,3},{2,0},{3,1},{4,6},{5,7},{6,4},{7,5},{8,10},{9,11},{10,... | collective-permute-start | bytes 589832 | tf_op jit(solution)/shard_map/ppermute | solution.py:82
  195.4 11.2 %collective-permute-start.21 = (bf16[64,1536]{1,0:T(8,128)(2,1)S(1)}, bf16[64,1536]{1,0:T(8,128)(2,1)S(1)}, u32[]{:S(2)}, u32[]{:S(2)}) collective-permute-start(bf16[64,1536]{1,0:T(8,128)(2,1)S(1)} %get-tuple-element.166.refs_0_.hidden), channel_id=1, source_target_pairs={{0,1},{1,2},{2,3},{3,0},{4,5},{5,6},{6,7},{7,4},{8,9},{9,10},{10,1... | collective-permute-start | bytes 589832 | tf_op jit(solution)/shard_map/ppermute | solution.py:82
  215.7 7.7 %collective-permute-start.23 = (bf16[64,1536]{1,0:T(8,128)(2,1)S(1)}, bf16[64,1536]{1,0:T(8,128)(2,1)S(1)}, u32[]{:S(2)}, u32[]{:S(2)}) collective-permute-start(bf16[64,1536]{1,0:T(8,128)(2,1)S(1)} %get-tuple-element.169), channel_id=1, source_target_pairs={{0,1},{1,2},{2,3},{3,0},{4,5},{5,6},{6,7},{7,4},{8,9},{9,10},{10,1... | collective-permute-start | bytes 589832 | tf_op jit(solution)/shard_map/ppermute | solution.py:82
  217.1 9.3 %collective-permute-start.24 = (bf16[64,1536]{1,0:T(8,128)(2,1)S(1)}, bf16[64,1536]{1,0:T(8,128)(2,1)S(1)}, u32[]{:S(2)}, u32[]{:S(2)}) collective-permute-start(bf16[64,1536]{1,0:T(8,128)(2,1)S(1)} %get-tuple-element.170), channel_id=1, source_target_pairs={{0,2},{1,3},{2,0},{3,1},{4,6},{5,7},{6,4},{7,5},{8,10},{9,11},{10,... | collective-permute-start | bytes 589832 | tf_op jit(solution)/shard_map/ppermute | solution.py:82
  219.8 9.7 %collective-permute-start.25 = (bf16[64,1536]{1,0:T(8,128)(2,1)S(1)}, bf16[64,1536]{1,0:T(8,128)(2,1)S(1)}, u32[]{:S(2)}, u32[]{:S(2)}) collective-permute-start(bf16[64,1536]{1,0:T(8,128)(2,1)S(1)} %get-tuple-element.171), channel_id=1, source_target_pairs={{0,3},{1,0},{2,1},{3,2},{4,7},{5,4},{6,5},{7,6},{8,11},{9,8},{10,9... | collective-permute-start | bytes 589832 | tf_op jit(solution)/shard_map/ppermute | solution.py:82
  233.9 25.7 %collective-permute-start.26 = (bf16[768,3456]{1,0:T(8,128)(2,1)}, bf16[768,3456]{1,0:T(8,128)(2,1)}, u32[]{:S(2)}, u32[]{:S(2)}) collective-permute-start(bf16[768,3456]{1,0:T(8,128)(2,1)} %all-gather.11.cloned.1.call-done.up0.down0), channel_id=1, source_target_pairs={{0,4},{4,0},{1,5},{5,1},{2,6},{6,2},{3,7},{7,3},{8,12},{12,8},{9,1... | collective-permute-start | bytes 15925256 | tf_op jit(solution)/shard_map/ppermute | solution.py:82
  233.9 25.7 %all-to-all-start.3 = ((bf16[8,64,1536]{2,1,0:T(8,128)(2,1)}), bf16[8,64,1536]{2,1,0:T(8,128)(2,1)S(1)}, u32[]{:S(2)}, u32[]{:S(2)}) async-start(bf16[8,64,1536]{2,1,0:T(8,128)(2,1)} %bitcast.161), calls=%async_computation.3 | async-start | bytes 3145728 | tf_op jit(solution)/shard_map/all_to_all | solution.py:123
  239.7 137.0 %reduce-scatter.5.cloned.1.call-start = ((), (), s32[]{:S(2)}) async-start(), calls=%async_computation.15 | async-start | bytes 1769472 | tf_op jit(solution)/shard_map/reduce_scatter | solution.py:654
  292.8 9.1 %collective-permute-start.28 = (bf16[768,3456]{1,0:T(8,128)(2,1)}, bf16[768,3456]{1,0:T(8,128)(2,1)}, u32[]{:S(2)}, u32[]{:S(2)}) collective-permute-start(bf16[768,3456]{1,0:T(8,128)(2,1)} %shard_map.247), channel_id=1, source_target_pairs={{0,4},{4,0},{1,5},{5,1},{2,6},{6,2},{3,7},{7,3},{8,12},{12,8},{9,1... | collective-permute-start | bytes 15925256 | tf_op jit(solution)/shard_map/ppermute | solution.py:82
  292.8 33.0 %all-to-all-start.4 = ((bf16[8,64,1664]{2,1,0:T(8,128)(2,1)}), bf16[8,64,1664]{2,1,0:T(8,128)(2,1)}, u32[]{:S(2)}, u32[]{:S(2)}) async-start(bf16[8,64,1664]{2,1,0:T(8,128)(2,1)} %bitcast.158), calls=%async_computation.5 | async-start | bytes 3407872 | tf_op jit(solution)/shard_map/all_to_all | solution.py:123
  298.2 145.0 %reduce-scatter.7.cloned.1.call-start = ((), (), s32[]{:S(2)}) async-start(), calls=%async_computation.16 | async-start | bytes 6635520 | tf_op jit(solution)/shard_map/reduce_scatter | solution.py:516
  332.3 9.3 %collective-permute-start.29 = (bf16[64,1536]{1,0:T(8,128)(2,1)S(1)}, bf16[64,1536]{1,0:T(8,128)(2,1)S(1)}, u32[]{:S(2)}, u32[]{:S(2)}) collective-permute-start(bf16[64,1536]{1,0:T(8,128)(2,1)S(1)} %get-tuple-element.191.refs_0_), channel_id=1, source_target_pairs={{0,3},{1,0},{2,1},{3,2},{4,7},{5,4},{6,5},{7,6},{8,11},{9,8},{10,9... | collective-permute-start | bytes 589832 | tf_op jit(solution)/shard_map/ppermute | solution.py:82
  332.6 14.8 %collective-permute-start.30 = (bf16[64,1536]{1,0:T(8,128)(2,1)S(1)}, bf16[64,1536]{1,0:T(8,128)(2,1)S(1)}, u32[]{:S(2)}, u32[]{:S(2)}) collective-permute-start(bf16[64,1536]{1,0:T(8,128)(2,1)S(1)} %get-tuple-element.191.refs_0_), channel_id=1, source_target_pairs={{0,2},{1,3},{2,0},{3,1},{4,6},{5,7},{6,4},{7,5},{8,10},{9,11},{10,... | collective-permute-start | bytes 589832 | tf_op jit(solution)/shard_map/ppermute | solution.py:82
  336.6 11.7 %collective-permute-start.31 = (bf16[64,1536]{1,0:T(8,128)(2,1)S(1)}, bf16[64,1536]{1,0:T(8,128)(2,1)S(1)}, u32[]{:S(2)}, u32[]{:S(2)}) collective-permute-start(bf16[64,1536]{1,0:T(8,128)(2,1)S(1)} %get-tuple-element.191.refs_0_), channel_id=1, source_target_pairs={{0,1},{1,2},{2,3},{3,0},{4,5},{5,6},{6,7},{7,4},{8,9},{9,10},{10,1... | collective-permute-start | bytes 589832 | tf_op jit(solution)/shard_map/ppermute | solution.py:82
  353.9 22.8 %collective-permute-start.35 = (bf16[768,1024]{1,0:T(8,128)(2,1)}, bf16[768,1024]{1,0:T(8,128)(2,1)}, u32[]{:S(2)}, u32[]{:S(2)}) collective-permute-start(bf16[768,1024]{1,0:T(8,128)(2,1)} %shard_map.251), channel_id=1, source_target_pairs={{0,4},{4,0},{1,5},{5,1},{2,6},{6,2},{3,7},{7,3},{8,12},{12,8},{9,1... | collective-permute-start | bytes 4718600 | tf_op jit(solution)/shard_map/ppermute | solution.py:82
  353.9 8.3 %collective-permute-start.32 = (bf16[64,1536]{1,0:T(8,128)(2,1)S(1)}, bf16[64,1536]{1,0:T(8,128)(2,1)S(1)}, u32[]{:S(2)}, u32[]{:S(2)}) collective-permute-start(bf16[64,1536]{1,0:T(8,128)(2,1)S(1)} %get-tuple-element.195), channel_id=1, source_target_pairs={{0,1},{1,2},{2,3},{3,0},{4,5},{5,6},{6,7},{7,4},{8,9},{9,10},{10,1... | collective-permute-start | bytes 589832 | tf_op jit(solution)/shard_map/ppermute | solution.py:82
  354.7 9.5 %collective-permute-start.33 = (bf16[64,1536]{1,0:T(8,128)(2,1)S(1)}, bf16[64,1536]{1,0:T(8,128)(2,1)S(1)}, u32[]{:S(2)}, u32[]{:S(2)}) collective-permute-start(bf16[64,1536]{1,0:T(8,128)(2,1)S(1)} %get-tuple-element.196), channel_id=1, source_target_pairs={{0,2},{1,3},{2,0},{3,1},{4,6},{5,7},{6,4},{7,5},{8,10},{9,11},{10,... | collective-permute-start | bytes 589832 | tf_op jit(solution)/shard_map/ppermute | solution.py:82
  358.5 9.4 %collective-permute-start.34 = (bf16[64,1536]{1,0:T(8,128)(2,1)S(1)}, bf16[64,1536]{1,0:T(8,128)(2,1)S(1)}, u32[]{:S(2)}, u32[]{:S(2)}) collective-permute-start(bf16[64,1536]{1,0:T(8,128)(2,1)S(1)} %get-tuple-element.197), channel_id=1, source_target_pairs={{0,3},{1,0},{2,1},{3,2},{4,7},{5,4},{6,5},{7,6},{8,11},{9,8},{10,9... | collective-permute-start | bytes 589832 | tf_op jit(solution)/shard_map/ppermute | solution.py:82
  370.8 25.1 %all-to-all-start.5 = ((bf16[8,64,1536]{2,1,0:T(8,128)(2,1)}), bf16[8,64,1536]{2,1,0:T(8,128)(2,1)S(1)}, u32[]{:S(2)}, u32[]{:S(2)}) async-start(bf16[8,64,1536]{2,1,0:T(8,128)(2,1)} %bitcast.160), calls=%async_computation.6 | async-start | bytes 3145728 | tf_op jit(solution)/shard_map/all_to_all | solution.py:123
  376.6 140.9 %reduce-scatter.11.cloned.1.call-start = ((), (), s32[]{:S(2)}) async-start(), calls=%async_computation.18 | async-start | bytes 1966080 | tf_op jit(solution)/shard_map/reduce_scatter | solution.py:516
  416.1 9.1 %collective-permute-start.36 = (bf16[768,3456]{1,0:T(8,128)(2,1)}, bf16[768,3456]{1,0:T(8,128)(2,1)}, u32[]{:S(2)}, u32[]{:S(2)}) collective-permute-start(bf16[768,3456]{1,0:T(8,128)(2,1)} %shard_map.255), channel_id=1, source_target_pairs={{0,4},{4,0},{1,5},{5,1},{2,6},{6,2},{3,7},{7,3},{8,12},{12,8},{9,1... | collective-permute-start | bytes 15925256 | tf_op jit(solution)/shard_map/ppermute | solution.py:82
  416.1 27.0 %all-to-all-start.6 = ((bf16[8,64,1664]{2,1,0:T(8,128)(2,1)}), bf16[8,64,1664]{2,1,0:T(8,128)(2,1)}, u32[]{:S(2)}, u32[]{:S(2)}) async-start(bf16[8,64,1664]{2,1,0:T(8,128)(2,1)} %bitcast.159), calls=%async_computation.7 | async-start | bytes 3407872 | tf_op jit(solution)/shard_map/all_to_all | solution.py:123
  421.4 98.5 %reduce-scatter.9.cloned.1.call-start = ((), (), s32[]{:S(2)}) async-start(), calls=%async_computation.17 | async-start | bytes 6635520 | tf_op jit(solution)/shard_map/reduce_scatter | solution.py:516
  449.0 10.0 %collective-permute-start.38 = (bf16[64,1536]{1,0:T(8,128)(2,1)S(1)}, bf16[64,1536]{1,0:T(8,128)(2,1)S(1)}, u32[]{:S(2)}, u32[]{:S(2)}) collective-permute-start(bf16[64,1536]{1,0:T(8,128)(2,1)S(1)} %get-tuple-element.217.refs_0_), channel_id=1, source_target_pairs={{0,2},{1,3},{2,0},{3,1},{4,6},{5,7},{6,4},{7,5},{8,10},{9,11},{10,... | collective-permute-start | bytes 589832 | tf_op jit(solution)/shard_map/ppermute | solution.py:82
  450.2 10.1 %collective-permute-start.39 = (bf16[64,1536]{1,0:T(8,128)(2,1)S(1)}, bf16[64,1536]{1,0:T(8,128)(2,1)S(1)}, u32[]{:S(2)}, u32[]{:S(2)}) collective-permute-start(bf16[64,1536]{1,0:T(8,128)(2,1)S(1)} %get-tuple-element.217.refs_0_), channel_id=1, source_target_pairs={{0,1},{1,2},{2,3},{3,0},{4,5},{5,6},{6,7},{7,4},{8,9},{9,10},{10,1... | collective-permute-start | bytes 589832 | tf_op jit(solution)/shard_map/ppermute | solution.py:82
  465.2 9.8 %collective-permute-start.43 = (bf16[768,1024]{1,0:T(8,128)(2,1)S(1)}, bf16[768,1024]{1,0:T(8,128)(2,1)}, u32[]{:S(2)}, u32[]{:S(2)}) collective-permute-start(bf16[768,1024]{1,0:T(8,128)(2,1)S(1)} %shard_map.259), channel_id=1, source_target_pairs={{0,4},{4,0},{1,5},{5,1},{2,6},{6,2},{3,7},{7,3},{8,12},{12,8},{9,1... | collective-permute-start | bytes 4718600 | tf_op jit(solution)/shard_map/ppermute | solution.py:82
  467.1 10.2 %collective-permute-start.40 = (bf16[64,1536]{1,0:T(8,128)(2,1)}, bf16[64,1536]{1,0:T(8,128)(2,1)S(1)}, u32[]{:S(2)}, u32[]{:S(2)}) collective-permute-start(bf16[64,1536]{1,0:T(8,128)(2,1)} %copy-done.90), channel_id=1, source_target_pairs={{0,1},{1,2},{2,3},{3,0},{4,5},{5,6},{6,7},{7,4},{8,9},{9,10},{10,1... | collective-permute-start | bytes 589832 | tf_op jit(solution)/shard_map/ppermute | solution.py:82
  468.7 9.5 %collective-permute-start.41 = (bf16[64,1536]{1,0:T(8,128)(2,1)}, bf16[64,1536]{1,0:T(8,128)(2,1)S(1)}, u32[]{:S(2)}, u32[]{:S(2)}) collective-permute-start(bf16[64,1536]{1,0:T(8,128)(2,1)} %copy-done.89), channel_id=1, source_target_pairs={{0,2},{1,3},{2,0},{3,1},{4,6},{5,7},{6,4},{7,5},{8,10},{9,11},{10,... | collective-permute-start | bytes 589832 | tf_op jit(solution)/shard_map/ppermute | solution.py:82
  471.8 9.7 %collective-permute-start.42 = (bf16[64,1536]{1,0:T(8,128)(2,1)}, bf16[64,1536]{1,0:T(8,128)(2,1)S(1)}, u32[]{:S(2)}, u32[]{:S(2)}) collective-permute-start(bf16[64,1536]{1,0:T(8,128)(2,1)} %copy-done.88), channel_id=1, source_target_pairs={{0,3},{1,0},{2,1},{3,2},{4,7},{5,4},{6,5},{7,6},{8,11},{9,8},{10,9... | collective-permute-start | bytes 589832 | tf_op jit(solution)/shard_map/ppermute | solution.py:82
  483.6 46.4 %collective-permute-start.27 = (bf16[64,1536]{1,0:T(8,128)(2,1)S(1)}, bf16[64,1536]{1,0:T(8,128)(2,1)S(1)}, u32[]{:S(2)}, u32[]{:S(2)}) collective-permute-start(bf16[64,1536]{1,0:T(8,128)(2,1)S(1)} %get-tuple-element.312), channel_id=1, source_target_pairs={{0,64},{64,0},{1,65},{65,1},{2,66},{66,2},{3,67},{67,3},{4,68},{68... | collective-permute-start | bytes 589832 | tf_op jit(solution)/shard_map/ppermute | solution.py:82
  490.0 17.7 %collective-permute-start.47 = (bf16[192,1024]{1,0:T(8,128)(2,1)S(1)}, bf16[192,1024]{1,0:T(8,128)(2,1)S(1)}, u32[]{:S(2)}, u32[]{:S(2)}) collective-permute-start(bf16[192,1024]{1,0:T(8,128)(2,1)S(1)} %get-tuple-element.304), channel_id=1, source_target_pairs={{0,24},{8,0},{16,8},{24,16},{1,25},{9,1},{17,9},{25,17},{2,26},{10... | collective-permute-start | bytes 1179656 | tf_op jit(solution)/shard_map/ppermute | solution.py:82
  492.5 17.1 %collective-permute-start.46 = (bf16[192,1024]{1,0:T(8,128)(2,1)S(1)}, bf16[192,1024]{1,0:T(8,128)(2,1)S(1)}, u32[]{:S(2)}, u32[]{:S(2)}) collective-permute-start(bf16[192,1024]{1,0:T(8,128)(2,1)S(1)} %get-tuple-element.303), channel_id=1, source_target_pairs={{0,16},{8,24},{16,0},{24,8},{1,17},{9,25},{17,1},{25,9},{2,18},{10... | collective-permute-start | bytes 1179656 | tf_op jit(solution)/shard_map/ppermute | solution.py:82
  494.6 22.7 %collective-permute-start.45 = (bf16[192,1024]{1,0:T(8,128)(2,1)S(1)}, bf16[192,1024]{1,0:T(8,128)(2,1)S(1)}, u32[]{:S(2)}, u32[]{:S(2)}) collective-permute-start(bf16[192,1024]{1,0:T(8,128)(2,1)S(1)} %get-tuple-element.302), channel_id=1, source_target_pairs={{0,8},{8,16},{16,24},{24,0},{1,9},{9,17},{17,25},{25,1},{2,10},{10... | collective-permute-start | bytes 1179656 | tf_op jit(solution)/shard_map/ppermute | solution.py:82
  525.5 24.2 %collective-permute-start.52 = (bf16[96,4608]{1,0:T(8,128)(2,1)S(1)}, bf16[96,4608]{1,0:T(8,128)(2,1)S(1)}, u32[]{:S(2)}, u32[]{:S(2)}) collective-permute-start(bf16[96,4608]{1,0:T(8,128)(2,1)S(1)} %get-tuple-element.300), channel_id=1, source_target_pairs={{0,32},{32,0},{64,96},{96,64},{1,33},{33,1},{65,97},{97,65},{2,34}... | collective-permute-start | bytes 2654216 | tf_op jit(solution)/shard_map/ppermute | solution.py:82
  528.6 40.0 %collective-permute-start.53 = (bf16[96,4608]{1,0:T(8,128)(2,1)S(1)}, bf16[96,4608]{1,0:T(8,128)(2,1)S(1)}, u32[]{:S(2)}, u32[]{:S(2)}) collective-permute-start(bf16[96,4608]{1,0:T(8,128)(2,1)S(1)} %get-tuple-element.299), channel_id=1, source_target_pairs={{0,64},{32,96},{64,0},{96,32},{1,65},{33,97},{65,1},{97,33},{2,66}... | collective-permute-start | bytes 2654216 | tf_op jit(solution)/shard_map/ppermute | solution.py:82
  529.3 39.3 %collective-permute-start.54 = (bf16[96,4608]{1,0:T(8,128)(2,1)S(1)}, bf16[96,4608]{1,0:T(8,128)(2,1)S(1)}, u32[]{:S(2)}, u32[]{:S(2)}) collective-permute-start(bf16[96,4608]{1,0:T(8,128)(2,1)S(1)} %get-tuple-element.298), channel_id=1, source_target_pairs={{0,96},{32,64},{64,32},{96,0},{1,97},{33,65},{65,33},{97,1},{2,98}... | collective-permute-start | bytes 2654216 | tf_op jit(solution)/shard_map/ppermute | solution.py:82
  532.9 41.8 %collective-permute-start.44 = (bf16[64,1536]{1,0:T(8,128)(2,1)S(1)}, bf16[64,1536]{1,0:T(8,128)(2,1)S(1)}, u32[]{:S(2)}, u32[]{:S(2)}) collective-permute-start(bf16[64,1536]{1,0:T(8,128)(2,1)S(1)} %get-tuple-element.310), channel_id=1, source_target_pairs={{0,64},{64,0},{1,65},{65,1},{2,66},{66,2},{3,67},{67,3},{4,68},{68... | collective-permute-start | bytes 589832 | tf_op jit(solution)/shard_map/ppermute | solution.py:82
  569.9 8.9 %collective-permute-start.57 = (f32[24,128]{1,0:T(8,128)S(1)}, f32[24,128]{1,0:T(8,128)S(1)}, u32[]{:S(2)}, u32[]{:S(2)}) collective-permute-start(f32[24,128]{1,0:T(8,128)S(1)} %get-tuple-element.330), channel_id=1, source_target_pairs={{0,3},{1,0},{2,1},{3,2},{4,7},{5,4},{6,5},{7,6},{8,11},{9,8},{10,9... | collective-permute-start | bytes 36872 | tf_op jit(solution)/shard_map/ppermute | solution.py:82
  570.5 8.3 %collective-permute-start.56 = (f32[24,128]{1,0:T(8,128)S(1)}, f32[24,128]{1,0:T(8,128)S(1)}, u32[]{:S(2)}, u32[]{:S(2)}) collective-permute-start(f32[24,128]{1,0:T(8,128)S(1)} %get-tuple-element.329), channel_id=1, source_target_pairs={{0,2},{1,3},{2,0},{3,1},{4,6},{5,7},{6,4},{7,5},{8,10},{9,11},{10,... | collective-permute-start | bytes 36872 | tf_op jit(solution)/shard_map/ppermute | solution.py:82
  (118 other events, 890.3 us)
Sparse Core Ops, SparseCore 0:
  43.3 29.0 all-gather.4
  87.9 57.3 all-gather.6
  147.6 27.0 all-gather.8
  176.2 57.6 all-gather.10
  292.9 52.3 reduce-scatter.4
  347.6 57.2 reduce-scatter.6
  416.3 25.2 reduce-scatter.10
  444.1 69.6 reduce-scatter.8

commit v4 on v3

--- a/solution.py
+++ b/solution.py
@@ -81,7 +81,6 @@
     walk(())
     return lax.ppermute(block, axes, pairs)
 
-VMEM = pl.BlockSpec(memory_space=pltpu.VMEM)
 SMEM = pl.BlockSpec(memory_space=pltpu.SMEM)
 
 
@@ -89,20 +88,42 @@
     return jax.ShapeDtypeStruct(shape, dtype)
 
 
-def run(kernel, outs, operands, scalars=0, flops=0, in_specs=None, out_specs=None, grid=(), scratch=()):
+def whole(array):
+    return pl.BlockSpec(array.shape, lambda i: (0,) * array.ndim)
+
+
+def run(
+    kernel,
+    outs,
+    operands,
+    scalars=0,
+    flops=0,
+    in_specs=None,
+    out_specs=None,
+    grid=(),
+    scratch=(),
+    far_in=(),
+    far_out=(),
+):
     if in_specs is None:
-        in_specs = [SMEM] * scalars + [VMEM] * (len(operands) - scalars)
+        in_specs = [SMEM] * scalars + [whole(x) for x in operands[scalars:]]
     if out_specs is None:
-        out_specs = [VMEM] * len(outs)
+        grid = (1,)
+        out_specs = [whole(x) for x in outs]
+    limit = 28 if len(grid) and grid[0] == 3 else 12
     moved = sum(x.size * x.dtype.itemsize for x in list(operands) + list(outs))
+    operands = [
+        pltpu.with_memory_space_constraint(x, pltpu.HBM) if i in far_in else x
+        for i, x in enumerate(operands)
+    ]
     return pl.pallas_call(
         kernel,
-        out_shape=list(outs),
+        out_shape=[pltpu.HBM(x.shape, x.dtype) if i in far_out else x for i, x in enumerate(outs)],
         in_specs=in_specs,
         out_specs=out_specs,
         grid=grid,
         scratch_shapes=list(scratch),
-        compiler_params=pltpu.CompilerParams(vmem_limit_bytes=48 * 1024 * 1024),
+        compiler_params=pltpu.CompilerParams(vmem_limit_bytes=limit * 1024 * 1024),
         cost_estimate=pl.CostEstimate(flops=flops, bytes_accessed=moved, transcendentals=0),
     )(*operands)
 
@@ -198,7 +219,7 @@
     outs = [shaped((ROWS, D))] * 4
     outs += [shaped((LEN, D)), shaped((LEN, QKV)), shaped((GROUPS, LEN, LEN)), shaped((LEN, STEP))]
     flops = 2 * LEN * D * ATT + 4 * GROUPS * LEN * LEN * HD
-    got = run(attention_forward_kernel, outs, [t, *hidden_blocks, gain, *weights], 1, flops)
+    got = run(attention_forward_kernel, outs, [t, *hidden_blocks, gain, *weights], 1, flops, far_out=(4, 5, 6, 7))
     return got[:4], got[4:]
 
 
@@ -235,7 +256,7 @@
 def attention_backward(grad_blocks, weights, qkv, probs):
     outs = [shaped((ROWS, D))] * 4 + [shaped((LEN, D)), shaped((LEN, QKV))]
     flops = 2 * LEN * D * ATT + 10 * GROUPS * LEN * LEN * HD
-    got = run(attention_backward_kernel, outs, [*grad_blocks, *weights, qkv, probs], 0, flops)
+    got = run(attention_backward_kernel, outs, [*grad_blocks, *weights, qkv, probs], 0, flops, far_in=(6, 7))
     return got[:4], got[4], got[5]
 
 
@@ -333,6 +354,7 @@
         + [by_step(ROUTES, 2 * STEP), by_step(ROUTES, STEP)],
         grid=(STEPS,),
         scratch=[pltpu.VMEM((ROUTES, D), F32)],
+        far_out=(1, 2, 3, 4),
     )
 
 
@@ -479,6 +501,23 @@
     both[32 : 32 + SMALL, :] = second[...]
     own[...] = both[:, :HALF].T.astype(BF)
     other[...] = both[:, HALF:].T.astype(BF)
+
+
+def pack_kernel(s_ref, ffn0, ffn1, att1, *refs):
+    outs = refs[4:]
+    total = add_up(refs[:4])
+    att0, small = total[:, :ATT].astype(BF), total[:, ATT:]
+    smalls = (small.astype(BF), pltpu.roll(small, HD - 32, 1).astype(BF))
+    for layer, ffn, att in ((0, ffn0, att0), (1, ffn1, att1[...])):
+        for index in (0, 1):
+            cut = slice(index * DBLK, (index + 1) * DBLK)
+            for mine in (0, 1):
+
+                @pl.when((s_ref[0] == layer) == (mine == 0))
+                def _(out=outs[2 * mine + index]):
+                    out[:, :PIECE] = ffn[cut, :]
+                    out[:, PIECE : PIECE + ATT] = att[cut]
+                    out[:, PIECE + ATT :] = smalls[layer][cut]
 
 
 def final_kernel(s_ref, own, beside, straight, across, *outs):
@@ -549,7 +588,7 @@
     small = jnp.concatenate([gain_attn[0][:, None], gain_ffn[0][:, None], w_router[0]], axis=1)
     small = jnp.pad(small, ((0, 0), (0, HD - 2 - E)))
     small = rolled(jnp.stack(tensor_gather(small)), (4 - t) % 4).reshape(DBLK, HD)
-    att_piece = jnp.concatenate([w_query[0], w_key[0], w_value[0], w_out[0].T, small], axis=1)
+    att_piece = jnp.concatenate([w_query[0], w_key[0], w_value[0], w_out[0].T], axis=1)
 
     expert_in = w_expert_in[0].reshape(DBLK, 2, HALF_E, 2, HD)
     shared_in = w_shared_in[0].reshape(DBLK, 2, 2, HD)
@@ -564,16 +603,33 @@
     ffn_own = jnp.where(first, ffn_piece(0), ffn_piece(1))
     ffn_other = jnp.where(first, ffn_piece(1), ffn_piece(0))
 
+    place = jnp.arange(D, dtype=jnp.int32)
+    at_core = (place // HALF + core) % 2
+    at_z = (place // (2 * DBLK)) % 4
+    at_x = (place // DBLK + xhi) % 2
+    column = at_x * HALF + at_z * (2 * DBLK) + at_core * DBLK + place % DBLK
+    order = (place[:, None] == column[None, :]).astype(BF)
+
+    own_tokens = lax.dynamic_index_in_dim(tokens, s, 0, keepdims=False)
+    own_rows = nn(own_tokens, order).astype(BF)
+    grad_rows = lax.all_gather(cotangent.reshape(2 * ROWS, D), "tensor", axis=0, tiled=True)
+
     named = jnp.sum((route_experts[0][:, :, :, None] == jnp.arange(E)).astype(F32), axis=2)
     named = named.astype(BF).reshape(ROUTES, E)
     named_else = move(named, SECTION, lambda s: (s + 1,))
-    att_piece, named_else = together(att_piece, named_else)
+    small, named_else, own_rows = together(small, named_else, own_rows)
     masks = [jnp.where(s == layer, named, named_else).astype(F32) for layer in (0, 1)]
 
     att_beside = move(att_piece, SIDE, lambda s, x: (s, x + 1))
     att_straight = move(att_piece, SIDE, lambda s, x: (s + 1, x))
     att_across = move(att_piece, SIDE, lambda s, x: (s + 1, x + 1))
-    att_straight, ffn_own, ffn_other = together(att_straight, ffn_own, ffn_other)
+    small_x = [
+        small,
+        move(small, SIDE, lambda s, x: (s, x + 1)),
+        move(small, SIDE, lambda s, x: (s + 1, x)),
+        move(small, SIDE, lambda s, x: (s + 1, x + 1)),
+    ]
+    att_straight, small_x, ffn_own, ffn_other = together(att_straight, small_x, ffn_own, ffn_other)
     att_same = jnp.concatenate([att_piece, att_beside], axis=0)
     att_else = jnp.concatenate([att_straight, att_across], axis=0)
     att_pairs = [jnp.where(first, att_same, att_else), jnp.where(first, att_else, att_same)]
@@ -581,38 +637,33 @@
     ffn_across = move(ffn_other, SIDE, lambda s, x: (s + 1, x + 1))
     ffn_beside0 = move(ffn_own, SIDE, lambda s, x: (s, x + 1), lambda s, x: s == 0)
 
-    smalls = [pair[:, ATT : ATT + 32] for pair in att_pairs]
+    small_same = jnp.concatenate(small_x[:2], axis=0)[:, :32]
+    small_else = jnp.concatenate(small_x[2:], axis=0)[:, :32]
     att_pair0 = jnp.concatenate(
-        [att_pairs[0][:, :ATT], *smalls, jnp.zeros((2 * DBLK, HD - 64), BF)], axis=1
-    )
-    att_pair1 = att_pairs[1][:, :ATT]
+        [
+            att_pairs[0],
+            jnp.where(first, small_same, small_else),
+            jnp.where(first, small_else, small_same),
+            jnp.zeros((2 * DBLK, HD - 64), BF),
+        ],
+        axis=1,
+    )
+    att_pair1 = att_pairs[1]
+    att_pair0, grad_rows = together(att_pair0, grad_rows)
     att_row0 = gather_row(att_pair0)
 
-    place = jnp.arange(D, dtype=jnp.int32)
-    at_core = (place // HALF + core) % 2
-    at_z = (place // (2 * DBLK)) % 4
-    at_x = (place // DBLK + xhi) % 2
-    column = at_x * HALF + at_z * (2 * DBLK) + at_core * DBLK + place % DBLK
-    order = (place[:, None] == column[None, :]).astype(BF)
-
-    own_tokens = lax.dynamic_index_in_dim(tokens, s, 0, keepdims=False)
-    own_rows = jnp.concatenate([own_tokens, cotangent.reshape(2 * ROWS, D)], axis=0)
-    own_rows = nn(own_rows, order).astype(BF)
-    hidden_blocks = tensor_gather(own_rows[:ROWS])
-    both_cotangents = own_rows[ROWS:]
-    own_cotangent = lax.dynamic_slice_in_dim(both_cotangents, s * ROWS, ROWS, 0)
-    grad_rows = lax.all_to_all(jnp.tile(both_cotangents, (4, 1)), "tensor", 0, 0, tiled=True)
+    hidden_blocks = tensor_gather(own_rows)
+    grad_rows = nn(grad_rows, order).astype(BF)
+    grad_rows = grad_rows.reshape(4, 2, ROWS, D).swapaxes(0, 1).reshape(ROUTES, D)
+    own_cotangent = lax.dynamic_slice_in_dim(grad_rows, (4 * s + t) * ROWS, ROWS, 0)
 
     from_x = (ffn_straight, ffn_across, ffn_beside0)
-    from_x, hidden_blocks, grad_rows, att_row0 = together(
-        from_x, hidden_blocks, grad_rows, att_row0
-    )
+    from_x, hidden_blocks, att_row0 = together(from_x, hidden_blocks, att_row0)
     ffn_straight, ffn_across, ffn_beside0 = from_x
     ffn_else = jnp.concatenate([ffn_straight, ffn_across], axis=0)
     ffn_pair0 = jnp.where(first, jnp.concatenate([ffn_own, ffn_beside0], axis=0), ffn_else)
     ffn_pair0, hidden_blocks = together(ffn_pair0, hidden_blocks)
     ffn_row0 = gather_row(ffn_pair0)
-    grad_rows = grad_rows.reshape(4, 2, ROWS, D).swapaxes(0, 1).reshape(ROUTES, D)
     att_w = [(att_row0, swap_core(att_row0)), None]
     small = run(
         small_forward_kernel,
@@ -634,6 +685,7 @@
             mid_kernel,
             [shaped((ROWS, D), F32), shaped((ROWS, D)), shaped((ROUTES, D))],
             [hidden_blocks[0], ffn_gain, parts[0], *tensor_send(parts)],
+            far_out=(1,),
         )
         rows = group_exchange(copies)
         if layer == 0:
@@ -683,6 +735,8 @@
             mid_backward_kernel,
             [shaped((ROWS, D), F32), shaped((ROWS, D)), shaped((SMALL, D), F32)],
             [mid, own_gates, out_low, ffn_gain, router, normed_ffn, got],
+            far_in=(0, 1, 2, 3, 4, 5),
+            far_out=(0, 2),
         )
         mid_blocks = tensor_gather(mid_low)
         parts, mid_rows, qkv_grad = attention_backward(mid_blocks, att_w[layer], qkv, probs)
@@ -698,17 +752,16 @@
             hidden_backward_kernel,
             [shaped((ROWS, D)), shaped((SMALL, D), F32), shaped((ROUTES, D))],
             [hidden, attn_gain, mid_grad, small, parts[0], *got],
+            far_in=(0, 1, 2, 3),
+            far_out=(0, 1),
         )
         in_grads[layer] = out_low
         if layer == 1:
             grad_rows, att_own = together(group_exchange(copies), att_own)
             att_sums[1] = sum_row(att_own)
-    def sum_z(part):
+    def spread_z(part):
         blocks = rolled(part.reshape(4, 2 * DBLK, -1), z)
-        total = blocks[0].astype(F32)
-        for k in (1, 2, 3):
-            total = total + move(blocks[k], ROW, lambda at, k=k: (at + k,)).astype(F32)
-        return total.astype(BF)
+        return [blocks[0]] + [move(blocks[k], ROW, lambda at, k=k: (at + k,)) for k in (1, 2, 3)]
 
     small_own, small_other = run(
         small_backward_kernel,
@@ -716,22 +769,19 @@
         small_grads,
         scratch=[pltpu.VMEM((HD, D), F32)],
     )
-    small_own = small_own.astype(F32) + swap_core(small_other).astype(F32)
-    small_sum = sum_z(small_own.astype(BF))
-    att_sums[0] = jnp.concatenate([sum_z(att_own), small_sum[:, :32]], axis=1)
-    att_sums[1] = jnp.concatenate([att_sums[1], small_sum[:, 32:64]], axis=1)
+    small_own = (small_own.astype(F32) + swap_core(small_other).astype(F32)).astype(BF)
+    att_blocks = spread_z(jnp.concatenate([att_own, small_own], axis=1))
     result1 = run(last_kernel, [shaped((ROWS, D))], [kept[3][0], sum1])[0]
-    sums = [
-        jnp.concatenate([ffn, att, jnp.zeros((2 * DBLK, HD - 32), BF)], axis=1)
-        for ffn, att in zip(ffn_sums, att_sums)
-    ]
-    sums = together(*sums)
-
-    same = jnp.where(first, sums[0], sums[1]).reshape(2, DBLK, -1)
-    other = jnp.where(first, sums[1], sums[0]).reshape(2, DBLK, -1)
-    beside = move(same[1], SIDE, lambda s, x: (s, x + 1))
-    straight = move(other[0], SIDE, lambda s, x: (s + 1, x))
-    across = move(other[1], SIDE, lambda s, x: (s + 1, x + 1))
+
+    same0, same1, other0, other1 = run(
+        pack_kernel,
+        [shaped((DBLK, PIECE + ATT_PAD))] * 4,
+        [s_arg, *ffn_sums, att_sums[1], *att_blocks],
+        1,
+    )
+    beside = move(same1, SIDE, lambda s, x: (s, x + 1))
+    straight = move(other0, SIDE, lambda s, x: (s + 1, x))
+    across = move(other1, SIDE, lambda s, x: (s + 1, x + 1))
     grads = run(
         final_kernel,
         [
@@ -748,7 +798,7 @@
                 (DBLK, HD),
             )
         ],
-        [s_arg, same[0], beside, straight, across],
+        [s_arg, same0, beside, straight, across],
         1,
     )
     grad_query, grad_key, grad_value, grad_out, grad_shared_in, grad_shared_down = grads[:6]

time: 598 us -> 590 us (0.987)
  waiting for transfers between devices: 233 us -> 244 us
  local copies, waits for them, and re-layouts: 73.4 us -> 63 us
  starting transfers between devices: 111 us -> 103 us
    all_gather x4, waiting for transfers between devices: 4.49 us -> 11.1 us  [gather_row(): return lax.all_gather(part, 'z', axis=0, tiled=True)]
    ppermute x58, waiting for transfers between devices: 160 us -> 167 us  [move(): return lax.ppermute(block, axes, pairs)]
    concatenate x5 -> x1, local copies, waits for them, and re-layouts: 6.95 us -> 0.88 us  [per_device(): jnp.concatenate([att_pairs[0], jnp.where(first, small_same, small_else),...]
    pallas_call x27 -> x28, Pallas kernels: 107 us -> 106 us  [run(): pl.pallas_call(kernel, out_shape=[pltpu.HBM(x.shape, x.dtype) if i in far...]
    unnamed x237 -> x178, local copies, waits for them, and re-layouts: 47 us -> 47.5 us
  transfers between devices with their start and end apart: 72 -> 72, of which waited for: 44 -> 41; matrix products, arithmetic and copies ran while one was open for 8% -> 6% of each run, Pallas kernels for 13% -> 13%
where the time goes in v4:
time: 590 us; the launch traced here: 580 us
  waiting for transfers between devices  244 us (41%)
  Pallas kernels  106 us (18%)
  starting transfers between devices  103 us (17%)
  local copies, waits for them, and re-layouts  63 us (11%)
  blocking collectives  25.2 us (4%)
  between operations  15.4 us (3%)
  other arithmetic  14.6 us (2%)
  matrix products  8.7 us (1%)
    ppermute x58, waiting for transfers between devices, move(): return lax.ppermute(block, axes, pairs)  167 us
    pallas_call x28, Pallas kernels, run(): pl.pallas_call(kernel, out_shape=[pltpu.HBM(x.shape, x.dtype) if i in far...  106 us
    ppermute x58, starting transfers between devices, move(): return lax.ppermute(block, axes, pairs)  74.2 us
    all_to_all x5, waiting for transfers between devices, group_exchange(): return lax.all_to_all(rows, GROUP, 0, 0, tiled=True)  65 us
    unnamed x178, local copies, waits for them, and re-layouts  47.5 us
    all_to_all x5, starting transfers between devices, group_exchange(): return lax.all_to_all(rows, GROUP, 0, 0, tiled=True)  28.6 us
    all_to_all x1, blocking collectives, group_exchange(): return lax.all_to_all(rows, GROUP, 0, 0, tiled=True)  25.2 us
  transfers between devices with their start and end apart: 72, of which 41 were waited for; matrix products, arithmetic and copies ran while one was open for 6% of the time, Pallas kernels for 13%

profile of v4, /device:TPU:8, one launch (start us, length us, event | category | flops | bytes accessed | tf_op | source)
XLA Modules:
  0.0 580.0 jit_solution(14980451043842595015)
XLA Ops:
  10.0 2.7 collective-permute-start.2
  28.7 4.4 collective-permute-done.4
  39.0 2.8 collective-permute-done.7
  48.8 4.9 collective-permute-start.10
  55.1 6.6 %collective-permute-done.11.refs_1_ = bf16[64,1536]{1,0:T(8,128)(2,1)S(1)} collective-permute-done((bf16[64,1536]{1,0:T(8,128)(2,1)S(1)}, bf16[64,1536]{1,0:T(8,128)(2,1)S(1)}, u32[]{:S(2)}, u32[]{:S(2)}) %collective-permute-start.11) | collective-permute-done | bytes 196640 | tf_op jit(solution)/shard_map/ppermute | solution.py:82
  61.6 5.7 collective-permute-done.13.refs_3_
  67.3 10.3 %collective-permute-done.9 = bf16[96,3456]{1,0:T(8,128)(2,1)S(1)} collective-permute-done((bf16[96,3456]{1,0:T(8,128)(2,1)}, bf16[96,3456]{1,0:T(8,128)(2,1)S(1)}, u32[]{:S(2)}, u32[]{:S(2)}) %collective-permute-start.9) | collective-permute-done | bytes 663584 | tf_op jit(solution)/shard_map/ppermute | solution.py:82
  78.9 2.9 maximum_select_fusion
  82.1 3.7 collective-permute-done.16.other.refs_6_.refs_5_
  87.0 2.9 shard_map.238
  92.2 2.9 collective-permute-start.18
  95.9 3.3 collective-permute-done.17.refs_1_
  101.6 3.0 collective-permute-done.19.refs_3_
  106.7 6.0 %all-to-all-start = ((bf16[8,64,1536]{2,1,0:T(8,128)(2,1)}), bf16[8,64,1536]{2,1,0:T(8,128)(2,1)S(1)}, u32[]{:S(2)}, u32[]{:S(2)}) async-start(bf16[8,64,1536]{2,1,0:T(8,128)(2,1)} %bitcast.141), calls=%async_computation | async-start | bytes 3145728 | tf_op jit(solution)/shard_map/all_to_all | solution.py:144
  112.7 3.1 maximum_select_fusion.1
  115.8 15.8 %all-to-all-done = bf16[8,64,1536]{2,1,0:T(8,128)(2,1)S(1)} async-done(((bf16[8,64,1536]{2,1,0:T(8,128)(2,1)}), bf16[8,64,1536]{2,1,0:T(8,128)(2,1)S(1)}, u32[]{:S(2)}, u32[]{:S(2)}) %all-to-all-start) | async-done | bytes 1572896 | tf_op jit(solution)/shard_map/all_to_all | solution.py:144
  131.6 7.3 %all-gather.10.cloned.1.call-done.up0.down0 = bf16[768,3456]{1,0:T(8,128)(2,1)} async-done(((bf16[192,3456]{1,0:T(8,128)(2,1)}), bf16[768,3456]{1,0:T(8,128)(2,1)}) %all-gather.10.cloned.1.call-update) | async-done | bytes 5308432 | tf_op jit(solution)/shard_map/all_gather | solution.py:559
  140.9 7.2 %collective-permute-done.21.up1.down1 = bf16[768,3456]{1,0:T(8,128)(2,1)} collective-permute-done((bf16[768,3456]{1,0:T(8,128)(2,1)}, bf16[768,3456]{1,0:T(8,128)(2,1)}, u32[]{:S(2)}, u32[]{:S(2)}) %collective-permute-start.21) | collective-permute-done | bytes 5308448 | tf_op jit(solution)/shard_map/ppermute | solution.py:82
  150.7 12.3 %shard_map.240 = (bf16[512,1536]{1,0:T(8,128)(2,1)S(1)}, f32[512,16]{1,0:T(8,128)}, f32[64,16]{1,0:T(8,128)}, bf16[512,2304]{1,0:T(8,128)(2,1)}, bf16[512,1152]{1,0:T(8,128)(2,1)}) custom-call(s32[1]{0:T(128)} %bitcast.35.s_ref, s32[1]{0:T(128)} %bitcast.32.t_ref, bf16[512,1536]{1,0:T(8,128)(2,1)S(1)} %bitcast.130, ...), custom_call_target="tpu_custom_call" | custom-call | flops 5435817984 | bytes 28037128 | tf_op jit(solution)/shard_map/pallas_call | solution.py:119
  163.0 25.2 %all_to_all.70 = bf16[8,64,1536]{2,1,0:T(8,128)(2,1)S(1)} all-to-all(bf16[8,64,1536]{2,1,0:T(8,128)(2,1)S(1)} %bitcast.142), channel_id=1, replica_groups=mesh['section'=2,'xhi'=2,'z'=4,'core'=2,'tensor'=4] {'section','tensor'}, dimensions={0} | all-to-all | bytes 3145728 | tf_op jit(solution)/shard_map/all_to_all | solution.py:144
  193.3 3.5 collective-permute-done.22.refs_1_
  196.8 4.0 collective-permute-done.23.refs_2_
  204.6 3.0 shard_map.242
  212.1 3.2 collective-permute-done.26.refs_1_
  215.3 3.0 collective-permute-done.27.refs_2_
  218.3 3.0 collective-permute-done.28.refs_3_
  223.5 3.8 all-gather.14.cloned.1.call-done.up0.down0
  227.3 5.9 %all-to-all-start.2 = ((bf16[8,64,1536]{2,1,0:T(8,128)(2,1)}), bf16[8,64,1536]{2,1,0:T(8,128)(2,1)}, u32[]{:S(2)}, u32[]{:S(2)}) async-start(bf16[8,64,1536]{2,1,0:T(8,128)(2,1)} %bitcast.140), calls=%async_computation.2 | async-start | bytes 3145728 | tf_op jit(solution)/shard_map/all_to_all | solution.py:144
  233.2 2.7 fusion.8
  236.1 17.1 %all-to-all-done.2 = bf16[8,64,1536]{2,1,0:T(8,128)(2,1)} async-done(((bf16[8,64,1536]{2,1,0:T(8,128)(2,1)}), bf16[8,64,1536]{2,1,0:T(8,128)(2,1)}, u32[]{:S(2)}, u32[]{:S(2)}) %all-to-all-start.2) | async-done | bytes 1572896 | tf_op jit(solution)/shard_map/all_to_all | solution.py:144
  255.7 12.8 %shard_map.244 = (bf16[512,1536]{1,0:T(8,128)(2,1)S(1)}, f32[512,16]{1,0:T(8,128)}, f32[64,16]{1,0:T(8,128)}, bf16[512,2304]{1,0:T(8,128)(2,1)}, bf16[512,1152]{1,0:T(8,128)(2,1)}) custom-call(s32[1]{0:T(128)} %bitcast.35.s_ref, s32[1]{0:T(128)} %bitcast.32.t_ref, bf16[512,1536]{1,0:T(8,128)(2,1)} %bitcast.39.rows_ref.rows, bf16[16,1536]{1,0:T(8,128)(2,1)S(1)} %copy-done.53, ...), custom_call_target="tpu_custom_call" | custom-call | flops 5435817984 | bytes 28037128 | tf_op jit(solution)/shard_map/pallas_call | solution.py:119
  272.3 10.3 %shard_map.246 = (bf16[512,1664]{1,0:T(8,128)(2,1)S(1)}, bf16[512,2304]{1,0:T(8,128)(2,1)S(1)}) custom-call(s32[1]{0:T(128)} %bitcast.35.s_ref, bf16[512,1536]{1,0:T(8,128)(2,1)S(1)} %bitcast.126, f32[512,16]{1,0:T(8,128)S(1)} %copy-done.56, bf16[512,2304]{1,0:T(8,128)(2,1)S(1)} %copy-done.32, bf16[768,3456]{1,0:T(8,128)(2,1)S(1)} %copy-done.4, ...), custom_call_target="tpu_custom_call" | custom-call | flops 5435817984 | bytes 29261828 | tf_op jit(solution)/shard_map/pallas_call | solution.py:119
  282.7 6.9 %shard_map.247 = bf16[768,3456]{1,0:T(8,128)(2,1)} custom-call(bf16[512,1536]{1,0:T(8,128)(2,1)} %bitcast.39.rows_ref.rows, bf16[512,1536]{1,0:T(8,128)(2,1)S(1)} %bitcast.127, bf16[512,2304]{1,0:T(8,128)(2,1)S(1)} %get-tuple-element.200.gate_up_grad, bf16[512,1152]{1,0:T(8,128)(2,1)S(1)} %copy-done.22), custom_call_target="tpu_custom_call" | custom-call | flops 2717908992 | bytes 11993088 | tf_op jit(solution)/shard_map/pallas_call | solution.py:119
  289.6 5.4 all-to-all-start.3
  295.1 3.5 collective-permute-done.31.refs_0_
  301.6 6.0 %shard_map.248 = bf16[768,3456]{1,0:T(8,128)(2,1)S(1)} custom-call(bf16[512,1536]{1,0:T(8,128)(2,1)} %bitcast.39.rows_ref.rows, bf16[512,1536]{1,0:T(8,128)(2,1)S(1)} %bitcast.128, bf16[512,2304]{1,0:T(8,128)(2,1)S(1)} %copy-done.12, bf16[512,1152]{1,0:T(8,128)(2,1)S(1)} %copy-done.23, bf16[768,3456]{1,0:T(8,128)(2,1)} %collective-permute-done.31.refs_0_), custom_call_target="tpu_custom_call" | custom-call | flops 2717908992 | bytes 17301504 | tf_op jit(solution)/shard_map/pallas_call | solution.py:119
  309.9 12.6 %all-to-all-done.3 = bf16[8,64,1664]{2,1,0:T(8,128)(2,1)} async-done(((bf16[8,64,1664]{2,1,0:T(8,128)(2,1)}), bf16[8,64,1664]{2,1,0:T(8,128)(2,1)}, u32[]{:S(2)}, u32[]{:S(2)}) %all-to-all-start.3) | async-done | bytes 1703968 | tf_op jit(solution)/shard_map/all_to_all | solution.py:144
  323.3 3.2 shard_map.249
  326.6 4.0 collective-permute-start.33
  333.2 3.7 collective-permute-done.32.refs_1_
  336.9 6.4 %collective-permute-done.33.refs_2_ = bf16[64,1536]{1,0:T(8,128)(2,1)S(1)} collective-permute-done((bf16[64,1536]{1,0:T(8,128)(2,1)S(1)}, bf16[64,1536]{1,0:T(8,128)(2,1)S(1)}, u32[]{:S(2)}, u32[]{:S(2)}) %collective-permute-start.33) | collective-permute-done | bytes 196640 | tf_op jit(solution)/shard_map/ppermute | solution.py:82
  345.5 3.3 shard_map.250
  351.3 3.6 collective-permute-start.36
  355.0 3.6 collective-permute-done.35.refs_1_
  360.6 3.7 collective-permute-done.37.refs_3_
  367.8 6.0 %all-to-all-start.4 = ((bf16[8,64,1536]{2,1,0:T(8,128)(2,1)}), bf16[8,64,1536]{2,1,0:T(8,128)(2,1)S(1)}, u32[]{:S(2)}, u32[]{:S(2)}) async-start(bf16[8,64,1536]{2,1,0:T(8,128)(2,1)} %bitcast.139), calls=%async_computation.5 | async-start | bytes 3145728 | tf_op jit(solution)/shard_map/all_to_all | solution.py:144
  380.5 12.5 %all-to-all-done.4 = bf16[8,64,1536]{2,1,0:T(8,128)(2,1)S(1)} async-done(((bf16[8,64,1536]{2,1,0:T(8,128)(2,1)}), bf16[8,64,1536]{2,1,0:T(8,128)(2,1)S(1)}, u32[]{:S(2)}, u32[]{:S(2)}) %all-to-all-start.4) | async-done | bytes 1572896 | tf_op jit(solution)/shard_map/all_to_all | solution.py:144
  398.2 10.3 %shard_map.254 = (bf16[512,1664]{1,0:T(8,128)(2,1)S(1)}, bf16[512,2304]{1,0:T(8,128)(2,1)S(1)}) custom-call(s32[1]{0:T(128)} %bitcast.35.s_ref, bf16[512,1536]{1,0:T(8,128)(2,1)S(1)} %bitcast.133, f32[512,16]{1,0:T(8,128)S(1)} %copy-done.55, bf16[512,2304]{1,0:T(8,128)(2,1)S(1)} %copy-done.31, bf16[768,3456]{1,0:T(8,128)(2,1)S(1)} %copy-done.3, ...), custom_call_target="tpu_custom_call" | custom-call | flops 5435817984 | bytes 29261828 | tf_op jit(solution)/shard_map/pallas_call | solution.py:119
  408.6 5.4 shard_map.255
  414.0 5.4 all-to-all-start.5
  419.4 3.7 collective-permute-done.39.refs_0_
  426.0 5.8 %shard_map.256 = bf16[768,3456]{1,0:T(8,128)(2,1)S(1)} custom-call(bf16[512,1536]{1,0:T(8,128)(2,1)S(1)} %bitcast.132, bf16[512,1536]{1,0:T(8,128)(2,1)S(1)} %bitcast.135, bf16[512,2304]{1,0:T(8,128)(2,1)S(1)} %copy-done.14, bf16[512,1152]{1,0:T(8,128)(2,1)S(1)} %copy-done.21, bf16[768,3456]{1,0:T(8,128)(2,1)} %collective-permute-done.39.refs_0_), custom_call_target="tpu_custom_call" | custom-call | flops 2717908992 | bytes 17301504 | tf_op jit(solution)/shard_map/pallas_call | solution.py:119
  434.1 7.0 %all-to-all-done.5 = bf16[8,64,1664]{2,1,0:T(8,128)(2,1)} async-done(((bf16[8,64,1664]{2,1,0:T(8,128)(2,1)}), bf16[8,64,1664]{2,1,0:T(8,128)(2,1)}, u32[]{:S(2)}, u32[]{:S(2)}) %all-to-all-start.5) | async-done | bytes 1703968 | tf_op jit(solution)/shard_map/all_to_all | solution.py:144
  441.1 3.3 shard_map.257
  451.8 3.7 collective-permute-done.41.refs_2_
  457.0 4.1 shard_map.258
  463.6 3.1 collective-permute-start.44
  473.2 3.4 collective-permute-done.45.refs_3_
  476.5 2.9 shard_map.261
  492.2 13.4 %collective-permute-done.49.refs_1_ = bf16[192,1152]{1,0:T(8,128)(2,1)S(1)} collective-permute-done((bf16[192,1152]{1,0:T(8,128)(2,1)}, bf16[192,1152]{1,0:T(8,128)(2,1)S(1)}, u32[]{:S(2)}, u32[]{:S(2)}) %collective-permute-start.49) | collective-permute-done | bytes 442400 | tf_op jit(solution)/shard_map/ppermute | solution.py:82
  505.6 9.7 %collective-permute-done.50.refs_2_ = bf16[192,1152]{1,0:T(8,128)(2,1)S(1)} collective-permute-done((bf16[192,1152]{1,0:T(8,128)(2,1)}, bf16[192,1152]{1,0:T(8,128)(2,1)S(1)}, u32[]{:S(2)}, u32[]{:S(2)}) %collective-permute-start.50) | collective-permute-done | bytes 442400 | tf_op jit(solution)/shard_map/ppermute | solution.py:82
  518.3 3.1 collective-permute-start.52
  528.2 14.2 %collective-permute-done.52.beside = bf16[96,4608]{1,0:T(8,128)(2,1)S(1)} collective-permute-done((bf16[96,4608]{1,0:T(8,128)(2,1)S(1)}, bf16[96,4608]{1,0:T(8,128)(2,1)S(1)}, u32[]{:S(2)}, u32[]{:S(2)}) %collective-permute-start.52) | collective-permute-done | bytes 884768 | tf_op jit(solution)/shard_map/ppermute | solution.py:82
  542.4 19.0 %collective-permute-done.53.straight = bf16[96,4608]{1,0:T(8,128)(2,1)S(1)} collective-permute-done((bf16[96,4608]{1,0:T(8,128)(2,1)S(1)}, bf16[96,4608]{1,0:T(8,128)(2,1)S(1)}, u32[]{:S(2)}, u32[]{:S(2)}) %collective-permute-start.53) | collective-permute-done | bytes 884768 | tf_op jit(solution)/shard_map/ppermute | solution.py:82
  (356 shorter events, 157.4 us)
Async XLA Ops:
  7.2 40.3 %all-gather.6.cloned.1.call-start = ((), (), s32[]{:S(2)}) async-start(), calls=%async_computation.10 | async-start | bytes 1966080 | tf_op jit(solution)/shard_map/all_gather | solution.py:615
  9.6 18.3 %collective-permute-start.1 = (bf16[24,128]{1,0:T(8,128)(2,1)S(1)}, bf16[24,128]{1,0:T(8,128)(2,1)S(1)}, u32[]{:S(2)}, u32[]{:S(2)}) collective-permute-start(bf16[24,128]{1,0:T(8,128)(2,1)S(1)} %get-tuple-element.311), channel_id=1, source_target_pairs={{0,3},{1,0},{2,1},{3,2},{4,7},{5,4},{6,5},{7,6},{8,11},{9,8},{10,9... | collective-permute-start | bytes 18440 | tf_op jit(solution)/shard_map/ppermute | solution.py:82
  10.0 18.6 %collective-permute-start.2 = (bf16[24,128]{1,0:T(8,128)(2,1)S(1)}, bf16[24,128]{1,0:T(8,128)(2,1)S(1)}, u32[]{:S(2)}, u32[]{:S(2)}) collective-permute-start(bf16[24,128]{1,0:T(8,128)(2,1)S(1)} %get-tuple-element.311), channel_id=1, source_target_pairs={{0,2},{1,3},{2,0},{3,1},{4,6},{5,7},{6,4},{7,5},{8,10},{9,11},{10,... | collective-permute-start | bytes 18440 | tf_op jit(solution)/shard_map/ppermute | solution.py:82
  12.7 15.9 %collective-permute-start.3 = (bf16[24,128]{1,0:T(8,128)(2,1)S(1)}, bf16[24,128]{1,0:T(8,128)(2,1)S(1)}, u32[]{:S(2)}, u32[]{:S(2)}) collective-permute-start(bf16[24,128]{1,0:T(8,128)(2,1)S(1)} %get-tuple-element.311), channel_id=1, source_target_pairs={{0,1},{1,2},{2,3},{3,0},{4,5},{5,6},{6,7},{7,4},{8,9},{9,10},{10,1... | collective-permute-start | bytes 18440 | tf_op jit(solution)/shard_map/ppermute | solution.py:82
  15.5 26.3 %collective-permute-start = (bf16[96,1024]{1,0:T(8,128)(2,1)S(1)}, bf16[96,1024]{1,0:T(8,128)(2,1)}, u32[]{:S(2)}, u32[]{:S(2)}) collective-permute-start(bf16[96,1024]{1,0:T(8,128)(2,1)S(1)} %pad_maximum_fusion.6), channel_id=1, source_target_pairs={{0,64},{32,96},{64,0},{96,32},{1,65},{33,97},{65,1},{97,33},{2,66}... | collective-permute-start | bytes 589832 | tf_op jit(solution)/shard_map/ppermute | solution.py:82
  17.1 25.7 %collective-permute-start.15 = (bf16[96,1024]{1,0:T(8,128)(2,1)S(1)}, bf16[96,1024]{1,0:T(8,128)(2,1)}, u32[]{:S(2)}, u32[]{:S(2)}) collective-permute-start(bf16[96,1024]{1,0:T(8,128)(2,1)S(1)} %pad_maximum_fusion.6), channel_id=1, source_target_pairs={{0,96},{32,64},{64,32},{96,0},{1,97},{33,65},{65,33},{97,1},{2,98}... | collective-permute-start | bytes 589832 | tf_op jit(solution)/shard_map/ppermute | solution.py:82
  19.2 58.4 %all-gather.8.cloned.1.call-start = ((), (), s32[]{:S(2)}) async-start(), calls=%async_computation.11 | async-start | bytes 2211840 | tf_op jit(solution)/shard_map/all_gather | solution.py:559
  34.9 6.9 %collective-permute-start.7 = (bf16[96,128]{1,0:T(8,128)(2,1)S(1)}, bf16[96,128]{1,0:T(8,128)(2,1)S(1)}, u32[]{:S(2)}, u32[]{:S(2)}) collective-permute-start(bf16[96,128]{1,0:T(8,128)(2,1)S(1)} %bitcast.159), channel_id=1, source_target_pairs={{0,96},{32,64},{64,32},{96,0},{1,97},{33,65},{65,33},{97,1},{2,98}... | collective-permute-start | bytes 73736 | tf_op jit(solution)/shard_map/ppermute | solution.py:82
  38.5 7.2 %collective-permute-start.14 = (bf16[96,1024]{1,0:T(8,128)(2,1)S(1)}, bf16[96,1024]{1,0:T(8,128)(2,1)S(1)}, u32[]{:S(2)}, u32[]{:S(2)}) collective-permute-start(bf16[96,1024]{1,0:T(8,128)(2,1)S(1)} %pad_maximum_fusion.6), channel_id=1, source_target_pairs={{0,32},{32,0},{64,96},{96,64},{1,33},{33,1},{65,97},{97,65},{2,34}... | collective-permute-start | bytes 589832 | tf_op jit(solution)/shard_map/ppermute | solution.py:82
  47.5 91.4 %all-gather.10.cloned.1.call-start = ((), (), s32[]{:S(2)}) async-start(), calls=%async_computation.12 | async-start | bytes 6635520 | tf_op jit(solution)/shard_map/all_gather | solution.py:559
  47.6 19.7 %collective-permute-start.8 = (bf16[96,3456]{1,0:T(8,128)(2,1)}, bf16[96,3456]{1,0:T(8,128)(2,1)S(1)}, u32[]{:S(2)}, u32[]{:S(2)}) collective-permute-start(bf16[96,3456]{1,0:T(8,128)(2,1)} %get-tuple-element.143), channel_id=1, source_target_pairs={{0,64},{32,96},{64,0},{96,32},{1,65},{33,97},{65,1},{97,33},{2,66}... | collective-permute-start | bytes 1990664 | tf_op jit(solution)/shard_map/ppermute | solution.py:82
  48.1 29.5 %collective-permute-start.9 = (bf16[96,3456]{1,0:T(8,128)(2,1)}, bf16[96,3456]{1,0:T(8,128)(2,1)S(1)}, u32[]{:S(2)}, u32[]{:S(2)}) collective-permute-start(bf16[96,3456]{1,0:T(8,128)(2,1)} %get-tuple-element.143), channel_id=1, source_target_pairs={{0,96},{32,64},{64,32},{96,0},{1,97},{33,65},{65,33},{97,1},{2,98}... | collective-permute-start | bytes 1990664 | tf_op jit(solution)/shard_map/ppermute | solution.py:82
  48.8 28.9 %collective-permute-start.10 = (bf16[96,3456]{1,0:T(8,128)(2,1)}, bf16[96,3456]{1,0:T(8,128)(2,1)}, u32[]{:S(2)}, u32[]{:S(2)}) collective-permute-start(bf16[96,3456]{1,0:T(8,128)(2,1)} %get-tuple-element.170), channel_id=1, source_target_pairs={{0,32},{32,0},{1,33},{33,1},{2,34},{34,2},{3,35},{35,3},{4,36},{36... | collective-permute-start | bytes 1990664 | tf_op jit(solution)/shard_map/ppermute | solution.py:82
  53.6 8.0 %collective-permute-start.11 = (bf16[64,1536]{1,0:T(8,128)(2,1)S(1)}, bf16[64,1536]{1,0:T(8,128)(2,1)S(1)}, u32[]{:S(2)}, u32[]{:S(2)}) collective-permute-start(bf16[64,1536]{1,0:T(8,128)(2,1)S(1)} %fusion.11.refs_0_.hidden), channel_id=1, source_target_pairs={{0,3},{1,0},{2,1},{3,2},{4,7},{5,4},{6,5},{7,6},{8,11},{9,8},{10,9... | collective-permute-start | bytes 589832 | tf_op jit(solution)/shard_map/ppermute | solution.py:82
  53.8 7.8 %collective-permute-start.12 = (bf16[64,1536]{1,0:T(8,128)(2,1)S(1)}, bf16[64,1536]{1,0:T(8,128)(2,1)S(1)}, u32[]{:S(2)}, u32[]{:S(2)}) collective-permute-start(bf16[64,1536]{1,0:T(8,128)(2,1)S(1)} %fusion.11.refs_0_.hidden), channel_id=1, source_target_pairs={{0,2},{1,3},{2,0},{3,1},{4,6},{5,7},{6,4},{7,5},{8,10},{9,11},{10,... | collective-permute-start | bytes 589832 | tf_op jit(solution)/shard_map/ppermute | solution.py:82
  90.0 22.7 %collective-permute-start.20 = (bf16[96,3456]{1,0:T(8,128)(2,1)}, bf16[96,3456]{1,0:T(8,128)(2,1)}, u32[]{:S(2)}, u32[]{:S(2)}) collective-permute-start(bf16[96,3456]{1,0:T(8,128)(2,1)} %get-tuple-element.170), channel_id=1, source_target_pairs={{64,96},{96,64},{65,97},{97,65},{66,98},{98,66},{67,99},{99,67},{6... | collective-permute-start | bytes 1990664 | tf_op jit(solution)/shard_map/ppermute | solution.py:82
  91.5 7.7 %collective-permute-start.17 = (bf16[64,1536]{1,0:T(8,128)(2,1)S(1)}, bf16[64,1536]{1,0:T(8,128)(2,1)S(1)}, u32[]{:S(2)}, u32[]{:S(2)}) collective-permute-start(bf16[64,1536]{1,0:T(8,128)(2,1)S(1)} %get-tuple-element.165), channel_id=1, source_target_pairs={{0,1},{1,2},{2,3},{3,0},{4,5},{5,6},{6,7},{7,4},{8,9},{9,10},{10,1... | collective-permute-start | bytes 589832 | tf_op jit(solution)/shard_map/ppermute | solution.py:82
  92.2 9.3 %collective-permute-start.18 = (bf16[64,1536]{1,0:T(8,128)(2,1)S(1)}, bf16[64,1536]{1,0:T(8,128)(2,1)S(1)}, u32[]{:S(2)}, u32[]{:S(2)}) collective-permute-start(bf16[64,1536]{1,0:T(8,128)(2,1)S(1)} %get-tuple-element.166), channel_id=1, source_target_pairs={{0,2},{1,3},{2,0},{3,1},{4,6},{5,7},{6,4},{7,5},{8,10},{9,11},{10,... | collective-permute-start | bytes 589832 | tf_op jit(solution)/shard_map/ppermute | solution.py:82
  95.1 9.5 %collective-permute-start.19 = (bf16[64,1536]{1,0:T(8,128)(2,1)S(1)}, bf16[64,1536]{1,0:T(8,128)(2,1)S(1)}, u32[]{:S(2)}, u32[]{:S(2)}) collective-permute-start(bf16[64,1536]{1,0:T(8,128)(2,1)S(1)} %get-tuple-element.167), channel_id=1, source_target_pairs={{0,3},{1,0},{2,1},{3,2},{4,7},{5,4},{6,5},{7,6},{8,11},{9,8},{10,9... | collective-permute-start | bytes 589832 | tf_op jit(solution)/shard_map/ppermute | solution.py:82
  106.7 24.9 %all-to-all-start = ((bf16[8,64,1536]{2,1,0:T(8,128)(2,1)}), bf16[8,64,1536]{2,1,0:T(8,128)(2,1)S(1)}, u32[]{:S(2)}, u32[]{:S(2)}) async-start(bf16[8,64,1536]{2,1,0:T(8,128)(2,1)} %bitcast.141), calls=%async_computation | async-start | bytes 3145728 | tf_op jit(solution)/shard_map/all_to_all | solution.py:144
  112.7 76.5 %all-gather.12.cloned.1.call-start = ((), (), s32[]{:S(2)}) async-start(), calls=%async_computation.13 | async-start | bytes 1966080 | tf_op jit(solution)/shard_map/all_gather | solution.py:559
  138.9 88.4 %all-gather.14.cloned.1.call-start = ((), (), s32[]{:S(2)}) async-start(), calls=%async_computation.14 | async-start | bytes 6635520 | tf_op jit(solution)/shard_map/all_gather | solution.py:559
  139.0 9.2 %collective-permute-start.21 = (bf16[768,3456]{1,0:T(8,128)(2,1)}, bf16[768,3456]{1,0:T(8,128)(2,1)}, u32[]{:S(2)}, u32[]{:S(2)}) collective-permute-start(bf16[768,3456]{1,0:T(8,128)(2,1)} %all-gather.10.cloned.1.call-done.up0.down0), channel_id=1, source_target_pairs={{0,4},{4,0},{1,5},{5,1},{2,6},{6,2},{3,7},{7,3},{8,12},{12,8},{9,1... | collective-permute-start | bytes 15925256 | tf_op jit(solution)/shard_map/ppermute | solution.py:82
  189.2 13.4 %collective-permute-start.25 = (bf16[768,1024]{1,0:T(8,128)(2,1)}, bf16[768,1024]{1,0:T(8,128)(2,1)S(1)}, u32[]{:S(2)}, u32[]{:S(2)}) collective-permute-start(bf16[768,1024]{1,0:T(8,128)(2,1)} %all-gather.12.cloned.1.call-done.refs_5_.refs_4_), channel_id=1, source_target_pairs={{0,4},{4,0},{1,5},{5,1},{2,6},{6,2},{3,7},{7,3},{8,12},{12,8},{9,1... | collective-permute-start | bytes 4718600 | tf_op jit(solution)/shard_map/ppermute | solution.py:82
  189.2 7.6 %collective-permute-start.22 = (bf16[64,1536]{1,0:T(8,128)(2,1)S(1)}, bf16[64,1536]{1,0:T(8,128)(2,1)S(1)}, u32[]{:S(2)}, u32[]{:S(2)}) collective-permute-start(bf16[64,1536]{1,0:T(8,128)(2,1)S(1)} %get-tuple-element.180.refs_0_.hidden), channel_id=1, source_target_pairs={{0,3},{1,0},{2,1},{3,2},{4,7},{5,4},{6,5},{7,6},{8,11},{9,8},{10,9... | collective-permute-start | bytes 589832 | tf_op jit(solution)/shard_map/ppermute | solution.py:82
  191.0 9.8 %collective-permute-start.23 = (bf16[64,1536]{1,0:T(8,128)(2,1)S(1)}, bf16[64,1536]{1,0:T(8,128)(2,1)S(1)}, u32[]{:S(2)}, u32[]{:S(2)}) collective-permute-start(bf16[64,1536]{1,0:T(8,128)(2,1)S(1)} %get-tuple-element.180.refs_0_.hidden), channel_id=1, source_target_pairs={{0,2},{1,3},{2,0},{3,1},{4,6},{5,7},{6,4},{7,5},{8,10},{9,11},{10,... | collective-permute-start | bytes 589832 | tf_op jit(solution)/shard_map/ppermute | solution.py:82
  191.3 11.2 %collective-permute-start.24 = (bf16[64,1536]{1,0:T(8,128)(2,1)S(1)}, bf16[64,1536]{1,0:T(8,128)(2,1)S(1)}, u32[]{:S(2)}, u32[]{:S(2)}) collective-permute-start(bf16[64,1536]{1,0:T(8,128)(2,1)S(1)} %get-tuple-element.180.refs_0_.hidden), channel_id=1, source_target_pairs={{0,1},{1,2},{2,3},{3,0},{4,5},{5,6},{6,7},{7,4},{8,9},{9,10},{10,1... | collective-permute-start | bytes 589832 | tf_op jit(solution)/shard_map/ppermute | solution.py:82
  207.6 7.7 %collective-permute-start.26 = (bf16[64,1536]{1,0:T(8,128)(2,1)S(1)}, bf16[64,1536]{1,0:T(8,128)(2,1)S(1)}, u32[]{:S(2)}, u32[]{:S(2)}) collective-permute-start(bf16[64,1536]{1,0:T(8,128)(2,1)S(1)} %get-tuple-element.183), channel_id=1, source_target_pairs={{0,1},{1,2},{2,3},{3,0},{4,5},{5,6},{6,7},{7,4},{8,9},{9,10},{10,1... | collective-permute-start | bytes 589832 | tf_op jit(solution)/shard_map/ppermute | solution.py:82
  209.0 9.3 %collective-permute-start.27 = (bf16[64,1536]{1,0:T(8,128)(2,1)S(1)}, bf16[64,1536]{1,0:T(8,128)(2,1)S(1)}, u32[]{:S(2)}, u32[]{:S(2)}) collective-permute-start(bf16[64,1536]{1,0:T(8,128)(2,1)S(1)} %get-tuple-element.184), channel_id=1, source_target_pairs={{0,2},{1,3},{2,0},{3,1},{4,6},{5,7},{6,4},{7,5},{8,10},{9,11},{10,... | collective-permute-start | bytes 589832 | tf_op jit(solution)/shard_map/ppermute | solution.py:82
  211.7 9.7 %collective-permute-start.28 = (bf16[64,1536]{1,0:T(8,128)(2,1)S(1)}, bf16[64,1536]{1,0:T(8,128)(2,1)S(1)}, u32[]{:S(2)}, u32[]{:S(2)}) collective-permute-start(bf16[64,1536]{1,0:T(8,128)(2,1)S(1)} %get-tuple-element.185), channel_id=1, source_target_pairs={{0,3},{1,0},{2,1},{3,2},{4,7},{5,4},{6,5},{7,6},{8,11},{9,8},{10,9... | collective-permute-start | bytes 589832 | tf_op jit(solution)/shard_map/ppermute | solution.py:82
  227.3 25.9 %collective-permute-start.29 = (bf16[768,3456]{1,0:T(8,128)(2,1)}, bf16[768,3456]{1,0:T(8,128)(2,1)}, u32[]{:S(2)}, u32[]{:S(2)}) collective-permute-start(bf16[768,3456]{1,0:T(8,128)(2,1)} %all-gather.14.cloned.1.call-done.up0.down0), channel_id=1, source_target_pairs={{0,4},{4,0},{1,5},{5,1},{2,6},{6,2},{3,7},{7,3},{8,12},{12,8},{9,1... | collective-permute-start | bytes 15925256 | tf_op jit(solution)/shard_map/ppermute | solution.py:82
  227.3 25.9 %all-to-all-start.2 = ((bf16[8,64,1536]{2,1,0:T(8,128)(2,1)}), bf16[8,64,1536]{2,1,0:T(8,128)(2,1)}, u32[]{:S(2)}, u32[]{:S(2)}) async-start(bf16[8,64,1536]{2,1,0:T(8,128)(2,1)} %bitcast.140), calls=%async_computation.2 | async-start | bytes 3145728 | tf_op jit(solution)/shard_map/all_to_all | solution.py:144
  233.2 140.8 %reduce-scatter.5.cloned.1.call-start = ((), (), s32[]{:S(2)}) async-start(), calls=%async_computation.15 | async-start | bytes 1769472 | tf_op jit(solution)/shard_map/reduce_scatter | solution.py:706
  289.5 9.1 %collective-permute-start.31 = (bf16[768,3456]{1,0:T(8,128)(2,1)}, bf16[768,3456]{1,0:T(8,128)(2,1)}, u32[]{:S(2)}, u32[]{:S(2)}) collective-permute-start(bf16[768,3456]{1,0:T(8,128)(2,1)} %shard_map.247), channel_id=1, source_target_pairs={{0,4},{4,0},{1,5},{5,1},{2,6},{6,2},{3,7},{7,3},{8,12},{12,8},{9,1... | collective-permute-start | bytes 15925256 | tf_op jit(solution)/shard_map/ppermute | solution.py:82
  289.6 33.0 %all-to-all-start.3 = ((bf16[8,64,1664]{2,1,0:T(8,128)(2,1)}), bf16[8,64,1664]{2,1,0:T(8,128)(2,1)}, u32[]{:S(2)}, u32[]{:S(2)}) async-start(bf16[8,64,1664]{2,1,0:T(8,128)(2,1)} %bitcast.137), calls=%async_computation.4 | async-start | bytes 3407872 | tf_op jit(solution)/shard_map/all_to_all | solution.py:144
  294.9 146.2 %reduce-scatter.7.cloned.1.call-start = ((), (), s32[]{:S(2)}) async-start(), calls=%async_computation.16 | async-start | bytes 6635520 | tf_op jit(solution)/shard_map/reduce_scatter | solution.py:555
  326.5 10.3 %collective-permute-start.32 = (bf16[64,1536]{1,0:T(8,128)(2,1)S(1)}, bf16[64,1536]{1,0:T(8,128)(2,1)S(1)}, u32[]{:S(2)}, u32[]{:S(2)}) collective-permute-start(bf16[64,1536]{1,0:T(8,128)(2,1)S(1)} %get-tuple-element.205.refs_0_), channel_id=1, source_target_pairs={{0,3},{1,0},{2,1},{3,2},{4,7},{5,4},{6,5},{7,6},{8,11},{9,8},{10,9... | collective-permute-start | bytes 589832 | tf_op jit(solution)/shard_map/ppermute | solution.py:82
  326.6 16.7 %collective-permute-start.33 = (bf16[64,1536]{1,0:T(8,128)(2,1)S(1)}, bf16[64,1536]{1,0:T(8,128)(2,1)S(1)}, u32[]{:S(2)}, u32[]{:S(2)}) collective-permute-start(bf16[64,1536]{1,0:T(8,128)(2,1)S(1)} %get-tuple-element.205.refs_0_), channel_id=1, source_target_pairs={{0,2},{1,3},{2,0},{3,1},{4,6},{5,7},{6,4},{7,5},{8,10},{9,11},{10,... | collective-permute-start | bytes 589832 | tf_op jit(solution)/shard_map/ppermute | solution.py:82
  330.6 13.6 %collective-permute-start.34 = (bf16[64,1536]{1,0:T(8,128)(2,1)S(1)}, bf16[64,1536]{1,0:T(8,128)(2,1)S(1)}, u32[]{:S(2)}, u32[]{:S(2)}) collective-permute-start(bf16[64,1536]{1,0:T(8,128)(2,1)S(1)} %get-tuple-element.205.refs_0_), channel_id=1, source_target_pairs={{0,1},{1,2},{2,3},{3,0},{4,5},{5,6},{6,7},{7,4},{8,9},{9,10},{10,1... | collective-permute-start | bytes 589832 | tf_op jit(solution)/shard_map/ppermute | solution.py:82
  350.8 23.2 %collective-permute-start.38 = (bf16[768,1024]{1,0:T(8,128)(2,1)}, bf16[768,1024]{1,0:T(8,128)(2,1)}, u32[]{:S(2)}, u32[]{:S(2)}) collective-permute-start(bf16[768,1024]{1,0:T(8,128)(2,1)} %shard_map.251), channel_id=1, source_target_pairs={{0,4},{4,0},{1,5},{5,1},{2,6},{6,2},{3,7},{7,3},{8,12},{12,8},{9,1... | collective-permute-start | bytes 4718600 | tf_op jit(solution)/shard_map/ppermute | solution.py:82
  350.8 7.8 %collective-permute-start.35 = (bf16[64,1536]{1,0:T(8,128)(2,1)S(1)}, bf16[64,1536]{1,0:T(8,128)(2,1)S(1)}, u32[]{:S(2)}, u32[]{:S(2)}) collective-permute-start(bf16[64,1536]{1,0:T(8,128)(2,1)S(1)} %get-tuple-element.209), channel_id=1, source_target_pairs={{0,1},{1,2},{2,3},{3,0},{4,5},{5,6},{6,7},{7,4},{8,9},{9,10},{10,1... | collective-permute-start | bytes 589832 | tf_op jit(solution)/shard_map/ppermute | solution.py:82
  351.3 9.3 %collective-permute-start.36 = (bf16[64,1536]{1,0:T(8,128)(2,1)S(1)}, bf16[64,1536]{1,0:T(8,128)(2,1)S(1)}, u32[]{:S(2)}, u32[]{:S(2)}) collective-permute-start(bf16[64,1536]{1,0:T(8,128)(2,1)S(1)} %get-tuple-element.210), channel_id=1, source_target_pairs={{0,2},{1,3},{2,0},{3,1},{4,6},{5,7},{6,4},{7,5},{8,10},{9,11},{10,... | collective-permute-start | bytes 589832 | tf_op jit(solution)/shard_map/ppermute | solution.py:82
  354.9 9.4 %collective-permute-start.37 = (bf16[64,1536]{1,0:T(8,128)(2,1)S(1)}, bf16[64,1536]{1,0:T(8,128)(2,1)S(1)}, u32[]{:S(2)}, u32[]{:S(2)}) collective-permute-start(bf16[64,1536]{1,0:T(8,128)(2,1)S(1)} %get-tuple-element.211), channel_id=1, source_target_pairs={{0,3},{1,0},{2,1},{3,2},{4,7},{5,4},{6,5},{7,6},{8,11},{9,8},{10,9... | collective-permute-start | bytes 589832 | tf_op jit(solution)/shard_map/ppermute | solution.py:82
  367.8 25.3 %all-to-all-start.4 = ((bf16[8,64,1536]{2,1,0:T(8,128)(2,1)}), bf16[8,64,1536]{2,1,0:T(8,128)(2,1)S(1)}, u32[]{:S(2)}, u32[]{:S(2)}) async-start(bf16[8,64,1536]{2,1,0:T(8,128)(2,1)} %bitcast.139), calls=%async_computation.5 | async-start | bytes 3145728 | tf_op jit(solution)/shard_map/all_to_all | solution.py:144
  373.7 118.5 %reduce-scatter.11.cloned.1.call-start = ((), (), s32[]{:S(2)}) async-start(), calls=%async_computation.18 | async-start | bytes 1966080 | tf_op jit(solution)/shard_map/reduce_scatter | solution.py:555
  414.0 9.1 %collective-permute-start.39 = (bf16[768,3456]{1,0:T(8,128)(2,1)}, bf16[768,3456]{1,0:T(8,128)(2,1)}, u32[]{:S(2)}, u32[]{:S(2)}) collective-permute-start(bf16[768,3456]{1,0:T(8,128)(2,1)} %shard_map.255), channel_id=1, source_target_pairs={{0,4},{4,0},{1,5},{5,1},{2,6},{6,2},{3,7},{7,3},{8,12},{12,8},{9,1... | collective-permute-start | bytes 15925256 | tf_op jit(solution)/shard_map/ppermute | solution.py:82
  414.0 27.1 %all-to-all-start.5 = ((bf16[8,64,1664]{2,1,0:T(8,128)(2,1)}), bf16[8,64,1664]{2,1,0:T(8,128)(2,1)}, u32[]{:S(2)}, u32[]{:S(2)}) async-start(bf16[8,64,1664]{2,1,0:T(8,128)(2,1)} %bitcast.138), calls=%async_computation.6 | async-start | bytes 3407872 | tf_op jit(solution)/shard_map/all_to_all | solution.py:144
  419.4 95.9 %reduce-scatter.9.cloned.1.call-start = ((), (), s32[]{:S(2)}) async-start(), calls=%async_computation.17 | async-start | bytes 6635520 | tf_op jit(solution)/shard_map/reduce_scatter | solution.py:555
  444.4 7.4 %collective-permute-start.40 = (bf16[64,1536]{1,0:T(8,128)(2,1)S(1)}, bf16[64,1536]{1,0:T(8,128)(2,1)S(1)}, u32[]{:S(2)}, u32[]{:S(2)}) collective-permute-start(bf16[64,1536]{1,0:T(8,128)(2,1)S(1)} %get-tuple-element.231.refs_0_), channel_id=1, source_target_pairs={{0,3},{1,0},{2,1},{3,2},{4,7},{5,4},{6,5},{7,6},{8,11},{9,8},{10,9... | collective-permute-start | bytes 589832 | tf_op jit(solution)/shard_map/ppermute | solution.py:82
  445.6 10.0 %collective-permute-start.41 = (bf16[64,1536]{1,0:T(8,128)(2,1)S(1)}, bf16[64,1536]{1,0:T(8,128)(2,1)S(1)}, u32[]{:S(2)}, u32[]{:S(2)}) collective-permute-start(bf16[64,1536]{1,0:T(8,128)(2,1)S(1)} %get-tuple-element.231.refs_0_), channel_id=1, source_target_pairs={{0,2},{1,3},{2,0},{3,1},{4,6},{5,7},{6,4},{7,5},{8,10},{9,11},{10,... | collective-permute-start | bytes 589832 | tf_op jit(solution)/shard_map/ppermute | solution.py:82
  446.9 10.1 %collective-permute-start.42 = (bf16[64,1536]{1,0:T(8,128)(2,1)S(1)}, bf16[64,1536]{1,0:T(8,128)(2,1)S(1)}, u32[]{:S(2)}, u32[]{:S(2)}) collective-permute-start(bf16[64,1536]{1,0:T(8,128)(2,1)S(1)} %get-tuple-element.231.refs_0_), channel_id=1, source_target_pairs={{0,1},{1,2},{2,3},{3,0},{4,5},{5,6},{6,7},{7,4},{8,9},{9,10},{10,1... | collective-permute-start | bytes 589832 | tf_op jit(solution)/shard_map/ppermute | solution.py:82
  462.0 9.1 %collective-permute-start.43 = (bf16[64,1536]{1,0:T(8,128)(2,1)}, bf16[64,1536]{1,0:T(8,128)(2,1)S(1)}, u32[]{:S(2)}, u32[]{:S(2)}) collective-permute-start(bf16[64,1536]{1,0:T(8,128)(2,1)} %get-tuple-element.235), channel_id=1, source_target_pairs={{0,1},{1,2},{2,3},{3,0},{4,5},{5,6},{6,7},{7,4},{8,9},{9,10},{10,1... | collective-permute-start | bytes 589832 | tf_op jit(solution)/shard_map/ppermute | solution.py:82
  463.6 9.6 %collective-permute-start.44 = (bf16[64,1536]{1,0:T(8,128)(2,1)}, bf16[64,1536]{1,0:T(8,128)(2,1)}, u32[]{:S(2)}, u32[]{:S(2)}) collective-permute-start(bf16[64,1536]{1,0:T(8,128)(2,1)} %get-tuple-element.236), channel_id=1, source_target_pairs={{0,2},{1,3},{2,0},{3,1},{4,6},{5,7},{6,4},{7,5},{8,10},{9,11},{10,... | collective-permute-start | bytes 589832 | tf_op jit(solution)/shard_map/ppermute | solution.py:82
  466.7 9.9 %collective-permute-start.45 = (bf16[64,1536]{1,0:T(8,128)(2,1)}, bf16[64,1536]{1,0:T(8,128)(2,1)}, u32[]{:S(2)}, u32[]{:S(2)}) collective-permute-start(bf16[64,1536]{1,0:T(8,128)(2,1)} %get-tuple-element.237), channel_id=1, source_target_pairs={{0,3},{1,0},{2,1},{3,2},{4,7},{5,4},{6,5},{7,6},{8,11},{9,8},{10,9... | collective-permute-start | bytes 589832 | tf_op jit(solution)/shard_map/ppermute | solution.py:82
  484.8 20.8 %collective-permute-start.49 = (bf16[192,1152]{1,0:T(8,128)(2,1)}, bf16[192,1152]{1,0:T(8,128)(2,1)S(1)}, u32[]{:S(2)}, u32[]{:S(2)}) collective-permute-start(bf16[192,1152]{1,0:T(8,128)(2,1)} %get-tuple-element.314), channel_id=1, source_target_pairs={{0,8},{8,16},{16,24},{24,0},{1,9},{9,17},{17,25},{25,1},{2,10},{10... | collective-permute-start | bytes 1327112 | tf_op jit(solution)/shard_map/ppermute | solution.py:82
  485.6 29.7 %collective-permute-start.50 = (bf16[192,1152]{1,0:T(8,128)(2,1)}, bf16[192,1152]{1,0:T(8,128)(2,1)S(1)}, u32[]{:S(2)}, u32[]{:S(2)}) collective-permute-start(bf16[192,1152]{1,0:T(8,128)(2,1)} %get-tuple-element.313), channel_id=1, source_target_pairs={{0,16},{8,24},{16,0},{24,8},{1,17},{9,25},{17,1},{25,9},{2,18},{10... | collective-permute-start | bytes 1327112 | tf_op jit(solution)/shard_map/ppermute | solution.py:82
  487.0 28.3 %collective-permute-start.51 = (bf16[192,1152]{1,0:T(8,128)(2,1)}, bf16[192,1152]{1,0:T(8,128)(2,1)S(1)}, u32[]{:S(2)}, u32[]{:S(2)}) collective-permute-start(bf16[192,1152]{1,0:T(8,128)(2,1)} %get-tuple-element.312), channel_id=1, source_target_pairs={{0,24},{8,0},{16,8},{24,16},{1,25},{9,1},{17,9},{25,17},{2,26},{10... | collective-permute-start | bytes 1327112 | tf_op jit(solution)/shard_map/ppermute | solution.py:82
  490.4 32.4 %collective-permute-start.30 = (bf16[64,1536]{1,0:T(8,128)(2,1)}, bf16[64,1536]{1,0:T(8,128)(2,1)}, u32[]{:S(2)}, u32[]{:S(2)}) collective-permute-start(bf16[64,1536]{1,0:T(8,128)(2,1)} %get-tuple-element.325), channel_id=1, source_target_pairs={{0,64},{64,0},{1,65},{65,1},{2,66},{66,2},{3,67},{67,3},{4,68},{68... | collective-permute-start | bytes 589832 | tf_op jit(solution)/shard_map/ppermute | solution.py:82
  518.3 24.1 %collective-permute-start.52 = (bf16[96,4608]{1,0:T(8,128)(2,1)S(1)}, bf16[96,4608]{1,0:T(8,128)(2,1)S(1)}, u32[]{:S(2)}, u32[]{:S(2)}) collective-permute-start(bf16[96,4608]{1,0:T(8,128)(2,1)S(1)} %get-tuple-element.257), channel_id=1, source_target_pairs={{0,32},{32,0},{64,96},{96,64},{1,33},{33,1},{65,97},{97,65},{2,34}... | collective-permute-start | bytes 2654216 | tf_op jit(solution)/shard_map/ppermute | solution.py:82
  521.3 40.0 %collective-permute-start.53 = (bf16[96,4608]{1,0:T(8,128)(2,1)S(1)}, bf16[96,4608]{1,0:T(8,128)(2,1)S(1)}, u32[]{:S(2)}, u32[]{:S(2)}) collective-permute-start(bf16[96,4608]{1,0:T(8,128)(2,1)S(1)} %get-tuple-element.258), channel_id=1, source_target_pairs={{0,64},{32,96},{64,0},{96,32},{1,65},{33,97},{65,1},{97,33},{2,66}... | collective-permute-start | bytes 2654216 | tf_op jit(solution)/shard_map/ppermute | solution.py:82
  521.9 39.5 %collective-permute-start.54 = (bf16[96,4608]{1,0:T(8,128)(2,1)S(1)}, bf16[96,4608]{1,0:T(8,128)(2,1)S(1)}, u32[]{:S(2)}, u32[]{:S(2)}) collective-permute-start(bf16[96,4608]{1,0:T(8,128)(2,1)S(1)} %get-tuple-element.259), channel_id=1, source_target_pairs={{0,96},{32,64},{64,32},{96,0},{1,97},{33,65},{65,33},{97,1},{2,98}... | collective-permute-start | bytes 2654216 | tf_op jit(solution)/shard_map/ppermute | solution.py:82
  526.7 40.8 %collective-permute-start.47 = (bf16[64,1536]{1,0:T(8,128)(2,1)S(1)}, bf16[64,1536]{1,0:T(8,128)(2,1)S(1)}, u32[]{:S(2)}, u32[]{:S(2)}) collective-permute-start(bf16[64,1536]{1,0:T(8,128)(2,1)S(1)} %get-tuple-element.323), channel_id=1, source_target_pairs={{0,64},{64,0},{1,65},{65,1},{2,66},{66,2},{3,67},{67,3},{4,68},{68... | collective-permute-start | bytes 589832 | tf_op jit(solution)/shard_map/ppermute | solution.py:82
  562.6 8.9 %collective-permute-start.57 = (f32[24,128]{1,0:T(8,128)S(1)}, f32[24,128]{1,0:T(8,128)S(1)}, u32[]{:S(2)}, u32[]{:S(2)}) collective-permute-start(f32[24,128]{1,0:T(8,128)S(1)} %get-tuple-element.342), channel_id=1, source_target_pairs={{0,3},{1,0},{2,1},{3,2},{4,7},{5,4},{6,5},{7,6},{8,11},{9,8},{10,9... | collective-permute-start | bytes 36872 | tf_op jit(solution)/shard_map/ppermute | solution.py:82
  563.3 8.3 %collective-permute-start.56 = (f32[24,128]{1,0:T(8,128)S(1)}, f32[24,128]{1,0:T(8,128)S(1)}, u32[]{:S(2)}, u32[]{:S(2)}) collective-permute-start(f32[24,128]{1,0:T(8,128)S(1)} %get-tuple-element.341), channel_id=1, source_target_pairs={{0,2},{1,3},{2,0},{3,1},{4,6},{5,7},{6,4},{7,5},{8,10},{9,11},{10,... | collective-permute-start | bytes 36872 | tf_op jit(solution)/shard_map/ppermute | solution.py:82
  (91 other events, 923.9 us)
Sparse Core Ops, SparseCore 0:
  19.3 24.6 all-gather.5
  47.6 28.0 all-gather.7
  81.9 56.8 all-gather.9
  141.0 27.0 all-gather.11
  169.6 57.6 all-gather.13
  289.7 54.5 reduce-scatter.4
  346.7 55.2 reduce-scatter.6
  414.1 25.2 reduce-scatter.10
  442.0 64.8 reduce-scatter.8

commit v5 on v4

--- a/solution.py
+++ b/solution.py
@@ -354,6 +354,7 @@
         + [by_step(ROUTES, 2 * STEP), by_step(ROUTES, STEP)],
         grid=(STEPS,),
         scratch=[pltpu.VMEM((ROUTES, D), F32)],
+        far_in=(5, 6, 7, 8),
         far_out=(1, 2, 3, 4),
     )
 
@@ -397,7 +398,7 @@
         part[:, D:] = extra.astype(BF)
 
 
-def ffn_backward(s, rows, gates, gate_up, weights):
+def ffn_backward(s, rows, gates, gate_up, weights, far_rows):
     return run(
         ffn_backward_kernel,
         [shaped((ROUTES, WIDE)), shaped((ROUTES, UP))],
@@ -408,6 +409,7 @@
         out_specs=[fixed(ROUTES, WIDE), by_step(ROUTES, 2 * STEP)],
         grid=(STEPS,),
         scratch=[pltpu.VMEM((ROUTES, D), F32), pltpu.VMEM((ROUTES, HD), F32)],
+        far_in=(1, 2, 3) if far_rows else (2, 3),
     )
 
 
@@ -617,8 +619,7 @@
     named = jnp.sum((route_experts[0][:, :, :, None] == jnp.arange(E)).astype(F32), axis=2)
     named = named.astype(BF).reshape(ROUTES, E)
     named_else = move(named, SECTION, lambda s: (s + 1,))
-    small, named_else, own_rows = together(small, named_else, own_rows)
-    masks = [jnp.where(s == layer, named, named_else).astype(F32) for layer in (0, 1)]
+    small, own_rows = together(small, own_rows)
 
     att_beside = move(att_piece, SIDE, lambda s, x: (s, x + 1))
     att_straight = move(att_piece, SIDE, lambda s, x: (s + 1, x))
@@ -649,7 +650,8 @@
         axis=1,
     )
     att_pair1 = att_pairs[1]
-    att_pair0, grad_rows = together(att_pair0, grad_rows)
+    att_pair0, grad_rows, named_else = together(att_pair0, grad_rows, named_else)
+    masks = [jnp.where(s == layer, named, named_else).astype(F32) for layer in (0, 1)]
     att_row0 = gather_row(att_pair0)
 
     hidden_blocks = tensor_gather(own_rows)
@@ -723,7 +725,9 @@
         mid, ffn_gain, router, normed_ffn, rows, gates, own_gates, gate_up, gated = kept[2 * layer + 1]
         if layer == 0:
             gated, sum1 = together(gated, sum1)
-        part_grad, gate_up_grad = ffn_backward(s_arg, grad_rows, gates, gate_up, ffn_w[layer])
+        part_grad, gate_up_grad = ffn_backward(
+            s_arg, grad_rows, gates, gate_up, ffn_w[layer], layer == 1
+        )
         ffn_parts = (rows, grad_rows, gate_up_grad, gated)
         got = group_exchange(part_grad)
         own = ffn_weights(0, *ffn_parts, swap_core(ffn_weights(1, *ffn_parts)))
@@ -778,6 +782,7 @@
         [shaped((DBLK, PIECE + ATT_PAD))] * 4,
         [s_arg, *ffn_sums, att_sums[1], *att_blocks],
         1,
+        far_in=(1, 2, 3),
     )
     beside = move(same1, SIDE, lambda s, x: (s, x + 1))
     straight = move(other0, SIDE, lambda s, x: (s + 1, x))

time: 590 us -> 583 us (0.988)
  local copies, waits for them, and re-layouts: 63 us -> 53.1 us
    unnamed x178 -> x168, local copies, waits for them, and re-layouts: 47.5 us -> 37.3 us
  transfers between devices with their start and end apart: 72 -> 72, of which waited for: 41 -> 42; matrix products, arithmetic and copies ran while one was open for 6% -> 7% of each run, Pallas kernels for 13% -> 14%
where the time goes in v5:
time: 583 us; the launch traced here: 573 us
  waiting for transfers between devices  240 us (41%)
  Pallas kernels  108 us (19%)
  starting transfers between devices  106 us (18%)
  local copies, waits for them, and re-layouts  53.1 us (9%)
  blocking collectives  25.3 us (4%)
  other arithmetic  15.9 us (3%)
  between operations  15.4 us (3%)
  matrix products  10.1 us (2%)
    ppermute x58, waiting for transfers between devices, move(): return lax.ppermute(block, axes, pairs)  164 us
    pallas_call x28, Pallas kernels, run(): pl.pallas_call(kernel, out_shape=[pltpu.HBM(x.shape, x.dtype) if i in far...  108 us
    ppermute x58, starting transfers between devices, move(): return lax.ppermute(block, axes, pairs)  76.4 us
    all_to_all x5, waiting for transfers between devices, group_exchange(): return lax.all_to_all(rows, GROUP, 0, 0, tiled=True)  61.3 us
    unnamed x168, local copies, waits for them, and re-layouts  37.3 us
    all_to_all x5, starting transfers between devices, group_exchange(): return lax.all_to_all(rows, GROUP, 0, 0, tiled=True)  28.6 us
    all_to_all x1, blocking collectives, group_exchange(): return lax.all_to_all(rows, GROUP, 0, 0, tiled=True)  25.3 us
    all_gather x4, waiting for transfers between devices, gather_row(): return lax.all_gather(part, 'z', axis=0, tiled=True)  13.3 us
  transfers between devices with their start and end apart: 72, of which 42 were waited for; matrix products, arithmetic and copies ran while one was open for 7% of the time, Pallas kernels for 14%

profile of v5, /device:TPU:8, one launch (start us, length us, event | category | flops | bytes accessed | tf_op | source)
XLA Modules:
  0.0 572.7 jit_solution(13314904480054025733)
XLA Ops:
  10.6 2.7 collective-permute-start.2
  48.9 3.3 collective-permute-start.9
  54.3 5.5 collective-permute-done.10.refs_1_
  62.2 3.3 collective-permute-done.12.refs_3_
  65.5 13.4 %collective-permute-done.8 = bf16[96,3456]{1,0:T(8,128)(2,1)S(1)} collective-permute-done((bf16[96,3456]{1,0:T(8,128)(2,1)}, bf16[96,3456]{1,0:T(8,128)(2,1)S(1)}, u32[]{:S(2)}, u32[]{:S(2)}) %collective-permute-start.8) | collective-permute-done | bytes 663584 | tf_op jit(solution)/shard_map/ppermute | solution.py:82
  80.1 3.0 maximum_select_fusion
  83.4 3.7 collective-permute-done.16.other.refs_6_.refs_5_
  88.3 3.0 shard_map.238
  93.5 2.9 collective-permute-start.18
  97.2 3.3 collective-permute-done.17.refs_1_
  102.8 3.0 collective-permute-done.19.refs_3_
  108.0 6.0 %all-to-all-start = ((bf16[8,64,1536]{2,1,0:T(8,128)(2,1)}), bf16[8,64,1536]{2,1,0:T(8,128)(2,1)S(1)}, u32[]{:S(2)}, u32[]{:S(2)}) async-start(bf16[8,64,1536]{2,1,0:T(8,128)(2,1)} %bitcast.146), calls=%async_computation | async-start | bytes 3145728 | tf_op jit(solution)/shard_map/all_to_all | solution.py:144
  114.0 3.1 maximum_select_fusion.1
  117.0 15.8 %all-to-all-done = bf16[8,64,1536]{2,1,0:T(8,128)(2,1)S(1)} async-done(((bf16[8,64,1536]{2,1,0:T(8,128)(2,1)}), bf16[8,64,1536]{2,1,0:T(8,128)(2,1)S(1)}, u32[]{:S(2)}, u32[]{:S(2)}) %all-to-all-start) | async-done | bytes 1572896 | tf_op jit(solution)/shard_map/all_to_all | solution.py:144
  132.9 7.2 %all-gather.10.cloned.1.call-done.up0.down0 = bf16[768,3456]{1,0:T(8,128)(2,1)} async-done(((bf16[192,3456]{1,0:T(8,128)(2,1)}), bf16[768,3456]{1,0:T(8,128)(2,1)}) %all-gather.10.cloned.1.call-update) | async-done | bytes 5308432 | tf_op jit(solution)/shard_map/all_gather | solution.py:561
  142.2 7.2 %collective-permute-done.21.up1.down1 = bf16[768,3456]{1,0:T(8,128)(2,1)} collective-permute-done((bf16[768,3456]{1,0:T(8,128)(2,1)}, bf16[768,3456]{1,0:T(8,128)(2,1)}, u32[]{:S(2)}, u32[]{:S(2)}) %collective-permute-start.21) | collective-permute-done | bytes 5308448 | tf_op jit(solution)/shard_map/ppermute | solution.py:82
  149.4 12.6 %shard_map.240 = (bf16[512,1536]{1,0:T(8,128)(2,1)S(1)}, f32[512,16]{1,0:T(8,128)}, f32[64,16]{1,0:T(8,128)}, bf16[512,2304]{1,0:T(8,128)(2,1)}, bf16[512,1152]{1,0:T(8,128)(2,1)}) custom-call(s32[1]{0:T(128)} %bitcast.35.s_ref, s32[1]{0:T(128)} %bitcast.32.t_ref, bf16[512,1536]{1,0:T(8,128)(2,1)S(1)} %bitcast.132, ...), custom_call_target="tpu_custom_call" | custom-call | flops 5435817984 | bytes 28037128 | tf_op jit(solution)/shard_map/pallas_call | solution.py:119
  162.0 25.3 %all_to_all.70 = bf16[8,64,1536]{2,1,0:T(8,128)(2,1)S(1)} all-to-all(bf16[8,64,1536]{2,1,0:T(8,128)(2,1)S(1)} %bitcast.147), channel_id=1, replica_groups=mesh['section'=2,'xhi'=2,'z'=4,'core'=2,'tensor'=4] {'section','tensor'}, dimensions={0} | all-to-all | bytes 3145728 | tf_op jit(solution)/shard_map/all_to_all | solution.py:144
  192.3 3.5 collective-permute-done.22.refs_1_
  195.8 4.0 collective-permute-done.23.refs_2_
  203.5 3.0 shard_map.242
  208.0 2.7 collective-permute-start.27
  211.1 3.2 collective-permute-done.26.refs_1_
  214.3 3.0 collective-permute-done.27.refs_2_
  217.3 3.0 collective-permute-done.28.refs_3_
  222.5 6.1 %all-gather.14.cloned.1.call-done.up0.down0 = bf16[768,3456]{1,0:T(8,128)(2,1)} async-done(((bf16[192,3456]{1,0:T(8,128)(2,1)}), bf16[768,3456]{1,0:T(8,128)(2,1)}) %all-gather.14.cloned.1.call-update) | async-done | bytes 5308432 | tf_op jit(solution)/shard_map/all_gather | solution.py:561
  228.6 5.9 %all-to-all-start.2 = ((bf16[8,64,1536]{2,1,0:T(8,128)(2,1)}), bf16[8,64,1536]{2,1,0:T(8,128)(2,1)S(1)}, u32[]{:S(2)}, u32[]{:S(2)}) async-start(bf16[8,64,1536]{2,1,0:T(8,128)(2,1)} %bitcast.145), calls=%async_computation.2 | async-start | bytes 3145728 | tf_op jit(solution)/shard_map/all_to_all | solution.py:144
  234.4 4.1 fusion.8
  239.9 14.5 %all-to-all-done.2 = bf16[8,64,1536]{2,1,0:T(8,128)(2,1)S(1)} async-done(((bf16[8,64,1536]{2,1,0:T(8,128)(2,1)}), bf16[8,64,1536]{2,1,0:T(8,128)(2,1)S(1)}, u32[]{:S(2)}, u32[]{:S(2)}) %all-to-all-start.2) | async-done | bytes 1572896 | tf_op jit(solution)/shard_map/all_to_all | solution.py:144
  254.4 13.2 %shard_map.244 = (bf16[512,1536]{1,0:T(8,128)(2,1)S(1)}, f32[512,16]{1,0:T(8,128)}, f32[64,16]{1,0:T(8,128)}, bf16[512,2304]{1,0:T(8,128)(2,1)}, bf16[512,1152]{1,0:T(8,128)(2,1)}) custom-call(s32[1]{0:T(128)} %bitcast.35.s_ref, s32[1]{0:T(128)} %bitcast.32.t_ref, bf16[512,1536]{1,0:T(8,128)(2,1)S(1)} %bitcast.135, bf16[16,1536]{1,0:T(8,128)(2,1)S(1)} %copy-done.51, ...), custom_call_target="tpu_custom_call" | custom-call | flops 5435817984 | bytes 28037128 | tf_op jit(solution)/shard_map/pallas_call | solution.py:119
  268.8 10.9 %shard_map.246 = (bf16[512,1664]{1,0:T(8,128)(2,1)S(1)}, bf16[512,2304]{1,0:T(8,128)(2,1)S(1)}) custom-call(s32[1]{0:T(128)} %bitcast.35.s_ref, bf16[512,1536]{1,0:T(8,128)(2,1)} %bitcast.128, f32[512,16]{1,0:T(8,128)} %get-tuple-element.197.gates_ref, bf16[512,2304]{1,0:T(8,128)(2,1)} %get-tuple-element.198.gate_up_ref, bf16[768,3456]{1,0:T(8,128)(2,1)S(1)} %bitcast.127, ...), custom_call_target="tpu_custom_call" | custom-call | flops 5435817984 | bytes 29261828 | tf_op jit(solution)/shard_map/pallas_call | solution.py:119
  279.8 5.4 shard_map.247
  285.2 5.4 all-to-all-start.3
  290.7 3.5 collective-permute-done.31.refs_0_
  298.6 5.8 %shard_map.248 = bf16[768,3456]{1,0:T(8,128)(2,1)S(1)} custom-call(bf16[512,1536]{1,0:T(8,128)(2,1)S(1)} %bitcast.137, bf16[512,1536]{1,0:T(8,128)(2,1)S(1)} %bitcast.130, bf16[512,2304]{1,0:T(8,128)(2,1)S(1)} %copy-done.14, bf16[512,1152]{1,0:T(8,128)(2,1)S(1)} %copy-done.25, bf16[768,3456]{1,0:T(8,128)(2,1)} %collective-permute-done.31.refs_0_), custom_call_target="tpu_custom_call" | custom-call | flops 2717908992 | bytes 17301504 | tf_op jit(solution)/shard_map/pallas_call | solution.py:119
  306.8 11.4 %all-to-all-done.3 = bf16[8,64,1664]{2,1,0:T(8,128)(2,1)} async-done(((bf16[8,64,1664]{2,1,0:T(8,128)(2,1)}), bf16[8,64,1664]{2,1,0:T(8,128)(2,1)}, u32[]{:S(2)}, u32[]{:S(2)}) %all-to-all-start.3) | async-done | bytes 1703968 | tf_op jit(solution)/shard_map/all_to_all | solution.py:144
  318.9 3.2 shard_map.249
  322.2 4.0 collective-permute-start.33
  326.2 2.6 collective-permute-start.34
  328.8 3.7 collective-permute-done.32.refs_1_
  332.5 6.4 %collective-permute-done.33.refs_2_ = bf16[64,1536]{1,0:T(8,128)(2,1)S(1)} collective-permute-done((bf16[64,1536]{1,0:T(8,128)(2,1)S(1)}, bf16[64,1536]{1,0:T(8,128)(2,1)S(1)}, u32[]{:S(2)}, u32[]{:S(2)}) %collective-permute-start.33) | collective-permute-done | bytes 196640 | tf_op jit(solution)/shard_map/ppermute | solution.py:82
  341.2 3.3 shard_map.250
  346.9 3.6 collective-permute-start.36
  350.7 3.6 collective-permute-done.35.refs_1_
  356.3 3.7 collective-permute-done.37.refs_3_
  363.4 6.0 %all-to-all-start.4 = ((bf16[8,64,1536]{2,1,0:T(8,128)(2,1)}), bf16[8,64,1536]{2,1,0:T(8,128)(2,1)S(1)}, u32[]{:S(2)}, u32[]{:S(2)}) async-start(bf16[8,64,1536]{2,1,0:T(8,128)(2,1)} %bitcast.144), calls=%async_computation.5 | async-start | bytes 3145728 | tf_op jit(solution)/shard_map/all_to_all | solution.py:144
  376.1 12.5 %all-to-all-done.4 = bf16[8,64,1536]{2,1,0:T(8,128)(2,1)S(1)} async-done(((bf16[8,64,1536]{2,1,0:T(8,128)(2,1)}), bf16[8,64,1536]{2,1,0:T(8,128)(2,1)S(1)}, u32[]{:S(2)}, u32[]{:S(2)}) %all-to-all-start.4) | async-done | bytes 1572896 | tf_op jit(solution)/shard_map/all_to_all | solution.py:144
  391.3 10.4 %shard_map.254 = (bf16[512,1664]{1,0:T(8,128)(2,1)S(1)}, bf16[512,2304]{1,0:T(8,128)(2,1)S(1)}) custom-call(s32[1]{0:T(128)} %bitcast.35.s_ref, bf16[512,1536]{1,0:T(8,128)(2,1)S(1)} %bitcast.138, f32[512,16]{1,0:T(8,128)} %get-tuple-element.223.gates_ref, bf16[512,2304]{1,0:T(8,128)(2,1)} %get-tuple-element.224.gate_up_ref, ...), custom_call_target="tpu_custom_call" | custom-call | flops 5435817984 | bytes 29261828 | tf_op jit(solution)/shard_map/pallas_call | solution.py:119
  401.7 5.4 shard_map.255
  407.2 5.4 all-to-all-start.5
  412.6 3.6 collective-permute-done.39.refs_0_
  419.2 5.8 %shard_map.256 = bf16[768,3456]{1,0:T(8,128)(2,1)S(1)} custom-call(bf16[512,1536]{1,0:T(8,128)(2,1)S(1)} %bitcast.134, bf16[512,1536]{1,0:T(8,128)(2,1)S(1)} %bitcast.140, bf16[512,2304]{1,0:T(8,128)(2,1)S(1)} %copy-done.16, bf16[512,1152]{1,0:T(8,128)(2,1)S(1)} %copy-done.23, bf16[768,3456]{1,0:T(8,128)(2,1)} %collective-permute-done.39.refs_0_), custom_call_target="tpu_custom_call" | custom-call | flops 2717908992 | bytes 17301504 | tf_op jit(solution)/shard_map/pallas_call | solution.py:119
  427.3 7.0 %all-to-all-done.5 = bf16[8,64,1664]{2,1,0:T(8,128)(2,1)} async-done(((bf16[8,64,1664]{2,1,0:T(8,128)(2,1)}), bf16[8,64,1664]{2,1,0:T(8,128)(2,1)}, u32[]{:S(2)}, u32[]{:S(2)}) %all-to-all-start.5) | async-done | bytes 1703968 | tf_op jit(solution)/shard_map/all_to_all | solution.py:144
  434.3 3.3 shard_map.257
  445.1 3.7 collective-permute-done.41.refs_2_
  450.2 4.1 shard_map.258
  456.8 3.1 collective-permute-start.44
  466.4 3.3 collective-permute-done.45.refs_3_
  469.7 2.9 shard_map.261
  484.6 14.1 %collective-permute-done.49.refs_1_ = bf16[192,1152]{1,0:T(8,128)(2,1)S(1)} collective-permute-done((bf16[192,1152]{1,0:T(8,128)(2,1)S(1)}, bf16[192,1152]{1,0:T(8,128)(2,1)S(1)}, u32[]{:S(2)}, u32[]{:S(2)}) %collective-permute-start.49) | collective-permute-done | bytes 442400 | tf_op jit(solution)/shard_map/ppermute | solution.py:82
  498.7 9.7 %collective-permute-done.50.refs_2_ = bf16[192,1152]{1,0:T(8,128)(2,1)S(1)} collective-permute-done((bf16[192,1152]{1,0:T(8,128)(2,1)S(1)}, bf16[192,1152]{1,0:T(8,128)(2,1)S(1)}, u32[]{:S(2)}, u32[]{:S(2)}) %collective-permute-start.50) | collective-permute-done | bytes 442400 | tf_op jit(solution)/shard_map/ppermute | solution.py:82
  510.9 3.1 collective-permute-start.52
  520.8 14.2 %collective-permute-done.52.beside = bf16[96,4608]{1,0:T(8,128)(2,1)S(1)} collective-permute-done((bf16[96,4608]{1,0:T(8,128)(2,1)S(1)}, bf16[96,4608]{1,0:T(8,128)(2,1)S(1)}, u32[]{:S(2)}, u32[]{:S(2)}) %collective-permute-start.52) | collective-permute-done | bytes 884768 | tf_op jit(solution)/shard_map/ppermute | solution.py:82
  535.0 19.0 %collective-permute-done.53.straight = bf16[96,4608]{1,0:T(8,128)(2,1)S(1)} collective-permute-done((bf16[96,4608]{1,0:T(8,128)(2,1)S(1)}, bf16[96,4608]{1,0:T(8,128)(2,1)S(1)}, u32[]{:S(2)}, u32[]{:S(2)}) %collective-permute-start.53) | collective-permute-done | bytes 884768 | tf_op jit(solution)/shard_map/ppermute | solution.py:82
  (347 shorter events, 153.5 us)
Async XLA Ops:
  7.2 38.9 %all-gather.6.cloned.1.call-start = ((), (), s32[]{:S(2)}) async-start(), calls=%async_computation.10 | async-start | bytes 1966080 | tf_op jit(solution)/shard_map/all_gather | solution.py:617
  10.2 19.1 %collective-permute-start.1 = (bf16[24,128]{1,0:T(8,128)(2,1)}, bf16[24,128]{1,0:T(8,128)(2,1)S(1)}, u32[]{:S(2)}, u32[]{:S(2)}) collective-permute-start(bf16[24,128]{1,0:T(8,128)(2,1)} %get-tuple-element.311), channel_id=1, source_target_pairs={{0,3},{1,0},{2,1},{3,2},{4,7},{5,4},{6,5},{7,6},{8,11},{9,8},{10,9... | collective-permute-start | bytes 18440 | tf_op jit(solution)/shard_map/ppermute | solution.py:82
  10.6 18.7 %collective-permute-start.2 = (bf16[24,128]{1,0:T(8,128)(2,1)}, bf16[24,128]{1,0:T(8,128)(2,1)S(1)}, u32[]{:S(2)}, u32[]{:S(2)}) collective-permute-start(bf16[24,128]{1,0:T(8,128)(2,1)} %get-tuple-element.311), channel_id=1, source_target_pairs={{0,2},{1,3},{2,0},{3,1},{4,6},{5,7},{6,4},{7,5},{8,10},{9,11},{10,... | collective-permute-start | bytes 18440 | tf_op jit(solution)/shard_map/ppermute | solution.py:82
  13.3 16.1 %collective-permute-start.3 = (bf16[24,128]{1,0:T(8,128)(2,1)}, bf16[24,128]{1,0:T(8,128)(2,1)}, u32[]{:S(2)}, u32[]{:S(2)}) collective-permute-start(bf16[24,128]{1,0:T(8,128)(2,1)} %get-tuple-element.311), channel_id=1, source_target_pairs={{0,1},{1,2},{2,3},{3,0},{4,5},{5,6},{6,7},{7,4},{8,9},{9,10},{10,1... | collective-permute-start | bytes 18440 | tf_op jit(solution)/shard_map/ppermute | solution.py:82
  16.8 23.8 %collective-permute-start = (bf16[96,1024]{1,0:T(8,128)(2,1)}, bf16[96,1024]{1,0:T(8,128)(2,1)}, u32[]{:S(2)}, u32[]{:S(2)}) collective-permute-start(bf16[96,1024]{1,0:T(8,128)(2,1)} %pad_maximum_fusion.6), channel_id=1, source_target_pairs={{0,64},{32,96},{64,0},{96,32},{1,65},{33,97},{65,1},{97,33},{2,66}... | collective-permute-start | bytes 589832 | tf_op jit(solution)/shard_map/ppermute | solution.py:82
  18.3 23.3 %collective-permute-start.14 = (bf16[96,1024]{1,0:T(8,128)(2,1)}, bf16[96,1024]{1,0:T(8,128)(2,1)}, u32[]{:S(2)}, u32[]{:S(2)}) collective-permute-start(bf16[96,1024]{1,0:T(8,128)(2,1)} %pad_maximum_fusion.6), channel_id=1, source_target_pairs={{0,96},{32,64},{64,32},{96,0},{1,97},{33,65},{65,33},{97,1},{2,98}... | collective-permute-start | bytes 589832 | tf_op jit(solution)/shard_map/ppermute | solution.py:82
  20.4 58.4 %all-gather.8.cloned.1.call-start = ((), (), s32[]{:S(2)}) async-start(), calls=%async_computation.11 | async-start | bytes 2211840 | tf_op jit(solution)/shard_map/all_gather | solution.py:561
  36.8 7.4 %collective-permute-start.13 = (bf16[96,1024]{1,0:T(8,128)(2,1)}, bf16[96,1024]{1,0:T(8,128)(2,1)S(1)}, u32[]{:S(2)}, u32[]{:S(2)}) collective-permute-start(bf16[96,1024]{1,0:T(8,128)(2,1)} %pad_maximum_fusion.6), channel_id=1, source_target_pairs={{0,32},{32,0},{64,96},{96,64},{1,33},{33,1},{65,97},{97,65},{2,34}... | collective-permute-start | bytes 589832 | tf_op jit(solution)/shard_map/ppermute | solution.py:82
  37.4 8.6 %collective-permute-start.15 = (bf16[512,16]{1,0:T(8,128)(2,1)S(1)}, bf16[512,16]{1,0:T(8,128)(2,1)S(1)}, u32[]{:S(2)}, u32[]{:S(2)}) collective-permute-start(bf16[512,16]{1,0:T(8,128)(2,1)S(1)} %bitcast.154), channel_id=1, source_target_pairs={{0,64},{64,0},{1,65},{65,1},{2,66},{66,2},{3,67},{67,3},{4,68},{68... | collective-permute-start | bytes 49160 | tf_op jit(solution)/shard_map/ppermute | solution.py:82
  46.1 94.0 %all-gather.10.cloned.1.call-start = ((), (), s32[]{:S(2)}) async-start(), calls=%async_computation.12 | async-start | bytes 6635520 | tf_op jit(solution)/shard_map/all_gather | solution.py:561
  46.1 19.3 %collective-permute-start.7 = (bf16[96,3456]{1,0:T(8,128)(2,1)}, bf16[96,3456]{1,0:T(8,128)(2,1)S(1)}, u32[]{:S(2)}, u32[]{:S(2)}) collective-permute-start(bf16[96,3456]{1,0:T(8,128)(2,1)} %get-tuple-element.143), channel_id=1, source_target_pairs={{0,64},{32,96},{64,0},{96,32},{1,65},{33,97},{65,1},{97,33},{2,66}... | collective-permute-start | bytes 1990664 | tf_op jit(solution)/shard_map/ppermute | solution.py:82
  46.9 32.0 %collective-permute-start.8 = (bf16[96,3456]{1,0:T(8,128)(2,1)}, bf16[96,3456]{1,0:T(8,128)(2,1)S(1)}, u32[]{:S(2)}, u32[]{:S(2)}) collective-permute-start(bf16[96,3456]{1,0:T(8,128)(2,1)} %get-tuple-element.143), channel_id=1, source_target_pairs={{0,96},{32,64},{64,32},{96,0},{1,97},{33,65},{65,33},{97,1},{2,98}... | collective-permute-start | bytes 1990664 | tf_op jit(solution)/shard_map/ppermute | solution.py:82
  48.9 29.9 %collective-permute-start.9 = (bf16[96,3456]{1,0:T(8,128)(2,1)}, bf16[96,3456]{1,0:T(8,128)(2,1)}, u32[]{:S(2)}, u32[]{:S(2)}) collective-permute-start(bf16[96,3456]{1,0:T(8,128)(2,1)} %get-tuple-element.170), channel_id=1, source_target_pairs={{0,32},{32,0},{1,33},{33,1},{2,34},{34,2},{3,35},{35,3},{4,36},{36... | collective-permute-start | bytes 1990664 | tf_op jit(solution)/shard_map/ppermute | solution.py:82
  52.2 7.6 %collective-permute-start.10 = (bf16[64,1536]{1,0:T(8,128)(2,1)S(1)}, bf16[64,1536]{1,0:T(8,128)(2,1)S(1)}, u32[]{:S(2)}, u32[]{:S(2)}) collective-permute-start(bf16[64,1536]{1,0:T(8,128)(2,1)S(1)} %fusion.11.refs_0_.hidden), channel_id=1, source_target_pairs={{0,3},{1,0},{2,1},{3,2},{4,7},{5,4},{6,5},{7,6},{8,11},{9,8},{10,9... | collective-permute-start | bytes 589832 | tf_op jit(solution)/shard_map/ppermute | solution.py:82
  53.1 9.0 %collective-permute-start.11 = (bf16[64,1536]{1,0:T(8,128)(2,1)S(1)}, bf16[64,1536]{1,0:T(8,128)(2,1)S(1)}, u32[]{:S(2)}, u32[]{:S(2)}) collective-permute-start(bf16[64,1536]{1,0:T(8,128)(2,1)S(1)} %fusion.11.refs_0_.hidden), channel_id=1, source_target_pairs={{0,2},{1,3},{2,0},{3,1},{4,6},{5,7},{6,4},{7,5},{8,10},{9,11},{10,... | collective-permute-start | bytes 589832 | tf_op jit(solution)/shard_map/ppermute | solution.py:82
  91.2 22.7 %collective-permute-start.20 = (bf16[96,3456]{1,0:T(8,128)(2,1)}, bf16[96,3456]{1,0:T(8,128)(2,1)}, u32[]{:S(2)}, u32[]{:S(2)}) collective-permute-start(bf16[96,3456]{1,0:T(8,128)(2,1)} %get-tuple-element.170), channel_id=1, source_target_pairs={{64,96},{96,64},{65,97},{97,65},{66,98},{98,66},{67,99},{99,67},{6... | collective-permute-start | bytes 1990664 | tf_op jit(solution)/shard_map/ppermute | solution.py:82
  92.7 7.7 %collective-permute-start.17 = (bf16[64,1536]{1,0:T(8,128)(2,1)S(1)}, bf16[64,1536]{1,0:T(8,128)(2,1)S(1)}, u32[]{:S(2)}, u32[]{:S(2)}) collective-permute-start(bf16[64,1536]{1,0:T(8,128)(2,1)S(1)} %get-tuple-element.165), channel_id=1, source_target_pairs={{0,1},{1,2},{2,3},{3,0},{4,5},{5,6},{6,7},{7,4},{8,9},{9,10},{10,1... | collective-permute-start | bytes 589832 | tf_op jit(solution)/shard_map/ppermute | solution.py:82
  93.5 9.3 %collective-permute-start.18 = (bf16[64,1536]{1,0:T(8,128)(2,1)S(1)}, bf16[64,1536]{1,0:T(8,128)(2,1)S(1)}, u32[]{:S(2)}, u32[]{:S(2)}) collective-permute-start(bf16[64,1536]{1,0:T(8,128)(2,1)S(1)} %get-tuple-element.166), channel_id=1, source_target_pairs={{0,2},{1,3},{2,0},{3,1},{4,6},{5,7},{6,4},{7,5},{8,10},{9,11},{10,... | collective-permute-start | bytes 589832 | tf_op jit(solution)/shard_map/ppermute | solution.py:82
  96.4 9.5 %collective-permute-start.19 = (bf16[64,1536]{1,0:T(8,128)(2,1)S(1)}, bf16[64,1536]{1,0:T(8,128)(2,1)S(1)}, u32[]{:S(2)}, u32[]{:S(2)}) collective-permute-start(bf16[64,1536]{1,0:T(8,128)(2,1)S(1)} %get-tuple-element.167), channel_id=1, source_target_pairs={{0,3},{1,0},{2,1},{3,2},{4,7},{5,4},{6,5},{7,6},{8,11},{9,8},{10,9... | collective-permute-start | bytes 589832 | tf_op jit(solution)/shard_map/ppermute | solution.py:82
  108.0 24.9 %all-to-all-start = ((bf16[8,64,1536]{2,1,0:T(8,128)(2,1)}), bf16[8,64,1536]{2,1,0:T(8,128)(2,1)S(1)}, u32[]{:S(2)}, u32[]{:S(2)}) async-start(bf16[8,64,1536]{2,1,0:T(8,128)(2,1)} %bitcast.146), calls=%async_computation | async-start | bytes 3145728 | tf_op jit(solution)/shard_map/all_to_all | solution.py:144
  113.9 74.2 %all-gather.12.cloned.1.call-start = ((), (), s32[]{:S(2)}) async-start(), calls=%async_computation.13 | async-start | bytes 1966080 | tf_op jit(solution)/shard_map/all_gather | solution.py:561
  140.2 88.4 %all-gather.14.cloned.1.call-start = ((), (), s32[]{:S(2)}) async-start(), calls=%async_computation.14 | async-start | bytes 6635520 | tf_op jit(solution)/shard_map/all_gather | solution.py:561
  140.2 9.2 %collective-permute-start.21 = (bf16[768,3456]{1,0:T(8,128)(2,1)}, bf16[768,3456]{1,0:T(8,128)(2,1)}, u32[]{:S(2)}, u32[]{:S(2)}) collective-permute-start(bf16[768,3456]{1,0:T(8,128)(2,1)} %all-gather.10.cloned.1.call-done.up0.down0), channel_id=1, source_target_pairs={{0,4},{4,0},{1,5},{5,1},{2,6},{6,2},{3,7},{7,3},{8,12},{12,8},{9,1... | collective-permute-start | bytes 15925256 | tf_op jit(solution)/shard_map/ppermute | solution.py:82
  188.2 13.4 %collective-permute-start.25 = (bf16[768,1024]{1,0:T(8,128)(2,1)}, bf16[768,1024]{1,0:T(8,128)(2,1)S(1)}, u32[]{:S(2)}, u32[]{:S(2)}) collective-permute-start(bf16[768,1024]{1,0:T(8,128)(2,1)} %all-gather.12.cloned.1.call-done.refs_5_.refs_4_), channel_id=1, source_target_pairs={{0,4},{4,0},{1,5},{5,1},{2,6},{6,2},{3,7},{7,3},{8,12},{12,8},{9,1... | collective-permute-start | bytes 4718600 | tf_op jit(solution)/shard_map/ppermute | solution.py:82
  188.2 7.6 %collective-permute-start.22 = (bf16[64,1536]{1,0:T(8,128)(2,1)S(1)}, bf16[64,1536]{1,0:T(8,128)(2,1)S(1)}, u32[]{:S(2)}, u32[]{:S(2)}) collective-permute-start(bf16[64,1536]{1,0:T(8,128)(2,1)S(1)} %get-tuple-element.180.refs_0_.hidden), channel_id=1, source_target_pairs={{0,3},{1,0},{2,1},{3,2},{4,7},{5,4},{6,5},{7,6},{8,11},{9,8},{10,9... | collective-permute-start | bytes 589832 | tf_op jit(solution)/shard_map/ppermute | solution.py:82
  190.0 9.8 %collective-permute-start.23 = (bf16[64,1536]{1,0:T(8,128)(2,1)S(1)}, bf16[64,1536]{1,0:T(8,128)(2,1)S(1)}, u32[]{:S(2)}, u32[]{:S(2)}) collective-permute-start(bf16[64,1536]{1,0:T(8,128)(2,1)S(1)} %get-tuple-element.180.refs_0_.hidden), channel_id=1, source_target_pairs={{0,2},{1,3},{2,0},{3,1},{4,6},{5,7},{6,4},{7,5},{8,10},{9,11},{10,... | collective-permute-start | bytes 589832 | tf_op jit(solution)/shard_map/ppermute | solution.py:82
  190.3 11.2 %collective-permute-start.24 = (bf16[64,1536]{1,0:T(8,128)(2,1)S(1)}, bf16[64,1536]{1,0:T(8,128)(2,1)S(1)}, u32[]{:S(2)}, u32[]{:S(2)}) collective-permute-start(bf16[64,1536]{1,0:T(8,128)(2,1)S(1)} %get-tuple-element.180.refs_0_.hidden), channel_id=1, source_target_pairs={{0,1},{1,2},{2,3},{3,0},{4,5},{5,6},{6,7},{7,4},{8,9},{9,10},{10,1... | collective-permute-start | bytes 589832 | tf_op jit(solution)/shard_map/ppermute | solution.py:82
  206.6 7.7 %collective-permute-start.26 = (bf16[64,1536]{1,0:T(8,128)(2,1)S(1)}, bf16[64,1536]{1,0:T(8,128)(2,1)S(1)}, u32[]{:S(2)}, u32[]{:S(2)}) collective-permute-start(bf16[64,1536]{1,0:T(8,128)(2,1)S(1)} %get-tuple-element.183), channel_id=1, source_target_pairs={{0,1},{1,2},{2,3},{3,0},{4,5},{5,6},{6,7},{7,4},{8,9},{9,10},{10,1... | collective-permute-start | bytes 589832 | tf_op jit(solution)/shard_map/ppermute | solution.py:82
  208.0 9.3 %collective-permute-start.27 = (bf16[64,1536]{1,0:T(8,128)(2,1)S(1)}, bf16[64,1536]{1,0:T(8,128)(2,1)S(1)}, u32[]{:S(2)}, u32[]{:S(2)}) collective-permute-start(bf16[64,1536]{1,0:T(8,128)(2,1)S(1)} %get-tuple-element.184), channel_id=1, source_target_pairs={{0,2},{1,3},{2,0},{3,1},{4,6},{5,7},{6,4},{7,5},{8,10},{9,11},{10,... | collective-permute-start | bytes 589832 | tf_op jit(solution)/shard_map/ppermute | solution.py:82
  210.7 9.7 %collective-permute-start.28 = (bf16[64,1536]{1,0:T(8,128)(2,1)S(1)}, bf16[64,1536]{1,0:T(8,128)(2,1)S(1)}, u32[]{:S(2)}, u32[]{:S(2)}) collective-permute-start(bf16[64,1536]{1,0:T(8,128)(2,1)S(1)} %get-tuple-element.185), channel_id=1, source_target_pairs={{0,3},{1,0},{2,1},{3,2},{4,7},{5,4},{6,5},{7,6},{8,11},{9,8},{10,9... | collective-permute-start | bytes 589832 | tf_op jit(solution)/shard_map/ppermute | solution.py:82
  228.6 25.8 %collective-permute-start.29 = (bf16[768,3456]{1,0:T(8,128)(2,1)}, bf16[768,3456]{1,0:T(8,128)(2,1)}, u32[]{:S(2)}, u32[]{:S(2)}) collective-permute-start(bf16[768,3456]{1,0:T(8,128)(2,1)} %all-gather.14.cloned.1.call-done.up0.down0), channel_id=1, source_target_pairs={{0,4},{4,0},{1,5},{5,1},{2,6},{6,2},{3,7},{7,3},{8,12},{12,8},{9,1... | collective-permute-start | bytes 15925256 | tf_op jit(solution)/shard_map/ppermute | solution.py:82
  228.6 25.8 %all-to-all-start.2 = ((bf16[8,64,1536]{2,1,0:T(8,128)(2,1)}), bf16[8,64,1536]{2,1,0:T(8,128)(2,1)S(1)}, u32[]{:S(2)}, u32[]{:S(2)}) async-start(bf16[8,64,1536]{2,1,0:T(8,128)(2,1)} %bitcast.145), calls=%async_computation.2 | async-start | bytes 3145728 | tf_op jit(solution)/shard_map/all_to_all | solution.py:144
  234.4 135.2 %reduce-scatter.5.cloned.1.call-start = ((), (), s32[]{:S(2)}) async-start(), calls=%async_computation.15 | async-start | bytes 1769472 | tf_op jit(solution)/shard_map/reduce_scatter | solution.py:708
  285.2 9.1 %collective-permute-start.31 = (bf16[768,3456]{1,0:T(8,128)(2,1)}, bf16[768,3456]{1,0:T(8,128)(2,1)}, u32[]{:S(2)}, u32[]{:S(2)}) collective-permute-start(bf16[768,3456]{1,0:T(8,128)(2,1)} %shard_map.247), channel_id=1, source_target_pairs={{0,4},{4,0},{1,5},{5,1},{2,6},{6,2},{3,7},{7,3},{8,12},{12,8},{9,1... | collective-permute-start | bytes 15925256 | tf_op jit(solution)/shard_map/ppermute | solution.py:82
  285.2 33.0 %all-to-all-start.3 = ((bf16[8,64,1664]{2,1,0:T(8,128)(2,1)}), bf16[8,64,1664]{2,1,0:T(8,128)(2,1)}, u32[]{:S(2)}, u32[]{:S(2)}) async-start(bf16[8,64,1664]{2,1,0:T(8,128)(2,1)} %bitcast.142), calls=%async_computation.4 | async-start | bytes 3407872 | tf_op jit(solution)/shard_map/all_to_all | solution.py:144
  290.6 143.7 %reduce-scatter.7.cloned.1.call-start = ((), (), s32[]{:S(2)}) async-start(), calls=%async_computation.16 | async-start | bytes 6635520 | tf_op jit(solution)/shard_map/reduce_scatter | solution.py:557
  322.2 10.3 %collective-permute-start.32 = (bf16[64,1536]{1,0:T(8,128)(2,1)S(1)}, bf16[64,1536]{1,0:T(8,128)(2,1)S(1)}, u32[]{:S(2)}, u32[]{:S(2)}) collective-permute-start(bf16[64,1536]{1,0:T(8,128)(2,1)S(1)} %get-tuple-element.205.refs_0_), channel_id=1, source_target_pairs={{0,3},{1,0},{2,1},{3,2},{4,7},{5,4},{6,5},{7,6},{8,11},{9,8},{10,9... | collective-permute-start | bytes 589832 | tf_op jit(solution)/shard_map/ppermute | solution.py:82
  322.2 16.7 %collective-permute-start.33 = (bf16[64,1536]{1,0:T(8,128)(2,1)S(1)}, bf16[64,1536]{1,0:T(8,128)(2,1)S(1)}, u32[]{:S(2)}, u32[]{:S(2)}) collective-permute-start(bf16[64,1536]{1,0:T(8,128)(2,1)S(1)} %get-tuple-element.205.refs_0_), channel_id=1, source_target_pairs={{0,2},{1,3},{2,0},{3,1},{4,6},{5,7},{6,4},{7,5},{8,10},{9,11},{10,... | collective-permute-start | bytes 589832 | tf_op jit(solution)/shard_map/ppermute | solution.py:82
  326.2 13.6 %collective-permute-start.34 = (bf16[64,1536]{1,0:T(8,128)(2,1)S(1)}, bf16[64,1536]{1,0:T(8,128)(2,1)S(1)}, u32[]{:S(2)}, u32[]{:S(2)}) collective-permute-start(bf16[64,1536]{1,0:T(8,128)(2,1)S(1)} %get-tuple-element.205.refs_0_), channel_id=1, source_target_pairs={{0,1},{1,2},{2,3},{3,0},{4,5},{5,6},{6,7},{7,4},{8,9},{9,10},{10,1... | collective-permute-start | bytes 589832 | tf_op jit(solution)/shard_map/ppermute | solution.py:82
  346.4 23.2 %collective-permute-start.38 = (bf16[768,1024]{1,0:T(8,128)(2,1)}, bf16[768,1024]{1,0:T(8,128)(2,1)}, u32[]{:S(2)}, u32[]{:S(2)}) collective-permute-start(bf16[768,1024]{1,0:T(8,128)(2,1)} %shard_map.251), channel_id=1, source_target_pairs={{0,4},{4,0},{1,5},{5,1},{2,6},{6,2},{3,7},{7,3},{8,12},{12,8},{9,1... | collective-permute-start | bytes 4718600 | tf_op jit(solution)/shard_map/ppermute | solution.py:82
  346.4 7.8 %collective-permute-start.35 = (bf16[64,1536]{1,0:T(8,128)(2,1)S(1)}, bf16[64,1536]{1,0:T(8,128)(2,1)S(1)}, u32[]{:S(2)}, u32[]{:S(2)}) collective-permute-start(bf16[64,1536]{1,0:T(8,128)(2,1)S(1)} %get-tuple-element.209), channel_id=1, source_target_pairs={{0,1},{1,2},{2,3},{3,0},{4,5},{5,6},{6,7},{7,4},{8,9},{9,10},{10,1... | collective-permute-start | bytes 589832 | tf_op jit(solution)/shard_map/ppermute | solution.py:82
  346.9 9.3 %collective-permute-start.36 = (bf16[64,1536]{1,0:T(8,128)(2,1)S(1)}, bf16[64,1536]{1,0:T(8,128)(2,1)S(1)}, u32[]{:S(2)}, u32[]{:S(2)}) collective-permute-start(bf16[64,1536]{1,0:T(8,128)(2,1)S(1)} %get-tuple-element.210), channel_id=1, source_target_pairs={{0,2},{1,3},{2,0},{3,1},{4,6},{5,7},{6,4},{7,5},{8,10},{9,11},{10,... | collective-permute-start | bytes 589832 | tf_op jit(solution)/shard_map/ppermute | solution.py:82
  350.5 9.4 %collective-permute-start.37 = (bf16[64,1536]{1,0:T(8,128)(2,1)S(1)}, bf16[64,1536]{1,0:T(8,128)(2,1)S(1)}, u32[]{:S(2)}, u32[]{:S(2)}) collective-permute-start(bf16[64,1536]{1,0:T(8,128)(2,1)S(1)} %get-tuple-element.211), channel_id=1, source_target_pairs={{0,3},{1,0},{2,1},{3,2},{4,7},{5,4},{6,5},{7,6},{8,11},{9,8},{10,9... | collective-permute-start | bytes 589832 | tf_op jit(solution)/shard_map/ppermute | solution.py:82
  363.4 25.3 %all-to-all-start.4 = ((bf16[8,64,1536]{2,1,0:T(8,128)(2,1)}), bf16[8,64,1536]{2,1,0:T(8,128)(2,1)S(1)}, u32[]{:S(2)}, u32[]{:S(2)}) async-start(bf16[8,64,1536]{2,1,0:T(8,128)(2,1)} %bitcast.144), calls=%async_computation.5 | async-start | bytes 3145728 | tf_op jit(solution)/shard_map/all_to_all | solution.py:144
  369.4 115.2 %reduce-scatter.11.cloned.1.call-start = ((), (), s32[]{:S(2)}) async-start(), calls=%async_computation.18 | async-start | bytes 1966080 | tf_op jit(solution)/shard_map/reduce_scatter | solution.py:557
  407.1 9.1 %collective-permute-start.39 = (bf16[768,3456]{1,0:T(8,128)(2,1)}, bf16[768,3456]{1,0:T(8,128)(2,1)}, u32[]{:S(2)}, u32[]{:S(2)}) collective-permute-start(bf16[768,3456]{1,0:T(8,128)(2,1)} %shard_map.255), channel_id=1, source_target_pairs={{0,4},{4,0},{1,5},{5,1},{2,6},{6,2},{3,7},{7,3},{8,12},{12,8},{9,1... | collective-permute-start | bytes 15925256 | tf_op jit(solution)/shard_map/ppermute | solution.py:82
  407.2 27.1 %all-to-all-start.5 = ((bf16[8,64,1664]{2,1,0:T(8,128)(2,1)}), bf16[8,64,1664]{2,1,0:T(8,128)(2,1)}, u32[]{:S(2)}, u32[]{:S(2)}) async-start(bf16[8,64,1664]{2,1,0:T(8,128)(2,1)} %bitcast.143), calls=%async_computation.6 | async-start | bytes 3407872 | tf_op jit(solution)/shard_map/all_to_all | solution.py:144
  412.6 95.8 %reduce-scatter.9.cloned.1.call-start = ((), (), s32[]{:S(2)}) async-start(), calls=%async_computation.17 | async-start | bytes 6635520 | tf_op jit(solution)/shard_map/reduce_scatter | solution.py:557
  437.7 7.4 %collective-permute-start.40 = (bf16[64,1536]{1,0:T(8,128)(2,1)S(1)}, bf16[64,1536]{1,0:T(8,128)(2,1)S(1)}, u32[]{:S(2)}, u32[]{:S(2)}) collective-permute-start(bf16[64,1536]{1,0:T(8,128)(2,1)S(1)} %get-tuple-element.231.refs_0_), channel_id=1, source_target_pairs={{0,3},{1,0},{2,1},{3,2},{4,7},{5,4},{6,5},{7,6},{8,11},{9,8},{10,9... | collective-permute-start | bytes 589832 | tf_op jit(solution)/shard_map/ppermute | solution.py:82
  438.8 10.0 %collective-permute-start.41 = (bf16[64,1536]{1,0:T(8,128)(2,1)S(1)}, bf16[64,1536]{1,0:T(8,128)(2,1)S(1)}, u32[]{:S(2)}, u32[]{:S(2)}) collective-permute-start(bf16[64,1536]{1,0:T(8,128)(2,1)S(1)} %get-tuple-element.231.refs_0_), channel_id=1, source_target_pairs={{0,2},{1,3},{2,0},{3,1},{4,6},{5,7},{6,4},{7,5},{8,10},{9,11},{10,... | collective-permute-start | bytes 589832 | tf_op jit(solution)/shard_map/ppermute | solution.py:82
  440.1 10.1 %collective-permute-start.42 = (bf16[64,1536]{1,0:T(8,128)(2,1)S(1)}, bf16[64,1536]{1,0:T(8,128)(2,1)S(1)}, u32[]{:S(2)}, u32[]{:S(2)}) collective-permute-start(bf16[64,1536]{1,0:T(8,128)(2,1)S(1)} %get-tuple-element.231.refs_0_), channel_id=1, source_target_pairs={{0,1},{1,2},{2,3},{3,0},{4,5},{5,6},{6,7},{7,4},{8,9},{9,10},{10,1... | collective-permute-start | bytes 589832 | tf_op jit(solution)/shard_map/ppermute | solution.py:82
  455.2 9.1 %collective-permute-start.43 = (bf16[64,1536]{1,0:T(8,128)(2,1)}, bf16[64,1536]{1,0:T(8,128)(2,1)S(1)}, u32[]{:S(2)}, u32[]{:S(2)}) collective-permute-start(bf16[64,1536]{1,0:T(8,128)(2,1)} %get-tuple-element.235), channel_id=1, source_target_pairs={{0,1},{1,2},{2,3},{3,0},{4,5},{5,6},{6,7},{7,4},{8,9},{9,10},{10,1... | collective-permute-start | bytes 589832 | tf_op jit(solution)/shard_map/ppermute | solution.py:82
  456.8 9.6 %collective-permute-start.44 = (bf16[64,1536]{1,0:T(8,128)(2,1)}, bf16[64,1536]{1,0:T(8,128)(2,1)}, u32[]{:S(2)}, u32[]{:S(2)}) collective-permute-start(bf16[64,1536]{1,0:T(8,128)(2,1)} %get-tuple-element.236), channel_id=1, source_target_pairs={{0,2},{1,3},{2,0},{3,1},{4,6},{5,7},{6,4},{7,5},{8,10},{9,11},{10,... | collective-permute-start | bytes 589832 | tf_op jit(solution)/shard_map/ppermute | solution.py:82
  459.9 9.8 %collective-permute-start.45 = (bf16[64,1536]{1,0:T(8,128)(2,1)}, bf16[64,1536]{1,0:T(8,128)(2,1)}, u32[]{:S(2)}, u32[]{:S(2)}) collective-permute-start(bf16[64,1536]{1,0:T(8,128)(2,1)} %get-tuple-element.237), channel_id=1, source_target_pairs={{0,3},{1,0},{2,1},{3,2},{4,7},{5,4},{6,5},{7,6},{8,11},{9,8},{10,9... | collective-permute-start | bytes 589832 | tf_op jit(solution)/shard_map/ppermute | solution.py:82
  477.1 21.7 %collective-permute-start.49 = (bf16[192,1152]{1,0:T(8,128)(2,1)S(1)}, bf16[192,1152]{1,0:T(8,128)(2,1)S(1)}, u32[]{:S(2)}, u32[]{:S(2)}) collective-permute-start(bf16[192,1152]{1,0:T(8,128)(2,1)S(1)} %get-tuple-element.314), channel_id=1, source_target_pairs={{0,8},{8,16},{16,24},{24,0},{1,9},{9,17},{17,25},{25,1},{2,10},{10... | collective-permute-start | bytes 1327112 | tf_op jit(solution)/shard_map/ppermute | solution.py:82
  478.1 30.3 %collective-permute-start.50 = (bf16[192,1152]{1,0:T(8,128)(2,1)S(1)}, bf16[192,1152]{1,0:T(8,128)(2,1)S(1)}, u32[]{:S(2)}, u32[]{:S(2)}) collective-permute-start(bf16[192,1152]{1,0:T(8,128)(2,1)S(1)} %get-tuple-element.313), channel_id=1, source_target_pairs={{0,16},{8,24},{16,0},{24,8},{1,17},{9,25},{17,1},{25,9},{2,18},{10... | collective-permute-start | bytes 1327112 | tf_op jit(solution)/shard_map/ppermute | solution.py:82
  479.6 28.9 %collective-permute-start.51 = (bf16[192,1152]{1,0:T(8,128)(2,1)S(1)}, bf16[192,1152]{1,0:T(8,128)(2,1)S(1)}, u32[]{:S(2)}, u32[]{:S(2)}) collective-permute-start(bf16[192,1152]{1,0:T(8,128)(2,1)S(1)} %get-tuple-element.312), channel_id=1, source_target_pairs={{0,24},{8,0},{16,8},{24,16},{1,25},{9,1},{17,9},{25,17},{2,26},{10... | collective-permute-start | bytes 1327112 | tf_op jit(solution)/shard_map/ppermute | solution.py:82
  482.8 32.6 %collective-permute-start.30 = (bf16[64,1536]{1,0:T(8,128)(2,1)}, bf16[64,1536]{1,0:T(8,128)(2,1)}, u32[]{:S(2)}, u32[]{:S(2)}) collective-permute-start(bf16[64,1536]{1,0:T(8,128)(2,1)} %get-tuple-element.325), channel_id=1, source_target_pairs={{0,64},{64,0},{1,65},{65,1},{2,66},{66,2},{3,67},{67,3},{4,68},{68... | collective-permute-start | bytes 589832 | tf_op jit(solution)/shard_map/ppermute | solution.py:82
  510.9 24.1 %collective-permute-start.52 = (bf16[96,4608]{1,0:T(8,128)(2,1)S(1)}, bf16[96,4608]{1,0:T(8,128)(2,1)S(1)}, u32[]{:S(2)}, u32[]{:S(2)}) collective-permute-start(bf16[96,4608]{1,0:T(8,128)(2,1)S(1)} %get-tuple-element.257), channel_id=1, source_target_pairs={{0,32},{32,0},{64,96},{96,64},{1,33},{33,1},{65,97},{97,65},{2,34}... | collective-permute-start | bytes 2654216 | tf_op jit(solution)/shard_map/ppermute | solution.py:82
  514.0 40.0 %collective-permute-start.53 = (bf16[96,4608]{1,0:T(8,128)(2,1)S(1)}, bf16[96,4608]{1,0:T(8,128)(2,1)S(1)}, u32[]{:S(2)}, u32[]{:S(2)}) collective-permute-start(bf16[96,4608]{1,0:T(8,128)(2,1)S(1)} %get-tuple-element.258), channel_id=1, source_target_pairs={{0,64},{32,96},{64,0},{96,32},{1,65},{33,97},{65,1},{97,33},{2,66}... | collective-permute-start | bytes 2654216 | tf_op jit(solution)/shard_map/ppermute | solution.py:82
  514.5 39.5 %collective-permute-start.54 = (bf16[96,4608]{1,0:T(8,128)(2,1)S(1)}, bf16[96,4608]{1,0:T(8,128)(2,1)S(1)}, u32[]{:S(2)}, u32[]{:S(2)}) collective-permute-start(bf16[96,4608]{1,0:T(8,128)(2,1)S(1)} %get-tuple-element.259), channel_id=1, source_target_pairs={{0,96},{32,64},{64,32},{96,0},{1,97},{33,65},{65,33},{97,1},{2,98}... | collective-permute-start | bytes 2654216 | tf_op jit(solution)/shard_map/ppermute | solution.py:82
  519.3 40.8 %collective-permute-start.47 = (bf16[64,1536]{1,0:T(8,128)(2,1)S(1)}, bf16[64,1536]{1,0:T(8,128)(2,1)S(1)}, u32[]{:S(2)}, u32[]{:S(2)}) collective-permute-start(bf16[64,1536]{1,0:T(8,128)(2,1)S(1)} %get-tuple-element.323), channel_id=1, source_target_pairs={{0,64},{64,0},{1,65},{65,1},{2,66},{66,2},{3,67},{67,3},{4,68},{68... | collective-permute-start | bytes 589832 | tf_op jit(solution)/shard_map/ppermute | solution.py:82
  555.3 8.9 %collective-permute-start.57 = (f32[24,128]{1,0:T(8,128)S(1)}, f32[24,128]{1,0:T(8,128)S(1)}, u32[]{:S(2)}, u32[]{:S(2)}) collective-permute-start(f32[24,128]{1,0:T(8,128)S(1)} %get-tuple-element.342), channel_id=1, source_target_pairs={{0,3},{1,0},{2,1},{3,2},{4,7},{5,4},{6,5},{7,6},{8,11},{9,8},{10,9... | collective-permute-start | bytes 36872 | tf_op jit(solution)/shard_map/ppermute | solution.py:82
  555.9 8.3 %collective-permute-start.56 = (f32[24,128]{1,0:T(8,128)S(1)}, f32[24,128]{1,0:T(8,128)S(1)}, u32[]{:S(2)}, u32[]{:S(2)}) collective-permute-start(f32[24,128]{1,0:T(8,128)S(1)} %get-tuple-element.341), channel_id=1, source_target_pairs={{0,2},{1,3},{2,0},{3,1},{4,6},{5,7},{6,4},{7,5},{8,10},{9,11},{10,... | collective-permute-start | bytes 36872 | tf_op jit(solution)/shard_map/ppermute | solution.py:82
  (86 other events, 939.6 us)
Sparse Core Ops, SparseCore 0:
  20.5 24.6 all-gather.5
  47.5 29.4 all-gather.7
  83.2 56.8 all-gather.9
  142.2 27.0 all-gather.11
  170.9 57.6 all-gather.13
  285.3 54.5 reduce-scatter.4
  342.3 55.3 reduce-scatter.6
  407.3 25.1 reduce-scatter.10
  435.0 65.9 reduce-scatter.8
